TPU v7x, 256 devices: a whole 4x4x8 slice. The times are simulated.
256 devices in a mesh: items: 64 (over z, y, core), rep: 4 (over x).
Axes of the slice: x: 4, y: 4, z: 8, core: 2. Of those that a mesh axis runs over, the one named last changes fastest.
Arguments:
- queries: bfloat16 [131072, 256], P(('items', 'rep')), may hold values from -60 to 60
- clusters: int32 [4096, 4], P(('items', 'rep')), may hold values from 0 to 63, all different within a row; in each aligned block of 16 rows (0 to 15, 16 to 31, ...) at most 2 rows name the same one
- positives: int32 [131072], P(('items', 'rep')), may hold values from 0 to 4095
- owner_of: int32 [64], replicated, may hold values from 0 to 63, each once
- table: float32 [64, 1024, 256], P('items'), may hold values from -1.2 to 1.2
- accum: float32 [64, 1024, 256], P('items'), may hold values from 0.1 to 10
Outputs:
- losses: float32 [131072], P(('items', 'rep'))
- query_grads: float32 [131072, 256], P(('items', 'rep'))
- new_table: float32 [64, 1024, 256], P('items')
- new_accum: float32 [64, 1024, 256], P('items')
Inputs may be any that keep to these rules, and one draw needn't show every extreme that they name: Each row names 4 different clusters; within the rows of one device no cluster is named more than 2 times. `owner_of`: each cluster has its own slot. `positives`: a candidate index of the query's block.
All inputs are finite; a program needn't handle non-finite values.
Results may differ from a plain program's by a relative error of at most 0.0045.
The roundings to bfloat16 on the way count: a program that leaves them out, or rounds other values in their place, can miss the bound.
Values may be sent and summed in bfloat16 or wider, within the bound.
No kernel may reach another device: no remote copies, remote signals or barrier semaphores. Data moves between devices by JAX's collectives and lax.ppermute only.
A program may use at most 128 MiB of HBM per device.

v0:
```python
import jax
import jax.numpy as jnp
from jax import lax
from jax.sharding import PartitionSpec as P

MOST = 2


def local(queries, clusters, positives, owner_of, table, accum):
    peer_count = lax.axis_size("items")
    local_rows, features = queries.shape
    block_count, picks = clusters.shape
    block_rows = local_rows // block_count
    cluster_items = table.shape[1]
    pair_count = block_count * picks
    flat_lists = clusters.reshape(pair_count)
    catalog_ids = jnp.arange(owner_of.shape[0], dtype=jnp.int32)
    lookup = flat_lists[:, None] == catalog_ids[None, :]
    destination = jnp.sum(jnp.where(lookup, owner_of[None, :], 0), axis=1)
    pair_ids = jnp.arange(pair_count, dtype=jnp.int32)
    earlier = (destination[:, None] == destination[None, :]) & (
        pair_ids[:, None] > pair_ids[None, :]
    )
    rank_in = jnp.sum(earlier.astype(jnp.int32), axis=1)
    lanes = MOST
    slot_of_pair = destination * MOST + rank_in
    slot_count = peer_count * lanes
    matches = slot_of_pair[None, :] == jnp.arange(slot_count, dtype=jnp.int32)[:, None]
    filled = jnp.any(matches, axis=1)
    source_pair = jnp.sum(jnp.where(matches, pair_ids[None, :], 0), axis=1)
    which_block = source_pair // picks
    which_pick = source_pair % picks
    query_blocks = queries.reshape(block_count, block_rows, features)
    send_rows = jnp.where(
        filled[:, None, None], query_blocks[which_block], jnp.zeros((), jnp.bfloat16)
    )
    target_blocks = positives.reshape(block_count, block_rows)
    chosen = target_blocks[which_block]
    inside = filled[:, None] & (chosen // cluster_items == which_pick[:, None])
    send_targets = jnp.where(inside, chosen - which_pick[:, None] * cluster_items, -1)
    rows_out = send_rows.reshape(peer_count, lanes, block_rows, features)
    targets_out = send_targets.reshape(peer_count, lanes, block_rows)
    got_rows, got_targets = (
        lax.all_to_all(rows_out, "items", split_axis=0, concat_axis=0, tiled=True),
        lax.all_to_all(targets_out, "items", split_axis=0, concat_axis=0, tiled=True),
    )
    total_rows = slot_count * block_rows
    span = 512
    steps_count = total_rows // span
    owner_rows = got_rows.reshape(steps_count, span, features)
    owner_targets = got_targets.reshape(steps_count, span)
    weights16 = table[0].astype(jnp.bfloat16)
    columns = jnp.arange(cluster_items, dtype=jnp.int32)

    def score_rows(rows):
        return lax.dot_general(
            rows, weights16, (((1,), (1,)), ((), ())), preferred_element_type=jnp.float32
        )

    def summarize(scores, targets):
        highest = jnp.max(scores, axis=1)
        mass = jnp.sum(jnp.exp(scores - highest[:, None]), axis=1)
        picked = jnp.sum(
            jnp.where(columns[None, :] == targets[:, None], scores, jnp.float32(0.0)), axis=1
        )
        return (highest, mass, picked)

    def first_keep(inputs):
        scores = score_rows(inputs[0])
        highest, mass, picked = summarize(scores, inputs[1])
        return (highest, mass, picked, scores)

    highest, mass, picked, stored = lax.map(first_keep, (owner_rows, owner_targets))

    def to_peers(values):
        return values.reshape(peer_count, lanes, block_rows)

    back_high, back_mass, back_pick = (
        lax.all_to_all(to_peers(highest), "items", split_axis=0, concat_axis=0, tiled=True),
        lax.all_to_all(to_peers(mass), "items", split_axis=0, concat_axis=0, tiled=True),
        lax.all_to_all(to_peers(picked), "items", split_axis=0, concat_axis=0, tiled=True),
    )

    def per_pair(values):
        return values.reshape(slot_count, block_rows)[slot_of_pair].reshape(
            block_count, picks, block_rows
        )

    pair_high = per_pair(back_high)
    pair_mass = per_pair(back_mass)
    pair_pick = per_pair(back_pick)
    block_high = jnp.max(pair_high, axis=1)
    block_mass = jnp.sum(pair_mass * jnp.exp(pair_high - block_high[:, None, :]), axis=1)
    block_lse = block_high + jnp.log(block_mass)
    losses = (block_lse - jnp.sum(pair_pick, axis=1)).reshape(local_rows)
    send_lse = jnp.where(filled[:, None], block_lse[which_block], jnp.float32(0.0))
    lse_out = send_lse.reshape(peer_count, lanes, block_rows)
    got_lse = lax.all_to_all(lse_out, "items", split_axis=0, concat_axis=0, tiled=True)
    owner_lse = got_lse.reshape(steps_count, span)

    def backward_rows(grads, rows, targets, lse_rows, scores):
        is_target = columns[None, :] == targets[:, None]
        coeffs = (jnp.exp(scores - lse_rows[:, None]) - is_target.astype(jnp.float32)).astype(
            jnp.bfloat16
        )
        grad_rows = jnp.dot(coeffs, weights16, preferred_element_type=jnp.float32)
        grads = grads + lax.dot_general(
            coeffs, rows, (((0,), (0,)), ((), ())), preferred_element_type=jnp.float32
        )
        return (grads, grad_rows)

    grad_start = jnp.zeros((cluster_items, features), jnp.float32)

    def second_keep(grads, inputs):
        return backward_rows(grads, inputs[0], inputs[1], inputs[2], inputs[3])

    item_grads, owner_grads = lax.scan(
        second_keep, grad_start, (owner_rows, owner_targets, owner_lse, stored)
    )
    grads_out = owner_grads.reshape(peer_count, lanes, block_rows, features)
    got_grads = lax.all_to_all(grads_out, "items", split_axis=0, concat_axis=0, tiled=True)
    pair_grads = got_grads.reshape(slot_count, block_rows, features)[slot_of_pair].reshape(
        block_count, picks, block_rows, features
    )
    query_grads = jnp.sum(pair_grads, axis=1).reshape(local_rows, features)
    summed = lax.psum(item_grads, "rep")
    new_accum = accum[0] + summed * summed
    new_table = table[0] - 0.5 * summed / jnp.sqrt(new_accum)
    return (losses, query_grads, new_table[None], new_accum[None])


def solution(mesh):
    placed = (
        P(("items", "rep"), None),
        P(("items", "rep"), None),
        P(("items", "rep")),
        P(),
        P("items", None, None),
        P("items", None, None),
    )
    return jax.shard_map(
        local,
        mesh=mesh,
        in_specs=placed,
        out_specs=(
            P(("items", "rep")),
            P(("items", "rep"), None),
            P("items", None, None),
            P("items", None, None),
        ),
        check_vma=False,
    )
```

profile of v0, /device:TPU:6, one launch (start us, length us, event | category | flops | bytes accessed | tf_op | source)
XLA Modules:
  0.0 345.6 jit_solution(2844988465353706585)
XLA Ops:
  12.0 12.1 %all-to-all-start.1 = ((s32[64,2,32]{2,1,0:T(2,128)}), s32[64,2,32]{2,1,0:T(2,128)S(1)}, u32[]{:S(2)}, u32[]{:S(2)}) async-start(s32[64,2,32]{2,1,0:T(2,128)} %and_select_fusion), calls=%async_computation.1 | async-start | bytes 131072 | tf_op jit(solution)/shard_map/all_to_all | solution.py:45
  26.3 7.8 %all-to-all-done.1 = s32[64,2,32]{2,1,0:T(2,128)S(1)} async-done(((s32[64,2,32]{2,1,0:T(2,128)}), s32[64,2,32]{2,1,0:T(2,128)S(1)}, u32[]{:S(2)}, u32[]{:S(2)}) %all-to-all-start.1) | async-done | bytes 16416 | tf_op jit(solution)/shard_map/all_to_all | solution.py:45
  34.1 5.6 %all-to-all-start = ((bf16[64,2,32,256]{3,2,1,0:T(8,128)(2,1)}), bf16[64,2,32,256]{3,2,1,0:T(8,128)(2,1)}, u32[]{:S(2)}, u32[]{:S(2)}) async-start(bf16[64,2,32,256]{3,2,1,0:T(8,128)(2,1)} %broadcast_select_fusion), calls=%async_computation | async-start | bytes 4194304 | tf_op jit(solution)/shard_map/all_to_all | solution.py:44
  39.9 51.0 %all-to-all-done = bf16[64,2,32,256]{3,2,1,0:T(8,128)(2,1)} async-done(((bf16[64,2,32,256]{3,2,1,0:T(8,128)(2,1)}), bf16[64,2,32,256]{3,2,1,0:T(8,128)(2,1)}, u32[]{:S(2)}, u32[]{:S(2)}) %all-to-all-start) | async-done | bytes 2097184 | tf_op jit(solution)/shard_map/all_to_all | solution.py:44
  90.9 32.9 %while.31 = (s32[]{:T(128)}, f32[8,512]{1,0:T(8,128)S(1)}, f32[8,512]{1,0:T(8,128)S(1)}, f32[8,512]{1,0:T(8,128)S(1)}, f32[8,512,1024]{2,1,0:T(8,128)}, /*index=...) while((s32[]{:T(128)}, f32[8,512]{1,0:T(8,128)S(1)}, ...), condition=%wide.region_8.9_spmd.clone, body=%wide.region_4.8_spmd.clone.sunk | while | flops 271579648 | bytes 9201797 | solution.py:73
  124.5 5.3 %all-to-all-start.4 = ((f32[64,2,32]{2,1,0:T(2,128)}), f32[64,2,32]{2,1,0:T(2,128)S(1)}, u32[]{:S(2)}, u32[]{:S(2)}) async-start(f32[64,2,32]{2,1,0:T(2,128)} %reshape.289), calls=%async_computation.4 | async-start | bytes 131072 | tf_op jit(solution)/shard_map/all_to_all | solution.py:81
  130.6 9.3 %all-to-all-done.4 = f32[64,2,32]{2,1,0:T(2,128)S(1)} async-done(((f32[64,2,32]{2,1,0:T(2,128)}), f32[64,2,32]{2,1,0:T(2,128)S(1)}, u32[]{:S(2)}, u32[]{:S(2)}) %all-to-all-start.4) | async-done | bytes 16416 | tf_op jit(solution)/shard_map/all_to_all | solution.py:81
  139.8 4.6 %all-to-all-start.2 = ((f32[64,2,32]{2,1,0:T(2,128)}), f32[64,2,32]{2,1,0:T(2,128)S(1)}, u32[]{:S(2)}, u32[]{:S(2)}) async-start(f32[64,2,32]{2,1,0:T(2,128)} %reshape.283), calls=%async_computation.2 | async-start | bytes 131072 | tf_op jit(solution)/shard_map/all_to_all | solution.py:79
  145.2 9.2 %all-to-all-done.2 = f32[64,2,32]{2,1,0:T(2,128)S(1)} async-done(((f32[64,2,32]{2,1,0:T(2,128)}), f32[64,2,32]{2,1,0:T(2,128)S(1)}, u32[]{:S(2)}, u32[]{:S(2)}) %all-to-all-start.2) | async-done | bytes 16416 | tf_op jit(solution)/shard_map/all_to_all | solution.py:79
  154.4 4.6 %all-to-all-start.3 = ((f32[64,2,32]{2,1,0:T(2,128)}), f32[64,2,32]{2,1,0:T(2,128)S(1)}, u32[]{:S(2)}, u32[]{:S(2)}) async-start(f32[64,2,32]{2,1,0:T(2,128)} %reshape.286), calls=%async_computation.3 | async-start | bytes 131072 | tf_op jit(solution)/shard_map/all_to_all | solution.py:80
  160.3 8.7 %all-to-all-done.3 = f32[64,2,32]{2,1,0:T(2,128)S(1)} async-done(((f32[64,2,32]{2,1,0:T(2,128)}), f32[64,2,32]{2,1,0:T(2,128)S(1)}, u32[]{:S(2)}, u32[]{:S(2)}) %all-to-all-start.3) | async-done | bytes 16416 | tf_op jit(solution)/shard_map/all_to_all | solution.py:80
  171.1 4.6 %all-to-all-start.5 = ((f32[64,2,32]{2,1,0:T(2,128)}), f32[64,2,32]{2,1,0:T(2,128)S(1)}, u32[]{:S(2)}, u32[]{:S(2)}) async-start(f32[64,2,32]{2,1,0:T(2,128)} %broadcast_select_fusion.1), calls=%async_computation.5 | async-start | bytes 131072 | tf_op jit(solution)/shard_map/all_to_all | solution.py:98
  175.8 9.9 %all-to-all-done.5 = f32[64,2,32]{2,1,0:T(2,128)S(1)} async-done(((f32[64,2,32]{2,1,0:T(2,128)}), f32[64,2,32]{2,1,0:T(2,128)S(1)}, u32[]{:S(2)}, u32[]{:S(2)}) %all-to-all-start.5) | async-done | bytes 16416 | tf_op jit(solution)/shard_map/all_to_all | solution.py:98
  185.8 46.0 %while.32 = (s32[]{:T(128)}, f32[1024,256]{1,0:T(8,128)S(1)}, f32[8,512,256]{2,1,0:T(8,128)}, f32[8,512,1024]{2,1,0:T(8,128)}, f32[8,512]{1,0:T(8,128)S(1)}, /*i...) while((s32[]{:T(128)}, f32[1024,256]{1,0:T(8,128)S(1)}, ...), condition=%wide.region_13.14_spmd.clone.clone, body=%wide.region_12.13_spmd.clone.clone.sunk | while | flops 542638080 | bytes 7621246 | solution.py:117
  185.9 2.6 convolution_add_fusion.2
  188.5 3.1 fusion.46
  191.6 2.6 convolution_add_fusion.2
  194.3 3.1 fusion.46
  200.0 3.1 fusion.46
  203.1 2.6 convolution_add_fusion.2
  205.8 3.1 fusion.46
  211.6 3.1 fusion.46
  214.6 2.6 convolution_add_fusion.2
  217.3 3.1 fusion.46
  220.4 2.6 convolution_add_fusion.2
  223.1 3.1 fusion.46
  228.8 3.1 fusion.46
  232.8 5.8 %all-to-all-start.6 = ((f32[64,2,32,256]{3,2,1,0:T(8,128)}), f32[64,2,32,256]{3,2,1,0:T(8,128)}, u32[]{:S(2)}, u32[]{:S(2)}) async-start(f32[64,2,32,256]{3,2,1,0:T(8,128)} %bitcast.111), calls=%async_computation.6 | async-start | bytes 8388608 | tf_op jit(solution)/shard_map/all_to_all | solution.py:121
  240.0 53.5 %all-reduce.2.cloned.1.call-done = f32[1024,256]{1,0:T(8,128)} async-done(((f32[1024,256]{1,0:T(8,128)}), f32[1024,256]{1,0:T(8,128)}) %all-reduce.2.cloned.1.call-update) | async-done | bytes 1048592 | tf_op jit(solution)/shard_map/psum | solution.py:126
  293.6 2.8 fusion.23
  296.4 38.5 %all-to-all-done.6 = f32[64,2,32,256]{3,2,1,0:T(8,128)} async-done(((f32[64,2,32,256]{3,2,1,0:T(8,128)}), f32[64,2,32,256]{3,2,1,0:T(8,128)}, u32[]{:S(2)}, u32[]{:S(2)}) %all-to-all-start.6) | async-done | bytes 4194336 | tf_op jit(solution)/shard_map/all_to_all | solution.py:121
  334.9 2.9 gather_fusion.6
  (128 shorter events, 56.8 us)
Async XLA Ops:
  7.2 16.9 %copy-start = (bf16[512,256]{1,0:T(8,128)(2,1)S(1)}, bf16[512,256]{1,0:T(8,128)(2,1)}, u32[]{:S(2)}) copy-start(bf16[512,256]{1,0:T(8,128)(2,1)} %param.10) | copy-start | bytes 786436
  12.0 22.1 %all-to-all-start.1 = ((s32[64,2,32]{2,1,0:T(2,128)}), s32[64,2,32]{2,1,0:T(2,128)S(1)}, u32[]{:S(2)}, u32[]{:S(2)}) async-start(s32[64,2,32]{2,1,0:T(2,128)} %and_select_fusion), calls=%async_computation.1 | async-start | bytes 131072 | tf_op jit(solution)/shard_map/all_to_all | solution.py:45
  26.3 13.4 %copy-start.1 = (f32[1,1024,256]{2,1,0:T(8,128)S(1)}, f32[1,1024,256]{2,1,0:T(8,128)}, u32[]{:S(2)}) copy-start(f32[1,1024,256]{2,1,0:T(8,128)} %param.14) | copy-start | bytes 3145732
  34.1 56.8 %all-to-all-start = ((bf16[64,2,32,256]{3,2,1,0:T(8,128)(2,1)}), bf16[64,2,32,256]{3,2,1,0:T(8,128)(2,1)}, u32[]{:S(2)}, u32[]{:S(2)}) async-start(bf16[64,2,32,256]{3,2,1,0:T(8,128)(2,1)} %broadcast_select_fusion), calls=%async_computation | async-start | bytes 4194304 | tf_op jit(solution)/shard_map/all_to_all | solution.py:44
  124.5 15.4 %all-to-all-start.4 = ((f32[64,2,32]{2,1,0:T(2,128)}), f32[64,2,32]{2,1,0:T(2,128)S(1)}, u32[]{:S(2)}, u32[]{:S(2)}) async-start(f32[64,2,32]{2,1,0:T(2,128)} %reshape.289), calls=%async_computation.4 | async-start | bytes 131072 | tf_op jit(solution)/shard_map/all_to_all | solution.py:81
  139.8 14.6 %all-to-all-start.2 = ((f32[64,2,32]{2,1,0:T(2,128)}), f32[64,2,32]{2,1,0:T(2,128)S(1)}, u32[]{:S(2)}, u32[]{:S(2)}) async-start(f32[64,2,32]{2,1,0:T(2,128)} %reshape.283), calls=%async_computation.2 | async-start | bytes 131072 | tf_op jit(solution)/shard_map/all_to_all | solution.py:79
  154.4 14.6 %all-to-all-start.3 = ((f32[64,2,32]{2,1,0:T(2,128)}), f32[64,2,32]{2,1,0:T(2,128)S(1)}, u32[]{:S(2)}, u32[]{:S(2)}) async-start(f32[64,2,32]{2,1,0:T(2,128)} %reshape.286), calls=%async_computation.3 | async-start | bytes 131072 | tf_op jit(solution)/shard_map/all_to_all | solution.py:80
  171.1 14.6 %all-to-all-start.5 = ((f32[64,2,32]{2,1,0:T(2,128)}), f32[64,2,32]{2,1,0:T(2,128)S(1)}, u32[]{:S(2)}, u32[]{:S(2)}) async-start(f32[64,2,32]{2,1,0:T(2,128)} %broadcast_select_fusion.1), calls=%async_computation.5 | async-start | bytes 131072 | tf_op jit(solution)/shard_map/all_to_all | solution.py:98
  231.9 1.0 copy-start.4
  232.8 60.7 %copy-start.2 = (f32[1,1024,256]{2,1,0:T(8,128)S(1)}, f32[1,1024,256]{2,1,0:T(8,128)}, u32[]{:S(2)}) copy-start(f32[1,1024,256]{2,1,0:T(8,128)} %param.14) | copy-start | bytes 3145732
  232.8 60.7 %copy-start.3 = (f32[1,1024,256]{2,1,0:T(8,128)S(1)}, f32[1,1024,256]{2,1,0:T(8,128)}, u32[]{:S(2)}) copy-start(f32[1,1024,256]{2,1,0:T(8,128)} %param.15) | copy-start | bytes 3145732
  232.8 102.0 %all-to-all-start.6 = ((f32[64,2,32,256]{3,2,1,0:T(8,128)}), f32[64,2,32,256]{3,2,1,0:T(8,128)}, u32[]{:S(2)}, u32[]{:S(2)}) async-start(f32[64,2,32,256]{3,2,1,0:T(8,128)} %bitcast.111), calls=%async_computation.6 | async-start | bytes 8388608 | tf_op jit(solution)/shard_map/all_to_all | solution.py:121
  238.6 54.9 %all-reduce.2.cloned.1.call-start = ((), (), s32[]{:S(2)}) async-start(), calls=%async_computation.7 | async-start | bytes 2097152 | tf_op jit(solution)/shard_map/psum | solution.py:126
Sparse Core Ops, SparseCore 0:
  242.4 51.1 all-reduce.1
where the time goes:
time: 347 us; the launch traced here: 346 us
  waiting for transfers between devices  189 us (54%)
  matrix products  57.8 us (17%)
  starting transfers between devices  42.7 us (12%)
  local copies, waits for them, and re-layouts  27 us (8%)
  other arithmetic  14.8 us (4%)
  between operations  14.3 us (4%)
    psum x1, waiting for transfers between devices, local(): summed = lax.psum(item_grads, 'rep')  53.5 us
    all_to_all x1, waiting for transfers between devices, local(): lax.all_to_all(rows_out, 'items', split_axis=0, concat_axis=0, tiled=True)  51 us
    all_to_all x1, waiting for transfers between devices, local(): lax.all_to_all(grads_out, 'items', split_axis=0, concat_axis=0, tiled=True)  38.5 us
    dot_general x8, matrix products, backward_rows(): grad_rows = jnp.dot(coeffs, weights16, preferred_element_type=jnp.float32)  24.6 us
    dot_general x8, matrix products, backward_rows(): lax.dot_general(coeffs, rows, (((0,), (0,)), ((), ())), preferred_element...  21.2 us
    dynamic_update_slice x32, local copies, waits for them, and re-layouts, local(): lax.map(first_keep, (owner_rows, owner_targets))  14.2 us
    all_to_all x1, starting transfers between devices, local(): lax.all_to_all(targets_out, 'items', split_axis=0, concat_axis=0, tiled=T...  12.1 us
    dot_general x8, matrix products, score_rows(): lax.dot_general(rows, weights16, (((1,), (1,)), ((), ())), preferred_elem...  12 us
  transfers between devices with their start and end apart: 8, of which 8 were waited for; matrix products, arithmetic and copies ran while one was open for 2% of the time, Pallas kernels for 0%

commit v1 on v0

v1 whole, which is shorter than its diff:
```python
import jax
import jax.numpy as jnp
from jax import lax
from jax.experimental import pallas as pl
from jax.experimental.pallas import tpu as pltpu
from jax.sharding import Mesh, PartitionSpec as P

MOST = 2
EMPTY = 1e30
NEAR = (0, 1, 7, 2)
FAR = (6, 3, 5, 4)
ORDER = NEAR + FAR
PLANE = ("y", "c")
F32 = jnp.float32
BF16 = jnp.bfloat16
NT = (((1,), (1,)), ((), ()))
TN = (((0,), (0,)), ((), ()))
TILE = 256


def shift(value, axis, step):
    size = lax.axis_size(axis)
    return lax.ppermute(value, axis, [(i, (i + step) % size) for i in range(size)])


def tile_ids(start, shape):
    return lax.broadcasted_iota(jnp.int32, shape, 0) + start


def forward_kernel(blk, q0, q1, q2, q3, t_ref, tgt_ref, p_ref, stat_ref, s_ref):
    step = pl.program_id(0)
    sources = (q0, q1, q2, q3)
    block_rows = q0.shape[1]
    for slot in range(8):
        b = blk[step * 8 + slot]
        p_ref[0, pl.ds(slot * block_rows, block_rows), :] = sources[slot // MOST][b]
    q = p_ref[0]
    items = t_ref.shape[1]
    width = q.shape[0]
    tgt = tgt_ref[0]
    high = jnp.full((8, width), -jnp.inf, F32)
    pick = jnp.zeros((8, width), F32)
    for start in range(0, items, TILE):
        s = lax.dot_general(t_ref[0, pl.ds(start, TILE), :], q, NT, preferred_element_type=F32)
        s_ref[pl.ds(start, TILE), :] = s
        high = jnp.maximum(high, jnp.max(s.reshape(TILE // 8, 8, width), axis=0))
        hit = jnp.where(tile_ids(start, s.shape) == tgt, s, 0.0)
        pick = pick + jnp.sum(hit.reshape(TILE // 8, 8, width), axis=0)
    top = jnp.max(high, axis=0, keepdims=True)
    mass = jnp.zeros((8, width), F32)
    for start in range(0, items, TILE):
        e = jnp.exp(s_ref[pl.ds(start, TILE), :] - top)
        mass = mass + jnp.sum(e.reshape(TILE // 8, 8, width), axis=0)
    stat_ref[0, 0:1, :] = top + jnp.log(jnp.sum(mass, axis=0, keepdims=True))
    stat_ref[0, 1:2, :] = jnp.sum(pick, axis=0, keepdims=True)


def forward(sources, blk, targets, tables):
    planes, items, features = tables.shape
    width = targets.shape[2]
    whole = pl.BlockSpec(sources[0].shape, lambda j, blk: (0, 0, 0))
    return pl.pallas_call(
        forward_kernel,
        grid_spec=pltpu.PrefetchScalarGridSpec(
            num_scalar_prefetch=1,
            grid=(planes,),
            in_specs=[whole] * 4
            + [
                pl.BlockSpec((1, items, features), lambda j, blk: (j, 0, 0)),
                pl.BlockSpec((1, 1, width), lambda j, blk: (j, 0, 0)),
            ],
            out_specs=[
                pl.BlockSpec((1, width, features), lambda j, blk: (j, 0, 0)),
                pl.BlockSpec((1, 2, width), lambda j, blk: (j, 0, 0)),
            ],
            scratch_shapes=[pltpu.VMEM((items, width), F32)],
        ),
        out_shape=[
            jax.ShapeDtypeStruct((planes, width, features), BF16),
            jax.ShapeDtypeStruct((planes, 2, width), F32),
        ],
        compiler_params=pltpu.CompilerParams(vmem_limit_bytes=24 << 20),
        cost_estimate=pl.CostEstimate(
            flops=2 * planes * width * items * features,
            bytes_accessed=planes * items * features * 2 + 3 * planes * width * features * 2,
            transcendentals=planes * width * items,
        ),
        name="forward",
    )(blk, *sources, tables, targets)


def query_kernel(blk, p_ref, t_ref, lse_ref, tgt_ref, g0, g1, g2, g3, c_ref, acc_ref):
    step = pl.program_id(0)

    @pl.when(step == 0)
    def _():
        acc_ref[...] = jnp.zeros_like(acc_ref)

    q = p_ref[0]
    lse = lse_ref[0]
    tgt = tgt_ref[0]
    items = t_ref.shape[1]
    for start in range(0, items, TILE):
        s = lax.dot_general(t_ref[0, pl.ds(start, TILE), :], q, NT, preferred_element_type=F32)
        e = jnp.exp(s - lse)
        c = jnp.where(tile_ids(start, s.shape) == tgt, e - 1.0, e)
        c_ref[pl.ds(start, TILE), :] = c.astype(BF16)
    g = lax.dot_general(c_ref[...], t_ref[0], TN, preferred_element_type=F32)
    block_rows = g0.shape[1]
    for slot in range(8):
        b = blk[step * 8 + slot]
        acc_ref[slot // MOST, b] += g[slot * block_rows:(slot + 1) * block_rows, :]

    @pl.when(step == pl.num_programs(0) - 1)
    def _():
        for i, out in enumerate((g0, g1, g2, g3)):
            out[...] = acc_ref[i].astype(BF16)


def query_parts(packed, blk, lse, targets, tables, blocks, block_rows):
    planes, items, features = tables.shape
    width = targets.shape[2]
    line = pl.BlockSpec((1, 1, width), lambda j, blk: (j, 0, 0))
    out = jax.ShapeDtypeStruct((blocks, block_rows, features), BF16)
    return pl.pallas_call(
        query_kernel,
        grid_spec=pltpu.PrefetchScalarGridSpec(
            num_scalar_prefetch=1,
            grid=(planes,),
            in_specs=[
                pl.BlockSpec((1, width, features), lambda j, blk: (j, 0, 0)),
                pl.BlockSpec((1, items, features), lambda j, blk: (j, 0, 0)),
                line,
                line,
            ],
            out_specs=[pl.BlockSpec(out.shape, lambda j, blk: (0, 0, 0))] * 4,
            scratch_shapes=[
                pltpu.VMEM((items, width), BF16),
                pltpu.VMEM((4, blocks, block_rows, features), F32),
            ],
        ),
        out_shape=[out] * 4,
        compiler_params=pltpu.CompilerParams(vmem_limit_bytes=24 << 20),
        cost_estimate=pl.CostEstimate(
            flops=4 * planes * width * items * features,
            bytes_accessed=planes * items * features * 2 + 2 * planes * width * features * 2,
            transcendentals=planes * width * items,
        ),
        name="query_parts",
    )(blk, packed, tables, lse, targets)


def item_kernel(x_ref, a_ref, b_ref, line_ref, t_ref, w_ref):
    step = pl.program_id(0)
    quarters = w_ref.shape[0]
    rows = w_ref.shape[1]
    mine = x_ref[0]
    pairs = []
    for i, ref in enumerate((a_ref, b_ref)):
        pairs.append((ref[0], line_ref[0, 2 * i:2 * i + 1, :], line_ref[0, 2 * i + 1:2 * i + 2, :]))
    for tile in range(quarters):
        total = None
        for q, lse, tgt in pairs:
            s = lax.dot_general(
                t_ref[pl.ds(tile * rows, rows), :], q, NT, preferred_element_type=F32
            )
            e = jnp.exp(s - lse)
            ids = tile_ids(tile * rows, s.shape)
            c = jnp.where(ids == tgt.astype(jnp.int32), e - 1.0, e).astype(BF16)
            part = jnp.dot(c, q, preferred_element_type=F32)
            total = part if total is None else total + part
        place = lax.rem(tile - mine + quarters, quarters)

        @pl.when(step == 0)
        def _():
            w_ref[place] = total

        @pl.when(step > 0)
        def _():
            w_ref[place] += total


def item_parts(mine, near, far, lines, table16, quarters):
    sources, width, features = near.shape
    items = table16.shape[0]
    return pl.pallas_call(
        item_kernel,
        grid_spec=pltpu.PrefetchScalarGridSpec(
            num_scalar_prefetch=1,
            grid=(sources,),
            in_specs=[
                pl.BlockSpec((1, width, features), lambda j, x: (j, 0, 0)),
                pl.BlockSpec((1, width, features), lambda j, x: (j, 0, 0)),
                pl.BlockSpec((1, 4, width), lambda j, x: (j, 0, 0)),
                pl.BlockSpec((items, features), lambda j, x: (0, 0)),
            ],
            out_specs=pl.BlockSpec((quarters, items // quarters, features), lambda j, x: (0, 0, 0)),
        ),
        out_shape=jax.ShapeDtypeStruct((quarters, items // quarters, features), F32),
        compiler_params=pltpu.CompilerParams(vmem_limit_bytes=24 << 20),
        cost_estimate=pl.CostEstimate(
            flops=8 * sources * width * items * features,
            bytes_accessed=4 * sources * width * features + items * features * 6,
            transcendentals=2 * sources * width * items,
        ),
        name="item_parts",
    )(mine, near, far, lines, table16)


def local(queries, clusters, positives, owner_of, table, accum):
    z_size = lax.axis_size("z")
    x_size = lax.axis_size("x")
    z = lax.axis_index("z")
    x = lax.axis_index("x")
    local_rows, features = queries.shape
    block_count, picks = clusters.shape
    block_rows = local_rows // block_count
    items = table.shape[1]
    owners = owner_of.shape[0]
    plane = owners // z_size
    pair_count = block_count * picks

    table16 = table[0].astype(BF16)
    tables = lax.all_gather(table16, PLANE)

    here = queries.reshape(block_count, block_rows, features)
    half = block_count // 2
    right = [here]
    left = [here]
    for _ in range(3):
        right.append(shift(right[-1], "z", 1))
        left.append(shift(left[-1], "z", -1))
    opposite = jnp.concatenate(
        [shift(right[3][:half], "z", 1), shift(left[3][half:], "z", -1)], axis=0
    )
    by_source = {0: here, 4: opposite}
    for hop in range(1, 4):
        by_source[z_size - hop] = right[hop]
        by_source[hop] = left[hop]

    flat_lists = clusters.reshape(pair_count)
    catalog_ids = jnp.arange(owners, dtype=jnp.int32)
    lookup = flat_lists[:, None] == catalog_ids[None, :]
    destination = jnp.sum(jnp.where(lookup, owner_of[None, :], 0), axis=1)
    pair_ids = jnp.arange(pair_count, dtype=jnp.int32)
    earlier = (destination[:, None] == destination[None, :]) & (
        pair_ids[:, None] > pair_ids[None, :]
    )
    rank_in = jnp.sum(earlier.astype(jnp.int32), axis=1)
    slot_of_pair = destination * MOST + rank_in
    slot_count = owners * MOST
    matches = slot_of_pair[None, :] == jnp.arange(slot_count, dtype=jnp.int32)[:, None]
    filled = jnp.any(matches, axis=1)
    source_pair = jnp.sum(jnp.where(matches, pair_ids[None, :], 0), axis=1)
    which_block = source_pair // picks
    which_pick = source_pair % picks
    chosen = positives.reshape(block_count, block_rows)[which_block]
    inside = filled[:, None] & (chosen // items == which_pick[:, None])
    send_targets = jnp.where(inside, chosen - which_pick[:, None] * items, -1)
    meta = jnp.concatenate([send_targets, which_block[:, None]], axis=1)
    per_plane = plane * MOST
    got_meta = lax.all_to_all(
        meta.reshape(z_size, per_plane, block_rows + 1), "z", 0, 0, tiled=True
    )
    order = jnp.array(ORDER, jnp.int32)
    arrive = (z + order) % z_size
    place_of = [ORDER.index(d) for d in range(z_size)]
    leave = jnp.array(place_of, jnp.int32)[(jnp.arange(z_size) - z) % z_size]

    def to_slots(values):
        ordered = values[arrive].reshape(2, 4, plane, MOST, -1)
        return ordered.transpose(0, 2, 1, 3, 4)

    slots = to_slots(got_meta)
    width = 4 * MOST * block_rows
    targets = slots[..., :block_rows].reshape(2, plane, 1, width)
    blk = slots[..., block_rows].reshape(2, plane * 4 * MOST)

    near_q = [by_source[d] for d in NEAR]
    far_q = [by_source[d] for d in FAR]
    near_packed, near_stat = forward(near_q, blk[0], targets[0], tables)
    near_rows = lax.all_to_all(near_packed, PLANE, 0, 0, tiled=True)
    far_packed, far_stat = forward(far_q, blk[1], targets[1], tables)
    far_rows = lax.all_to_all(far_packed, PLANE, 0, 0, tiled=True)

    stats = jnp.stack([near_stat, far_stat]).reshape(2, plane, 2, 4, MOST, block_rows)
    stats = stats.transpose(0, 3, 1, 4, 2, 5).reshape(z_size, per_plane * 2 * block_rows)
    home = lax.all_to_all(stats[leave], "z", 0, 0, tiled=True)
    pair_stats = home.reshape(slot_count, 2 * block_rows)[slot_of_pair].reshape(
        block_count, picks, 2, block_rows
    )
    part = pair_stats[:, :, 0]
    top = jnp.max(part, axis=1)
    lse = top + jnp.log(jnp.sum(jnp.exp(part - top[:, None]), axis=1))
    losses = (lse - jnp.sum(pair_stats[:, :, 1], axis=1)).reshape(local_rows)
    slot_lse = jnp.where(filled[:, None], lse[which_block], F32(EMPTY))
    got_lse = lax.all_to_all(
        slot_lse.reshape(z_size, per_plane, block_rows), "z", 0, 0, tiled=True
    )
    lse_lines = to_slots(got_lse).reshape(2, plane, 1, width)
    lines = jnp.concatenate(
        [lse_lines[0], targets[0].astype(F32), lse_lines[1], targets[1].astype(F32)], axis=1
    )
    got_lines = lax.all_to_all(lines, PLANE, 0, 0, tiled=True)

    far_g = query_parts(
        far_packed, blk[1], lse_lines[1], targets[1], tables, block_count, block_rows
    )
    near_g = query_parts(
        near_packed, blk[0], lse_lines[0], targets[0], tables, block_count, block_rows
    )
    grads = dict(zip(ORDER, list(near_g) + list(far_g)))

    def add(a, b):
        return (a.astype(F32) + b.astype(F32)).astype(BF16)

    go_right = shift(grads[4][:half], "z", 1)
    go_left = shift(grads[4][half:], "z", -1)
    go_right = jnp.concatenate([add(go_right, grads[3][:half]), grads[3][half:]], axis=0)
    go_left = jnp.concatenate([grads[5][:half], add(go_left, grads[5][half:])], axis=0)
    for hop in (2, 1):
        go_right = add(shift(go_right, "z", 1), grads[hop])
        go_left = add(shift(go_left, "z", -1), grads[z_size - hop])
    go_right = shift(go_right, "z", 1)
    go_left = shift(go_left, "z", -1)
    query_grads = (
        grads[0].astype(F32) + go_right.astype(F32) + go_left.astype(F32)
    ).reshape(local_rows, features)

    parts = item_parts(x.reshape(1), near_rows, far_rows, got_lines, table16, x_size)
    summed = parts[0]
    for hop in range(1, x_size):
        summed = summed + shift(parts[hop], "x", hop)
    all_sums = jnp.stack([summed] + [shift(summed, "x", -hop) for hop in range(1, x_size)])
    summed = all_sums[(jnp.arange(x_size) - x) % x_size].reshape(items, features)
    new_accum = accum[0] + summed * summed
    new_table = table[0] - 0.5 * summed / jnp.sqrt(new_accum)
    return (losses, query_grads, new_table[None], new_accum[None])


def solution(mesh):
    axes = ("z", "y", "c", "x")
    split = Mesh(mesh.devices.reshape(8, 4, 2, 4), axes)
    placed = (
        P(axes, None),
        P(axes, None),
        P(axes),
        P(),
        P(axes[:3], None, None),
        P(axes[:3], None, None),
    )
    return jax.shard_map(
        local,
        mesh=split,
        in_specs=placed,
        out_specs=(
            P(axes),
            P(axes, None),
            P(axes[:3], None, None),
            P(axes[:3], None, None),
        ),
        check_vma=False,
    )
```

time: 347 us -> 221 us (0.64)
  waiting for transfers between devices: 189 us -> 54.2 us
  matrix products: 57.8 us -> 0 us
  Pallas kernels: 0 us -> 43.1 us
  starting transfers between devices: 42.7 us -> 63 us
  other arithmetic: 14.8 us -> 20.2 us
    all_to_all x7 -> x6, waiting for transfers between devices: 134 us -> 21.3 us  [the longest x1 8.02 us: local(): home = lax.all_to_all(stats[leave], 'z', 0, 0, tiled=True)]
    dot_general x24 -> x0, matrix products: 57.8 us -> none  [the longest x8 24.6 us: backward_rows(): grad_rows = jnp.dot(coeffs, weights16, preferred_element_type=jnp.float32)]
    psum x1 -> x0, waiting for transfers between devices: 53.5 us -> none  [local(): summed = lax.psum(item_grads, 'rep')]
    pallas_call x0 -> x5, Pallas kernels: none -> 43.1 us  [the longest x1 17.1 us: item_parts(): pl.pallas_call(item_kernel, grid_spec=pltpu.PrefetchScalarGridSpec(num_sc...]
    ppermute x0 -> x22, starting transfers between devices: none -> 34.2 us  [shift(): lax.ppermute(value, axis, [(i, (i + step) % size) for i in range(size)])]
    ppermute x0 -> x22, waiting for transfers between devices: none -> 32.9 us  [shift(): lax.ppermute(value, axis, [(i, (i + step) % size) for i in range(size)])]
    dynamic_update_slice x32 -> x0, local copies, waits for them, and re-layouts: 14.2 us -> none  [local(): lax.map(first_keep, (owner_rows, owner_targets))]
    all_to_all x7 -> x6, starting transfers between devices: 42.6 us -> 28.7 us  [the longest x1 6.76 us: local(): home = lax.all_to_all(stats[leave], 'z', 0, 0, tiled=True)]
  transfers between devices with their start and end apart: 8 -> 29, of which waited for: 8 -> 12; matrix products, arithmetic and copies ran while one was open for 2% -> 10% of each run, Pallas kernels for 0% -> 15%
where the time goes in v1:
time: 221 us; the launch traced here: 219 us
  starting transfers between devices  63 us (29%)
  waiting for transfers between devices  54.2 us (25%)
  Pallas kernels  43.1 us (20%)
  local copies, waits for them, and re-layouts  24.4 us (11%)
  other arithmetic  20.2 us (9%)
  between operations  14.6 us (7%)
    ppermute x22, starting transfers between devices, shift(): lax.ppermute(value, axis, [(i, (i + step) % size) for i in range(size)])  34.2 us
    ppermute x22, waiting for transfers between devices, shift(): lax.ppermute(value, axis, [(i, (i + step) % size) for i in range(size)])  32.9 us
    pallas_call x1, Pallas kernels, item_parts(): pl.pallas_call(item_kernel, grid_spec=pltpu.PrefetchScalarGridSpec(num_sc...  17.1 us
    pallas_call x2, Pallas kernels, query_parts(): pl.pallas_call(query_kernel, grid_spec=pltpu.PrefetchScalarGridSpec(num_s...  15.9 us
    unnamed x27, local copies, waits for them, and re-layouts  11.8 us
    pallas_call x2, Pallas kernels, forward(): pl.pallas_call(forward_kernel, grid_spec=pltpu.PrefetchScalarGridSpec(num...  10.2 us
    all_to_all x1, waiting for transfers between devices, local(): home = lax.all_to_all(stats[leave], 'z', 0, 0, tiled=True)  8.02 us
    all_to_all x1, waiting for transfers between devices, local(): lax.all_to_all(slot_lse.reshape(z_size, per_plane, block_rows), 'z', 0, 0...  7.66 us
  transfers between devices with their start and end apart: 29, of which 12 were waited for; matrix products, arithmetic and copies ran while one was open for 10% of the time, Pallas kernels for 15%

profile of v1, /device:TPU:6, one launch (start us, length us, event | category | flops | bytes accessed | tf_op | source)
XLA Modules:
  0.0 219.4 jit_solution(4924266956768560149)
XLA Ops:
  11.3 4.0 %collective-permute-start = (bf16[16,32,256]{2,1,0:T(8,128)(2,1)}, bf16[16,32,256]{2,1,0:T(8,128)(2,1)S(1)}, u32[]{:S(2)}, u32[]{:S(2)}) collective-permute-start(bf16[16,32,256]{2,1,0:T(8,128)(2,1)} %bitcast.72), channel_id=1, source_target_pairs={{0,224},{32,0},{64,32},{96,64},{128,96},{160,128},{192,160},{224,1... | collective-permute-start | bytes 786440 | tf_op jit(solution)/shard_map/ppermute | solution.py:23
  20.2 5.8 %all-to-all-start = ((s32[8,1,528]{2,1,0:T(1,128)}), s32[8,1,528]{2,1,0:T(1,128)S(1)}, u32[]{:S(2)}, u32[]{:S(2)}) async-start(s32[8,1,528]{2,1,0:T(1,128)} %reshape.511), calls=%async_computation | async-start | bytes 40960 | tf_op jit(solution)/shard_map/all_to_all | solution.py:262
  31.4 4.2 %collective-permute-done.2.q3 = bf16[16,32,256]{2,1,0:T(8,128)(2,1)S(1)} collective-permute-done((bf16[16,32,256]{2,1,0:T(8,128)(2,1)S(1)}, bf16[16,32,256]{2,1,0:T(8,128)(2,1)S(1)}, u32[]{:S(2)}, u32[]{:S(2)}) %collective-permute-start.2) | collective-permute-done | bytes 262176 | tf_op jit(solution)/shard_map/ppermute | solution.py:23
  35.6 2.7 %collective-permute-start.4 = (bf16[16,32,256]{2,1,0:T(8,128)(2,1)S(1)}, bf16[16,32,256]{2,1,0:T(8,128)(2,1)S(1)}, u32[]{:S(2)}, u32[]{:S(2)}) collective-permute-start(bf16[16,32,256]{2,1,0:T(8,128)(2,1)S(1)} %collective-permute-done.2.q3), channel_id=1, source_target_pairs={{0,224},{32,0},{64,32},{96,64},{128,96},{160,128},{192,160},{224,1... | collective-permute-start | bytes 786440 | tf_op jit(solution)/shard_map/ppermute | solution.py:23
  42.2 3.8 %collective-permute-start.7 = (bf16[8,32,256]{2,1,0:T(8,128)(2,1)S(1)}, bf16[8,32,256]{2,1,0:T(8,128)(2,1)S(1)}, u32[]{:S(2)}, u32[]{:S(2)}) collective-permute-start(bf16[8,32,256]{2,1,0:T(8,128)(2,1)S(1)} %slice.120), channel_id=1, source_target_pairs={{0,224},{32,0},{64,32},{96,64},{128,96},{160,128},{192,160},{224,1... | collective-permute-start | bytes 393224 | tf_op jit(solution)/shard_map/ppermute | solution.py:23
  48.5 3.8 %collective-permute-done.6 = bf16[8,32,256]{2,1,0:T(8,128)(2,1)S(1)} collective-permute-done((bf16[8,32,256]{2,1,0:T(8,128)(2,1)S(1)}, bf16[8,32,256]{2,1,0:T(8,128)(2,1)S(1)}, u32[]{:S(2)}, u32[]{:S(2)}) %collective-permute-start.6) | collective-permute-done | bytes 131104 | tf_op jit(solution)/shard_map/ppermute | solution.py:23
  52.3 2.2 copy-done
  54.5 5.1 %forward.3 = (bf16[8,256,256]{2,1,0:T(8,128)(2,1)}, f32[8,2,256]{2,1,0:T(2,128)S(1)}) custom-call(s32[64]{0:T(128)S(1)} %squeeze.47.blk, bf16[16,32,256]{2,1,0:T(8,128)(2,1)S(1)} %collective-permute-done.3.q0, bf16[16,32,256]{2,1,0:T(8,128)(2,1)S(1)} %collective-permute-done.4.q1, bf16[16,32,256]{2,1,0:T(8,128)(2,1)S(1)} %collective-permute-done.5.q2, ...), custom_call_target="tpu_custom_call" | custom-call | flops 1073741824 | bytes 7340032 | tf_op jit(solution)/shard_map/forward/pallas_call | solution.py:62
  59.7 2.2 copy-done.1
  61.9 5.1 %forward.2 = (bf16[8,256,256]{2,1,0:T(8,128)(2,1)}, f32[8,2,256]{2,1,0:T(2,128)S(1)}) custom-call(s32[64]{0:T(128)S(1)} %squeeze.22.blk, bf16[16,32,256]{2,1,0:T(8,128)(2,1)S(1)} %bitcast.73, bf16[16,32,256]{2,1,0:T(8,128)(2,1)S(1)} %collective-permute-done.q1, bf16[16,32,256]{2,1,0:T(8,128)(2,1)S(1)} %collective-permute-done.1.q2, ...), custom_call_target="tpu_custom_call" | custom-call | flops 1073741824 | bytes 7340032 | tf_op jit(solution)/shard_map/forward/pallas_call | solution.py:62
  68.6 6.8 %all-to-all-start.1 = ((f32[8,1,1024]{2,1,0:T(1,128)}), f32[8,1,1024]{2,1,0:T(1,128)S(1)}, u32[]{:S(2)}, u32[]{:S(2)}) async-start(f32[8,1,1024]{2,1,0:T(1,128)} %copy.43), calls=%async_computation.1 | async-start | bytes 65536 | tf_op jit(solution)/shard_map/all_to_all | solution.py:288
  75.4 8.0 %all-to-all-done.1 = f32[8,1,1024]{2,1,0:T(1,128)S(1)} async-done(((f32[8,1,1024]{2,1,0:T(1,128)}), f32[8,1,1024]{2,1,0:T(1,128)S(1)}, u32[]{:S(2)}, u32[]{:S(2)}) %all-to-all-start.1) | async-done | bytes 32800 | tf_op jit(solution)/shard_map/all_to_all | solution.py:288
  85.9 3.3 %all-to-all-start.2 = ((f32[8,1,512]{2,1,0:T(1,128)}), f32[8,1,512]{2,1,0:T(1,128)S(1)}, u32[]{:S(2)}, u32[]{:S(2)}) async-start(f32[8,1,512]{2,1,0:T(1,128)} %reshape.513), calls=%async_computation.2 | async-start | bytes 32768 | tf_op jit(solution)/shard_map/all_to_all | solution.py:297
  89.3 7.7 %all-to-all-done.2 = f32[8,1,512]{2,1,0:T(1,128)S(1)} async-done(((f32[8,1,512]{2,1,0:T(1,128)}), f32[8,1,512]{2,1,0:T(1,128)S(1)}, u32[]{:S(2)}, u32[]{:S(2)}) %all-to-all-start.2) | async-done | bytes 16416 | tf_op jit(solution)/shard_map/all_to_all | solution.py:297
  99.7 4.5 %all-to-all-start.5 = ((f32[8,4,256]{2,1,0:T(4,128)}), f32[8,4,256]{2,1,0:T(4,128)S(1)}, u32[]{:S(2)}, u32[]{:S(2)}) async-start(f32[8,4,256]{2,1,0:T(4,128)} %pad_maximum_fusion.4), calls=%async_computation.5 | async-start | bytes 65536 | tf_op jit(solution)/shard_map/all_to_all | solution.py:304
  104.2 2.2 copy-done.2
  106.4 7.9 %query_parts.3 = (bf16[16,32,256]{2,1,0:T(8,128)(2,1)S(1)}, bf16[16,32,256]{2,1,0:T(8,128)(2,1)S(1)}, bf16[16,32,256]{2,1,0:T(8,128)(2,1)S(1)}, bf16[16,32,256]{2,1,0:T(8,128)(2,1)S(1)}) custom-call(s32[64]{0:T(128)S(1)} %squeeze.47.blk, bf16[8,256,256]{2,1,0:T(8,128)(2,1)} %get-tuple-element.20.p_ref, bf16[8,1024,256]{2,1,0:T(8,128)(2,1)S(1)} %copy-done.2, ...), custom_call_target="tpu_custom_call" | custom-call | flops 2147483648 | bytes 6291456 | tf_op jit(solution)/shard_map/query_parts/pallas_call | solution.py:125
  114.3 4.8 %all-to-all-start.3 = ((bf16[8,256,256]{2,1,0:T(8,128)(2,1)}), bf16[8,256,256]{2,1,0:T(8,128)(2,1)S(1)}, u32[]{:S(2)}, u32[]{:S(2)}) async-start(bf16[8,256,256]{2,1,0:T(8,128)(2,1)} %get-tuple-element.18.p_ref), calls=%async_computation.3 | async-start | bytes 2097152 | tf_op jit(solution)/shard_map/all_to_all | solution.py:282
  122.6 3.5 %collective-permute-done.12 = bf16[8,32,256]{2,1,0:T(8,128)(2,1)} collective-permute-done((bf16[8,32,256]{2,1,0:T(8,128)(2,1)}, bf16[8,32,256]{2,1,0:T(8,128)(2,1)}, u32[]{:S(2)}, u32[]{:S(2)}) %collective-permute-start.12) | collective-permute-done | bytes 131104 | tf_op jit(solution)/shard_map/ppermute | solution.py:23
  129.5 5.6 %all-to-all-done.3.a_ref = bf16[8,256,256]{2,1,0:T(8,128)(2,1)S(1)} async-done(((bf16[8,256,256]{2,1,0:T(8,128)(2,1)}), bf16[8,256,256]{2,1,0:T(8,128)(2,1)S(1)}, u32[]{:S(2)}, u32[]{:S(2)}) %all-to-all-start.3) | async-done | bytes 1048608 | tf_op jit(solution)/shard_map/all_to_all | solution.py:282
  135.1 3.6 %all-to-all-start.4 = ((bf16[8,256,256]{2,1,0:T(8,128)(2,1)}), bf16[8,256,256]{2,1,0:T(8,128)(2,1)S(1)}, u32[]{:S(2)}, u32[]{:S(2)}) async-start(bf16[8,256,256]{2,1,0:T(8,128)(2,1)} %get-tuple-element.20.p_ref), calls=%async_computation.4 | async-start | bytes 2097152 | tf_op jit(solution)/shard_map/all_to_all | solution.py:284
  141.2 2.2 copy-done.3
  143.4 7.9 %query_parts.2 = (bf16[16,32,256]{2,1,0:T(8,128)(2,1)S(1)}, bf16[16,32,256]{2,1,0:T(8,128)(2,1)S(1)}, bf16[16,32,256]{2,1,0:T(8,128)(2,1)S(1)}, bf16[16,32,256]{2,1,0:T(8,128)(2,1)S(1)}) custom-call(s32[64]{0:T(128)S(1)} %squeeze.22.blk, bf16[8,256,256]{2,1,0:T(8,128)(2,1)} %get-tuple-element.18.p_ref, bf16[8,1024,256]{2,1,0:T(8,128)(2,1)S(1)} %copy-done.3, ...), custom_call_target="tpu_custom_call" | custom-call | flops 2147483648 | bytes 6291456 | tf_op jit(solution)/shard_map/query_parts/pallas_call | solution.py:125
  153.2 2.6 %collective-permute-start.14 = (bf16[16,32,256]{2,1,0:T(8,128)(2,1)}, bf16[16,32,256]{2,1,0:T(8,128)(2,1)}, u32[]{:S(2)}, u32[]{:S(2)}) collective-permute-start(bf16[16,32,256]{2,1,0:T(8,128)(2,1)} %add_convert_fusion.1), channel_id=1, source_target_pairs={{0,224},{32,0},{64,32},{96,64},{128,96},{160,128},{192,160},{224,1... | collective-permute-start | bytes 786440 | tf_op jit(solution)/shard_map/ppermute | solution.py:23
  156.6 17.1 %item_parts.1 = f32[4,256,256]{2,1,0:T(8,128)S(1)} custom-call(s32[1]{0:T(128)} %bitcast.20.x_ref, bf16[8,256,256]{2,1,0:T(8,128)(2,1)S(1)} %all-to-all-done.3.a_ref, bf16[8,256,256]{2,1,0:T(8,128)(2,1)S(1)} %all-to-all-done.4.b_ref, f32[8,4,256]{2,1,0:T(4,128)S(1)} %all-to-all-done.5.line_ref, bf16[1024,256]{1,0:T(8,128)(2,1)S(1)} %convert_bitcast_fusion.t_ref), custom_call_target="tpu_custom_call" | custom-call | flops 4294967296 | bytes 3670016 | tf_op jit(solution)/shard_map/item_parts/pallas_call | solution.py:186
  175.8 2.1 collective-permute-start.16
  179.0 3.3 %collective-permute-start.15 = (bf16[16,32,256]{2,1,0:T(8,128)(2,1)S(1)}, bf16[16,32,256]{2,1,0:T(8,128)(2,1)S(1)}, u32[]{:S(2)}, u32[]{:S(2)}) collective-permute-start(bf16[16,32,256]{2,1,0:T(8,128)(2,1)S(1)} %add_convert_fusion), channel_id=1, source_target_pairs={{0,224},{32,0},{64,32},{96,64},{128,96},{160,128},{192,160},{224,1... | collective-permute-start | bytes 786440 | tf_op jit(solution)/shard_map/ppermute | solution.py:23
  183.4 5.4 %collective-permute-done.18 = f32[256,256]{1,0:T(8,128)S(1)} collective-permute-done((f32[256,256]{1,0:T(8,128)S(1)}, f32[256,256]{1,0:T(8,128)S(1)}, u32[]{:S(2)}, u32[]{:S(2)}) %collective-permute-start.18) | collective-permute-done | bytes 262176 | tf_op jit(solution)/shard_map/ppermute | solution.py:23
  189.5 2.7 %collective-permute-start.21 = (f32[256,256]{1,0:T(8,128)S(1)}, f32[256,256]{1,0:T(8,128)}, u32[]{:S(2)}, u32[]{:S(2)}) collective-permute-start(f32[256,256]{1,0:T(8,128)S(1)} %fusion.3), channel_id=1, source_target_pairs={{0,1},{1,2},{2,3},{3,0},{4,5},{5,6},{6,7},{7,4},{8,9},{9,10},{10,1... | collective-permute-start | bytes 786440 | tf_op jit(solution)/shard_map/ppermute | solution.py:23
  194.7 8.8 %collective-permute-done.21 = f32[256,256]{1,0:T(8,128)} collective-permute-done((f32[256,256]{1,0:T(8,128)S(1)}, f32[256,256]{1,0:T(8,128)}, u32[]{:S(2)}, u32[]{:S(2)}) %collective-permute-start.21) | collective-permute-done | bytes 262176 | tf_op jit(solution)/shard_map/ppermute | solution.py:23
  203.6 3.4 %collective-permute-done.19 = f32[256,256]{1,0:T(8,128)S(1)} collective-permute-done((f32[256,256]{1,0:T(8,128)S(1)}, f32[256,256]{1,0:T(8,128)S(1)}, u32[]{:S(2)}, u32[]{:S(2)}) %collective-permute-start.19) | collective-permute-done | bytes 262176 | tf_op jit(solution)/shard_map/ppermute | solution.py:23
  209.7 2.9 %fusion = (f32[1,1024,256]{2,1,0:T(8,128)}, f32[1,1024,256]{2,1,0:T(8,128)}) fusion(f32[1,1024,256]{2,1,0:T(8,128)S(1)} %copy-done.8, f32[1,1024,256]{2,1,0:T(8,128)} %param.13, f32[1,1024,256]{2,1,0:T(8,128)S(1)} %bitcast.74, f32[1,1024,256]{2,1,0:T(8,128)S(1)} %bitcast.75), kind=kLoop, calls=%fused_computation.11 | loop fusion | flops 786432 | bytes 6291456 | tf_op jit(solution)/shard_map/sub | solution.py:337
  (151 shorter events, 49.9 us)
Async XLA Ops:
  7.2 45.1 %all-gather.2.cloned.1.call-start = ((), (), s32[]{:S(2)}) async-start(), calls=%async_computation.6 | async-start | bytes 4718592 | tf_op jit(solution)/shard_map/all_gather | solution.py:224
  9.3 17.3 %collective-permute-start.1 = (bf16[16,32,256]{2,1,0:T(8,128)(2,1)}, bf16[16,32,256]{2,1,0:T(8,128)(2,1)S(1)}, u32[]{:S(2)}, u32[]{:S(2)}) collective-permute-start(bf16[16,32,256]{2,1,0:T(8,128)(2,1)} %bitcast.71), channel_id=1, source_target_pairs={{0,32},{32,64},{64,96},{96,128},{128,160},{160,192},{192,224},{224... | collective-permute-start | bytes 786440 | tf_op jit(solution)/shard_map/ppermute | solution.py:23
  11.3 17.5 %collective-permute-start = (bf16[16,32,256]{2,1,0:T(8,128)(2,1)}, bf16[16,32,256]{2,1,0:T(8,128)(2,1)S(1)}, u32[]{:S(2)}, u32[]{:S(2)}) collective-permute-start(bf16[16,32,256]{2,1,0:T(8,128)(2,1)} %bitcast.72), channel_id=1, source_target_pairs={{0,224},{32,0},{64,32},{96,64},{128,96},{160,128},{192,160},{224,1... | collective-permute-start | bytes 786440 | tf_op jit(solution)/shard_map/ppermute | solution.py:23
  19.2 40.4 %copy-start.6 = (bf16[512,256]{1,0:T(8,128)(2,1)S(1)}, bf16[512,256]{1,0:T(8,128)(2,1)}, u32[]{:S(2)}) copy-start(bf16[512,256]{1,0:T(8,128)(2,1)} %param.8) | copy-start | bytes 786436
  20.2 18.1 %all-to-all-start = ((s32[8,1,528]{2,1,0:T(1,128)}), s32[8,1,528]{2,1,0:T(1,128)S(1)}, u32[]{:S(2)}, u32[]{:S(2)}) async-start(s32[8,1,528]{2,1,0:T(1,128)} %reshape.511), calls=%async_computation | async-start | bytes 40960 | tf_op jit(solution)/shard_map/all_to_all | solution.py:262
  26.7 11.6 %collective-permute-start.3 = (bf16[16,32,256]{2,1,0:T(8,128)(2,1)S(1)}, bf16[16,32,256]{2,1,0:T(8,128)(2,1)S(1)}, u32[]{:S(2)}, u32[]{:S(2)}) collective-permute-start(bf16[16,32,256]{2,1,0:T(8,128)(2,1)S(1)} %collective-permute-done.1.q2), channel_id=1, source_target_pairs={{0,32},{32,64},{64,96},{96,128},{128,160},{160,192},{192,224},{224... | collective-permute-start | bytes 786440 | tf_op jit(solution)/shard_map/ppermute | solution.py:23
  28.8 6.8 %collective-permute-start.2 = (bf16[16,32,256]{2,1,0:T(8,128)(2,1)S(1)}, bf16[16,32,256]{2,1,0:T(8,128)(2,1)S(1)}, u32[]{:S(2)}, u32[]{:S(2)}) collective-permute-start(bf16[16,32,256]{2,1,0:T(8,128)(2,1)S(1)} %collective-permute-done.q1), channel_id=1, source_target_pairs={{0,224},{32,0},{64,32},{96,64},{128,96},{160,128},{192,160},{224,1... | collective-permute-start | bytes 786440 | tf_op jit(solution)/shard_map/ppermute | solution.py:23
  35.6 6.6 %collective-permute-start.4 = (bf16[16,32,256]{2,1,0:T(8,128)(2,1)S(1)}, bf16[16,32,256]{2,1,0:T(8,128)(2,1)S(1)}, u32[]{:S(2)}, u32[]{:S(2)}) collective-permute-start(bf16[16,32,256]{2,1,0:T(8,128)(2,1)S(1)} %collective-permute-done.2.q3), channel_id=1, source_target_pairs={{0,224},{32,0},{64,32},{96,64},{128,96},{160,128},{192,160},{224,1... | collective-permute-start | bytes 786440 | tf_op jit(solution)/shard_map/ppermute | solution.py:23
  38.3 7.7 %collective-permute-start.5 = (bf16[16,32,256]{2,1,0:T(8,128)(2,1)S(1)}, bf16[16,32,256]{2,1,0:T(8,128)(2,1)S(1)}, u32[]{:S(2)}, u32[]{:S(2)}) collective-permute-start(bf16[16,32,256]{2,1,0:T(8,128)(2,1)S(1)} %collective-permute-done.3.q0), channel_id=1, source_target_pairs={{0,32},{32,64},{64,96},{96,128},{128,160},{160,192},{192,224},{224... | collective-permute-start | bytes 786440 | tf_op jit(solution)/shard_map/ppermute | solution.py:23
  42.2 6.3 %collective-permute-start.7 = (bf16[8,32,256]{2,1,0:T(8,128)(2,1)S(1)}, bf16[8,32,256]{2,1,0:T(8,128)(2,1)S(1)}, u32[]{:S(2)}, u32[]{:S(2)}) collective-permute-start(bf16[8,32,256]{2,1,0:T(8,128)(2,1)S(1)} %slice.120), channel_id=1, source_target_pairs={{0,224},{32,0},{64,32},{96,64},{128,96},{160,128},{192,160},{224,1... | collective-permute-start | bytes 393224 | tf_op jit(solution)/shard_map/ppermute | solution.py:23
  46.0 6.3 %collective-permute-start.6 = (bf16[8,32,256]{2,1,0:T(8,128)(2,1)S(1)}, bf16[8,32,256]{2,1,0:T(8,128)(2,1)S(1)}, u32[]{:S(2)}, u32[]{:S(2)}) collective-permute-start(bf16[8,32,256]{2,1,0:T(8,128)(2,1)S(1)} %slice.119), channel_id=1, source_target_pairs={{0,32},{32,64},{64,96},{96,128},{128,160},{160,192},{192,224},{224... | collective-permute-start | bytes 393224 | tf_op jit(solution)/shard_map/ppermute | solution.py:23
  68.6 14.8 %all-to-all-start.1 = ((f32[8,1,1024]{2,1,0:T(1,128)}), f32[8,1,1024]{2,1,0:T(1,128)S(1)}, u32[]{:S(2)}, u32[]{:S(2)}) async-start(f32[8,1,1024]{2,1,0:T(1,128)} %copy.43), calls=%async_computation.1 | async-start | bytes 65536 | tf_op jit(solution)/shard_map/all_to_all | solution.py:288
  85.9 11.0 %all-to-all-start.2 = ((f32[8,1,512]{2,1,0:T(1,128)}), f32[8,1,512]{2,1,0:T(1,128)S(1)}, u32[]{:S(2)}, u32[]{:S(2)}) async-start(f32[8,1,512]{2,1,0:T(1,128)} %reshape.513), calls=%async_computation.2 | async-start | bytes 32768 | tf_op jit(solution)/shard_map/all_to_all | solution.py:297
  99.7 14.6 %all-to-all-start.5 = ((f32[8,4,256]{2,1,0:T(4,128)}), f32[8,4,256]{2,1,0:T(4,128)S(1)}, u32[]{:S(2)}, u32[]{:S(2)}) async-start(f32[8,4,256]{2,1,0:T(4,128)} %pad_maximum_fusion.4), calls=%async_computation.5 | async-start | bytes 65536 | tf_op jit(solution)/shard_map/all_to_all | solution.py:304
  114.3 20.8 %all-to-all-start.3 = ((bf16[8,256,256]{2,1,0:T(8,128)(2,1)}), bf16[8,256,256]{2,1,0:T(8,128)(2,1)S(1)}, u32[]{:S(2)}, u32[]{:S(2)}) async-start(bf16[8,256,256]{2,1,0:T(8,128)(2,1)} %get-tuple-element.18.p_ref), calls=%async_computation.3 | async-start | bytes 2097152 | tf_op jit(solution)/shard_map/all_to_all | solution.py:282
  119.8 6.2 %collective-permute-start.12 = (bf16[8,32,256]{2,1,0:T(8,128)(2,1)}, bf16[8,32,256]{2,1,0:T(8,128)(2,1)}, u32[]{:S(2)}, u32[]{:S(2)}) collective-permute-start(bf16[8,32,256]{2,1,0:T(8,128)(2,1)} %get-tuple-element.42), channel_id=1, source_target_pairs={{0,224},{32,0},{64,32},{96,64},{128,96},{160,128},{192,160},{224,1... | collective-permute-start | bytes 393224 | tf_op jit(solution)/shard_map/ppermute | solution.py:23
  121.1 17.5 %collective-permute-start.8 = (bf16[8,32,256]{2,1,0:T(8,128)(2,1)}, bf16[8,32,256]{2,1,0:T(8,128)(2,1)}, u32[]{:S(2)}, u32[]{:S(2)}) collective-permute-start(bf16[8,32,256]{2,1,0:T(8,128)(2,1)} %get-tuple-element.41), channel_id=1, source_target_pairs={{0,32},{32,64},{64,96},{96,128},{128,160},{160,192},{192,224},{224... | collective-permute-start | bytes 393224 | tf_op jit(solution)/shard_map/ppermute | solution.py:23
  127.7 23.6 %collective-permute-start.13 = (bf16[16,32,256]{2,1,0:T(8,128)(2,1)}, bf16[16,32,256]{2,1,0:T(8,128)(2,1)}, u32[]{:S(2)}, u32[]{:S(2)}) collective-permute-start(bf16[16,32,256]{2,1,0:T(8,128)(2,1)} %pad_maximum_fusion.3), channel_id=1, source_target_pairs={{0,224},{32,0},{64,32},{96,64},{128,96},{160,128},{192,160},{224,1... | collective-permute-start | bytes 786440 | tf_op jit(solution)/shard_map/ppermute | solution.py:23
  135.1 21.5 %all-to-all-start.4 = ((bf16[8,256,256]{2,1,0:T(8,128)(2,1)}), bf16[8,256,256]{2,1,0:T(8,128)(2,1)S(1)}, u32[]{:S(2)}, u32[]{:S(2)}) async-start(bf16[8,256,256]{2,1,0:T(8,128)(2,1)} %get-tuple-element.20.p_ref), calls=%async_computation.4 | async-start | bytes 2097152 | tf_op jit(solution)/shard_map/all_to_all | solution.py:284
  140.5 15.3 %collective-permute-start.9 = (bf16[16,32,256]{2,1,0:T(8,128)(2,1)S(1)}, bf16[16,32,256]{2,1,0:T(8,128)(2,1)S(1)}, u32[]{:S(2)}, u32[]{:S(2)}) collective-permute-start(bf16[16,32,256]{2,1,0:T(8,128)(2,1)S(1)} %pad_maximum_fusion.2), channel_id=1, source_target_pairs={{0,32},{32,64},{64,96},{96,128},{128,160},{160,192},{192,224},{224... | collective-permute-start | bytes 786440 | tf_op jit(solution)/shard_map/ppermute | solution.py:23
  153.2 24.7 %collective-permute-start.14 = (bf16[16,32,256]{2,1,0:T(8,128)(2,1)}, bf16[16,32,256]{2,1,0:T(8,128)(2,1)}, u32[]{:S(2)}, u32[]{:S(2)}) collective-permute-start(bf16[16,32,256]{2,1,0:T(8,128)(2,1)} %add_convert_fusion.1), channel_id=1, source_target_pairs={{0,224},{32,0},{64,32},{96,64},{128,96},{160,128},{192,160},{224,1... | collective-permute-start | bytes 786440 | tf_op jit(solution)/shard_map/ppermute | solution.py:23
  156.6 25.6 %collective-permute-start.10 = (bf16[16,32,256]{2,1,0:T(8,128)(2,1)}, bf16[16,32,256]{2,1,0:T(8,128)(2,1)}, u32[]{:S(2)}, u32[]{:S(2)}) collective-permute-start(bf16[16,32,256]{2,1,0:T(8,128)(2,1)} %add_convert_fusion.3), channel_id=1, source_target_pairs={{0,32},{32,64},{64,96},{96,128},{128,160},{160,192},{192,224},{224... | collective-permute-start | bytes 786440 | tf_op jit(solution)/shard_map/ppermute | solution.py:23
  156.6 21.3 %copy-start.5 = (bf16[16,32,256]{2,1,0:T(8,128)(2,1)S(1)}, bf16[16,32,256]{2,1,0:T(8,128)(2,1)}, u32[]{:S(2)}) copy-start(bf16[16,32,256]{2,1,0:T(8,128)(2,1)} %copy-done.4) | copy-start | bytes 786436
  173.8 15.0 %collective-permute-start.18 = (f32[256,256]{1,0:T(8,128)S(1)}, f32[256,256]{1,0:T(8,128)S(1)}, u32[]{:S(2)}, u32[]{:S(2)}) collective-permute-start(f32[256,256]{1,0:T(8,128)S(1)} %get-tuple-element.39), channel_id=1, source_target_pairs={{0,3},{1,0},{2,1},{3,2},{4,7},{5,4},{6,5},{7,6},{8,11},{9,8},{10,9... | collective-permute-start | bytes 786440 | tf_op jit(solution)/shard_map/ppermute | solution.py:23
  174.7 14.1 %collective-permute-start.17 = (f32[256,256]{1,0:T(8,128)S(1)}, f32[256,256]{1,0:T(8,128)S(1)}, u32[]{:S(2)}, u32[]{:S(2)}) collective-permute-start(f32[256,256]{1,0:T(8,128)S(1)} %get-tuple-element.40), channel_id=1, source_target_pairs={{0,2},{1,3},{2,0},{3,1},{4,6},{5,7},{6,4},{7,5},{8,10},{9,11},{10,... | collective-permute-start | bytes 786440 | tf_op jit(solution)/shard_map/ppermute | solution.py:23
  175.8 13.6 %collective-permute-start.16 = (f32[256,256]{1,0:T(8,128)S(1)}, f32[256,256]{1,0:T(8,128)S(1)}, u32[]{:S(2)}, u32[]{:S(2)}) collective-permute-start(f32[256,256]{1,0:T(8,128)S(1)} %get-tuple-element.38), channel_id=1, source_target_pairs={{0,1},{1,2},{2,3},{3,0},{4,5},{5,6},{6,7},{7,4},{8,9},{9,10},{10,1... | collective-permute-start | bytes 786440 | tf_op jit(solution)/shard_map/ppermute | solution.py:23
  179.0 14.8 %collective-permute-start.15 = (bf16[16,32,256]{2,1,0:T(8,128)(2,1)S(1)}, bf16[16,32,256]{2,1,0:T(8,128)(2,1)S(1)}, u32[]{:S(2)}, u32[]{:S(2)}) collective-permute-start(bf16[16,32,256]{2,1,0:T(8,128)(2,1)S(1)} %add_convert_fusion), channel_id=1, source_target_pairs={{0,224},{32,0},{64,32},{96,64},{128,96},{160,128},{192,160},{224,1... | collective-permute-start | bytes 786440 | tf_op jit(solution)/shard_map/ppermute | solution.py:23
  183.3 10.5 %collective-permute-start.11 = (bf16[16,32,256]{2,1,0:T(8,128)(2,1)S(1)}, bf16[16,32,256]{2,1,0:T(8,128)(2,1)S(1)}, u32[]{:S(2)}, u32[]{:S(2)}) collective-permute-start(bf16[16,32,256]{2,1,0:T(8,128)(2,1)S(1)} %add_convert_fusion.2), channel_id=1, source_target_pairs={{0,32},{32,64},{64,96},{96,128},{128,160},{160,192},{192,224},{224... | collective-permute-start | bytes 786440 | tf_op jit(solution)/shard_map/ppermute | solution.py:23
  189.5 14.1 %collective-permute-start.21 = (f32[256,256]{1,0:T(8,128)S(1)}, f32[256,256]{1,0:T(8,128)}, u32[]{:S(2)}, u32[]{:S(2)}) collective-permute-start(f32[256,256]{1,0:T(8,128)S(1)} %fusion.3), channel_id=1, source_target_pairs={{0,1},{1,2},{2,3},{3,0},{4,5},{5,6},{6,7},{7,4},{8,9},{9,10},{10,1... | collective-permute-start | bytes 786440 | tf_op jit(solution)/shard_map/ppermute | solution.py:23
  192.2 11.4 %collective-permute-start.20 = (f32[256,256]{1,0:T(8,128)S(1)}, f32[256,256]{1,0:T(8,128)S(1)}, u32[]{:S(2)}, u32[]{:S(2)}) collective-permute-start(f32[256,256]{1,0:T(8,128)S(1)} %fusion.3), channel_id=1, source_target_pairs={{0,2},{1,3},{2,0},{3,1},{4,6},{5,7},{6,4},{7,5},{8,10},{9,11},{10,... | collective-permute-start | bytes 786440 | tf_op jit(solution)/shard_map/ppermute | solution.py:23
  192.4 14.6 %collective-permute-start.19 = (f32[256,256]{1,0:T(8,128)S(1)}, f32[256,256]{1,0:T(8,128)S(1)}, u32[]{:S(2)}, u32[]{:S(2)}) collective-permute-start(f32[256,256]{1,0:T(8,128)S(1)} %fusion.3), channel_id=1, source_target_pairs={{0,3},{1,0},{2,1},{3,2},{4,7},{5,4},{6,5},{7,6},{8,11},{9,8},{10,9... | collective-permute-start | bytes 786440 | tf_op jit(solution)/shard_map/ppermute | solution.py:23
  193.8 15.9 %copy-start.8 = (f32[1,1024,256]{2,1,0:T(8,128)S(1)}, f32[1,1024,256]{2,1,0:T(8,128)}, u32[]{:S(2)}) copy-start(f32[1,1024,256]{2,1,0:T(8,128)} %param.12) | copy-start | bytes 3145732
  (8 other events, 32.2 us)
Sparse Core Ops, SparseCore 0:
  10.4 37.5 all-gather.1

commit v2 on v1

v2 whole, which is shorter than its diff:
```python
import jax
import jax.numpy as jnp
from jax import lax
from jax.experimental import pallas as pl
from jax.experimental.pallas import tpu as pltpu
from jax.sharding import Mesh, PartitionSpec as P

MOST = 2
EMPTY = 1e30
NEAR = (0, 1, 7, 2)
FAR = (6, 3, 5, 4)
ORDER = NEAR + FAR
PLANE = ("y", "c")
F32 = jnp.float32
BF16 = jnp.bfloat16
NT = (((1,), (1,)), ((), ()))
TN = (((0,), (0,)), ((), ()))
TILE = 256
VMEM = 56 << 20


def shift(value, axis, step):
    size = lax.axis_size(axis)
    return lax.ppermute(value, axis, [(i, (i + step) % size) for i in range(size)])


def tile_ids(start, shape):
    return lax.broadcasted_iota(jnp.int32, shape, 0) + start


def shift_plane(value, dy, dc):
    ys, cs = lax.axis_size("y"), lax.axis_size("c")
    moves = []
    for y in range(ys):
        for c in range(cs):
            moves.append((y * cs + c, (y + dy) % ys * cs + (c + dc) % cs))
    return lax.ppermute(value, PLANE, moves)


def forward_kernel(blk, q0, q1, q2, q3, t_ref, tgt_ref, *rest):
    p_ref, stat_ref, s_ref = rest[-3:]
    step = pl.program_id(0)
    sources = (q0, q1, q2, q3)
    block_rows = q0.shape[1]
    for slot in range(8):
        b = blk[step * 8 + slot]
        p_ref[0, pl.ds(slot * block_rows, block_rows), :] = sources[slot // MOST][b]
    q = p_ref[0]
    items = t_ref.shape[1]
    width = q.shape[0]
    tgt = tgt_ref[0]
    high = jnp.full((8, width), -jnp.inf, F32)
    pick = jnp.zeros((8, width), F32)
    for start in range(0, items, TILE):
        s = lax.dot_general(t_ref[0, pl.ds(start, TILE), :], q, NT, preferred_element_type=F32)
        s_ref[pl.ds(start, TILE), :] = s
        high = jnp.maximum(high, jnp.max(s.reshape(TILE // 8, 8, width), axis=0))
        hit = jnp.where(tile_ids(start, s.shape) == tgt, s, 0.0)
        pick = pick + jnp.sum(hit.reshape(TILE // 8, 8, width), axis=0)
    top = jnp.max(high, axis=0, keepdims=True)
    mass = jnp.zeros((8, width), F32)
    for start in range(0, items, TILE):
        e = jnp.exp(s_ref[pl.ds(start, TILE), :] - top)
        mass = mass + jnp.sum(e.reshape(TILE // 8, 8, width), axis=0)
    stat_ref[0, 0, 0:1, :] = top + jnp.log(jnp.sum(mass, axis=0, keepdims=True))
    stat_ref[0, 0, 1:2, :] = jnp.sum(pick, axis=0, keepdims=True)


def forward(sources, blk, targets, tables, half, held=None):
    planes, items, features = tables.shape
    width = targets.shape[2]
    whole = pl.BlockSpec(sources[0].shape, lambda j, blk: (0, 0, 0))
    anywhere = pl.BlockSpec(memory_space=pl.ANY)
    carried = [] if held is None else list(held)
    return pl.pallas_call(
        forward_kernel,
        grid_spec=pltpu.PrefetchScalarGridSpec(
            num_scalar_prefetch=1,
            grid=(planes,),
            in_specs=[whole] * 4
            + [
                pl.BlockSpec((1, items, features), lambda j, blk: (j, 0, 0)),
                pl.BlockSpec((1, 1, width), lambda j, blk: (j, 0, 0)),
            ]
            + [anywhere] * len(carried),
            out_specs=[
                pl.BlockSpec((1, width, features), lambda j, blk: (j, half, 0)),
                pl.BlockSpec((1, 1, 2, width), lambda j, blk: (j, half, 0, 0)),
            ],
            scratch_shapes=[pltpu.VMEM((items, width), F32)],
        ),
        out_shape=[
            jax.ShapeDtypeStruct((planes, 2 * width, features), BF16),
            jax.ShapeDtypeStruct((planes, 2, 2, width), F32),
        ],
        input_output_aliases={7: 0, 8: 1} if carried else {},
        compiler_params=pltpu.CompilerParams(vmem_limit_bytes=VMEM),
        cost_estimate=pl.CostEstimate(
            flops=2 * planes * width * items * features,
            bytes_accessed=planes * items * features * 2 + 3 * planes * width * features * 2,
            transcendentals=planes * width * items,
        ),
        name="forward",
    )(blk, *sources, tables, targets, *carried)


def query_kernel(blk, p_ref, t_ref, lse_ref, tgt_ref, g0, g1, g2, g3, c_ref, acc_ref):
    step = pl.program_id(0)

    @pl.when(step == 0)
    def _():
        acc_ref[...] = jnp.zeros_like(acc_ref)

    q = p_ref[0]
    lse = lse_ref[0]
    tgt = tgt_ref[0]
    items = t_ref.shape[1]
    for start in range(0, items, TILE):
        s = lax.dot_general(t_ref[0, pl.ds(start, TILE), :], q, NT, preferred_element_type=F32)
        e = jnp.exp(s - lse)
        c = jnp.where(tile_ids(start, s.shape) == tgt, e - 1.0, e)
        c_ref[pl.ds(start, TILE), :] = c.astype(BF16)
    g = lax.dot_general(c_ref[...], t_ref[0], TN, preferred_element_type=F32)
    block_rows = g0.shape[1]
    for slot in range(8):
        b = blk[step * 8 + slot]
        acc_ref[slot // MOST, b] += g[slot * block_rows:(slot + 1) * block_rows, :]

    @pl.when(step == pl.num_programs(0) - 1)
    def _():
        for i, out in enumerate((g0, g1, g2, g3)):
            out[...] = acc_ref[i].astype(BF16)


def query_parts(packed, blk, lse, targets, tables, half, blocks, block_rows):
    planes, items, features = tables.shape
    width = targets.shape[2]
    line = pl.BlockSpec((1, 1, width), lambda j, blk: (j, 0, 0))
    out = jax.ShapeDtypeStruct((blocks, block_rows, features), BF16)
    return pl.pallas_call(
        query_kernel,
        grid_spec=pltpu.PrefetchScalarGridSpec(
            num_scalar_prefetch=1,
            grid=(planes,),
            in_specs=[
                pl.BlockSpec((1, width, features), lambda j, blk: (j, half, 0)),
                pl.BlockSpec((1, items, features), lambda j, blk: (j, 0, 0)),
                line,
                line,
            ],
            out_specs=[pl.BlockSpec(out.shape, lambda j, blk: (0, 0, 0))] * 4,
            scratch_shapes=[
                pltpu.VMEM((items, width), BF16),
                pltpu.VMEM((4, blocks, block_rows, features), F32),
            ],
        ),
        out_shape=[out] * 4,
        compiler_params=pltpu.CompilerParams(vmem_limit_bytes=VMEM),
        cost_estimate=pl.CostEstimate(
            flops=4 * planes * width * items * features,
            bytes_accessed=planes * items * features * 2 + 2 * planes * width * features * 2,
            transcendentals=planes * width * items,
        ),
        name="query_parts",
    )(blk, packed, tables, lse, targets)


def item_kernel(order_ref, q_ref, line_ref, t_ref, w_ref):
    step = pl.program_id(0)

    @pl.when(step == 0)
    def _():
        w_ref[...] = jnp.zeros_like(w_ref)

    quarters = w_ref.shape[0]
    rows = w_ref.shape[1]
    mine = order_ref[0]
    q = q_ref[0]
    lse = line_ref[0, 0:1, :]
    tgt = line_ref[0, 1:2, :].astype(jnp.int32)
    for place in range(quarters):
        start = pl.multiple_of(lax.rem(place + mine, quarters) * rows, rows)
        s = lax.dot_general(t_ref[pl.ds(start, rows), :], q, NT, preferred_element_type=F32)
        e = jnp.exp(s - lse)
        c = jnp.where(tile_ids(start, s.shape) == tgt, e - 1.0, e).astype(BF16)
        w_ref[place] += jnp.dot(c, q, preferred_element_type=F32)


def item_parts(order, rows, lines, table16, quarters):
    sources, width, features = rows.shape
    items = table16.shape[0]
    return pl.pallas_call(
        item_kernel,
        grid_spec=pltpu.PrefetchScalarGridSpec(
            num_scalar_prefetch=1,
            grid=(sources,),
            in_specs=[
                pl.BlockSpec((1, width, features), lambda j, o: (j, 0, 0)),
                pl.BlockSpec((1, 2, width), lambda j, o: (o[j + 1], 0, 0)),
                pl.BlockSpec((items, features), lambda j, o: (0, 0)),
            ],
            out_specs=pl.BlockSpec((quarters, items // quarters, features), lambda j, o: (0, 0, 0)),
        ),
        out_shape=jax.ShapeDtypeStruct((quarters, items // quarters, features), F32),
        compiler_params=pltpu.CompilerParams(vmem_limit_bytes=VMEM),
        cost_estimate=pl.CostEstimate(
            flops=4 * sources * width * items * features,
            bytes_accessed=2 * sources * width * features + items * features * 6,
            transcendentals=sources * width * items,
        ),
        name="item_parts",
    )(order, rows, lines, table16)


def local(queries, clusters, positives, owner_of, table, accum):
    z_size = lax.axis_size("z")
    y_size = lax.axis_size("y")
    c_size = lax.axis_size("c")
    x_size = lax.axis_size("x")
    z = lax.axis_index("z")
    y = lax.axis_index("y")
    c = lax.axis_index("c")
    x = lax.axis_index("x")
    local_rows, features = queries.shape
    block_count, picks = clusters.shape
    block_rows = local_rows // block_count
    items = table.shape[1]
    owners = owner_of.shape[0]
    plane = owners // z_size
    pair_count = block_count * picks

    table16 = table[0].astype(BF16)
    tables = lax.all_gather(table16, PLANE)

    here = queries.reshape(block_count, block_rows, features)
    by_source = {0: here}
    right = left = here
    for hop in range(1, z_size // 2 + 1):
        right = shift(right, "z", 1)
        by_source[z_size - hop] = right
        if hop < z_size // 2:
            left = shift(left, "z", -1)
            by_source[hop] = left

    flat_lists = clusters.reshape(pair_count)
    catalog_ids = jnp.arange(owners, dtype=jnp.int32)
    lookup = flat_lists[:, None] == catalog_ids[None, :]
    destination = jnp.sum(jnp.where(lookup, owner_of[None, :], 0), axis=1)
    pair_ids = jnp.arange(pair_count, dtype=jnp.int32)
    earlier = (destination[:, None] == destination[None, :]) & (
        pair_ids[:, None] > pair_ids[None, :]
    )
    rank_in = jnp.sum(earlier.astype(jnp.int32), axis=1)
    slot_of_pair = destination * MOST + rank_in
    slot_count = owners * MOST
    matches = slot_of_pair[None, :] == jnp.arange(slot_count, dtype=jnp.int32)[:, None]
    filled = jnp.any(matches, axis=1)
    source_pair = jnp.sum(jnp.where(matches, pair_ids[None, :], 0), axis=1)
    which_block = source_pair // picks
    which_pick = source_pair % picks
    chosen = positives.reshape(block_count, block_rows)[which_block]
    inside = filled[:, None] & (chosen // items == which_pick[:, None])
    send_targets = jnp.where(inside, chosen - which_pick[:, None] * items, -1)
    block_or_none = jnp.where(filled, which_block, -1)
    per_plane = plane * MOST
    meta = jnp.concatenate(
        [
            send_targets.reshape(z_size, per_plane * block_rows),
            block_or_none.reshape(z_size, per_plane),
            jnp.broadcast_to(slot_of_pair[None, :], (z_size, pair_count)),
        ],
        axis=1,
    )
    got = lax.all_to_all(meta, "z", 0, 0, tiled=True)
    order = jnp.array(ORDER, jnp.int32)
    got = got[(z + order) % z_size]
    width = 4 * MOST * block_rows
    cut = per_plane * block_rows
    targets = got[:, :cut].reshape(2, 4, plane, MOST, block_rows)
    targets = targets.transpose(0, 2, 1, 3, 4).reshape(2, plane, 1, width)
    named = got[:, cut:cut + per_plane].reshape(2, 4, plane, MOST).transpose(0, 2, 1, 3)
    named = named.reshape(2, plane * 4 * MOST)
    blk = jnp.maximum(named, 0)

    pair_slot = got[:, cut + per_plane:]
    pair_owner = pair_slot // MOST
    pair_from = (pair_owner // plane - z) % z_size
    pair_rel = (order[:, None] - pair_from) % z_size
    pair_place = jnp.zeros_like(pair_rel)
    for place, d in enumerate(ORDER):
        pair_place = jnp.where(pair_rel == d, place, pair_place)
    pair_row = (pair_from * plane + pair_owner % plane) * 2 + pair_place // 4
    pair_row = pair_row * 2 * 4 * MOST + pair_place % 4 * MOST + pair_slot % MOST

    near_q = [by_source[d] for d in NEAR]
    far_q = [by_source[d] for d in FAR]
    held = forward(near_q, blk[0], targets[0], tables, 0)
    packed, stats = forward(far_q, blk[1], targets[1], tables, 1, held)
    rows = lax.all_to_all(packed, PLANE, 0, 0, tiled=True)

    all_stats = jnp.stack([stats] + [shift(stats, "z", -e) for e in range(1, z_size)])
    all_stats = all_stats.reshape(-1, block_rows)
    part = all_stats[pair_row.reshape(-1)].reshape(z_size, block_count, picks, block_rows)
    pick = all_stats[pair_row[0] + 4 * MOST].reshape(block_count, picks, block_rows)
    top = jnp.max(part, axis=2)
    lse = top + jnp.log(jnp.sum(jnp.exp(part - top[:, :, None]), axis=2))
    losses = (lse[0] - jnp.sum(pick, axis=1)).reshape(local_rows)
    lse_rows = lse.reshape(z_size * block_count, block_rows)
    first = jnp.arange(z_size, dtype=jnp.int32).reshape(2, 1, 4, 1) * block_count
    lse_at = (blk.reshape(2, plane, 4, MOST) + first).reshape(-1)
    lse_slots = jnp.where(named.reshape(-1, 1) < 0, F32(EMPTY), lse_rows[lse_at])
    lse_lines = lse_slots.reshape(2, plane, 1, width)

    lines = jnp.stack(
        [
            lse_lines.transpose(1, 2, 0, 3).reshape(plane, 2 * width),
            targets.transpose(1, 2, 0, 3).reshape(plane, 2 * width).astype(F32),
        ],
        axis=1,
    )
    line_parts = []
    ranks = []
    for dy in range(y_size):
        for dc in range(c_size):
            index = (y + dy) % y_size * c_size + (c + dc) % c_size
            mine = lax.dynamic_index_in_dim(lines, index, 0, keepdims=False)
            line_parts.append(shift_plane(mine, dy, dc) if dy or dc else mine)
    sources = jnp.arange(plane, dtype=jnp.int32)
    ranks = (y - sources // c_size) % y_size * c_size + (c - sources % c_size) % c_size
    got_lines = jnp.stack(line_parts)

    far_g = query_parts(
        packed, blk[1], lse_lines[1], targets[1], tables, 1, block_count, block_rows
    )
    near_g = query_parts(
        packed, blk[0], lse_lines[0], targets[0], tables, 0, block_count, block_rows
    )
    grads = dict(zip(ORDER, list(near_g) + list(far_g)))

    def add(a, b):
        return (a.astype(F32) + b.astype(F32)).astype(BF16)

    go_right = shift(grads[4], "z", 1)
    go_right = shift(add(go_right, grads[3]), "z", 1)
    go_left = shift(grads[5], "z", -1)
    go_right = shift(add(go_right, grads[2]), "z", 1)
    go_left = shift(add(go_left, grads[6]), "z", -1)
    go_right = shift(add(go_right, grads[1]), "z", 1)
    go_left = shift(add(go_left, grads[7]), "z", -1)
    query_grads = (
        grads[0].astype(F32) + go_right.astype(F32) + go_left.astype(F32)
    ).reshape(local_rows, features)

    item_order = jnp.concatenate([x.reshape(1), ranks])
    parts = item_parts(item_order, rows, got_lines, table16, x_size)
    summed = parts[0]
    for hop in range(1, x_size):
        summed = summed + shift(parts[hop], "x", hop)
    all_sums = jnp.stack([summed] + [shift(summed, "x", -hop) for hop in range(1, x_size)])
    summed = all_sums[(jnp.arange(x_size) - x) % x_size].reshape(items, features)
    new_accum = accum[0] + summed * summed
    new_table = table[0] - 0.5 * summed / jnp.sqrt(new_accum)
    return (losses, query_grads, new_table[None], new_accum[None])


def solution(mesh):
    axes = ("z", "y", "c", "x")
    split = Mesh(mesh.devices.reshape(8, 4, 2, 4), axes)
    placed = (
        P(axes, None),
        P(axes, None),
        P(axes),
        P(),
        P(axes[:3], None, None),
        P(axes[:3], None, None),
    )
    return jax.shard_map(
        local,
        mesh=split,
        in_specs=placed,
        out_specs=(
            P(axes),
            P(axes, None),
            P(axes[:3], None, None),
            P(axes[:3], None, None),
        ),
        check_vma=False,
    )
```

time: 221 us -> 201 us (0.910)
  waiting for transfers between devices: 54.2 us -> 42.8 us
  local copies, waits for them, and re-layouts: 24.4 us -> 16.5 us
  other arithmetic: 20.2 us -> 14.6 us
  Pallas kernels: 43.1 us -> 47.2 us
    all_to_all x6 -> x2, starting transfers between devices: 28.7 us -> 10.9 us  [the longest x1 5.76 us: local(): got = lax.all_to_all(meta, 'z', 0, 0, tiled=True)]
    all_to_all x6 -> x2, waiting for transfers between devices: 21.3 us -> 6.18 us  [the longest x1 6.18 us: local(): got = lax.all_to_all(meta, 'z', 0, 0, tiled=True)]
    unnamed x27 -> x57, local copies, waits for them, and re-layouts: 11.8 us -> 2.85 us
    ppermute x0 -> x7, starting transfers between devices: none -> 8.82 us  [shift_plane(): return lax.ppermute(value, PLANE, moves)]
    ppermute x22 -> x27, starting transfers between devices: 34.2 us -> 42.5 us  [shift(): lax.ppermute(value, axis, [(i, (i + step) % size) for i in range(size)])]
    pallas_call x2, Pallas kernels: 10.2 us -> 17.3 us  [forward(): pl.pallas_call(forward_kernel, grid_spec=pltpu.PrefetchScalarGridSpec(num...]
    pallas_call x1, Pallas kernels: 17.1 us -> 10.1 us  [item_parts(): pl.pallas_call(item_kernel, grid_spec=pltpu.PrefetchScalarGridSpec(num_sc...]
    pallas_call x2, Pallas kernels: 15.9 us -> 19.7 us  [query_parts(): pl.pallas_call(query_kernel, grid_spec=pltpu.PrefetchScalarGridSpec(num_s...]
  transfers between devices with their start and end apart: 29 -> 37, of which waited for: 12 -> 15; matrix products, arithmetic and copies ran while one was open for 10% -> 12% of each run, Pallas kernels for 15% -> 19%
where the time goes in v2:
time: 201 us; the launch traced here: 198 us
  starting transfers between devices  62.2 us (31%)
  Pallas kernels  47.2 us (23%)
  waiting for transfers between devices  42.8 us (21%)
  local copies, waits for them, and re-layouts  16.5 us (8%)
  between operations  14.7 us (7%)
  other arithmetic  14.6 us (7%)
    ppermute x27, starting transfers between devices, shift(): lax.ppermute(value, axis, [(i, (i + step) % size) for i in range(size)])  42.5 us
    ppermute x27, waiting for transfers between devices, shift(): lax.ppermute(value, axis, [(i, (i + step) % size) for i in range(size)])  35.1 us
    pallas_call x2, Pallas kernels, query_parts(): pl.pallas_call(query_kernel, grid_spec=pltpu.PrefetchScalarGridSpec(num_s...  19.7 us
    pallas_call x2, Pallas kernels, forward(): pl.pallas_call(forward_kernel, grid_spec=pltpu.PrefetchScalarGridSpec(num...  17.3 us
    pallas_call x1, Pallas kernels, item_parts(): pl.pallas_call(item_kernel, grid_spec=pltpu.PrefetchScalarGridSpec(num_sc...  10.1 us
    ppermute x7, starting transfers between devices, shift_plane(): return lax.ppermute(value, PLANE, moves)  8.82 us
    all_to_all x1, waiting for transfers between devices, local(): got = lax.all_to_all(meta, 'z', 0, 0, tiled=True)  6.18 us
    all_to_all x1, starting transfers between devices, local(): got = lax.all_to_all(meta, 'z', 0, 0, tiled=True)  5.76 us
  transfers between devices with their start and end apart: 37, of which 15 were waited for; matrix products, arithmetic and copies ran while one was open for 12% of the time, Pallas kernels for 19%

profile of v2, /device:TPU:6, one launch (start us, length us, event | category | flops | bytes accessed | tf_op | source)
XLA Modules:
  0.0 198.1 jit_solution(2928193079573989661)
XLA Ops:
  7.3 2.2 %convert_element_type.82 = bf16[1,1024,256]{2,1,0:T(8,128)(2,1)} convert(f32[1,1024,256]{2,1,0:T(8,128)} %param.11) | non-fusion elementwise | flops 262144 | bytes 1572864 | tf_op jit(solution)/shard_map/convert_element_type | solution.py:232
  9.5 2.0 %collective-permute-start = (bf16[16,32,256]{2,1,0:T(8,128)(2,1)S(1)}, bf16[16,32,256]{2,1,0:T(8,128)(2,1)S(1)}, u32[]{:S(2)}, u32[]{:S(2)}) collective-permute-start(bf16[16,32,256]{2,1,0:T(8,128)(2,1)S(1)} %bitcast.136), channel_id=1, source_target_pairs={{0,32},{32,64},{64,96},{96,128},{128,160},{160,192},{192,224},{224... | collective-permute-start | bytes 786440 | tf_op jit(solution)/shard_map/ppermute | solution.py:24
  11.5 4.0 %collective-permute-start.2 = (bf16[16,32,256]{2,1,0:T(8,128)(2,1)S(1)}, bf16[16,32,256]{2,1,0:T(8,128)(2,1)S(1)}, u32[]{:S(2)}, u32[]{:S(2)}) collective-permute-start(bf16[16,32,256]{2,1,0:T(8,128)(2,1)S(1)} %bitcast.137), channel_id=1, source_target_pairs={{0,224},{32,0},{64,32},{96,64},{128,96},{160,128},{192,160},{224,1... | collective-permute-start | bytes 786440 | tf_op jit(solution)/shard_map/ppermute | solution.py:24
  18.6 5.8 %all-to-all-start = ((s32[8,1,592]{2,1,0:T(1,128)}), s32[8,1,592]{2,1,0:T(1,128)S(1)}, u32[]{:S(2)}, u32[]{:S(2)}) async-start(s32[8,1,592]{2,1,0:T(1,128)} %copy.80), calls=%async_computation | async-start | bytes 40960 | tf_op jit(solution)/shard_map/all_to_all | solution.py:274
  25.9 6.2 %all-to-all-done = s32[8,1,592]{2,1,0:T(1,128)S(1)} async-done(((s32[8,1,592]{2,1,0:T(1,128)}), s32[8,1,592]{2,1,0:T(1,128)S(1)}, u32[]{:S(2)}, u32[]{:S(2)}) %all-to-all-start) | async-done | bytes 18976 | tf_op jit(solution)/shard_map/all_to_all | solution.py:274
  34.4 2.7 %collective-permute-start.3 = (bf16[16,32,256]{2,1,0:T(8,128)(2,1)S(1)}, bf16[16,32,256]{2,1,0:T(8,128)(2,1)S(1)}, u32[]{:S(2)}, u32[]{:S(2)}) collective-permute-start(bf16[16,32,256]{2,1,0:T(8,128)(2,1)S(1)} %collective-permute-done.2.q1), channel_id=1, source_target_pairs={{0,224},{32,0},{64,32},{96,64},{128,96},{160,128},{192,160},{224,1... | collective-permute-start | bytes 786440 | tf_op jit(solution)/shard_map/ppermute | solution.py:24
  37.0 3.7 %collective-permute-done.1.q0 = bf16[16,32,256]{2,1,0:T(8,128)(2,1)S(1)} collective-permute-done((bf16[16,32,256]{2,1,0:T(8,128)(2,1)S(1)}, bf16[16,32,256]{2,1,0:T(8,128)(2,1)S(1)}, u32[]{:S(2)}, u32[]{:S(2)}) %collective-permute-start.1) | collective-permute-done | bytes 262176 | tf_op jit(solution)/shard_map/ppermute | solution.py:24
  40.9 3.7 %collective-permute-start.4 = (bf16[16,32,256]{2,1,0:T(8,128)(2,1)S(1)}, bf16[16,32,256]{2,1,0:T(8,128)(2,1)S(1)}, u32[]{:S(2)}, u32[]{:S(2)}) collective-permute-start(bf16[16,32,256]{2,1,0:T(8,128)(2,1)S(1)} %collective-permute-done.3.q3), channel_id=1, source_target_pairs={{0,224},{32,0},{64,32},{96,64},{128,96},{160,128},{192,160},{224,1... | collective-permute-start | bytes 786440 | tf_op jit(solution)/shard_map/ppermute | solution.py:24
  44.6 3.7 %collective-permute-done.5.q2 = bf16[16,32,256]{2,1,0:T(8,128)(2,1)S(1)} collective-permute-done((bf16[16,32,256]{2,1,0:T(8,128)(2,1)S(1)}, bf16[16,32,256]{2,1,0:T(8,128)(2,1)S(1)}, u32[]{:S(2)}, u32[]{:S(2)}) %collective-permute-start.5) | collective-permute-done | bytes 262176 | tf_op jit(solution)/shard_map/ppermute | solution.py:24
  52.4 8.7 %forward.2 = (bf16[8,512,256]{2,1,0:T(8,128)(2,1)}, f32[8,2,2,256]{3,2,1,0:T(2,128)}) custom-call(s32[64]{0:T(128)} %squeeze.66.blk, bf16[16,32,256]{2,1,0:T(8,128)(2,1)} %bitcast.135, bf16[16,32,256]{2,1,0:T(8,128)(2,1)} %copy-done.13, bf16[16,32,256]{2,1,0:T(8,128)(2,1)} %copy-done.12, bf16[16,32,256]{2,1,0:T(8,128)(2,1)} %copy-done.14, ...), custom_call_target="tpu_custom_call" | custom-call | flops 1073741824 | bytes 7340032 | tf_op jit(solution)/shard_map/forward/pallas_call | solution.py:75
  61.9 8.6 %forward.3 = (bf16[8,512,256]{2,1,0:T(8,128)(2,1)}, f32[8,2,2,256]{3,2,1,0:T(2,128)}) custom-call(s32[64]{0:T(128)} %squeeze.64.blk, bf16[16,32,256]{2,1,0:T(8,128)(2,1)} %copy-done.7, bf16[16,32,256]{2,1,0:T(8,128)(2,1)} %copy-done.9, bf16[16,32,256]{2,1,0:T(8,128)(2,1)} %copy-done.8, ...), custom_call_target="tpu_custom_call", output_to_operand_aliasing={{0}: (7, {}), {1}: (8, {})} | custom-call | flops 1073741824 | bytes 7340032 | tf_op jit(solution)/shard_map/forward/pallas_call | solution.py:75
  70.5 3.2 %collective-permute-start.7 = (f32[8,2,2,256]{3,2,1,0:T(2,128)}, f32[8,2,2,256]{3,2,1,0:T(2,128)S(1)}, u32[]{:S(2)}, u32[]{:S(2)}) collective-permute-start(f32[8,2,2,256]{3,2,1,0:T(2,128)} %get-tuple-element.18), channel_id=1, source_target_pairs={{0,224},{32,0},{64,32},{96,64},{128,96},{160,128},{192,160},{224,1... | collective-permute-start | bytes 98312 | tf_op jit(solution)/shard_map/ppermute | solution.py:24
  75.4 5.1 %collective-permute-start.10 = (f32[8,2,2,256]{3,2,1,0:T(2,128)}, f32[8,2,2,256]{3,2,1,0:T(2,128)S(1)}, u32[]{:S(2)}, u32[]{:S(2)}) collective-permute-start(f32[8,2,2,256]{3,2,1,0:T(2,128)} %get-tuple-element.18), channel_id=1, source_target_pairs={{0,128},{32,160},{64,192},{96,224},{128,0},{160,32},{192,64},{224,... | collective-permute-start | bytes 98312 | tf_op jit(solution)/shard_map/ppermute | solution.py:24
  80.5 5.2 %all-to-all-start.1 = ((bf16[8,512,256]{2,1,0:T(8,128)(2,1)}), bf16[8,512,256]{2,1,0:T(8,128)(2,1)}, u32[]{:S(2)}, u32[]{:S(2)}) async-start(bf16[8,512,256]{2,1,0:T(8,128)(2,1)} %get-tuple-element.19.p_ref), calls=%async_computation.1 | async-start | bytes 4194304 | tf_op jit(solution)/shard_map/all_to_all | solution.py:299
  85.7 2.5 %collective-permute-start.12 = (f32[8,2,2,256]{3,2,1,0:T(2,128)S(1)}, f32[8,2,2,256]{3,2,1,0:T(2,128)S(1)}, u32[]{:S(2)}, u32[]{:S(2)}) collective-permute-start(f32[8,2,2,256]{3,2,1,0:T(2,128)S(1)} %copy-done.15), channel_id=1, source_target_pairs={{0,64},{32,96},{64,128},{96,160},{128,192},{160,224},{192,0},{224,... | collective-permute-start | bytes 98312 | tf_op jit(solution)/shard_map/ppermute | solution.py:24
  89.4 4.3 %collective-permute-done.12 = f32[8,2,2,256]{3,2,1,0:T(2,128)S(1)} collective-permute-done((f32[8,2,2,256]{3,2,1,0:T(2,128)S(1)}, f32[8,2,2,256]{3,2,1,0:T(2,128)S(1)}, u32[]{:S(2)}, u32[]{:S(2)}) %collective-permute-start.12) | collective-permute-done | bytes 32800 | tf_op jit(solution)/shard_map/ppermute | solution.py:24
  98.1 9.9 %query_parts.3 = (bf16[16,32,256]{2,1,0:T(8,128)(2,1)}, bf16[16,32,256]{2,1,0:T(8,128)(2,1)}, bf16[16,32,256]{2,1,0:T(8,128)(2,1)}, bf16[16,32,256]{2,1,0:T(8,128)(2,1)}) custom-call(s32[64]{0:T(128)} %squeeze.64.blk, bf16[8,512,256]{2,1,0:T(8,128)(2,1)} %get-tuple-element.19.p_ref, bf16[8,1024,256]{2,1,0:T(8,128)(2,1)} %all-gather.2.cloned.1.call-done.t_ref, ...), custom_call_target="tpu_custom_call" | custom-call | flops 2147483648 | bytes 6291456 | tf_op jit(solution)/shard_map/query_parts/pallas_call | solution.py:140
  110.3 1.9 collective-permute-start.22
  113.4 9.8 %query_parts.2 = (bf16[16,32,256]{2,1,0:T(8,128)(2,1)}, bf16[16,32,256]{2,1,0:T(8,128)(2,1)}, bf16[16,32,256]{2,1,0:T(8,128)(2,1)}, bf16[16,32,256]{2,1,0:T(8,128)(2,1)}) custom-call(s32[64]{0:T(128)} %squeeze.66.blk, bf16[8,512,256]{2,1,0:T(8,128)(2,1)} %get-tuple-element.19.p_ref, bf16[8,1024,256]{2,1,0:T(8,128)(2,1)} %all-gather.2.cloned.1.call-done.t_ref, ...), custom_call_target="tpu_custom_call" | custom-call | flops 2147483648 | bytes 6291456 | tf_op jit(solution)/shard_map/query_parts/pallas_call | solution.py:140
  123.2 1.7 collective-permute-start.24
  126.5 1.8 collective-permute-start.26
  131.6 2.4 %collective-permute-start.19 = (bf16[16,32,256]{2,1,0:T(8,128)(2,1)S(1)}, bf16[16,32,256]{2,1,0:T(8,128)(2,1)S(1)}, u32[]{:S(2)}, u32[]{:S(2)}) collective-permute-start(bf16[16,32,256]{2,1,0:T(8,128)(2,1)S(1)} %add_convert_fusion.1), channel_id=1, source_target_pairs={{0,224},{32,0},{64,32},{96,64},{128,96},{160,128},{192,160},{224,1... | collective-permute-start | bytes 786440 | tf_op jit(solution)/shard_map/ppermute | solution.py:24
  134.0 6.2 %collective-permute-done.15 = bf16[16,32,256]{2,1,0:T(8,128)(2,1)S(1)} collective-permute-done((bf16[16,32,256]{2,1,0:T(8,128)(2,1)S(1)}, bf16[16,32,256]{2,1,0:T(8,128)(2,1)S(1)}, u32[]{:S(2)}, u32[]{:S(2)}) %collective-permute-start.15) | collective-permute-done | bytes 262176 | tf_op jit(solution)/shard_map/ppermute | solution.py:24
  141.3 10.1 %item_parts.1 = f32[4,256,256]{2,1,0:T(8,128)} custom-call(s32[9]{0:T(128)} %pad_add_fusion.order_ref, bf16[8,512,256]{2,1,0:T(8,128)(2,1)} %all-to-all-done.1.q_ref, f32[8,2,512]{2,1,0:T(2,128)} %copy-done.19, bf16[1024,256]{1,0:T(8,128)(2,1)} %convert_bitcast_fusion.t_ref), custom_call_target="tpu_custom_call" | custom-call | flops 4294967296 | bytes 3670016 | tf_op jit(solution)/shard_map/item_parts/pallas_call | solution.py:192
  154.7 2.1 %collective-permute-start.28 = (f32[256,256]{1,0:T(8,128)S(1)}, f32[256,256]{1,0:T(8,128)S(1)}, u32[]{:S(2)}, u32[]{:S(2)}) collective-permute-start(f32[256,256]{1,0:T(8,128)S(1)} %get-tuple-element.32), channel_id=1, source_target_pairs={{0,1},{1,2},{2,3},{3,0},{4,5},{5,6},{6,7},{7,4},{8,9},{9,10},{10,1... | collective-permute-start | bytes 786440 | tf_op jit(solution)/shard_map/ppermute | solution.py:24
  156.9 3.3 %collective-permute-start.20 = (bf16[16,32,256]{2,1,0:T(8,128)(2,1)S(1)}, bf16[16,32,256]{2,1,0:T(8,128)(2,1)S(1)}, u32[]{:S(2)}, u32[]{:S(2)}) collective-permute-start(bf16[16,32,256]{2,1,0:T(8,128)(2,1)S(1)} %add_convert_fusion), channel_id=1, source_target_pairs={{0,224},{32,0},{64,32},{96,64},{128,96},{160,128},{192,160},{224,1... | collective-permute-start | bytes 786440 | tf_op jit(solution)/shard_map/ppermute | solution.py:24
  160.2 1.7 add_convert_fusion.2
  161.9 5.3 %collective-permute-done.30 = f32[256,256]{1,0:T(8,128)S(1)} collective-permute-done((f32[256,256]{1,0:T(8,128)S(1)}, f32[256,256]{1,0:T(8,128)S(1)}, u32[]{:S(2)}, u32[]{:S(2)}) %collective-permute-start.30) | collective-permute-done | bytes 262176 | tf_op jit(solution)/shard_map/ppermute | solution.py:24
  168.8 2.7 %collective-permute-start.33 = (f32[256,256]{1,0:T(8,128)S(1)}, f32[256,256]{1,0:T(8,128)}, u32[]{:S(2)}, u32[]{:S(2)}) collective-permute-start(f32[256,256]{1,0:T(8,128)S(1)} %fusion.3), channel_id=1, source_target_pairs={{0,1},{1,2},{2,3},{3,0},{4,5},{5,6},{6,7},{7,4},{8,9},{9,10},{10,1... | collective-permute-start | bytes 786440 | tf_op jit(solution)/shard_map/ppermute | solution.py:24
  173.9 1.9 convert_add_fusion
  175.7 7.3 %collective-permute-done.33 = f32[256,256]{1,0:T(8,128)} collective-permute-done((f32[256,256]{1,0:T(8,128)S(1)}, f32[256,256]{1,0:T(8,128)}, u32[]{:S(2)}, u32[]{:S(2)}) %collective-permute-start.33) | collective-permute-done | bytes 262176 | tf_op jit(solution)/shard_map/ppermute | solution.py:24
  183.0 3.5 %collective-permute-done.31 = f32[256,256]{1,0:T(8,128)} collective-permute-done((f32[256,256]{1,0:T(8,128)S(1)}, f32[256,256]{1,0:T(8,128)}, u32[]{:S(2)}, u32[]{:S(2)}) %collective-permute-start.31) | collective-permute-done | bytes 262176 | tf_op jit(solution)/shard_map/ppermute | solution.py:24
  (215 shorter events, 40.2 us)
Async XLA Ops:
  7.2 45.1 %all-gather.2.cloned.1.call-start = ((), (), s32[]{:S(2)}) async-start(), calls=%async_computation.2 | async-start | bytes 4718592 | tf_op jit(solution)/shard_map/all_gather | solution.py:233
  9.5 23.6 %collective-permute-start = (bf16[16,32,256]{2,1,0:T(8,128)(2,1)S(1)}, bf16[16,32,256]{2,1,0:T(8,128)(2,1)S(1)}, u32[]{:S(2)}, u32[]{:S(2)}) collective-permute-start(bf16[16,32,256]{2,1,0:T(8,128)(2,1)S(1)} %bitcast.136), channel_id=1, source_target_pairs={{0,32},{32,64},{64,96},{96,128},{128,160},{160,192},{192,224},{224... | collective-permute-start | bytes 786440 | tf_op jit(solution)/shard_map/ppermute | solution.py:24
  11.5 22.9 %collective-permute-start.2 = (bf16[16,32,256]{2,1,0:T(8,128)(2,1)S(1)}, bf16[16,32,256]{2,1,0:T(8,128)(2,1)S(1)}, u32[]{:S(2)}, u32[]{:S(2)}) collective-permute-start(bf16[16,32,256]{2,1,0:T(8,128)(2,1)S(1)} %bitcast.137), channel_id=1, source_target_pairs={{0,224},{32,0},{64,32},{96,64},{128,96},{160,128},{192,160},{224,1... | collective-permute-start | bytes 786440 | tf_op jit(solution)/shard_map/ppermute | solution.py:24
  18.6 13.6 %all-to-all-start = ((s32[8,1,592]{2,1,0:T(1,128)}), s32[8,1,592]{2,1,0:T(1,128)S(1)}, u32[]{:S(2)}, u32[]{:S(2)}) async-start(s32[8,1,592]{2,1,0:T(1,128)} %copy.80), calls=%async_computation | async-start | bytes 40960 | tf_op jit(solution)/shard_map/all_to_all | solution.py:274
  33.1 7.7 %collective-permute-start.1 = (bf16[16,32,256]{2,1,0:T(8,128)(2,1)S(1)}, bf16[16,32,256]{2,1,0:T(8,128)(2,1)S(1)}, u32[]{:S(2)}, u32[]{:S(2)}) collective-permute-start(bf16[16,32,256]{2,1,0:T(8,128)(2,1)S(1)} %collective-permute-done.q2), channel_id=1, source_target_pairs={{0,32},{32,64},{64,96},{96,128},{128,160},{160,192},{192,224},{224... | collective-permute-start | bytes 786440 | tf_op jit(solution)/shard_map/ppermute | solution.py:24
  34.4 6.6 %collective-permute-start.3 = (bf16[16,32,256]{2,1,0:T(8,128)(2,1)S(1)}, bf16[16,32,256]{2,1,0:T(8,128)(2,1)S(1)}, u32[]{:S(2)}, u32[]{:S(2)}) collective-permute-start(bf16[16,32,256]{2,1,0:T(8,128)(2,1)S(1)} %collective-permute-done.2.q1), channel_id=1, source_target_pairs={{0,224},{32,0},{64,32},{96,64},{128,96},{160,128},{192,160},{224,1... | collective-permute-start | bytes 786440 | tf_op jit(solution)/shard_map/ppermute | solution.py:24
  40.8 7.6 %collective-permute-start.5 = (bf16[16,32,256]{2,1,0:T(8,128)(2,1)S(1)}, bf16[16,32,256]{2,1,0:T(8,128)(2,1)S(1)}, u32[]{:S(2)}, u32[]{:S(2)}) collective-permute-start(bf16[16,32,256]{2,1,0:T(8,128)(2,1)S(1)} %collective-permute-done.1.q0), channel_id=1, source_target_pairs={{0,32},{32,64},{64,96},{96,128},{128,160},{160,192},{192,224},{224... | collective-permute-start | bytes 786440 | tf_op jit(solution)/shard_map/ppermute | solution.py:24
  40.9 20.1 %collective-permute-start.4 = (bf16[16,32,256]{2,1,0:T(8,128)(2,1)S(1)}, bf16[16,32,256]{2,1,0:T(8,128)(2,1)S(1)}, u32[]{:S(2)}, u32[]{:S(2)}) collective-permute-start(bf16[16,32,256]{2,1,0:T(8,128)(2,1)S(1)} %collective-permute-done.3.q3), channel_id=1, source_target_pairs={{0,224},{32,0},{64,32},{96,64},{128,96},{160,128},{192,160},{224,1... | collective-permute-start | bytes 786440 | tf_op jit(solution)/shard_map/ppermute | solution.py:24
  48.4 12.7 %collective-permute-start.6 = (bf16[16,32,256]{2,1,0:T(8,128)(2,1)S(1)}, bf16[16,32,256]{2,1,0:T(8,128)(2,1)S(1)}, u32[]{:S(2)}, u32[]{:S(2)}) collective-permute-start(bf16[16,32,256]{2,1,0:T(8,128)(2,1)S(1)} %collective-permute-done.5.q2), channel_id=1, source_target_pairs={{0,32},{32,64},{64,96},{96,128},{128,160},{160,192},{192,224},{224... | collective-permute-start | bytes 786440 | tf_op jit(solution)/shard_map/ppermute | solution.py:24
  70.5 15.1 %collective-permute-start.7 = (f32[8,2,2,256]{3,2,1,0:T(2,128)}, f32[8,2,2,256]{3,2,1,0:T(2,128)S(1)}, u32[]{:S(2)}, u32[]{:S(2)}) collective-permute-start(f32[8,2,2,256]{3,2,1,0:T(2,128)} %get-tuple-element.18), channel_id=1, source_target_pairs={{0,224},{32,0},{64,32},{96,64},{128,96},{160,128},{192,160},{224,1... | collective-permute-start | bytes 98312 | tf_op jit(solution)/shard_map/ppermute | solution.py:24
  74.6 13.6 %collective-permute-start.8 = (f32[8,2,2,256]{3,2,1,0:T(2,128)}, f32[8,2,2,256]{3,2,1,0:T(2,128)S(1)}, u32[]{:S(2)}, u32[]{:S(2)}) collective-permute-start(f32[8,2,2,256]{3,2,1,0:T(2,128)} %get-tuple-element.18), channel_id=1, source_target_pairs={{0,192},{32,224},{64,0},{96,32},{128,64},{160,96},{192,128},{224,1... | collective-permute-start | bytes 98312 | tf_op jit(solution)/shard_map/ppermute | solution.py:24
  74.6 14.8 %collective-permute-start.9 = (f32[8,2,2,256]{3,2,1,0:T(2,128)}, f32[8,2,2,256]{3,2,1,0:T(2,128)S(1)}, u32[]{:S(2)}, u32[]{:S(2)}) collective-permute-start(f32[8,2,2,256]{3,2,1,0:T(2,128)} %get-tuple-element.18), channel_id=1, source_target_pairs={{0,160},{32,192},{64,224},{96,0},{128,32},{160,64},{192,96},{224,1... | collective-permute-start | bytes 98312 | tf_op jit(solution)/shard_map/ppermute | solution.py:24
  75.4 14.0 %collective-permute-start.10 = (f32[8,2,2,256]{3,2,1,0:T(2,128)}, f32[8,2,2,256]{3,2,1,0:T(2,128)S(1)}, u32[]{:S(2)}, u32[]{:S(2)}) collective-permute-start(f32[8,2,2,256]{3,2,1,0:T(2,128)} %get-tuple-element.18), channel_id=1, source_target_pairs={{0,128},{32,160},{64,192},{96,224},{128,0},{160,32},{192,64},{224,... | collective-permute-start | bytes 98312 | tf_op jit(solution)/shard_map/ppermute | solution.py:24
  80.5 8.9 %collective-permute-start.11 = (f32[8,2,2,256]{3,2,1,0:T(2,128)}, f32[8,2,2,256]{3,2,1,0:T(2,128)S(1)}, u32[]{:S(2)}, u32[]{:S(2)}) collective-permute-start(f32[8,2,2,256]{3,2,1,0:T(2,128)} %get-tuple-element.18), channel_id=1, source_target_pairs={{0,96},{32,128},{64,160},{96,192},{128,224},{160,0},{192,32},{224,... | collective-permute-start | bytes 98312 | tf_op jit(solution)/shard_map/ppermute | solution.py:24
  80.5 60.8 %all-to-all-start.1 = ((bf16[8,512,256]{2,1,0:T(8,128)(2,1)}), bf16[8,512,256]{2,1,0:T(8,128)(2,1)}, u32[]{:S(2)}, u32[]{:S(2)}) async-start(bf16[8,512,256]{2,1,0:T(8,128)(2,1)} %get-tuple-element.19.p_ref), calls=%async_computation.1 | async-start | bytes 4194304 | tf_op jit(solution)/shard_map/all_to_all | solution.py:299
  85.7 8.0 %collective-permute-start.12 = (f32[8,2,2,256]{3,2,1,0:T(2,128)S(1)}, f32[8,2,2,256]{3,2,1,0:T(2,128)S(1)}, u32[]{:S(2)}, u32[]{:S(2)}) collective-permute-start(f32[8,2,2,256]{3,2,1,0:T(2,128)S(1)} %copy-done.15), channel_id=1, source_target_pairs={{0,64},{32,96},{64,128},{96,160},{128,192},{160,224},{192,0},{224,... | collective-permute-start | bytes 98312 | tf_op jit(solution)/shard_map/ppermute | solution.py:24
  108.1 23.4 %collective-permute-start.18 = (bf16[16,32,256]{2,1,0:T(8,128)(2,1)}, bf16[16,32,256]{2,1,0:T(8,128)(2,1)S(1)}, u32[]{:S(2)}, u32[]{:S(2)}) collective-permute-start(bf16[16,32,256]{2,1,0:T(8,128)(2,1)} %get-tuple-element.25), channel_id=1, source_target_pairs={{0,224},{32,0},{64,32},{96,64},{128,96},{160,128},{192,160},{224,1... | collective-permute-start | bytes 786440 | tf_op jit(solution)/shard_map/ppermute | solution.py:24
  109.0 21.2 %collective-permute-start.14 = (bf16[16,32,256]{2,1,0:T(8,128)(2,1)}, bf16[16,32,256]{2,1,0:T(8,128)(2,1)S(1)}, u32[]{:S(2)}, u32[]{:S(2)}) collective-permute-start(bf16[16,32,256]{2,1,0:T(8,128)(2,1)} %get-tuple-element.21), channel_id=1, source_target_pairs={{0,32},{32,64},{64,96},{96,128},{128,160},{160,192},{192,224},{224... | collective-permute-start | bytes 786440 | tf_op jit(solution)/shard_map/ppermute | solution.py:24
  110.2 13.0 %collective-permute-start.21 = (f32[2,512]{1,0:T(2,128)S(1)}, f32[2,512]{1,0:T(2,128)S(1)}, u32[]{:S(2)}, u32[]{:S(2)}) collective-permute-start(f32[2,512]{1,0:T(2,128)S(1)} %get-tuple-element.43), channel_id=1, source_target_pairs={{0,4},{4,0},{8,12},{12,8},{16,20},{20,16},{24,28},{28,24},{1,5},{5... | collective-permute-start | bytes 12296 | tf_op jit(solution)/shard_map/ppermute | solution.py:37
  110.3 14.7 %collective-permute-start.22 = (f32[2,512]{1,0:T(2,128)S(1)}, f32[2,512]{1,0:T(2,128)S(1)}, u32[]{:S(2)}, u32[]{:S(2)}) collective-permute-start(f32[2,512]{1,0:T(2,128)S(1)} %get-tuple-element.44), channel_id=1, source_target_pairs={{0,8},{4,12},{8,16},{12,20},{16,24},{20,28},{24,0},{28,4},{1,9},{5... | collective-permute-start | bytes 12296 | tf_op jit(solution)/shard_map/ppermute | solution.py:37
  112.1 14.4 %collective-permute-start.23 = (f32[2,512]{1,0:T(2,128)S(1)}, f32[2,512]{1,0:T(2,128)S(1)}, u32[]{:S(2)}, u32[]{:S(2)}) collective-permute-start(f32[2,512]{1,0:T(2,128)S(1)} %get-tuple-element.45), channel_id=1, source_target_pairs={{0,12},{4,8},{8,20},{12,16},{16,28},{20,24},{24,4},{28,0},{1,13},{... | collective-permute-start | bytes 12296 | tf_op jit(solution)/shard_map/ppermute | solution.py:37
  130.2 9.9 %collective-permute-start.15 = (bf16[16,32,256]{2,1,0:T(8,128)(2,1)S(1)}, bf16[16,32,256]{2,1,0:T(8,128)(2,1)S(1)}, u32[]{:S(2)}, u32[]{:S(2)}) collective-permute-start(bf16[16,32,256]{2,1,0:T(8,128)(2,1)S(1)} %add_convert_fusion.4), channel_id=1, source_target_pairs={{0,32},{32,64},{64,96},{96,128},{128,160},{160,192},{192,224},{224... | collective-permute-start | bytes 786440 | tf_op jit(solution)/shard_map/ppermute | solution.py:24
  131.6 25.2 %collective-permute-start.19 = (bf16[16,32,256]{2,1,0:T(8,128)(2,1)S(1)}, bf16[16,32,256]{2,1,0:T(8,128)(2,1)S(1)}, u32[]{:S(2)}, u32[]{:S(2)}) collective-permute-start(bf16[16,32,256]{2,1,0:T(8,128)(2,1)S(1)} %add_convert_fusion.1), channel_id=1, source_target_pairs={{0,224},{32,0},{64,32},{96,64},{128,96},{160,128},{192,160},{224,1... | collective-permute-start | bytes 786440 | tf_op jit(solution)/shard_map/ppermute | solution.py:24
  141.2 19.0 %collective-permute-start.16 = (bf16[16,32,256]{2,1,0:T(8,128)(2,1)S(1)}, bf16[16,32,256]{2,1,0:T(8,128)(2,1)}, u32[]{:S(2)}, u32[]{:S(2)}) collective-permute-start(bf16[16,32,256]{2,1,0:T(8,128)(2,1)S(1)} %add_convert_fusion.3), channel_id=1, source_target_pairs={{0,32},{32,64},{64,96},{96,128},{128,160},{160,192},{192,224},{224... | collective-permute-start | bytes 786440 | tf_op jit(solution)/shard_map/ppermute | solution.py:24
  152.7 14.5 %collective-permute-start.30 = (f32[256,256]{1,0:T(8,128)S(1)}, f32[256,256]{1,0:T(8,128)S(1)}, u32[]{:S(2)}, u32[]{:S(2)}) collective-permute-start(f32[256,256]{1,0:T(8,128)S(1)} %get-tuple-element.33), channel_id=1, source_target_pairs={{0,3},{1,0},{2,1},{3,2},{4,7},{5,4},{6,5},{7,6},{8,11},{9,8},{10,9... | collective-permute-start | bytes 786440 | tf_op jit(solution)/shard_map/ppermute | solution.py:24
  153.6 13.6 %collective-permute-start.29 = (f32[256,256]{1,0:T(8,128)S(1)}, f32[256,256]{1,0:T(8,128)S(1)}, u32[]{:S(2)}, u32[]{:S(2)}) collective-permute-start(f32[256,256]{1,0:T(8,128)S(1)} %get-tuple-element.34), channel_id=1, source_target_pairs={{0,2},{1,3},{2,0},{3,1},{4,6},{5,7},{6,4},{7,5},{8,10},{9,11},{10,... | collective-permute-start | bytes 786440 | tf_op jit(solution)/shard_map/ppermute | solution.py:24
  154.7 13.1 %collective-permute-start.28 = (f32[256,256]{1,0:T(8,128)S(1)}, f32[256,256]{1,0:T(8,128)S(1)}, u32[]{:S(2)}, u32[]{:S(2)}) collective-permute-start(f32[256,256]{1,0:T(8,128)S(1)} %get-tuple-element.32), channel_id=1, source_target_pairs={{0,1},{1,2},{2,3},{3,0},{4,5},{5,6},{6,7},{7,4},{8,9},{9,10},{10,1... | collective-permute-start | bytes 786440 | tf_op jit(solution)/shard_map/ppermute | solution.py:24
  156.9 17.0 %collective-permute-start.20 = (bf16[16,32,256]{2,1,0:T(8,128)(2,1)S(1)}, bf16[16,32,256]{2,1,0:T(8,128)(2,1)S(1)}, u32[]{:S(2)}, u32[]{:S(2)}) collective-permute-start(bf16[16,32,256]{2,1,0:T(8,128)(2,1)S(1)} %add_convert_fusion), channel_id=1, source_target_pairs={{0,224},{32,0},{64,32},{96,64},{128,96},{160,128},{192,160},{224,1... | collective-permute-start | bytes 786440 | tf_op jit(solution)/shard_map/ppermute | solution.py:24
  161.9 12.0 %collective-permute-start.17 = (bf16[16,32,256]{2,1,0:T(8,128)(2,1)}, bf16[16,32,256]{2,1,0:T(8,128)(2,1)}, u32[]{:S(2)}, u32[]{:S(2)}) collective-permute-start(bf16[16,32,256]{2,1,0:T(8,128)(2,1)} %add_convert_fusion.2), channel_id=1, source_target_pairs={{0,32},{32,64},{64,96},{96,128},{128,160},{160,192},{192,224},{224... | collective-permute-start | bytes 786440 | tf_op jit(solution)/shard_map/ppermute | solution.py:24
  168.8 14.2 %collective-permute-start.33 = (f32[256,256]{1,0:T(8,128)S(1)}, f32[256,256]{1,0:T(8,128)}, u32[]{:S(2)}, u32[]{:S(2)}) collective-permute-start(f32[256,256]{1,0:T(8,128)S(1)} %fusion.3), channel_id=1, source_target_pairs={{0,1},{1,2},{2,3},{3,0},{4,5},{5,6},{6,7},{7,4},{8,9},{9,10},{10,1... | collective-permute-start | bytes 786440 | tf_op jit(solution)/shard_map/ppermute | solution.py:24
  171.5 11.5 %collective-permute-start.32 = (f32[256,256]{1,0:T(8,128)S(1)}, f32[256,256]{1,0:T(8,128)}, u32[]{:S(2)}, u32[]{:S(2)}) collective-permute-start(f32[256,256]{1,0:T(8,128)S(1)} %fusion.3), channel_id=1, source_target_pairs={{0,2},{1,3},{2,0},{3,1},{4,6},{5,7},{6,4},{7,5},{8,10},{9,11},{10,... | collective-permute-start | bytes 786440 | tf_op jit(solution)/shard_map/ppermute | solution.py:24
  171.7 14.8 %collective-permute-start.31 = (f32[256,256]{1,0:T(8,128)S(1)}, f32[256,256]{1,0:T(8,128)}, u32[]{:S(2)}, u32[]{:S(2)}) collective-permute-start(f32[256,256]{1,0:T(8,128)S(1)} %fusion.3), channel_id=1, source_target_pairs={{0,3},{1,0},{2,1},{3,2},{4,7},{5,4},{6,5},{7,6},{8,11},{9,8},{10,9... | collective-permute-start | bytes 786440 | tf_op jit(solution)/shard_map/ppermute | solution.py:24
  (26 other events, 268.5 us)
Sparse Core Ops, SparseCore 0:
  10.5 37.5 all-gather.1

commit v3 on v2

v3 whole, which is shorter than its diff:
```python
import functools

import jax
import jax.numpy as jnp
from jax import lax
from jax.experimental import pallas as pl
from jax.experimental.pallas import tpu as pltpu
from jax.sharding import Mesh, PartitionSpec as P

MOST = 2
EMPTY = 1e30
NEAR = (0, 1, 7, 6)
FAR = (2, 3, 4, 5)
ORDER = NEAR + FAR
PLANE = ("y", "c")
F32 = jnp.float32
BF16 = jnp.bfloat16
NT = (((1,), (1,)), ((), ()))
TN = (((0,), (0,)), ((), ()))
TILE = 256
VMEM = 24 << 20


def shift(value, axis, step):
    size = lax.axis_size(axis)
    return lax.ppermute(value, axis, [(i, (i + step) % size) for i in range(size)])


def tile_ids(start, shape):
    return lax.broadcasted_iota(jnp.int32, shape, 0) + start


def pack_kernel(blk, *refs):
    sources, p_ref = refs[:-1], refs[-1]
    step = pl.program_id(0)
    block_rows = sources[0].shape[1]
    per_step = len(sources) * MOST
    for slot in range(per_step):
        b = blk[step * per_step + slot]
        p_ref[0, pl.ds(slot * block_rows, block_rows), :] = sources[slot // MOST][b]


def pack(sources, blk, plane):
    shape = sources[0].shape
    width = len(sources) * MOST * shape[1]
    return pl.pallas_call(
        pack_kernel,
        grid_spec=pltpu.PrefetchScalarGridSpec(
            num_scalar_prefetch=1,
            grid=(plane,),
            in_specs=[pl.BlockSpec(shape, lambda j, blk: (0, 0, 0))] * len(sources),
            out_specs=pl.BlockSpec((1, width, shape[2]), lambda j, blk: (j, 0, 0)),
        ),
        out_shape=jax.ShapeDtypeStruct((plane, width, shape[2]), BF16),
        compiler_params=pltpu.CompilerParams(vmem_limit_bytes=VMEM),
        cost_estimate=pl.CostEstimate(
            flops=0, bytes_accessed=4 * plane * width * shape[2], transcendentals=0
        ),
        name="pack",
    )(blk, *sources)


def forward_kernel(p_ref, t_ref, tgt_ref, stat_ref, s_ref):
    q = p_ref[0]
    items = t_ref.shape[1]
    width = q.shape[0]
    tgt = tgt_ref[0]
    high = jnp.full((8, width), -jnp.inf, F32)
    pick = jnp.zeros((8, width), F32)
    for start in range(0, items, TILE):
        s = lax.dot_general(t_ref[0, pl.ds(start, TILE), :], q, NT, preferred_element_type=F32)
        s_ref[pl.ds(start, TILE), :] = s
        high = jnp.maximum(high, jnp.max(s.reshape(TILE // 8, 8, width), axis=0))
        hit = jnp.where(tile_ids(start, s.shape) == tgt, s, 0.0)
        pick = pick + jnp.sum(hit.reshape(TILE // 8, 8, width), axis=0)
    top = jnp.max(high, axis=0, keepdims=True)
    mass = jnp.zeros((8, width), F32)
    for start in range(0, items, TILE):
        e = jnp.exp(s_ref[pl.ds(start, TILE), :] - top)
        mass = mass + jnp.sum(e.reshape(TILE // 8, 8, width), axis=0)
    stat_ref[0, 0:1, :] = top + jnp.log(jnp.sum(mass, axis=0, keepdims=True))
    stat_ref[0, 1:2, :] = jnp.sum(pick, axis=0, keepdims=True)


def forward(packed, targets, tables):
    planes, items, features = tables.shape
    width = packed.shape[1]
    return pl.pallas_call(
        forward_kernel,
        grid=(planes,),
        in_specs=[
            pl.BlockSpec((1, width, features), lambda j: (j, 0, 0)),
            pl.BlockSpec((1, items, features), lambda j: (j, 0, 0)),
            pl.BlockSpec((1, 1, width), lambda j: (j, 0, 0)),
        ],
        out_specs=pl.BlockSpec((1, 2, width), lambda j: (j, 0, 0)),
        out_shape=jax.ShapeDtypeStruct((planes, 2, width), F32),
        scratch_shapes=[pltpu.VMEM((items, width), F32)],
        compiler_params=pltpu.CompilerParams(vmem_limit_bytes=VMEM),
        cost_estimate=pl.CostEstimate(
            flops=2 * planes * width * items * features,
            bytes_accessed=planes * items * features * 2 + planes * width * features * 2,
            transcendentals=planes * width * items,
        ),
        name="forward",
    )(packed, tables, targets)


def query_kernel(half, blk, p_ref, t_ref, line_ref, g0, g1, g2, g3, c_ref, acc_ref):
    step = pl.program_id(0)

    @pl.when(step == 0)
    def _():
        acc_ref[...] = jnp.zeros_like(acc_ref)

    q = p_ref[0]
    lse = line_ref[0, 0:1, :]
    tgt = line_ref[0, 1:2, :].astype(jnp.int32)
    items = t_ref.shape[1]
    for start in range(0, items, TILE):
        s = lax.dot_general(t_ref[0, pl.ds(start, TILE), :], q, NT, preferred_element_type=F32)
        e = jnp.exp(s - lse)
        c = jnp.where(tile_ids(start, s.shape) == tgt, e - 1.0, e)
        c_ref[pl.ds(start, TILE), :] = c.astype(BF16)
    g = lax.dot_general(c_ref[...], t_ref[0], TN, preferred_element_type=F32)
    block_rows = g0.shape[1]
    for slot in range(8):
        b = blk[step * 16 + half * 8 + slot]
        acc_ref[slot // MOST, b] += g[slot * block_rows:(slot + 1) * block_rows, :]

    @pl.when(step == pl.num_programs(0) - 1)
    def _():
        for i, out in enumerate((g0, g1, g2, g3)):
            out[...] = acc_ref[i].astype(BF16)


def query_parts(packed, blk, lines, tables, half, blocks, block_rows):
    planes, items, features = tables.shape
    width = packed.shape[1] // 2
    out = jax.ShapeDtypeStruct((blocks, block_rows, features), BF16)
    return pl.pallas_call(
        functools.partial(query_kernel, half),
        grid_spec=pltpu.PrefetchScalarGridSpec(
            num_scalar_prefetch=1,
            grid=(planes,),
            in_specs=[
                pl.BlockSpec((1, width, features), lambda j, blk: (j, half, 0)),
                pl.BlockSpec((1, items, features), lambda j, blk: (j, 0, 0)),
                pl.BlockSpec((1, 2, width), lambda j, blk: (j, 0, half)),
            ],
            out_specs=[pl.BlockSpec(out.shape, lambda j, blk: (0, 0, 0))] * 4,
            scratch_shapes=[
                pltpu.VMEM((items, width), BF16),
                pltpu.VMEM((4, blocks, block_rows, features), F32),
            ],
        ),
        out_shape=[out] * 4,
        compiler_params=pltpu.CompilerParams(vmem_limit_bytes=VMEM),
        cost_estimate=pl.CostEstimate(
            flops=4 * planes * width * items * features,
            bytes_accessed=planes * items * features * 2 + 2 * planes * width * features * 2,
            transcendentals=planes * width * items,
        ),
        name="query_parts",
    )(blk, packed, tables, lines)


def item_kernel(places, quarters, x_ref, q_ref, line_ref, t_ref, *outs):
    step = pl.program_id(0)

    @pl.when(step == 0)
    def _():
        for out in outs:
            out[...] = jnp.zeros_like(out)

    rows = t_ref.shape[0] // quarters
    mine = x_ref[0]
    q = q_ref[0]
    lse = line_ref[0, 0:1, :]
    tgt = line_ref[0, 1:2, :].astype(jnp.int32)
    per_out = len(outs) // len(places)
    for i, place in enumerate(places):
        start = pl.multiple_of(lax.rem(place + mine, quarters) * rows, rows)
        s = lax.dot_general(t_ref[pl.ds(start, rows), :], q, NT, preferred_element_type=F32)
        e = jnp.exp(s - lse)
        c = jnp.where(tile_ids(start, s.shape) == tgt, e - 1.0, e).astype(BF16)
        part = jnp.dot(c, q, preferred_element_type=F32)
        cut = rows // per_out
        for n in range(per_out):
            outs[i * per_out + n][...] += part[n * cut:(n + 1) * cut]


def item_parts(places, pieces, x, rows, lines, table16, quarters):
    sources, width, features = rows.shape
    items = table16.shape[0]
    out = jax.ShapeDtypeStruct((items // quarters // pieces, features), F32)
    share = len(places)
    return pl.pallas_call(
        functools.partial(item_kernel, places, quarters),
        grid_spec=pltpu.PrefetchScalarGridSpec(
            num_scalar_prefetch=1,
            grid=(sources,),
            in_specs=[
                pl.BlockSpec((1, width, features), lambda j, o: (j, 0, 0)),
                pl.BlockSpec((1, 2, width), lambda j, o: (j, 0, 0)),
                pl.BlockSpec((items, features), lambda j, o: (0, 0)),
            ],
            out_specs=[pl.BlockSpec(out.shape, lambda j, o: (0, 0))] * (share * pieces),
        ),
        out_shape=[out] * (share * pieces),
        compiler_params=pltpu.CompilerParams(vmem_limit_bytes=VMEM),
        cost_estimate=pl.CostEstimate(
            flops=share * sources * width * items * features,
            bytes_accessed=2 * sources * width * features + items * features * 3,
            transcendentals=share * sources * width * items // 4,
        ),
        name="item_parts",
    )(x, rows, lines, table16)


def update_kernel(x_ref, own, after, before, far_a, far_b, t_ref, a_ref, nt_ref, na_ref):
    quarters = pl.num_programs(0)
    rel = lax.rem(pl.program_id(0) - x_ref[0] + quarters, quarters)
    cut = far_a.shape[0]

    def write(start, summed):
        span = pl.ds(start, summed.shape[0])
        accum = a_ref[span, :] + summed * summed
        na_ref[span, :] = accum
        nt_ref[span, :] = t_ref[span, :] - 0.5 * summed / jnp.sqrt(accum)

    for place, ref in ((0, own), (1, after), (3, before)):

        @pl.when(rel == place)
        def _():
            write(0, ref[...])

    @pl.when(rel == 2)
    def _():
        write(0, far_a[...])
        write(cut, far_b[...])


def update(x, own, after, before, far_a, far_b, table, accum, quarters):
    items, features = table.shape
    whole = pl.BlockSpec(own.shape, lambda i, x: (0, 0))
    part = pl.BlockSpec(far_a.shape, lambda i, x: (0, 0))
    block = pl.BlockSpec((items // quarters, features), lambda i, x: (i, 0))
    return pl.pallas_call(
        update_kernel,
        grid_spec=pltpu.PrefetchScalarGridSpec(
            num_scalar_prefetch=1,
            grid=(quarters,),
            in_specs=[whole] * 3 + [part] * 2 + [block] * 2,
            out_specs=[block] * 2,
        ),
        out_shape=[jax.ShapeDtypeStruct(table.shape, F32)] * 2,
        compiler_params=pltpu.CompilerParams(vmem_limit_bytes=VMEM),
        name="update",
    )(x, own, after, before, far_a, far_b, table, accum)


def local(queries, clusters, positives, owner_of, table, accum):
    z_size = lax.axis_size("z")
    x_size = lax.axis_size("x")
    z = lax.axis_index("z")
    x = lax.axis_index("x").reshape(1)
    local_rows, features = queries.shape
    block_count, picks = clusters.shape
    block_rows = local_rows // block_count
    items = table.shape[1]
    owners = owner_of.shape[0]
    plane = owners // z_size
    pair_count = block_count * picks

    table16 = table[0].astype(BF16)
    tables = lax.all_gather(table16, PLANE)

    here = queries.reshape(block_count, block_rows, features)
    by_source = {0: here, 7: shift(here, "z", 1), 1: shift(here, "z", -1)}
    clusters, positives, by_source[7], by_source[1] = lax.optimization_barrier(
        (clusters, positives, by_source[7], by_source[1])
    )
    by_source[6] = shift(by_source[7], "z", 1)
    by_source[2] = shift(by_source[1], "z", -1)
    by_source[5] = shift(by_source[6], "z", 1)
    by_source[3] = shift(by_source[2], "z", -1)

    flat_lists = clusters.reshape(pair_count)
    catalog_ids = jnp.arange(owners, dtype=jnp.int32)
    lookup = flat_lists[:, None] == catalog_ids[None, :]
    destination = jnp.sum(jnp.where(lookup, owner_of[None, :], 0), axis=1)
    pair_ids = jnp.arange(pair_count, dtype=jnp.int32)
    earlier = (destination[:, None] == destination[None, :]) & (
        pair_ids[:, None] > pair_ids[None, :]
    )
    rank_in = jnp.sum(earlier.astype(jnp.int32), axis=1)
    slot_of_pair = destination * MOST + rank_in
    slot_count = owners * MOST
    matches = slot_of_pair[None, :] == jnp.arange(slot_count, dtype=jnp.int32)[:, None]
    filled = jnp.any(matches, axis=1)
    source_pair = jnp.sum(jnp.where(matches, pair_ids[None, :], 0), axis=1)
    which_block = source_pair // picks
    which_pick = source_pair % picks
    chosen = positives.reshape(block_count, block_rows)[which_block]
    inside = filled[:, None] & (chosen // items == which_pick[:, None])
    send_targets = jnp.where(inside, chosen - which_pick[:, None] * items, -1)
    block_or_none = jnp.where(filled, which_block, -1)
    per_plane = plane * MOST
    meta = jnp.concatenate(
        [
            send_targets.reshape(z_size, per_plane * block_rows),
            block_or_none.reshape(z_size, per_plane),
            jnp.broadcast_to(slot_of_pair[None, :], (z_size, pair_count)),
        ],
        axis=1,
    )
    got = lax.all_to_all(meta, "z", 0, 0, tiled=True)
    got, last = lax.optimization_barrier((got, by_source[5]))
    by_source[4] = shift(last, "z", 1)
    order = jnp.array(ORDER, jnp.int32)
    got = got[(z + order) % z_size]
    width = z_size * MOST * block_rows
    cut = per_plane * block_rows
    targets = got[:, :cut].reshape(z_size, plane, MOST, block_rows)
    targets = targets.transpose(1, 0, 2, 3).reshape(plane, 1, width)
    named = got[:, cut:cut + per_plane].reshape(z_size, plane, MOST).transpose(1, 0, 2)
    named = named.reshape(plane * per_plane)
    blk = jnp.maximum(named, 0)

    pair_slot = got[:, cut + per_plane:]
    pair_owner = pair_slot // MOST
    pair_from = (pair_owner // plane - z) % z_size
    pair_rel = (order[:, None] - pair_from) % z_size
    pair_place = jnp.zeros_like(pair_rel)
    for place, d in enumerate(ORDER):
        pair_place = jnp.where(pair_rel == d, place, pair_place)
    pair_row = (pair_from % 2 * 4 + pair_from // 2) * plane + pair_owner % plane
    pair_row = (pair_row * 2 * z_size + pair_place) * MOST + pair_slot % MOST

    packed = pack([by_source[d] for d in ORDER], blk, plane)
    rows = lax.all_to_all(packed, PLANE, 0, 0, tiled=True)
    stats = forward(packed, targets, tables)

    even = jnp.stack([stats] + [shift(stats, "z", -e) for e in (2, 4, 6)])
    all_stats = jnp.stack([even, shift(even, "z", -1)]).reshape(-1, block_rows)
    part = all_stats[pair_row.reshape(-1)].reshape(z_size, block_count, picks, block_rows)
    pick = all_stats[pair_row[0] + z_size * MOST].reshape(block_count, picks, block_rows)
    top = jnp.max(part, axis=2)
    lse = top + jnp.log(jnp.sum(jnp.exp(part - top[:, :, None]), axis=2))
    losses = (lse[0] - jnp.sum(pick, axis=1)).reshape(local_rows)
    lse_rows = lse.reshape(z_size * block_count, block_rows)
    first = jnp.arange(z_size, dtype=jnp.int32).reshape(1, z_size, 1) * block_count
    lse_at = (blk.reshape(plane, z_size, MOST) + first).reshape(-1)
    lse_slots = jnp.where(named[:, None] < 0, F32(EMPTY), lse_rows[lse_at])
    lines = jnp.concatenate(
        [lse_slots.reshape(plane, 1, width), targets.astype(F32)], axis=1
    )
    got_lines = lax.all_to_all(lines, PLANE, 0, 0, tiled=True)

    far_g = query_parts(packed, blk, lines, tables, 1, block_count, block_rows)
    near_g = query_parts(packed, blk, lines, tables, 0, block_count, block_rows)
    grads = dict(zip(ORDER, list(near_g) + list(far_g)))

    def add(a, b):
        return (a.astype(F32) + b.astype(F32)).astype(BF16)

    go_right = shift(grads[4], "z", 1)
    go_right = shift(add(go_right, grads[3]), "z", 1)
    go_right = shift(add(go_right, grads[2]), "z", 1)
    go_right = shift(add(go_right, grads[1]), "z", 1)
    go_left = shift(grads[5], "z", -1)
    go_left = shift(add(go_left, grads[6]), "z", -1)
    go_left = shift(add(go_left, grads[7]), "z", -1)
    query_grads = (
        grads[0].astype(F32) + go_right.astype(F32) + go_left.astype(F32)
    ).reshape(local_rows, features)

    far_a, far_b = item_parts((2,), 2, x, rows, got_lines, table16, x_size)
    own, after, before = item_parts((0, 1, 3), 1, x, rows, got_lines, table16, x_size)
    half = far_a.shape[0]
    far_a = shift(far_a, "x", 1)
    far_b = shift(far_b, "x", -1)
    after = shift(jnp.concatenate([after[:half] + far_a, after[half:]]), "x", 1)
    before = shift(jnp.concatenate([before[:half], before[half:] + far_b]), "x", -1)
    own = own + after + before
    before = shift(own, "x", 1)
    after = shift(own, "x", -1)
    far_a = shift(before[:half], "x", 1)
    far_b = shift(after[half:], "x", -1)
    new_table, new_accum = update(
        x, own, after, before, far_a, far_b, table[0], accum[0], x_size
    )
    return (losses, query_grads, new_table[None], new_accum[None])


def solution(mesh):
    axes = ("z", "y", "c", "x")
    split = Mesh(mesh.devices.reshape(8, 4, 2, 4), axes)
    placed = (
        P(axes, None),
        P(axes, None),
        P(axes),
        P(),
        P(axes[:3], None, None),
        P(axes[:3], None, None),
    )
    return jax.shard_map(
        local,
        mesh=split,
        in_specs=placed,
        out_specs=(
            P(axes),
            P(axes, None),
            P(axes[:3], None, None),
            P(axes[:3], None, None),
        ),
        check_vma=False,
    )
```

time: 201 us -> 180 us (0.90)
  waiting for transfers between devices: 42.8 us -> 32 us
  Pallas kernels: 47.2 us -> 40.8 us
  starting transfers between devices: 62.2 us -> 57.1 us
  local copies, waits for them, and re-layouts: 16.5 us -> 21.5 us
  other arithmetic: 14.6 us -> 11 us
    ppermute x27 -> x26, waiting for transfers between devices: 35.1 us -> 24.1 us  [shift(): lax.ppermute(value, axis, [(i, (i + step) % size) for i in range(size)])]
    ppermute x7 -> x0, starting transfers between devices: 8.82 us -> none  [shift_plane(): return lax.ppermute(value, PLANE, moves)]
    pallas_call x5 -> x7, Pallas kernels: 47.2 us -> 40.8 us  [the longest x2 16.7 us: query_parts(): pl.pallas_call(functools.partial(query_kernel, half), grid_spec=pltpu.Pre...]
    unnamed x57 -> x39, local copies, waits for them, and re-layouts: 2.85 us -> 8.71 us
    squeeze x7 -> x0, local copies, waits for them, and re-layouts: 5.29 us -> none  [the longest x2 1.39 us: local(): held = forward(near_q, blk[0], targets[0], tables, 0)]
    all_to_all x0 -> x1, starting transfers between devices: none -> 4.45 us  [local(): got_lines = lax.all_to_all(lines, PLANE, 0, 0, tiled=True)]
    ppermute x27 -> x26, starting transfers between devices: 42.5 us -> 42.4 us  [shift(): lax.ppermute(value, axis, [(i, (i + step) % size) for i in range(size)])]
  transfers between devices with their start and end apart: 37 -> 30, of which waited for: 15 -> 12; matrix products, arithmetic and copies ran while one was open for 12% -> 11% of each run, Pallas kernels for 19% -> 23%
where the time goes in v3:
time: 180 us; the launch traced here: 177 us
  starting transfers between devices  57.1 us (32%)
  Pallas kernels  40.8 us (23%)
  waiting for transfers between devices  32 us (18%)
  local copies, waits for them, and re-layouts  21.5 us (12%)
  between operations  14.6 us (8%)
  other arithmetic  11 us (6%)
    ppermute x26, starting transfers between devices, shift(): lax.ppermute(value, axis, [(i, (i + step) % size) for i in range(size)])  42.4 us
    ppermute x26, waiting for transfers between devices, shift(): lax.ppermute(value, axis, [(i, (i + step) % size) for i in range(size)])  24.1 us
    pallas_call x2, Pallas kernels, query_parts(): pl.pallas_call(functools.partial(query_kernel, half), grid_spec=pltpu.Pre...  16.7 us
    pallas_call x2, Pallas kernels, item_parts(): pl.pallas_call(functools.partial(item_kernel, places, quarters), grid_spe...  9.58 us
    unnamed x39, local copies, waits for them, and re-layouts  8.71 us
    pallas_call x1, Pallas kernels, forward(): pl.pallas_call(forward_kernel, grid=(planes,), in_specs=[pl.BlockSpec((1,...  8.02 us
    all_to_all x1, waiting for transfers between devices, local(): got = lax.all_to_all(meta, 'z', 0, 0, tiled=True)  7.79 us
    all_to_all x1, starting transfers between devices, local(): got = lax.all_to_all(meta, 'z', 0, 0, tiled=True)  5.8 us
  transfers between devices with their start and end apart: 30, of which 12 were waited for; matrix products, arithmetic and copies ran while one was open for 11% of the time, Pallas kernels for 23%

profile of v3, /device:TPU:6, one launch (start us, length us, event | category | flops | bytes accessed | tf_op | source)
XLA Modules:
  0.0 177.0 jit_solution(13418622311045761752)
XLA Ops:
  7.3 2.5 %bitcast_convert_fusion = (bf16[1024,256]{1,0:T(8,128)(2,1)S(1)}, bf16[1,1024,256]{2,1,0:T(8,128)(2,1)}) fusion(f32[1,1024,256]{2,1,0:T(8,128)} %param.11), kind=kLoop, calls=%fused_computation.121 | loop fusion | flops 524288 | bytes 2097152 | tf_op jit(solution)/shard_map/convert_element_type | solution.py:276
  9.8 2.0 %collective-permute-start = (bf16[16,32,256]{2,1,0:T(8,128)(2,1)S(1)}, bf16[16,32,256]{2,1,0:T(8,128)(2,1)S(1)}, u32[]{:S(2)}, u32[]{:S(2)}) collective-permute-start(bf16[16,32,256]{2,1,0:T(8,128)(2,1)S(1)} %bitcast.59), channel_id=1, source_target_pairs={{0,32},{32,64},{64,96},{96,128},{128,160},{160,192},{192,224},{224... | collective-permute-start | bytes 786440 | tf_op jit(solution)/shard_map/ppermute | solution.py:26
  11.8 4.0 %collective-permute-start.1 = (bf16[16,32,256]{2,1,0:T(8,128)(2,1)S(1)}, bf16[16,32,256]{2,1,0:T(8,128)(2,1)S(1)}, u32[]{:S(2)}, u32[]{:S(2)}) collective-permute-start(bf16[16,32,256]{2,1,0:T(8,128)(2,1)S(1)} %bitcast.60), channel_id=1, source_target_pairs={{0,224},{32,0},{64,32},{96,64},{128,96},{160,128},{192,160},{224,1... | collective-permute-start | bytes 786440 | tf_op jit(solution)/shard_map/ppermute | solution.py:26
  15.8 6.2 %collective-permute-done.refs_2_ = bf16[16,32,256]{2,1,0:T(8,128)(2,1)S(1)} collective-permute-done((bf16[16,32,256]{2,1,0:T(8,128)(2,1)S(1)}, bf16[16,32,256]{2,1,0:T(8,128)(2,1)S(1)}, u32[]{:S(2)}, u32[]{:S(2)}) %collective-permute-start) | collective-permute-done | bytes 262176 | tf_op jit(solution)/shard_map/ppermute | solution.py:26
  24.5 3.2 %collective-permute-start.4 = (bf16[16,32,256]{2,1,0:T(8,128)(2,1)S(1)}, bf16[16,32,256]{2,1,0:T(8,128)(2,1)S(1)}, u32[]{:S(2)}, u32[]{:S(2)}) collective-permute-start(bf16[16,32,256]{2,1,0:T(8,128)(2,1)S(1)} %collective-permute-done.1.refs_1_), channel_id=1, source_target_pairs={{0,224},{32,0},{64,32},{96,64},{128,96},{160,128},{192,160},{224,1... | collective-permute-start | bytes 786440 | tf_op jit(solution)/shard_map/ppermute | solution.py:26
  27.7 3.9 %collective-permute-done.2.refs_3_ = bf16[16,32,256]{2,1,0:T(8,128)(2,1)S(1)} collective-permute-done((bf16[16,32,256]{2,1,0:T(8,128)(2,1)S(1)}, bf16[16,32,256]{2,1,0:T(8,128)(2,1)S(1)}, u32[]{:S(2)}, u32[]{:S(2)}) %collective-permute-start.2) | collective-permute-done | bytes 262176 | tf_op jit(solution)/shard_map/ppermute | solution.py:26
  32.3 5.8 %all-to-all-start = ((s32[8,1,592]{2,1,0:T(1,128)}), s32[8,1,592]{2,1,0:T(1,128)S(1)}, u32[]{:S(2)}, u32[]{:S(2)}) async-start(s32[8,1,592]{2,1,0:T(1,128)} %copy.41), calls=%async_computation | async-start | bytes 40960 | tf_op jit(solution)/shard_map/all_to_all | solution.py:318
  38.1 7.8 %all-to-all-done = s32[8,1,592]{2,1,0:T(1,128)S(1)} async-done(((s32[8,1,592]{2,1,0:T(1,128)}), s32[8,1,592]{2,1,0:T(1,128)S(1)}, u32[]{:S(2)}, u32[]{:S(2)}) %all-to-all-start) | async-done | bytes 18976 | tf_op jit(solution)/shard_map/all_to_all | solution.py:318
  49.6 2.6 %collective-permute-done.5.refs_5_ = bf16[16,32,256]{2,1,0:T(8,128)(2,1)S(1)} collective-permute-done((bf16[16,32,256]{2,1,0:T(8,128)(2,1)S(1)}, bf16[16,32,256]{2,1,0:T(8,128)(2,1)S(1)}, u32[]{:S(2)}, u32[]{:S(2)}) %collective-permute-start.5) | collective-permute-done | bytes 262176 | tf_op jit(solution)/shard_map/ppermute | solution.py:26
  52.3 2.4 %collective-permute-done.6.refs_6_ = bf16[16,32,256]{2,1,0:T(8,128)(2,1)S(1)} collective-permute-done((bf16[16,32,256]{2,1,0:T(8,128)(2,1)S(1)}, bf16[16,32,256]{2,1,0:T(8,128)(2,1)S(1)}, u32[]{:S(2)}, u32[]{:S(2)}) %collective-permute-start.6) | collective-permute-done | bytes 262176 | tf_op jit(solution)/shard_map/ppermute | solution.py:26
  54.7 3.6 %pack.1.p_ref = bf16[8,512,256]{2,1,0:T(8,128)(2,1)} custom-call(s32[128]{0:T(128)S(1)} %max.12.blk, bf16[16,32,256]{2,1,0:T(8,128)(2,1)S(1)} %bitcast.61, bf16[16,32,256]{2,1,0:T(8,128)(2,1)S(1)} %collective-permute-done.1.refs_1_, bf16[16,32,256]{2,1,0:T(8,128)(2,1)S(1)} %collective-permute-done.refs_2_, ...), custom_call_target="tpu_custom_call" | custom-call | bytes 4194304 | tf_op jit(solution)/shard_map/pack/pallas_call | solution.py:46
  58.3 4.5 %all-to-all-start.1 = ((bf16[8,512,256]{2,1,0:T(8,128)(2,1)}), bf16[8,512,256]{2,1,0:T(8,128)(2,1)S(1)}, u32[]{:S(2)}, u32[]{:S(2)}) async-start(bf16[8,512,256]{2,1,0:T(8,128)(2,1)} %pack.1.p_ref), calls=%async_computation.1 | async-start | bytes 4194304 | tf_op jit(solution)/shard_map/all_to_all | solution.py:342
  62.8 2.2 %copy-done.11 = bf16[8,1024,256]{2,1,0:T(8,128)(2,1)S(1)} copy-done((bf16[8,1024,256]{2,1,0:T(8,128)(2,1)S(1)}, bf16[8,1024,256]{2,1,0:T(8,128)(2,1)}, u32[]{:S(2)}) %copy-start.11) | copy-done | bytes 4194328
  65.0 8.0 %forward.1 = f32[8,2,512]{2,1,0:T(2,128)S(1)} custom-call(bf16[8,512,256]{2,1,0:T(8,128)(2,1)} %pack.1.p_ref, bf16[8,1024,256]{2,1,0:T(8,128)(2,1)S(1)} %copy-done.11, s32[8,1,512]{2,1,0:T(1,128)S(1)} %reshape.306.tgt_ref), custom_call_target="tpu_custom_call" | custom-call | flops 2147483648 | bytes 6291456 | tf_op jit(solution)/shard_map/forward/pallas_call | solution.py:88
  73.6 2.5 %collective-permute-start.8 = (f32[8,2,512]{2,1,0:T(2,128)S(1)}, f32[8,2,512]{2,1,0:T(2,128)S(1)}, u32[]{:S(2)}, u32[]{:S(2)}) collective-permute-start(f32[8,2,512]{2,1,0:T(2,128)S(1)} %forward.1), channel_id=1, source_target_pairs={{0,128},{32,160},{64,192},{96,224},{128,0},{160,32},{192,64},{224,... | collective-permute-start | bytes 98312 | tf_op jit(solution)/shard_map/ppermute | solution.py:26
  76.0 4.0 %collective-permute-start.7 = (f32[8,2,512]{2,1,0:T(2,128)S(1)}, f32[8,2,512]{2,1,0:T(2,128)S(1)}, u32[]{:S(2)}, u32[]{:S(2)}) collective-permute-start(f32[8,2,512]{2,1,0:T(2,128)S(1)} %forward.1), channel_id=1, source_target_pairs={{0,192},{32,224},{64,0},{96,32},{128,64},{160,96},{192,128},{224,1... | collective-permute-start | bytes 98312 | tf_op jit(solution)/shard_map/ppermute | solution.py:26
  85.5 3.1 %collective-permute-done.10 = f32[4,8,2,512]{3,2,1,0:T(2,128)S(1)} collective-permute-done((f32[4,8,2,512]{3,2,1,0:T(2,128)S(1)}, f32[4,8,2,512]{3,2,1,0:T(2,128)S(1)}, u32[]{:S(2)}, u32[]{:S(2)}) %collective-permute-start.10) | collective-permute-done | bytes 131104 | tf_op jit(solution)/shard_map/ppermute | solution.py:26
  90.2 2.3 %gather_fusion.2 = f32[512,32]{1,0:T(8,128)S(1)} fusion(f32[2048,32]{1,0:T(8,128)} %reshape.307, s32[1024]{0:T(1024)S(1)} %pad_clamp_fusion.2), kind=kCustom, calls=%fused_computation.2 | custom fusion | bytes 133120 | tf_op jit(solution)/shard_map/gather | solution.py:347
  94.3 2.2 %copy-done.12 = bf16[8,1024,256]{2,1,0:T(8,128)(2,1)S(1)} copy-done((bf16[8,1024,256]{2,1,0:T(8,128)(2,1)S(1)}, bf16[8,1024,256]{2,1,0:T(8,128)(2,1)}, u32[]{:S(2)}) %copy-start.12) | copy-done | bytes 4194328
  96.5 8.8 %query_parts.3 = (bf16[16,32,256]{2,1,0:T(8,128)(2,1)S(1)}, bf16[16,32,256]{2,1,0:T(8,128)(2,1)S(1)}, bf16[16,32,256]{2,1,0:T(8,128)(2,1)}, bf16[16,32,256]{2,1,0:T(8,128)(2,1)}) custom-call(s32[128]{0:T(128)S(1)} %max.12.blk, bf16[8,512,256]{2,1,0:T(8,128)(2,1)} %pack.1.p_ref, bf16[8,1024,256]{2,1,0:T(8,128)(2,1)S(1)} %copy-done.12, ...), custom_call_target="tpu_custom_call" | custom-call | flops 2147483648 | bytes 6291456 | tf_op jit(solution)/shard_map/query_parts/pallas_call | solution.py:141
  106.7 2.5 %collective-permute-start.15 = (bf16[16,32,256]{2,1,0:T(8,128)(2,1)}, bf16[16,32,256]{2,1,0:T(8,128)(2,1)}, u32[]{:S(2)}, u32[]{:S(2)}) collective-permute-start(bf16[16,32,256]{2,1,0:T(8,128)(2,1)} %get-tuple-element.36), channel_id=1, source_target_pairs={{0,224},{32,0},{64,32},{96,64},{128,96},{160,128},{192,160},{224,1... | collective-permute-start | bytes 786440 | tf_op jit(solution)/shard_map/ppermute | solution.py:26
  109.1 4.4 %all-to-all-start.2 = ((f32[8,2,512]{2,1,0:T(2,128)}), f32[8,2,512]{2,1,0:T(2,128)S(1)}, u32[]{:S(2)}, u32[]{:S(2)}) async-start(f32[8,2,512]{2,1,0:T(2,128)} %pad_maximum_fusion.4.line_ref), calls=%async_computation.2 | async-start | bytes 65536 | tf_op jit(solution)/shard_map/all_to_all | solution.py:359
  113.6 2.2 %copy-done.13 = bf16[8,1024,256]{2,1,0:T(8,128)(2,1)S(1)} copy-done((bf16[8,1024,256]{2,1,0:T(8,128)(2,1)S(1)}, bf16[8,1024,256]{2,1,0:T(8,128)(2,1)}, u32[]{:S(2)}) %copy-start.13) | copy-done | bytes 4194328
  115.8 7.9 %query_parts.2 = (bf16[16,32,256]{2,1,0:T(8,128)(2,1)S(1)}, bf16[16,32,256]{2,1,0:T(8,128)(2,1)S(1)}, bf16[16,32,256]{2,1,0:T(8,128)(2,1)S(1)}, bf16[16,32,256]{2,1,0:T(8,128)(2,1)S(1)}) custom-call(s32[128]{0:T(128)S(1)} %max.12.blk, bf16[8,512,256]{2,1,0:T(8,128)(2,1)} %pack.1.p_ref, bf16[8,1024,256]{2,1,0:T(8,128)(2,1)S(1)} %copy-done.13, ...), custom_call_target="tpu_custom_call" | custom-call | flops 2147483648 | bytes 6291456 | tf_op jit(solution)/shard_map/query_parts/pallas_call | solution.py:141
  124.4 3.7 %item_parts.3 = (f32[128,256]{1,0:T(8,128)S(1)}, f32[128,256]{1,0:T(8,128)S(1)}) custom-call(s32[1]{0:T(128)} %bitcast.24.x_ref, bf16[8,512,256]{2,1,0:T(8,128)(2,1)S(1)} %all-to-all-done.1.q_ref, f32[8,2,512]{2,1,0:T(2,128)S(1)} %all-to-all-done.2.line_ref, bf16[1024,256]{1,0:T(8,128)(2,1)S(1)} %get-tuple-element.46.t_ref), custom_call_target="tpu_custom_call" | custom-call | flops 1073741824 | bytes 2883584 | tf_op jit(solution)/shard_map/item_parts/pallas_call | solution.py:198
  130.2 5.9 %item_parts.2 = (f32[256,256]{1,0:T(8,128)S(1)}, f32[256,256]{1,0:T(8,128)S(1)}, f32[256,256]{1,0:T(8,128)S(1)}) custom-call(s32[1]{0:T(128)} %bitcast.24.x_ref, bf16[8,512,256]{2,1,0:T(8,128)(2,1)S(1)} %all-to-all-done.1.q_ref, f32[8,2,512]{2,1,0:T(2,128)S(1)} %all-to-all-done.2.line_ref, bf16[1024,256]{1,0:T(8,128)(2,1)S(1)} %get-tuple-element.46.t_ref), custom_call_target="tpu_custom_call" | custom-call | flops 3221225472 | bytes 2883584 | tf_op jit(solution)/shard_map/item_parts/pallas_call | solution.py:198
  137.2 2.5 %collective-permute-start.19 = (f32[256,256]{1,0:T(8,128)S(1)}, f32[256,256]{1,0:T(8,128)S(1)}, u32[]{:S(2)}, u32[]{:S(2)}) collective-permute-start(f32[256,256]{1,0:T(8,128)S(1)} %pad_maximum_fusion.1), channel_id=1, source_target_pairs={{0,1},{1,2},{2,3},{3,0},{4,5},{5,6},{6,7},{7,4},{8,9},{9,10},{10,1... | collective-permute-start | bytes 786440 | tf_op jit(solution)/shard_map/ppermute | solution.py:26
  142.7 2.6 %collective-permute-start.16 = (bf16[16,32,256]{2,1,0:T(8,128)(2,1)S(1)}, bf16[16,32,256]{2,1,0:T(8,128)(2,1)S(1)}, u32[]{:S(2)}, u32[]{:S(2)}) collective-permute-start(bf16[16,32,256]{2,1,0:T(8,128)(2,1)S(1)} %add_convert_fusion.1), channel_id=1, source_target_pairs={{0,224},{32,0},{64,32},{96,64},{128,96},{160,128},{192,160},{224,1... | collective-permute-start | bytes 786440 | tf_op jit(solution)/shard_map/ppermute | solution.py:26
  145.9 3.3 %collective-permute-start.23 = (f32[256,256]{1,0:T(8,128)S(1)}, f32[256,256]{1,0:T(8,128)S(1)}, u32[]{:S(2)}, u32[]{:S(2)}) collective-permute-start(f32[256,256]{1,0:T(8,128)S(1)} %add_add_fusion.own), channel_id=1, source_target_pairs={{0,1},{1,2},{2,3},{3,0},{4,5},{5,6},{6,7},{7,4},{8,9},{9,10},{10,1... | collective-permute-start | bytes 786440 | tf_op jit(solution)/shard_map/ppermute | solution.py:26
  151.1 3.7 %collective-permute-start.17 = (bf16[16,32,256]{2,1,0:T(8,128)(2,1)}, bf16[16,32,256]{2,1,0:T(8,128)(2,1)}, u32[]{:S(2)}, u32[]{:S(2)}) collective-permute-start(bf16[16,32,256]{2,1,0:T(8,128)(2,1)} %add_convert_fusion), channel_id=1, source_target_pairs={{0,224},{32,0},{64,32},{96,64},{128,96},{160,128},{192,160},{224,1... | collective-permute-start | bytes 786440 | tf_op jit(solution)/shard_map/ppermute | solution.py:26
  155.5 2.6 %collective-permute-start.24 = (f32[128,256]{1,0:T(8,128)}, f32[128,256]{1,0:T(8,128)S(1)}, u32[]{:S(2)}, u32[]{:S(2)}) collective-permute-start(f32[128,256]{1,0:T(8,128)} %slice.58), channel_id=1, source_target_pairs={{0,1},{1,2},{2,3},{3,0},{4,5},{5,6},{6,7},{7,4},{8,9},{9,10},{10,1... | collective-permute-start | bytes 393224 | tf_op jit(solution)/shard_map/ppermute | solution.py:26
  165.3 2.9 %update.1 = (f32[1024,256]{1,0:T(8,128)}, f32[1024,256]{1,0:T(8,128)}) custom-call(s32[1]{0:T(128)} %bitcast.24.x_ref, f32[256,256]{1,0:T(8,128)S(1)} %add_add_fusion.own, f32[256,256]{1,0:T(8,128)S(1)} %collective-permute-done.22.after, f32[256,256]{1,0:T(8,128)S(1)} %collective-permute-done.23.before, f32[128,256]{1,0:T(8,128)S(1)} %collective-permute-done.24.far_a, ...), custom_call_target="tpu_custom_call" | custom-call | tf_op jit(solution)/shard_map/update/pallas_call | solution.py:249
  (163 shorter events, 36.6 us)
Async XLA Ops:
  7.2 55.6 %all-gather.2.cloned.1.call-start = ((), (), s32[]{:S(2)}) async-start(), calls=%async_computation.3 | async-start | bytes 4718592 | tf_op jit(solution)/shard_map/all_gather | solution.py:277
  9.8 12.2 %collective-permute-start = (bf16[16,32,256]{2,1,0:T(8,128)(2,1)S(1)}, bf16[16,32,256]{2,1,0:T(8,128)(2,1)S(1)}, u32[]{:S(2)}, u32[]{:S(2)}) collective-permute-start(bf16[16,32,256]{2,1,0:T(8,128)(2,1)S(1)} %bitcast.59), channel_id=1, source_target_pairs={{0,32},{32,64},{64,96},{96,128},{128,160},{160,192},{192,224},{224... | collective-permute-start | bytes 786440 | tf_op jit(solution)/shard_map/ppermute | solution.py:26
  11.8 10.2 %collective-permute-start.1 = (bf16[16,32,256]{2,1,0:T(8,128)(2,1)S(1)}, bf16[16,32,256]{2,1,0:T(8,128)(2,1)S(1)}, u32[]{:S(2)}, u32[]{:S(2)}) collective-permute-start(bf16[16,32,256]{2,1,0:T(8,128)(2,1)S(1)} %bitcast.60), channel_id=1, source_target_pairs={{0,224},{32,0},{64,32},{96,64},{128,96},{160,128},{192,160},{224,1... | collective-permute-start | bytes 786440 | tf_op jit(solution)/shard_map/ppermute | solution.py:26
  22.9 8.7 %collective-permute-start.2 = (bf16[16,32,256]{2,1,0:T(8,128)(2,1)S(1)}, bf16[16,32,256]{2,1,0:T(8,128)(2,1)S(1)}, u32[]{:S(2)}, u32[]{:S(2)}) collective-permute-start(bf16[16,32,256]{2,1,0:T(8,128)(2,1)S(1)} %collective-permute-done.refs_2_), channel_id=1, source_target_pairs={{0,32},{32,64},{64,96},{96,128},{128,160},{160,192},{192,224},{224... | collective-permute-start | bytes 786440 | tf_op jit(solution)/shard_map/ppermute | solution.py:26
  24.5 21.4 %collective-permute-start.4 = (bf16[16,32,256]{2,1,0:T(8,128)(2,1)S(1)}, bf16[16,32,256]{2,1,0:T(8,128)(2,1)S(1)}, u32[]{:S(2)}, u32[]{:S(2)}) collective-permute-start(bf16[16,32,256]{2,1,0:T(8,128)(2,1)S(1)} %collective-permute-done.1.refs_1_), channel_id=1, source_target_pairs={{0,224},{32,0},{64,32},{96,64},{128,96},{160,128},{192,160},{224,1... | collective-permute-start | bytes 786440 | tf_op jit(solution)/shard_map/ppermute | solution.py:26
  31.7 14.8 %collective-permute-start.3 = (bf16[16,32,256]{2,1,0:T(8,128)(2,1)S(1)}, bf16[16,32,256]{2,1,0:T(8,128)(2,1)S(1)}, u32[]{:S(2)}, u32[]{:S(2)}) collective-permute-start(bf16[16,32,256]{2,1,0:T(8,128)(2,1)S(1)} %collective-permute-done.2.refs_3_), channel_id=1, source_target_pairs={{0,32},{32,64},{64,96},{96,128},{128,160},{160,192},{192,224},{224... | collective-permute-start | bytes 786440 | tf_op jit(solution)/shard_map/ppermute | solution.py:26
  32.3 13.6 %all-to-all-start = ((s32[8,1,592]{2,1,0:T(1,128)}), s32[8,1,592]{2,1,0:T(1,128)S(1)}, u32[]{:S(2)}, u32[]{:S(2)}) async-start(s32[8,1,592]{2,1,0:T(1,128)} %copy.41), calls=%async_computation | async-start | bytes 40960 | tf_op jit(solution)/shard_map/all_to_all | solution.py:318
  45.9 6.4 %collective-permute-start.5 = (bf16[16,32,256]{2,1,0:T(8,128)(2,1)S(1)}, bf16[16,32,256]{2,1,0:T(8,128)(2,1)S(1)}, u32[]{:S(2)}, u32[]{:S(2)}) collective-permute-start(bf16[16,32,256]{2,1,0:T(8,128)(2,1)S(1)} %collective-permute-done.4.refs_4_), channel_id=1, source_target_pairs={{0,224},{32,0},{64,32},{96,64},{128,96},{160,128},{192,160},{224,1... | collective-permute-start | bytes 786440 | tf_op jit(solution)/shard_map/ppermute | solution.py:26
  47.1 7.6 %collective-permute-start.6 = (bf16[16,32,256]{2,1,0:T(8,128)(2,1)S(1)}, bf16[16,32,256]{2,1,0:T(8,128)(2,1)S(1)}, u32[]{:S(2)}, u32[]{:S(2)}) collective-permute-start(bf16[16,32,256]{2,1,0:T(8,128)(2,1)S(1)} %collective-permute-done.3.refs_7_), channel_id=1, source_target_pairs={{0,32},{32,64},{64,96},{96,128},{128,160},{160,192},{192,224},{224... | collective-permute-start | bytes 786440 | tf_op jit(solution)/shard_map/ppermute | solution.py:26
  58.3 50.8 %all-to-all-start.1 = ((bf16[8,512,256]{2,1,0:T(8,128)(2,1)}), bf16[8,512,256]{2,1,0:T(8,128)(2,1)S(1)}, u32[]{:S(2)}, u32[]{:S(2)}) async-start(bf16[8,512,256]{2,1,0:T(8,128)(2,1)} %pack.1.p_ref), calls=%async_computation.1 | async-start | bytes 4194304 | tf_op jit(solution)/shard_map/all_to_all | solution.py:342
  73.0 7.0 %collective-permute-start.9 = (f32[8,2,512]{2,1,0:T(2,128)S(1)}, f32[8,2,512]{2,1,0:T(2,128)S(1)}, u32[]{:S(2)}, u32[]{:S(2)}) collective-permute-start(f32[8,2,512]{2,1,0:T(2,128)S(1)} %forward.1), channel_id=1, source_target_pairs={{0,64},{32,96},{64,128},{96,160},{128,192},{160,224},{192,0},{224,... | collective-permute-start | bytes 98312 | tf_op jit(solution)/shard_map/ppermute | solution.py:26
  73.6 7.9 %collective-permute-start.8 = (f32[8,2,512]{2,1,0:T(2,128)S(1)}, f32[8,2,512]{2,1,0:T(2,128)S(1)}, u32[]{:S(2)}, u32[]{:S(2)}) collective-permute-start(f32[8,2,512]{2,1,0:T(2,128)S(1)} %forward.1), channel_id=1, source_target_pairs={{0,128},{32,160},{64,192},{96,224},{128,0},{160,32},{192,64},{224,... | collective-permute-start | bytes 98312 | tf_op jit(solution)/shard_map/ppermute | solution.py:26
  76.0 6.8 %collective-permute-start.7 = (f32[8,2,512]{2,1,0:T(2,128)S(1)}, f32[8,2,512]{2,1,0:T(2,128)S(1)}, u32[]{:S(2)}, u32[]{:S(2)}) collective-permute-start(f32[8,2,512]{2,1,0:T(2,128)S(1)} %forward.1), channel_id=1, source_target_pairs={{0,192},{32,224},{64,0},{96,32},{128,64},{160,96},{192,128},{224,1... | collective-permute-start | bytes 98312 | tf_op jit(solution)/shard_map/ppermute | solution.py:26
  82.9 5.7 %collective-permute-start.10 = (f32[4,8,2,512]{3,2,1,0:T(2,128)S(1)}, f32[4,8,2,512]{3,2,1,0:T(2,128)S(1)}, u32[]{:S(2)}, u32[]{:S(2)}) collective-permute-start(f32[4,8,2,512]{3,2,1,0:T(2,128)S(1)} %pad_maximum_fusion.3), channel_id=1, source_target_pairs={{0,224},{32,0},{64,32},{96,64},{128,96},{160,128},{192,160},{224,1... | collective-permute-start | bytes 393224 | tf_op jit(solution)/shard_map/ppermute | solution.py:26
  106.7 34.9 %collective-permute-start.15 = (bf16[16,32,256]{2,1,0:T(8,128)(2,1)}, bf16[16,32,256]{2,1,0:T(8,128)(2,1)}, u32[]{:S(2)}, u32[]{:S(2)}) collective-permute-start(bf16[16,32,256]{2,1,0:T(8,128)(2,1)} %get-tuple-element.36), channel_id=1, source_target_pairs={{0,224},{32,0},{64,32},{96,64},{128,96},{160,128},{192,160},{224,1... | collective-permute-start | bytes 786440 | tf_op jit(solution)/shard_map/ppermute | solution.py:26
  109.1 30.6 %collective-permute-start.11 = (bf16[16,32,256]{2,1,0:T(8,128)(2,1)}, bf16[16,32,256]{2,1,0:T(8,128)(2,1)}, u32[]{:S(2)}, u32[]{:S(2)}) collective-permute-start(bf16[16,32,256]{2,1,0:T(8,128)(2,1)} %get-tuple-element.32), channel_id=1, source_target_pairs={{0,32},{32,64},{64,96},{96,128},{128,160},{160,192},{192,224},{224... | collective-permute-start | bytes 786440 | tf_op jit(solution)/shard_map/ppermute | solution.py:26
  109.1 15.3 %all-to-all-start.2 = ((f32[8,2,512]{2,1,0:T(2,128)}), f32[8,2,512]{2,1,0:T(2,128)S(1)}, u32[]{:S(2)}, u32[]{:S(2)}) async-start(f32[8,2,512]{2,1,0:T(2,128)} %pad_maximum_fusion.4.line_ref), calls=%async_computation.2 | async-start | bytes 65536 | tf_op jit(solution)/shard_map/all_to_all | solution.py:359
  128.1 8.1 %collective-permute-start.18 = (f32[128,256]{1,0:T(8,128)S(1)}, f32[128,256]{1,0:T(8,128)S(1)}, u32[]{:S(2)}, u32[]{:S(2)}) collective-permute-start(f32[128,256]{1,0:T(8,128)S(1)} %get-tuple-element.41), channel_id=1, source_target_pairs={{0,1},{1,2},{2,3},{3,0},{4,5},{5,6},{6,7},{7,4},{8,9},{9,10},{10,1... | collective-permute-start | bytes 393224 | tf_op jit(solution)/shard_map/ppermute | solution.py:26
  128.7 7.5 %collective-permute-start.20 = (f32[128,256]{1,0:T(8,128)S(1)}, f32[128,256]{1,0:T(8,128)S(1)}, u32[]{:S(2)}, u32[]{:S(2)}) collective-permute-start(f32[128,256]{1,0:T(8,128)S(1)} %get-tuple-element.43), channel_id=1, source_target_pairs={{0,3},{1,0},{2,1},{3,2},{4,7},{5,4},{6,5},{7,6},{8,11},{9,8},{10,9... | collective-permute-start | bytes 393224 | tf_op jit(solution)/shard_map/ppermute | solution.py:26
  136.3 9.4 %collective-permute-start.21 = (f32[256,256]{1,0:T(8,128)S(1)}, f32[256,256]{1,0:T(8,128)S(1)}, u32[]{:S(2)}, u32[]{:S(2)}) collective-permute-start(f32[256,256]{1,0:T(8,128)S(1)} %pad_maximum_fusion.2), channel_id=1, source_target_pairs={{0,3},{1,0},{2,1},{3,2},{4,7},{5,4},{6,5},{7,6},{8,11},{9,8},{10,9... | collective-permute-start | bytes 786440 | tf_op jit(solution)/shard_map/ppermute | solution.py:26
  137.2 8.5 %collective-permute-start.19 = (f32[256,256]{1,0:T(8,128)S(1)}, f32[256,256]{1,0:T(8,128)S(1)}, u32[]{:S(2)}, u32[]{:S(2)}) collective-permute-start(f32[256,256]{1,0:T(8,128)S(1)} %pad_maximum_fusion.1), channel_id=1, source_target_pairs={{0,1},{1,2},{2,3},{3,0},{4,5},{5,6},{6,7},{7,4},{8,9},{9,10},{10,1... | collective-permute-start | bytes 786440 | tf_op jit(solution)/shard_map/ppermute | solution.py:26
  140.8 9.2 %collective-permute-start.12 = (bf16[16,32,256]{2,1,0:T(8,128)(2,1)S(1)}, bf16[16,32,256]{2,1,0:T(8,128)(2,1)S(1)}, u32[]{:S(2)}, u32[]{:S(2)}) collective-permute-start(bf16[16,32,256]{2,1,0:T(8,128)(2,1)S(1)} %add_convert_fusion.4), channel_id=1, source_target_pairs={{0,32},{32,64},{64,96},{96,128},{128,160},{160,192},{192,224},{224... | collective-permute-start | bytes 786440 | tf_op jit(solution)/shard_map/ppermute | solution.py:26
  142.7 7.7 %collective-permute-start.16 = (bf16[16,32,256]{2,1,0:T(8,128)(2,1)S(1)}, bf16[16,32,256]{2,1,0:T(8,128)(2,1)S(1)}, u32[]{:S(2)}, u32[]{:S(2)}) collective-permute-start(bf16[16,32,256]{2,1,0:T(8,128)(2,1)S(1)} %add_convert_fusion.1), channel_id=1, source_target_pairs={{0,224},{32,0},{64,32},{96,64},{128,96},{160,128},{192,160},{224,1... | collective-permute-start | bytes 786440 | tf_op jit(solution)/shard_map/ppermute | solution.py:26
  145.8 19.5 %copy-start = (f32[1,1024,256]{2,1,0:T(8,128)S(1)}, f32[1,1024,256]{2,1,0:T(8,128)}, u32[]{:S(2)}) copy-start(f32[1,1024,256]{2,1,0:T(8,128)} %param.11) | copy-start | bytes 3145732
  145.8 19.5 %copy-start.1 = (f32[1,1024,256]{2,1,0:T(8,128)S(1)}, f32[1,1024,256]{2,1,0:T(8,128)}, u32[]{:S(2)}) copy-start(f32[1,1024,256]{2,1,0:T(8,128)} %param.12) | copy-start | bytes 3145732
  145.8 12.3 %collective-permute-start.22 = (f32[256,256]{1,0:T(8,128)S(1)}, f32[256,256]{1,0:T(8,128)S(1)}, u32[]{:S(2)}, u32[]{:S(2)}) collective-permute-start(f32[256,256]{1,0:T(8,128)S(1)} %add_add_fusion.own), channel_id=1, source_target_pairs={{0,3},{1,0},{2,1},{3,2},{4,7},{5,4},{6,5},{7,6},{8,11},{9,8},{10,9... | collective-permute-start | bytes 786440 | tf_op jit(solution)/shard_map/ppermute | solution.py:26
  145.9 8.9 %collective-permute-start.23 = (f32[256,256]{1,0:T(8,128)S(1)}, f32[256,256]{1,0:T(8,128)S(1)}, u32[]{:S(2)}, u32[]{:S(2)}) collective-permute-start(f32[256,256]{1,0:T(8,128)S(1)} %add_add_fusion.own), channel_id=1, source_target_pairs={{0,1},{1,2},{2,3},{3,0},{4,5},{5,6},{6,7},{7,4},{8,9},{9,10},{10,1... | collective-permute-start | bytes 786440 | tf_op jit(solution)/shard_map/ppermute | solution.py:26
  150.0 8.8 %collective-permute-start.13 = (bf16[16,32,256]{2,1,0:T(8,128)(2,1)S(1)}, bf16[16,32,256]{2,1,0:T(8,128)(2,1)S(1)}, u32[]{:S(2)}, u32[]{:S(2)}) collective-permute-start(bf16[16,32,256]{2,1,0:T(8,128)(2,1)S(1)} %add_convert_fusion.3), channel_id=1, source_target_pairs={{0,32},{32,64},{64,96},{96,128},{128,160},{160,192},{192,224},{224... | collective-permute-start | bytes 786440 | tf_op jit(solution)/shard_map/ppermute | solution.py:26
  151.1 17.1 %collective-permute-start.17 = (bf16[16,32,256]{2,1,0:T(8,128)(2,1)}, bf16[16,32,256]{2,1,0:T(8,128)(2,1)}, u32[]{:S(2)}, u32[]{:S(2)}) collective-permute-start(bf16[16,32,256]{2,1,0:T(8,128)(2,1)} %add_convert_fusion), channel_id=1, source_target_pairs={{0,224},{32,0},{64,32},{96,64},{128,96},{160,128},{192,160},{224,1... | collective-permute-start | bytes 786440 | tf_op jit(solution)/shard_map/ppermute | solution.py:26
  155.5 8.2 %collective-permute-start.24 = (f32[128,256]{1,0:T(8,128)}, f32[128,256]{1,0:T(8,128)S(1)}, u32[]{:S(2)}, u32[]{:S(2)}) collective-permute-start(f32[128,256]{1,0:T(8,128)} %slice.58), channel_id=1, source_target_pairs={{0,1},{1,2},{2,3},{3,0},{4,5},{5,6},{6,7},{7,4},{8,9},{9,10},{10,1... | collective-permute-start | bytes 393224 | tf_op jit(solution)/shard_map/ppermute | solution.py:26
  158.8 6.5 %collective-permute-start.25 = (f32[128,256]{1,0:T(8,128)}, f32[128,256]{1,0:T(8,128)}, u32[]{:S(2)}, u32[]{:S(2)}) collective-permute-start(f32[128,256]{1,0:T(8,128)} %slice.59), channel_id=1, source_target_pairs={{0,3},{1,0},{2,1},{3,2},{4,7},{5,4},{6,5},{7,6},{8,11},{9,8},{10,9... | collective-permute-start | bytes 393224 | tf_op jit(solution)/shard_map/ppermute | solution.py:26
  159.6 8.6 %collective-permute-start.14 = (bf16[16,32,256]{2,1,0:T(8,128)(2,1)}, bf16[16,32,256]{2,1,0:T(8,128)(2,1)}, u32[]{:S(2)}, u32[]{:S(2)}) collective-permute-start(bf16[16,32,256]{2,1,0:T(8,128)(2,1)} %add_convert_fusion.2), channel_id=1, source_target_pairs={{0,32},{32,64},{64,96},{96,128},{128,160},{160,192},{192,224},{224... | collective-permute-start | bytes 786440 | tf_op jit(solution)/shard_map/ppermute | solution.py:26
  (17 other events, 114.8 us)
Sparse Core Ops, SparseCore 0:
  10.5 37.5 all-gather.1

commit v4 on v3

--- a/solution.py
+++ b/solution.py
@@ -30,34 +30,49 @@
     return lax.broadcasted_iota(jnp.int32, shape, 0) + start
 
 
-def pack_kernel(blk, *refs):
-    sources, p_ref = refs[:-1], refs[-1]
-    step = pl.program_id(0)
+def shift_plane(value, dy, dc):
+    ys, cs = lax.axis_size("y"), lax.axis_size("c")
+    moves = []
+    for y in range(ys):
+        for c in range(cs):
+            moves.append((y * cs + c, (y + dy) % ys * cs + (c + dc) % cs))
+    return lax.ppermute(value, PLANE, moves)
+
+
+def pack_kernel(count, blk, *refs):
+    sources, p_ref, outs = refs[:count], refs[count], refs[count + 1:]
     block_rows = sources[0].shape[1]
-    per_step = len(sources) * MOST
-    for slot in range(per_step):
-        b = blk[step * per_step + slot]
-        p_ref[0, pl.ds(slot * block_rows, block_rows), :] = sources[slot // MOST][b]
-
-
-def pack(sources, blk, plane):
+    per_peer = count * MOST
+    for peer, out in enumerate(outs):
+        j = blk[len(outs) * per_peer + peer]
+        for slot in range(per_peer):
+            rows = sources[slot // MOST][blk[j * per_peer + slot]]
+            span = pl.ds(slot * block_rows, block_rows)
+            out[span, :] = rows
+            p_ref[j, span, :] = rows
+
+
+def pack(sources, blk, peers):
     shape = sources[0].shape
+    plane = peers.shape[0]
     width = len(sources) * MOST * shape[1]
+    out = jax.ShapeDtypeStruct((width, shape[2]), BF16)
     return pl.pallas_call(
-        pack_kernel,
+        functools.partial(pack_kernel, len(sources)),
         grid_spec=pltpu.PrefetchScalarGridSpec(
             num_scalar_prefetch=1,
-            grid=(plane,),
+            grid=(1,),
             in_specs=[pl.BlockSpec(shape, lambda j, blk: (0, 0, 0))] * len(sources),
-            out_specs=pl.BlockSpec((1, width, shape[2]), lambda j, blk: (j, 0, 0)),
-        ),
-        out_shape=jax.ShapeDtypeStruct((plane, width, shape[2]), BF16),
+            out_specs=[pl.BlockSpec((plane, width, shape[2]), lambda j, blk: (0, 0, 0))]
+            + [pl.BlockSpec(out.shape, lambda j, blk: (0, 0))] * plane,
+        ),
+        out_shape=[jax.ShapeDtypeStruct((plane, width, shape[2]), BF16)] + [out] * plane,
         compiler_params=pltpu.CompilerParams(vmem_limit_bytes=VMEM),
         cost_estimate=pl.CostEstimate(
-            flops=0, bytes_accessed=4 * plane * width * shape[2], transcendentals=0
+            flops=0, bytes_accessed=6 * plane * width * shape[2], transcendentals=0
         ),
         name="pack",
-    )(blk, *sources)
+    )(jnp.concatenate([blk, peers]), *sources)
 
 
 def forward_kernel(p_ref, t_ref, tgt_ref, stat_ref, s_ref):
@@ -165,57 +180,55 @@
     )(blk, packed, tables, lines)
 
 
-def item_kernel(places, quarters, x_ref, q_ref, line_ref, t_ref, *outs):
-    step = pl.program_id(0)
-
-    @pl.when(step == 0)
-    def _():
-        for out in outs:
-            out[...] = jnp.zeros_like(out)
-
-    rows = t_ref.shape[0] // quarters
-    mine = x_ref[0]
-    q = q_ref[0]
-    lse = line_ref[0, 0:1, :]
-    tgt = line_ref[0, 1:2, :].astype(jnp.int32)
-    per_out = len(outs) // len(places)
-    for i, place in enumerate(places):
-        start = pl.multiple_of(lax.rem(place + mine, quarters) * rows, rows)
-        s = lax.dot_general(t_ref[pl.ds(start, rows), :], q, NT, preferred_element_type=F32)
+def item_kernel(count, where, *refs):
+    rows_in, line_ref, t_ref, outs = refs[:count], refs[count], refs[count + 1], refs[count + 2:]
+    start = where[pl.program_id(0)] * t_ref.shape[0]
+    first = pl.num_programs(0)
+    total = None
+    for i, ref in enumerate(rows_in):
+        source = where[first + i]
+        q = ref[...]
+        line = line_ref[source]
+        lse = line[0:1, :]
+        tgt = line[1:2, :].astype(jnp.int32)
+        s = lax.dot_general(t_ref[...], q, NT, preferred_element_type=F32)
         e = jnp.exp(s - lse)
         c = jnp.where(tile_ids(start, s.shape) == tgt, e - 1.0, e).astype(BF16)
         part = jnp.dot(c, q, preferred_element_type=F32)
-        cut = rows // per_out
-        for n in range(per_out):
-            outs[i * per_out + n][...] += part[n * cut:(n + 1) * cut]
-
-
-def item_parts(places, pieces, x, rows, lines, table16, quarters):
-    sources, width, features = rows.shape
-    items = table16.shape[0]
-    out = jax.ShapeDtypeStruct((items // quarters // pieces, features), F32)
+        total = part if total is None else total + part
+    cut = t_ref.shape[0] // len(outs)
+    for n, out in enumerate(outs):
+        out[0] = total[n * cut:(n + 1) * cut]
+
+
+def item_parts(places, pieces, x, origin, rows, lines, table16, quarters):
+    width, features = rows[0].shape
+    count = len(rows)
+    span = table16.shape[0] // quarters
     share = len(places)
+    where = jnp.concatenate([(jnp.array(places, jnp.int32) + x) % quarters, origin])
+    out = jax.ShapeDtypeStruct((share, span // pieces, features), F32)
     return pl.pallas_call(
-        functools.partial(item_kernel, places, quarters),
+        functools.partial(item_kernel, count),
         grid_spec=pltpu.PrefetchScalarGridSpec(
             num_scalar_prefetch=1,
-            grid=(sources,),
-            in_specs=[
-                pl.BlockSpec((1, width, features), lambda j, o: (j, 0, 0)),
-                pl.BlockSpec((1, 2, width), lambda j, o: (j, 0, 0)),
-                pl.BlockSpec((items, features), lambda j, o: (0, 0)),
+            grid=(share,),
+            in_specs=[pl.BlockSpec((width, features), lambda i, o: (0, 0))] * count
+            + [
+                pl.BlockSpec(lines.shape, lambda i, o: (0, 0, 0)),
+                pl.BlockSpec((span, features), lambda i, o: (o[i], 0)),
             ],
-            out_specs=[pl.BlockSpec(out.shape, lambda j, o: (0, 0))] * (share * pieces),
-        ),
-        out_shape=[out] * (share * pieces),
+            out_specs=[pl.BlockSpec((1,) + out.shape[1:], lambda i, o: (i, 0, 0))] * pieces,
+        ),
+        out_shape=[out] * pieces,
         compiler_params=pltpu.CompilerParams(vmem_limit_bytes=VMEM),
         cost_estimate=pl.CostEstimate(
-            flops=share * sources * width * items * features,
-            bytes_accessed=2 * sources * width * features + items * features * 3,
-            transcendentals=share * sources * width * items // 4,
+            flops=4 * share * span * count * width * features,
+            bytes_accessed=2 * count * width * features + share * span * features * 6,
+            transcendentals=share * span * count * width,
         ),
         name="item_parts",
-    )(x, rows, lines, table16)
+    )(where, *rows, lines, table16)
 
 
 def update_kernel(x_ref, own, after, before, far_a, far_b, t_ref, a_ref, nt_ref, na_ref):
@@ -263,7 +276,11 @@
 def local(queries, clusters, positives, owner_of, table, accum):
     z_size = lax.axis_size("z")
     x_size = lax.axis_size("x")
+    y_size = lax.axis_size("y")
+    c_size = lax.axis_size("c")
     z = lax.axis_index("z")
+    y = lax.axis_index("y")
+    c = lax.axis_index("c")
     x = lax.axis_index("x").reshape(1)
     local_rows, features = queries.shape
     block_count, picks = clusters.shape
@@ -316,8 +333,7 @@
         axis=1,
     )
     got = lax.all_to_all(meta, "z", 0, 0, tiled=True)
-    got, last = lax.optimization_barrier((got, by_source[5]))
-    by_source[4] = shift(last, "z", 1)
+    by_source[4] = shift(by_source[5], "z", 1)
     order = jnp.array(ORDER, jnp.int32)
     got = got[(z + order) % z_size]
     width = z_size * MOST * block_rows
@@ -335,15 +351,20 @@
     pair_place = jnp.zeros_like(pair_rel)
     for place, d in enumerate(ORDER):
         pair_place = jnp.where(pair_rel == d, place, pair_place)
-    pair_row = (pair_from % 2 * 4 + pair_from // 2) * plane + pair_owner % plane
-    pair_row = (pair_row * 2 * z_size + pair_place) * MOST + pair_slot % MOST
-
-    packed = pack([by_source[d] for d in ORDER], blk, plane)
-    rows = lax.all_to_all(packed, PLANE, 0, 0, tiled=True)
+    pair_row = (pair_owner * 2 * z_size + pair_place) * MOST + pair_slot % MOST
+
+    hops = jnp.arange(plane, dtype=jnp.int32)
+    peers = (y + hops // c_size) % y_size * c_size + (c + hops % c_size) % c_size
+    origin = (y - hops // c_size) % y_size * c_size + (c - hops % c_size) % c_size
+    packed, *outgoing = pack([by_source[d] for d in ORDER], blk, peers)
+    rows = [
+        shift_plane(value, hop // c_size, hop % c_size) if hop else value
+        for hop, value in enumerate(outgoing)
+    ]
     stats = forward(packed, targets, tables)
 
-    even = jnp.stack([stats] + [shift(stats, "z", -e) for e in (2, 4, 6)])
-    all_stats = jnp.stack([even, shift(even, "z", -1)]).reshape(-1, block_rows)
+    spread = jnp.broadcast_to(stats[None], (z_size,) + stats.shape)
+    all_stats = lax.all_to_all(spread, "z", 0, 0, tiled=True).reshape(-1, block_rows)
     part = all_stats[pair_row.reshape(-1)].reshape(z_size, block_count, picks, block_rows)
     pick = all_stats[pair_row[0] + z_size * MOST].reshape(block_count, picks, block_rows)
     top = jnp.max(part, axis=2)
@@ -359,7 +380,10 @@
     got_lines = lax.all_to_all(lines, PLANE, 0, 0, tiled=True)
 
     far_g = query_parts(packed, blk, lines, tables, 1, block_count, block_rows)
-    near_g = query_parts(packed, blk, lines, tables, 0, block_count, block_rows)
+    far_a, far_b = item_parts((2,), 2, x, origin, rows, got_lines, table16, x_size)
+    (rest,) = item_parts((0, 1, 3), 1, x, origin, rows, got_lines, table16, x_size)
+    rest, late = lax.optimization_barrier((rest, blk))
+    near_g = query_parts(packed, late, lines, tables, 0, block_count, block_rows)
     grads = dict(zip(ORDER, list(near_g) + list(far_g)))
 
     def add(a, b):
@@ -376,14 +400,14 @@
         grads[0].astype(F32) + go_right.astype(F32) + go_left.astype(F32)
     ).reshape(local_rows, features)
 
-    far_a, far_b = item_parts((2,), 2, x, rows, got_lines, table16, x_size)
-    own, after, before = item_parts((0, 1, 3), 1, x, rows, got_lines, table16, x_size)
+    far_a, far_b = far_a[0], far_b[0]
+    own, after, before = rest[0], rest[1], rest[2]
     half = far_a.shape[0]
     far_a = shift(far_a, "x", 1)
     far_b = shift(far_b, "x", -1)
     after = shift(jnp.concatenate([after[:half] + far_a, after[half:]]), "x", 1)
     before = shift(jnp.concatenate([before[:half], before[half:] + far_b]), "x", -1)
-    own = own + after + before
+    own, losses = lax.optimization_barrier((own + after + before, losses))
     before = shift(own, "x", 1)
     after = shift(own, "x", -1)
     far_a = shift(before[:half], "x", 1)

time: 180 us -> 181 us (level)
  Pallas kernels: 40.8 us -> 34 us
  local copies, waits for them, and re-layouts: 21.5 us -> 27.8 us
  waiting for transfers between devices: 32 us -> 34 us
    ppermute x26 -> x22, starting transfers between devices: 42.4 us -> 31.6 us  [shift(): lax.ppermute(value, axis, [(i, (i + step) % size) for i in range(size)])]
    ppermute x0 -> x7, starting transfers between devices: none -> 8.38 us  [shift_plane(): return lax.ppermute(value, PLANE, moves)]
    unnamed x39 -> x49, local copies, waits for them, and re-layouts: 8.71 us -> 14.7 us
    all_to_all x1, waiting for transfers between devices: 7.79 us -> 4.66 us  [local(): got = lax.all_to_all(meta, 'z', 0, 0, tiled=True)]
    ppermute x26 -> x22, waiting for transfers between devices: 24.1 us -> 27 us  [shift(): lax.ppermute(value, axis, [(i, (i + step) % size) for i in range(size)])]
    pallas_call x2, Pallas kernels: 16.7 us -> 14.2 us  [query_parts(): pl.pallas_call(functools.partial(query_kernel, half), grid_spec=pltpu.Pre...]
    all_to_all x1, waiting for transfers between devices: 0.01 us -> 2.31 us  [local(): lax.all_to_all(spread, 'z', 0, 0, tiled=True).reshape(-1, block_rows)]
    pallas_call x3, Pallas kernels: 13.2 us -> 11.2 us  [the longest x2 10.3 us: item_parts(): pl.pallas_call(functools.partial(item_kernel, count), grid_spec=pltpu.Pre...]
  transfers between devices with their start and end apart: 30 -> 33, of which waited for: 12 -> 9; matrix products, arithmetic and copies ran while one was open for 11% -> 12% of each run, Pallas kernels for 23% -> 15%
where the time goes in v4:
time: 181 us; the launch traced here: 179 us
  starting transfers between devices  56.2 us (31%)
  waiting for transfers between devices  34 us (19%)
  Pallas kernels  34 us (19%)
  local copies, waits for them, and re-layouts  27.8 us (15%)
  between operations  14.6 us (8%)
  other arithmetic  12 us (7%)
    ppermute x22, starting transfers between devices, shift(): lax.ppermute(value, axis, [(i, (i + step) % size) for i in range(size)])  31.6 us
    ppermute x22, waiting for transfers between devices, shift(): lax.ppermute(value, axis, [(i, (i + step) % size) for i in range(size)])  27 us
    unnamed x49, local copies, waits for them, and re-layouts  14.7 us
    pallas_call x2, Pallas kernels, query_parts(): pl.pallas_call(functools.partial(query_kernel, half), grid_spec=pltpu.Pre...  14.2 us
    pallas_call x2, Pallas kernels, item_parts(): pl.pallas_call(functools.partial(item_kernel, count), grid_spec=pltpu.Pre...  10.3 us
    ppermute x7, starting transfers between devices, shift_plane(): return lax.ppermute(value, PLANE, moves)  8.38 us
    pallas_call x1, Pallas kernels, forward(): pl.pallas_call(forward_kernel, grid=(planes,), in_specs=[pl.BlockSpec((1,...  6.67 us
    all_to_all x1, starting transfers between devices, local(): lax.all_to_all(spread, 'z', 0, 0, tiled=True).reshape(-1, block_rows)  6.11 us
  transfers between devices with their start and end apart: 33, of which 9 were waited for; matrix products, arithmetic and copies ran while one was open for 12% of the time, Pallas kernels for 15%

profile of v4, /device:TPU:6, one launch (start us, length us, event | category | flops | bytes accessed | tf_op | source)
XLA Modules:
  0.0 178.6 jit_solution(6516133161258050253)
XLA Ops:
  7.2 2.5 %bitcast_convert_fusion = (bf16[1024,256]{1,0:T(8,128)(2,1)S(1)}, bf16[1,1024,256]{2,1,0:T(8,128)(2,1)}) fusion(f32[1,1024,256]{2,1,0:T(8,128)} %param.13), kind=kLoop, calls=%fused_computation.137 | loop fusion | flops 524288 | bytes 2097152 | tf_op jit(solution)/shard_map/convert_element_type | solution.py:293
  9.8 2.0 %collective-permute-start = (bf16[16,32,256]{2,1,0:T(8,128)(2,1)}, bf16[16,32,256]{2,1,0:T(8,128)(2,1)S(1)}, u32[]{:S(2)}, u32[]{:S(2)}) collective-permute-start(bf16[16,32,256]{2,1,0:T(8,128)(2,1)} %bitcast.66), channel_id=1, source_target_pairs={{0,32},{32,64},{64,96},{96,128},{128,160},{160,192},{192,224},{224... | collective-permute-start | bytes 786440 | tf_op jit(solution)/shard_map/ppermute | solution.py:26
  11.8 4.0 %collective-permute-start.1 = (bf16[16,32,256]{2,1,0:T(8,128)(2,1)}, bf16[16,32,256]{2,1,0:T(8,128)(2,1)S(1)}, u32[]{:S(2)}, u32[]{:S(2)}) collective-permute-start(bf16[16,32,256]{2,1,0:T(8,128)(2,1)} %bitcast.67), channel_id=1, source_target_pairs={{0,224},{32,0},{64,32},{96,64},{128,96},{160,128},{192,160},{224,1... | collective-permute-start | bytes 786440 | tf_op jit(solution)/shard_map/ppermute | solution.py:26
  17.3 5.0 %collective-permute-done.refs_2_ = bf16[16,32,256]{2,1,0:T(8,128)(2,1)S(1)} collective-permute-done((bf16[16,32,256]{2,1,0:T(8,128)(2,1)}, bf16[16,32,256]{2,1,0:T(8,128)(2,1)S(1)}, u32[]{:S(2)}, u32[]{:S(2)}) %collective-permute-start) | collective-permute-done | bytes 262176 | tf_op jit(solution)/shard_map/ppermute | solution.py:26
  27.3 5.8 %all-to-all-start = ((s32[8,1,592]{2,1,0:T(1,128)}), s32[8,1,592]{2,1,0:T(1,128)S(1)}, u32[]{:S(2)}, u32[]{:S(2)}) async-start(s32[8,1,592]{2,1,0:T(1,128)} %copy.43), calls=%async_computation | async-start | bytes 40960 | tf_op jit(solution)/shard_map/all_to_all | solution.py:335
  33.2 2.0 %collective-permute-start.2 = (bf16[16,32,256]{2,1,0:T(8,128)(2,1)S(1)}, bf16[16,32,256]{2,1,0:T(8,128)(2,1)S(1)}, u32[]{:S(2)}, u32[]{:S(2)}) collective-permute-start(bf16[16,32,256]{2,1,0:T(8,128)(2,1)S(1)} %collective-permute-done.refs_2_), channel_id=1, source_target_pairs={{0,32},{32,64},{64,96},{96,128},{128,160},{160,192},{192,224},{224... | collective-permute-start | bytes 786440 | tf_op jit(solution)/shard_map/ppermute | solution.py:26
  36.6 4.7 %all-to-all-done = s32[8,1,592]{2,1,0:T(1,128)S(1)} async-done(((s32[8,1,592]{2,1,0:T(1,128)}), s32[8,1,592]{2,1,0:T(1,128)S(1)}, u32[]{:S(2)}, u32[]{:S(2)}) %all-to-all-start) | async-done | bytes 18976 | tf_op jit(solution)/shard_map/all_to_all | solution.py:335
  43.1 2.7 %collective-permute-start.4 = (bf16[16,32,256]{2,1,0:T(8,128)(2,1)S(1)}, bf16[16,32,256]{2,1,0:T(8,128)(2,1)S(1)}, u32[]{:S(2)}, u32[]{:S(2)}) collective-permute-start(bf16[16,32,256]{2,1,0:T(8,128)(2,1)S(1)} %collective-permute-done.3.refs_4_), channel_id=1, source_target_pairs={{0,224},{32,0},{64,32},{96,64},{128,96},{160,128},{192,160},{224,1... | collective-permute-start | bytes 786440 | tf_op jit(solution)/shard_map/ppermute | solution.py:26
  45.7 3.9 %collective-permute-done.5.refs_7_ = bf16[16,32,256]{2,1,0:T(8,128)(2,1)S(1)} collective-permute-done((bf16[16,32,256]{2,1,0:T(8,128)(2,1)S(1)}, bf16[16,32,256]{2,1,0:T(8,128)(2,1)S(1)}, u32[]{:S(2)}, u32[]{:S(2)}) %collective-permute-start.5) | collective-permute-done | bytes 262176 | tf_op jit(solution)/shard_map/ppermute | solution.py:26
  50.0 7.3 %collective-permute-done.6.refs_6_ = bf16[16,32,256]{2,1,0:T(8,128)(2,1)S(1)} collective-permute-done((bf16[16,32,256]{2,1,0:T(8,128)(2,1)S(1)}, bf16[16,32,256]{2,1,0:T(8,128)(2,1)S(1)}, u32[]{:S(2)}, u32[]{:S(2)}) %collective-permute-start.6) | collective-permute-done | bytes 262176 | tf_op jit(solution)/shard_map/ppermute | solution.py:26
  63.0 2.2 %copy-done.3 = bf16[8,1024,256]{2,1,0:T(8,128)(2,1)S(1)} copy-done((bf16[8,1024,256]{2,1,0:T(8,128)(2,1)S(1)}, bf16[8,1024,256]{2,1,0:T(8,128)(2,1)}, u32[]{:S(2)}) %copy-start.3) | copy-done | bytes 4194328
  66.8 6.7 %forward.1 = f32[8,2,512]{2,1,0:T(2,128)S(1)} custom-call(bf16[8,512,256]{2,1,0:T(8,128)(2,1)S(1)} %copy-done.7, bf16[8,1024,256]{2,1,0:T(8,128)(2,1)S(1)} %copy-done.3, s32[8,1,512]{2,1,0:T(1,128)S(1)} %reshape.314.tgt_ref), custom_call_target="tpu_custom_call" | custom-call | flops 2147483648 | bytes 6291456 | tf_op jit(solution)/shard_map/forward/pallas_call | solution.py:103
  74.2 6.1 %all-to-all-start.1 = ((f32[8,8,2,512]{3,2,1,0:T(2,128)}), f32[8,8,2,512]{3,2,1,0:T(2,128)S(1)}, u32[]{:S(2)}, u32[]{:S(2)}) async-start(f32[8,8,2,512]{3,2,1,0:T(2,128)} %broadcast_in_dim.101), calls=%async_computation.1 | async-start | bytes 524288 | tf_op jit(solution)/shard_map/all_to_all | solution.py:367
  81.7 3.2 %collective-permute-start.10 = (bf16[512,256]{1,0:T(8,128)(2,1)S(1)}, bf16[512,256]{1,0:T(8,128)(2,1)S(1)}, u32[]{:S(2)}, u32[]{:S(2)}) collective-permute-start(bf16[512,256]{1,0:T(8,128)(2,1)S(1)} %copy-done.21), channel_id=1, source_target_pairs={{0,16},{4,20},{8,24},{12,28},{16,0},{20,4},{24,8},{28,12},{1,17},{... | collective-permute-start | bytes 786440 | tf_op jit(solution)/shard_map/ppermute | solution.py:39
  86.1 2.4 %collective-permute-start.13 = (bf16[512,256]{1,0:T(8,128)(2,1)S(1)}, bf16[512,256]{1,0:T(8,128)(2,1)}, u32[]{:S(2)}, u32[]{:S(2)}) collective-permute-start(bf16[512,256]{1,0:T(8,128)(2,1)S(1)} %copy-done.13), channel_id=1, source_target_pairs={{0,28},{4,24},{8,4},{12,0},{16,12},{20,8},{24,20},{28,16},{1,29},{... | collective-permute-start | bytes 786440 | tf_op jit(solution)/shard_map/ppermute | solution.py:39
  88.5 2.3 %all-to-all-done.1 = f32[8,8,2,512]{3,2,1,0:T(2,128)S(1)} async-done(((f32[8,8,2,512]{3,2,1,0:T(2,128)}), f32[8,8,2,512]{3,2,1,0:T(2,128)S(1)}, u32[]{:S(2)}, u32[]{:S(2)}) %all-to-all-start.1) | async-done | bytes 262176 | tf_op jit(solution)/shard_map/all_to_all | solution.py:367
  92.2 2.3 %gather_fusion.2 = f32[512,32]{1,0:T(8,128)S(1)} fusion(f32[2048,32]{1,0:T(8,128)} %reshape.315, s32[1024]{0:T(1024)S(1)} %pad_clamp_fusion.2), kind=kCustom, calls=%fused_computation.2 | custom fusion | bytes 133120 | tf_op jit(solution)/shard_map/gather | solution.py:368
  100.3 4.2 %all-to-all-start.2 = ((f32[8,2,512]{2,1,0:T(2,128)}), f32[8,2,512]{2,1,0:T(2,128)S(1)}, u32[]{:S(2)}, u32[]{:S(2)}) async-start(f32[8,2,512]{2,1,0:T(2,128)} %pad_maximum_fusion.2.line_ref), calls=%async_computation.2 | async-start | bytes 65536 | tf_op jit(solution)/shard_map/all_to_all | solution.py:380
  104.5 2.2 %copy-done.4 = bf16[8,1024,256]{2,1,0:T(8,128)(2,1)S(1)} copy-done((bf16[8,1024,256]{2,1,0:T(8,128)(2,1)S(1)}, bf16[8,1024,256]{2,1,0:T(8,128)(2,1)}, u32[]{:S(2)}) %copy-start.4) | copy-done | bytes 4194328
  108.3 7.1 %query_parts.3 = (bf16[16,32,256]{2,1,0:T(8,128)(2,1)S(1)}, bf16[16,32,256]{2,1,0:T(8,128)(2,1)S(1)}, bf16[16,32,256]{2,1,0:T(8,128)(2,1)S(1)}, bf16[16,32,256]{2,1,0:T(8,128)(2,1)S(1)}) custom-call(s32[128]{0:T(128)S(1)} %max.12.blk, bf16[8,512,256]{2,1,0:T(8,128)(2,1)S(1)} %copy-done.8, bf16[8,1024,256]{2,1,0:T(8,128)(2,1)S(1)} %copy-done.4, ...), custom_call_target="tpu_custom_call" | custom-call | flops 2147483648 | bytes 6291456 | tf_op jit(solution)/shard_map/query_parts/pallas_call | solution.py:156
  115.5 1.8 %gather_fusion.4 = f32[64,32]{1,0:T(8,128)S(1)} fusion(f32[2048,32]{1,0:T(8,128)} %reshape.315, s32[1024]{0:T(1024)S(1)} %pad_clamp_fusion), kind=kCustom, calls=%fused_computation.4 | custom fusion | bytes 16640 | tf_op jit(solution)/shard_map/gather | solution.py:369
  119.5 1.7 collective-permute-start.22
  122.2 6.7 %item_parts.2 = f32[3,256,256]{2,1,0:T(8,128)S(1)} custom-call(s32[11]{0:T(128)S(1)} %pad_add_fusion.1.where, bf16[512,256]{1,0:T(8,128)(2,1)S(1)} %get-tuple-element.37.refs_0_, bf16[512,256]{1,0:T(8,128)(2,1)} %collective-permute-done.7.refs_1_, bf16[512,256]{1,0:T(8,128)(2,1)} %collective-permute-done.8.refs_2_, ...), custom_call_target="tpu_custom_call" | custom-call | flops 3221225472 | bytes 3276800 | tf_op jit(solution)/shard_map/item_parts/pallas_call | solution.py:211
  128.9 3.6 %item_parts.3 = (f32[1,128,256]{2,1,0:T(8,128)S(1)}, f32[1,128,256]{2,1,0:T(8,128)S(1)}) custom-call(s32[9]{0:T(128)S(1)} %pad_add_fusion.2.where, bf16[512,256]{1,0:T(8,128)(2,1)S(1)} %get-tuple-element.37.refs_0_, bf16[512,256]{1,0:T(8,128)(2,1)} %collective-permute-done.7.refs_1_, bf16[512,256]{1,0:T(8,128)(2,1)} %collective-permute-done.8.refs_2_, ...), custom_call_target="tpu_custom_call" | custom-call | flops 1073741824 | bytes 2490368 | tf_op jit(solution)/shard_map/item_parts/pallas_call | solution.py:211
  134.7 7.1 %query_parts.2 = (bf16[16,32,256]{2,1,0:T(8,128)(2,1)S(1)}, bf16[16,32,256]{2,1,0:T(8,128)(2,1)S(1)}, bf16[16,32,256]{2,1,0:T(8,128)(2,1)S(1)}, bf16[16,32,256]{2,1,0:T(8,128)(2,1)S(1)}) custom-call(s32[128]{0:T(128)S(1)} %max.12.blk, bf16[8,512,256]{2,1,0:T(8,128)(2,1)S(1)} %copy-done.9, bf16[8,1024,256]{2,1,0:T(8,128)(2,1)S(1)} %copy-done.5, ...), custom_call_target="tpu_custom_call" | custom-call | flops 2147483648 | bytes 6291456 | tf_op jit(solution)/shard_map/query_parts/pallas_call | solution.py:156
  141.9 1.8 collective-permute-start.15
  146.8 3.0 %collective-permute-start.23 = (bf16[16,32,256]{2,1,0:T(8,128)(2,1)S(1)}, bf16[16,32,256]{2,1,0:T(8,128)(2,1)S(1)}, u32[]{:S(2)}, u32[]{:S(2)}) collective-permute-start(bf16[16,32,256]{2,1,0:T(8,128)(2,1)S(1)} %add_convert_fusion.1), channel_id=1, source_target_pairs={{0,224},{32,0},{64,32},{96,64},{128,96},{160,128},{192,160},{224,1... | collective-permute-start | bytes 786440 | tf_op jit(solution)/shard_map/ppermute | solution.py:26
  149.8 4.0 %collective-permute-done.19 = bf16[16,32,256]{2,1,0:T(8,128)(2,1)S(1)} collective-permute-done((bf16[16,32,256]{2,1,0:T(8,128)(2,1)S(1)}, bf16[16,32,256]{2,1,0:T(8,128)(2,1)S(1)}, u32[]{:S(2)}, u32[]{:S(2)}) %collective-permute-start.19) | collective-permute-done | bytes 262176 | tf_op jit(solution)/shard_map/ppermute | solution.py:26
  156.3 3.3 %collective-permute-start.24 = (bf16[16,32,256]{2,1,0:T(8,128)(2,1)S(1)}, bf16[16,32,256]{2,1,0:T(8,128)(2,1)S(1)}, u32[]{:S(2)}, u32[]{:S(2)}) collective-permute-start(bf16[16,32,256]{2,1,0:T(8,128)(2,1)S(1)} %add_convert_fusion), channel_id=1, source_target_pairs={{0,224},{32,0},{64,32},{96,64},{128,96},{160,128},{192,160},{224,1... | collective-permute-start | bytes 786440 | tf_op jit(solution)/shard_map/ppermute | solution.py:26
  159.5 2.3 %collective-permute-done.20 = bf16[16,32,256]{2,1,0:T(8,128)(2,1)S(1)} collective-permute-done((bf16[16,32,256]{2,1,0:T(8,128)(2,1)S(1)}, bf16[16,32,256]{2,1,0:T(8,128)(2,1)S(1)}, u32[]{:S(2)}, u32[]{:S(2)}) %collective-permute-start.20) | collective-permute-done | bytes 262176 | tf_op jit(solution)/shard_map/ppermute | solution.py:26
  164.2 2.8 %collective-permute-done.27.far_a = f32[128,256]{1,0:T(8,128)S(1)} collective-permute-done((f32[128,256]{1,0:T(8,128)S(1)}, f32[128,256]{1,0:T(8,128)S(1)}, u32[]{:S(2)}, u32[]{:S(2)}) %collective-permute-start.27) | collective-permute-done | bytes 131104 | tf_op jit(solution)/shard_map/ppermute | solution.py:26
  168.8 2.1 %update.1 = (f32[1024,256]{1,0:T(8,128)}, f32[1024,256]{1,0:T(8,128)}) custom-call(s32[1]{0:T(128)} %bitcast.16.x_ref, f32[256,256]{1,0:T(8,128)S(1)} %fusion.own, f32[256,256]{1,0:T(8,128)S(1)} %collective-permute-done.25.after, f32[256,256]{1,0:T(8,128)S(1)} %collective-permute-done.26.before, f32[128,256]{1,0:T(8,128)S(1)} %collective-permute-done.27.far_a, ...), custom_call_target="tpu_custom_call" | custom-call | tf_op jit(solution)/shard_map/update/pallas_call | solution.py:262
  (184 shorter events, 45.3 us)
Async XLA Ops:
  7.2 55.8 %all-gather.2.cloned.1.call-start = ((), (), s32[]{:S(2)}) async-start(), calls=%async_computation.3 | async-start | bytes 4718592 | tf_op jit(solution)/shard_map/all_gather | solution.py:294
  9.8 12.5 %collective-permute-start = (bf16[16,32,256]{2,1,0:T(8,128)(2,1)}, bf16[16,32,256]{2,1,0:T(8,128)(2,1)S(1)}, u32[]{:S(2)}, u32[]{:S(2)}) collective-permute-start(bf16[16,32,256]{2,1,0:T(8,128)(2,1)} %bitcast.66), channel_id=1, source_target_pairs={{0,32},{32,64},{64,96},{96,128},{128,160},{160,192},{192,224},{224... | collective-permute-start | bytes 786440 | tf_op jit(solution)/shard_map/ppermute | solution.py:26
  11.8 10.5 %collective-permute-start.1 = (bf16[16,32,256]{2,1,0:T(8,128)(2,1)}, bf16[16,32,256]{2,1,0:T(8,128)(2,1)S(1)}, u32[]{:S(2)}, u32[]{:S(2)}) collective-permute-start(bf16[16,32,256]{2,1,0:T(8,128)(2,1)} %bitcast.67), channel_id=1, source_target_pairs={{0,224},{32,0},{64,32},{96,64},{128,96},{160,128},{192,160},{224,1... | collective-permute-start | bytes 786440 | tf_op jit(solution)/shard_map/ppermute | solution.py:26
  27.3 13.9 %all-to-all-start = ((s32[8,1,592]{2,1,0:T(1,128)}), s32[8,1,592]{2,1,0:T(1,128)S(1)}, u32[]{:S(2)}, u32[]{:S(2)}) async-start(s32[8,1,592]{2,1,0:T(1,128)} %copy.43), calls=%async_computation | async-start | bytes 40960 | tf_op jit(solution)/shard_map/all_to_all | solution.py:335
  33.2 8.8 %collective-permute-start.2 = (bf16[16,32,256]{2,1,0:T(8,128)(2,1)S(1)}, bf16[16,32,256]{2,1,0:T(8,128)(2,1)S(1)}, u32[]{:S(2)}, u32[]{:S(2)}) collective-permute-start(bf16[16,32,256]{2,1,0:T(8,128)(2,1)S(1)} %collective-permute-done.refs_2_), channel_id=1, source_target_pairs={{0,32},{32,64},{64,96},{96,128},{128,160},{160,192},{192,224},{224... | collective-permute-start | bytes 786440 | tf_op jit(solution)/shard_map/ppermute | solution.py:26
  35.3 7.8 %collective-permute-start.3 = (bf16[16,32,256]{2,1,0:T(8,128)(2,1)S(1)}, bf16[16,32,256]{2,1,0:T(8,128)(2,1)S(1)}, u32[]{:S(2)}, u32[]{:S(2)}) collective-permute-start(bf16[16,32,256]{2,1,0:T(8,128)(2,1)S(1)} %collective-permute-done.1.refs_1_), channel_id=1, source_target_pairs={{0,224},{32,0},{64,32},{96,64},{128,96},{160,128},{192,160},{224,1... | collective-permute-start | bytes 786440 | tf_op jit(solution)/shard_map/ppermute | solution.py:26
  42.0 7.6 %collective-permute-start.5 = (bf16[16,32,256]{2,1,0:T(8,128)(2,1)S(1)}, bf16[16,32,256]{2,1,0:T(8,128)(2,1)S(1)}, u32[]{:S(2)}, u32[]{:S(2)}) collective-permute-start(bf16[16,32,256]{2,1,0:T(8,128)(2,1)S(1)} %collective-permute-done.2.refs_3_), channel_id=1, source_target_pairs={{0,32},{32,64},{64,96},{96,128},{128,160},{160,192},{192,224},{224... | collective-permute-start | bytes 786440 | tf_op jit(solution)/shard_map/ppermute | solution.py:26
  43.1 6.9 %collective-permute-start.4 = (bf16[16,32,256]{2,1,0:T(8,128)(2,1)S(1)}, bf16[16,32,256]{2,1,0:T(8,128)(2,1)S(1)}, u32[]{:S(2)}, u32[]{:S(2)}) collective-permute-start(bf16[16,32,256]{2,1,0:T(8,128)(2,1)S(1)} %collective-permute-done.3.refs_4_), channel_id=1, source_target_pairs={{0,224},{32,0},{64,32},{96,64},{128,96},{160,128},{192,160},{224,1... | collective-permute-start | bytes 786440 | tf_op jit(solution)/shard_map/ppermute | solution.py:26
  49.7 7.6 %collective-permute-start.6 = (bf16[16,32,256]{2,1,0:T(8,128)(2,1)S(1)}, bf16[16,32,256]{2,1,0:T(8,128)(2,1)S(1)}, u32[]{:S(2)}, u32[]{:S(2)}) collective-permute-start(bf16[16,32,256]{2,1,0:T(8,128)(2,1)S(1)} %collective-permute-done.5.refs_7_), channel_id=1, source_target_pairs={{0,32},{32,64},{64,96},{96,128},{128,160},{160,192},{192,224},{224... | collective-permute-start | bytes 786440 | tf_op jit(solution)/shard_map/ppermute | solution.py:26
  74.2 16.6 %all-to-all-start.1 = ((f32[8,8,2,512]{3,2,1,0:T(2,128)}), f32[8,8,2,512]{3,2,1,0:T(2,128)S(1)}, u32[]{:S(2)}, u32[]{:S(2)}) async-start(f32[8,8,2,512]{3,2,1,0:T(2,128)} %broadcast_in_dim.101), calls=%async_computation.1 | async-start | bytes 524288 | tf_op jit(solution)/shard_map/all_to_all | solution.py:367
  81.7 15.5 %collective-permute-start.10 = (bf16[512,256]{1,0:T(8,128)(2,1)S(1)}, bf16[512,256]{1,0:T(8,128)(2,1)S(1)}, u32[]{:S(2)}, u32[]{:S(2)}) collective-permute-start(bf16[512,256]{1,0:T(8,128)(2,1)S(1)} %copy-done.21), channel_id=1, source_target_pairs={{0,16},{4,20},{8,24},{12,28},{16,0},{20,4},{24,8},{28,12},{1,17},{... | collective-permute-start | bytes 786440 | tf_op jit(solution)/shard_map/ppermute | solution.py:39
  84.9 14.0 %collective-permute-start.11 = (bf16[512,256]{1,0:T(8,128)(2,1)S(1)}, bf16[512,256]{1,0:T(8,128)(2,1)S(1)}, u32[]{:S(2)}, u32[]{:S(2)}) collective-permute-start(bf16[512,256]{1,0:T(8,128)(2,1)S(1)} %copy-done.19), channel_id=1, source_target_pairs={{0,20},{4,16},{8,28},{12,24},{16,4},{20,0},{24,12},{28,8},{1,21},{... | collective-permute-start | bytes 786440 | tf_op jit(solution)/shard_map/ppermute | solution.py:39
  84.9 33.1 %collective-permute-start.12 = (bf16[512,256]{1,0:T(8,128)(2,1)S(1)}, bf16[512,256]{1,0:T(8,128)(2,1)}, u32[]{:S(2)}, u32[]{:S(2)}) collective-permute-start(bf16[512,256]{1,0:T(8,128)(2,1)S(1)} %copy-done.15), channel_id=1, source_target_pairs={{0,24},{4,28},{8,0},{12,4},{16,8},{20,12},{24,16},{28,20},{1,25},{... | collective-permute-start | bytes 786440 | tf_op jit(solution)/shard_map/ppermute | solution.py:39
  86.1 33.4 %collective-permute-start.13 = (bf16[512,256]{1,0:T(8,128)(2,1)S(1)}, bf16[512,256]{1,0:T(8,128)(2,1)}, u32[]{:S(2)}, u32[]{:S(2)}) collective-permute-start(bf16[512,256]{1,0:T(8,128)(2,1)S(1)} %copy-done.13), channel_id=1, source_target_pairs={{0,28},{4,24},{8,4},{12,0},{16,12},{20,8},{24,20},{28,16},{1,29},{... | collective-permute-start | bytes 786440 | tf_op jit(solution)/shard_map/ppermute | solution.py:39
  88.5 32.8 %collective-permute-start.7 = (bf16[512,256]{1,0:T(8,128)(2,1)S(1)}, bf16[512,256]{1,0:T(8,128)(2,1)}, u32[]{:S(2)}, u32[]{:S(2)}) collective-permute-start(bf16[512,256]{1,0:T(8,128)(2,1)S(1)} %copy-done.11), channel_id=1, source_target_pairs={{0,4},{4,0},{8,12},{12,8},{16,20},{20,16},{24,28},{28,24},{1,5},{5... | collective-permute-start | bytes 786440 | tf_op jit(solution)/shard_map/ppermute | solution.py:39
  97.3 24.0 %collective-permute-start.8 = (bf16[512,256]{1,0:T(8,128)(2,1)S(1)}, bf16[512,256]{1,0:T(8,128)(2,1)}, u32[]{:S(2)}, u32[]{:S(2)}) collective-permute-start(bf16[512,256]{1,0:T(8,128)(2,1)S(1)} %get-tuple-element.39), channel_id=1, source_target_pairs={{0,8},{4,12},{8,16},{12,20},{16,24},{20,28},{24,0},{28,4},{1,9},{5... | collective-permute-start | bytes 786440 | tf_op jit(solution)/shard_map/ppermute | solution.py:39
  99.7 21.6 %collective-permute-start.9 = (bf16[512,256]{1,0:T(8,128)(2,1)S(1)}, bf16[512,256]{1,0:T(8,128)(2,1)}, u32[]{:S(2)}, u32[]{:S(2)}) collective-permute-start(bf16[512,256]{1,0:T(8,128)(2,1)S(1)} %get-tuple-element.40), channel_id=1, source_target_pairs={{0,12},{4,8},{8,20},{12,16},{16,28},{20,24},{24,4},{28,0},{1,13},{... | collective-permute-start | bytes 786440 | tf_op jit(solution)/shard_map/ppermute | solution.py:39
  100.3 21.0 %all-to-all-start.2 = ((f32[8,2,512]{2,1,0:T(2,128)}), f32[8,2,512]{2,1,0:T(2,128)S(1)}, u32[]{:S(2)}, u32[]{:S(2)}) async-start(f32[8,2,512]{2,1,0:T(2,128)} %pad_maximum_fusion.2.line_ref), calls=%async_computation.2 | async-start | bytes 65536 | tf_op jit(solution)/shard_map/all_to_all | solution.py:380
  118.0 25.7 %collective-permute-start.18 = (bf16[16,32,256]{2,1,0:T(8,128)(2,1)S(1)}, bf16[16,32,256]{2,1,0:T(8,128)(2,1)}, u32[]{:S(2)}, u32[]{:S(2)}) collective-permute-start(bf16[16,32,256]{2,1,0:T(8,128)(2,1)S(1)} %get-tuple-element.52), channel_id=1, source_target_pairs={{0,32},{32,64},{64,96},{96,128},{128,160},{160,192},{192,224},{224... | collective-permute-start | bytes 786440 | tf_op jit(solution)/shard_map/ppermute | solution.py:26
  119.5 26.2 %collective-permute-start.22 = (bf16[16,32,256]{2,1,0:T(8,128)(2,1)S(1)}, bf16[16,32,256]{2,1,0:T(8,128)(2,1)}, u32[]{:S(2)}, u32[]{:S(2)}) collective-permute-start(bf16[16,32,256]{2,1,0:T(8,128)(2,1)S(1)} %get-tuple-element.56), channel_id=1, source_target_pairs={{0,224},{32,0},{64,32},{96,64},{128,96},{160,128},{192,160},{224,1... | collective-permute-start | bytes 786440 | tf_op jit(solution)/shard_map/ppermute | solution.py:26
  132.6 9.3 %collective-permute-start.14 = (f32[128,256]{1,0:T(8,128)S(1)}, f32[128,256]{1,0:T(8,128)S(1)}, u32[]{:S(2)}, u32[]{:S(2)}) collective-permute-start(f32[128,256]{1,0:T(8,128)S(1)} %bitcast.70), channel_id=1, source_target_pairs={{0,1},{1,2},{2,3},{3,0},{4,5},{5,6},{6,7},{7,4},{8,9},{9,10},{10,1... | collective-permute-start | bytes 393224 | tf_op jit(solution)/shard_map/ppermute | solution.py:26
  133.1 8.7 %collective-permute-start.16 = (f32[128,256]{1,0:T(8,128)S(1)}, f32[128,256]{1,0:T(8,128)S(1)}, u32[]{:S(2)}, u32[]{:S(2)}) collective-permute-start(f32[128,256]{1,0:T(8,128)S(1)} %bitcast.69), channel_id=1, source_target_pairs={{0,3},{1,0},{2,1},{3,2},{4,7},{5,4},{6,5},{7,6},{8,11},{9,8},{10,9... | collective-permute-start | bytes 393224 | tf_op jit(solution)/shard_map/ppermute | solution.py:26
  141.9 12.1 %collective-permute-start.15 = (f32[256,256]{1,0:T(8,128)S(1)}, f32[256,256]{1,0:T(8,128)S(1)}, u32[]{:S(2)}, u32[]{:S(2)}) collective-permute-start(f32[256,256]{1,0:T(8,128)S(1)} %pad_maximum_fusion), channel_id=1, source_target_pairs={{0,1},{1,2},{2,3},{3,0},{4,5},{5,6},{6,7},{7,4},{8,9},{9,10},{10,1... | collective-permute-start | bytes 786440 | tf_op jit(solution)/shard_map/ppermute | solution.py:26
  144.7 9.1 %collective-permute-start.19 = (bf16[16,32,256]{2,1,0:T(8,128)(2,1)S(1)}, bf16[16,32,256]{2,1,0:T(8,128)(2,1)S(1)}, u32[]{:S(2)}, u32[]{:S(2)}) collective-permute-start(bf16[16,32,256]{2,1,0:T(8,128)(2,1)S(1)} %add_convert_fusion.4), channel_id=1, source_target_pairs={{0,32},{32,64},{64,96},{96,128},{128,160},{160,192},{192,224},{224... | collective-permute-start | bytes 786440 | tf_op jit(solution)/shard_map/ppermute | solution.py:26
  145.3 8.7 %collective-permute-start.17 = (f32[256,256]{1,0:T(8,128)S(1)}, f32[256,256]{1,0:T(8,128)S(1)}, u32[]{:S(2)}, u32[]{:S(2)}) collective-permute-start(f32[256,256]{1,0:T(8,128)S(1)} %pad_maximum_fusion.1), channel_id=1, source_target_pairs={{0,3},{1,0},{2,1},{3,2},{4,7},{5,4},{6,5},{7,6},{8,11},{9,8},{10,9... | collective-permute-start | bytes 786440 | tf_op jit(solution)/shard_map/ppermute | solution.py:26
  146.8 9.4 %collective-permute-start.23 = (bf16[16,32,256]{2,1,0:T(8,128)(2,1)S(1)}, bf16[16,32,256]{2,1,0:T(8,128)(2,1)S(1)}, u32[]{:S(2)}, u32[]{:S(2)}) collective-permute-start(bf16[16,32,256]{2,1,0:T(8,128)(2,1)S(1)} %add_convert_fusion.1), channel_id=1, source_target_pairs={{0,224},{32,0},{64,32},{96,64},{128,96},{160,128},{192,160},{224,1... | collective-permute-start | bytes 786440 | tf_op jit(solution)/shard_map/ppermute | solution.py:26
  153.9 7.9 %collective-permute-start.20 = (bf16[16,32,256]{2,1,0:T(8,128)(2,1)S(1)}, bf16[16,32,256]{2,1,0:T(8,128)(2,1)S(1)}, u32[]{:S(2)}, u32[]{:S(2)}) collective-permute-start(bf16[16,32,256]{2,1,0:T(8,128)(2,1)S(1)} %add_convert_fusion.3), channel_id=1, source_target_pairs={{0,32},{32,64},{64,96},{96,128},{128,160},{160,192},{192,224},{224... | collective-permute-start | bytes 786440 | tf_op jit(solution)/shard_map/ppermute | solution.py:26
  154.1 7.9 %collective-permute-start.26 = (f32[256,256]{1,0:T(8,128)S(1)}, f32[256,256]{1,0:T(8,128)S(1)}, u32[]{:S(2)}, u32[]{:S(2)}) collective-permute-start(f32[256,256]{1,0:T(8,128)S(1)} %fusion.own), channel_id=1, source_target_pairs={{0,1},{1,2},{2,3},{3,0},{4,5},{5,6},{6,7},{7,4},{8,9},{9,10},{10,1... | collective-permute-start | bytes 786440 | tf_op jit(solution)/shard_map/ppermute | solution.py:26
  154.6 7.9 %collective-permute-start.25 = (f32[256,256]{1,0:T(8,128)S(1)}, f32[256,256]{1,0:T(8,128)S(1)}, u32[]{:S(2)}, u32[]{:S(2)}) collective-permute-start(f32[256,256]{1,0:T(8,128)S(1)} %fusion.own), channel_id=1, source_target_pairs={{0,3},{1,0},{2,1},{3,2},{4,7},{5,4},{6,5},{7,6},{8,11},{9,8},{10,9... | collective-permute-start | bytes 786440 | tf_op jit(solution)/shard_map/ppermute | solution.py:26
  156.3 14.6 %collective-permute-start.24 = (bf16[16,32,256]{2,1,0:T(8,128)(2,1)S(1)}, bf16[16,32,256]{2,1,0:T(8,128)(2,1)S(1)}, u32[]{:S(2)}, u32[]{:S(2)}) collective-permute-start(bf16[16,32,256]{2,1,0:T(8,128)(2,1)S(1)} %add_convert_fusion), channel_id=1, source_target_pairs={{0,224},{32,0},{64,32},{96,64},{128,96},{160,128},{192,160},{224,1... | collective-permute-start | bytes 786440 | tf_op jit(solution)/shard_map/ppermute | solution.py:26
  161.9 8.9 %collective-permute-start.21 = (bf16[16,32,256]{2,1,0:T(8,128)(2,1)S(1)}, bf16[16,32,256]{2,1,0:T(8,128)(2,1)S(1)}, u32[]{:S(2)}, u32[]{:S(2)}) collective-permute-start(bf16[16,32,256]{2,1,0:T(8,128)(2,1)S(1)} %add_convert_fusion.2), channel_id=1, source_target_pairs={{0,32},{32,64},{64,96},{96,128},{128,160},{160,192},{192,224},{224... | collective-permute-start | bytes 786440 | tf_op jit(solution)/shard_map/ppermute | solution.py:26
  162.5 6.3 %collective-permute-start.28 = (f32[128,256]{1,0:T(8,128)S(1)}, f32[128,256]{1,0:T(8,128)S(1)}, u32[]{:S(2)}, u32[]{:S(2)}) collective-permute-start(f32[128,256]{1,0:T(8,128)S(1)} %slice.85), channel_id=1, source_target_pairs={{0,3},{1,0},{2,1},{3,2},{4,7},{5,4},{6,5},{7,6},{8,11},{9,8},{10,9... | collective-permute-start | bytes 393224 | tf_op jit(solution)/shard_map/ppermute | solution.py:26
  (25 other events, 269.2 us)
Sparse Core Ops, SparseCore 0:
  10.5 37.5 all-gather.1

commit v5 on v4

--- a/solution.py
+++ b/solution.py
@@ -9,16 +9,14 @@
 
 MOST = 2
 EMPTY = 1e30
-NEAR = (0, 1, 7, 6)
-FAR = (2, 3, 4, 5)
-ORDER = NEAR + FAR
 PLANE = ("y", "c")
 F32 = jnp.float32
 BF16 = jnp.bfloat16
 NT = (((1,), (1,)), ((), ()))
 TN = (((0,), (0,)), ((), ()))
 TILE = 256
-VMEM = 24 << 20
+LARGE = 56 << 20
+SMALL = 20 << 20
 
 
 def shift(value, axis, step):
@@ -67,7 +65,7 @@
             + [pl.BlockSpec(out.shape, lambda j, blk: (0, 0))] * plane,
         ),
         out_shape=[jax.ShapeDtypeStruct((plane, width, shape[2]), BF16)] + [out] * plane,
-        compiler_params=pltpu.CompilerParams(vmem_limit_bytes=VMEM),
+        compiler_params=pltpu.CompilerParams(vmem_limit_bytes=LARGE),
         cost_estimate=pl.CostEstimate(
             flops=0, bytes_accessed=6 * plane * width * shape[2], transcendentals=0
         ),
@@ -75,15 +73,28 @@
     )(jnp.concatenate([blk, peers]), *sources)
 
 
-def forward_kernel(p_ref, t_ref, tgt_ref, stat_ref, s_ref):
+def fetch_table(t_hbm, t_all, sems):
+    step = pl.program_id(0)
+
+    @pl.when(step == 0)
+    def _():
+        for j in range(t_all.shape[0]):
+            pltpu.make_async_copy(t_hbm.at[j], t_all.at[j], sems.at[j]).start()
+
+    pltpu.make_async_copy(t_hbm.at[step], t_all.at[step], sems.at[step]).wait()
+    return t_all.at[step]
+
+
+def forward_kernel(p_ref, t_hbm, tgt_ref, stat_ref, s_ref, t_all, sems):
+    t_ref = fetch_table(t_hbm, t_all, sems)
     q = p_ref[0]
-    items = t_ref.shape[1]
+    items = t_ref.shape[0]
     width = q.shape[0]
     tgt = tgt_ref[0]
     high = jnp.full((8, width), -jnp.inf, F32)
     pick = jnp.zeros((8, width), F32)
     for start in range(0, items, TILE):
-        s = lax.dot_general(t_ref[0, pl.ds(start, TILE), :], q, NT, preferred_element_type=F32)
+        s = lax.dot_general(t_ref[pl.ds(start, TILE), :], q, NT, preferred_element_type=F32)
         s_ref[pl.ds(start, TILE), :] = s
         high = jnp.maximum(high, jnp.max(s.reshape(TILE // 8, 8, width), axis=0))
         hit = jnp.where(tile_ids(start, s.shape) == tgt, s, 0.0)
@@ -105,13 +116,17 @@
         grid=(planes,),
         in_specs=[
             pl.BlockSpec((1, width, features), lambda j: (j, 0, 0)),
-            pl.BlockSpec((1, items, features), lambda j: (j, 0, 0)),
+            pl.BlockSpec(memory_space=pl.ANY),
             pl.BlockSpec((1, 1, width), lambda j: (j, 0, 0)),
         ],
         out_specs=pl.BlockSpec((1, 2, width), lambda j: (j, 0, 0)),
         out_shape=jax.ShapeDtypeStruct((planes, 2, width), F32),
-        scratch_shapes=[pltpu.VMEM((items, width), F32)],
-        compiler_params=pltpu.CompilerParams(vmem_limit_bytes=VMEM),
+        scratch_shapes=[
+            pltpu.VMEM((items, width), F32),
+            pltpu.VMEM(tables.shape, BF16),
+            pltpu.SemaphoreType.DMA((planes,)),
+        ],
+        compiler_params=pltpu.CompilerParams(vmem_limit_bytes=LARGE),
         cost_estimate=pl.CostEstimate(
             flops=2 * planes * width * items * features,
             bytes_accessed=planes * items * features * 2 + planes * width * features * 2,
@@ -121,8 +136,81 @@
     )(packed, tables, targets)
 
 
-def query_kernel(half, blk, p_ref, t_ref, line_ref, g0, g1, g2, g3, c_ref, acc_ref):
+def combine_kernel(addr, named, a_ref, tgt_ref, line_ref, loss_ref, part_ref, lse_ref):
+    picks = part_ref.shape[0]
+    blocks = lse_ref.shape[0]
+    own_blocks = loss_ref.shape[0]
+    slots = line_ref.shape[2] // 32
+
+    def fetch(pair, kind):
+        a = addr[pair]
+        group = pl.multiple_of(lax.shift_right_logical(a, 2) % 4 * 128, 128)
+        row = a_ref[lax.shift_right_logical(a, 4), pl.ds(kind, 1), pl.ds(group, 128)]
+        return pltpu.roll(row, (4 - a % 4) % 4 * 32, 1)
+
+    def gather(i, carry):
+        for p in range(picks):
+            part_ref[p, pl.ds(i, 1), :] = fetch(i * picks + p, 0)
+        return carry
+
+    lax.fori_loop(0, blocks, gather, 0, unroll=4)
+    part = part_ref[...]
+    top = jnp.max(part, axis=0)
+    lse_ref[...] = top + jnp.log(jnp.sum(jnp.exp(part - top[None]), axis=0))
+
+    def loss(i, carry):
+        total = lse_ref[pl.ds(i, 1), :]
+        for p in range(picks):
+            total = total - fetch(i * picks + p, 1)
+        loss_ref[pl.ds(i, 1), :] = total
+        return carry
+
+    lax.fori_loop(0, own_blocks, loss, 0, unroll=4)
+    lane = lax.broadcasted_iota(jnp.int32, (1, 128), 1)
+
+    def lines(j, carry):
+        for group in range(slots // 4):
+            value = jnp.full((1, 128), EMPTY, F32)
+            for m in range(4):
+                slot = group * 4 + m
+                b = named[j * slots + slot]
+                row = lse_ref[pl.ds(slot // MOST * own_blocks + jnp.maximum(b, 0), 1), :]
+                if m:
+                    row = pltpu.roll(row, m * 32, 1)
+                keep = (lane >= m * 32) & (lane < m * 32 + 32) & (jnp.full((1, 128), b) >= 0)
+                value = jnp.where(keep, row, value)
+            line_ref[j, 0:1, group * 128:(group + 1) * 128] = value
+        line_ref[j, 1:2, :] = tgt_ref[j].astype(F32)
+        return carry
+
+    lax.fori_loop(0, line_ref.shape[0], lines, 0)
+
+
+def combine(addr, named, all_stats, targets, block_count, picks):
+    blocks = addr.shape[0] // picks
+    plane, _, width = targets.shape
+    whole = lambda shape: pl.BlockSpec(shape, lambda i, a, b: (0,) * len(shape))
+    lines = jax.ShapeDtypeStruct((plane, 2, width), F32)
+    loss = jax.ShapeDtypeStruct((block_count, 128), F32)
+    return pl.pallas_call(
+        combine_kernel,
+        grid_spec=pltpu.PrefetchScalarGridSpec(
+            num_scalar_prefetch=2,
+            grid=(1,),
+            in_specs=[whole(all_stats.shape), whole(targets.shape)],
+            out_specs=[whole(lines.shape), whole(loss.shape)],
+            scratch_shapes=[pltpu.VMEM((picks, blocks, 128), F32), pltpu.VMEM((blocks, 128), F32)],
+        ),
+        out_shape=[lines, loss],
+        compiler_params=pltpu.CompilerParams(vmem_limit_bytes=SMALL),
+        name="combine",
+    )(addr, named, all_stats, targets)
+
+
+def query_kernel(blk, p_ref, t_hbm, line_ref, g_ref, c_ref, acc_ref, t_all, sems):
     step = pl.program_id(0)
+    t_ref = fetch_table(t_hbm, t_all, sems)
+    sources, blocks, block_rows, _ = acc_ref.shape
 
     @pl.when(step == 0)
     def _():
@@ -131,46 +219,49 @@
     q = p_ref[0]
     lse = line_ref[0, 0:1, :]
     tgt = line_ref[0, 1:2, :].astype(jnp.int32)
-    items = t_ref.shape[1]
+    items = t_ref.shape[0]
     for start in range(0, items, TILE):
-        s = lax.dot_general(t_ref[0, pl.ds(start, TILE), :], q, NT, preferred_element_type=F32)
+        s = lax.dot_general(t_ref[pl.ds(start, TILE), :], q, NT, preferred_element_type=F32)
         e = jnp.exp(s - lse)
         c = jnp.where(tile_ids(start, s.shape) == tgt, e - 1.0, e)
         c_ref[pl.ds(start, TILE), :] = c.astype(BF16)
-    g = lax.dot_general(c_ref[...], t_ref[0], TN, preferred_element_type=F32)
-    block_rows = g0.shape[1]
-    for slot in range(8):
-        b = blk[step * 16 + half * 8 + slot]
+    g = lax.dot_general(c_ref[...], t_ref[...], TN, preferred_element_type=F32)
+    slots = sources * MOST
+    for slot in range(slots):
+        b = blk[step * slots + slot]
         acc_ref[slot // MOST, b] += g[slot * block_rows:(slot + 1) * block_rows, :]
 
     @pl.when(step == pl.num_programs(0) - 1)
     def _():
-        for i, out in enumerate((g0, g1, g2, g3)):
-            out[...] = acc_ref[i].astype(BF16)
-
-
-def query_parts(packed, blk, lines, tables, half, blocks, block_rows):
+        z = blk[pl.num_programs(0) * slots]
+        for i in range(sources):
+            g_ref[lax.rem(z + i, sources)] = acc_ref[i].astype(BF16)
+
+
+def query_parts(packed, blk, lines, tables, sources, blocks, block_rows):
     planes, items, features = tables.shape
-    width = packed.shape[1] // 2
-    out = jax.ShapeDtypeStruct((blocks, block_rows, features), BF16)
+    width = packed.shape[1]
+    out = jax.ShapeDtypeStruct((sources, blocks, block_rows, features), BF16)
     return pl.pallas_call(
-        functools.partial(query_kernel, half),
+        query_kernel,
         grid_spec=pltpu.PrefetchScalarGridSpec(
             num_scalar_prefetch=1,
             grid=(planes,),
             in_specs=[
-                pl.BlockSpec((1, width, features), lambda j, blk: (j, half, 0)),
-                pl.BlockSpec((1, items, features), lambda j, blk: (j, 0, 0)),
-                pl.BlockSpec((1, 2, width), lambda j, blk: (j, 0, half)),
+                pl.BlockSpec((1, width, features), lambda j, blk: (j, 0, 0)),
+                pl.BlockSpec(memory_space=pl.ANY),
+                pl.BlockSpec((1, 2, width), lambda j, blk: (j, 0, 0)),
             ],
-            out_specs=[pl.BlockSpec(out.shape, lambda j, blk: (0, 0, 0))] * 4,
+            out_specs=pl.BlockSpec(out.shape, lambda j, blk: (0, 0, 0, 0)),
             scratch_shapes=[
                 pltpu.VMEM((items, width), BF16),
-                pltpu.VMEM((4, blocks, block_rows, features), F32),
+                pltpu.VMEM(out.shape, F32),
+                pltpu.VMEM(tables.shape, BF16),
+                pltpu.SemaphoreType.DMA((planes,)),
             ],
         ),
-        out_shape=[out] * 4,
-        compiler_params=pltpu.CompilerParams(vmem_limit_bytes=VMEM),
+        out_shape=out,
+        compiler_params=pltpu.CompilerParams(vmem_limit_bytes=LARGE),
         cost_estimate=pl.CostEstimate(
             flops=4 * planes * width * items * features,
             bytes_accessed=planes * items * features * 2 + 2 * planes * width * features * 2,
@@ -221,7 +312,7 @@
             out_specs=[pl.BlockSpec((1,) + out.shape[1:], lambda i, o: (i, 0, 0))] * pieces,
         ),
         out_shape=[out] * pieces,
-        compiler_params=pltpu.CompilerParams(vmem_limit_bytes=VMEM),
+        compiler_params=pltpu.CompilerParams(vmem_limit_bytes=SMALL),
         cost_estimate=pl.CostEstimate(
             flops=4 * share * span * count * width * features,
             bytes_accessed=2 * count * width * features + share * span * features * 6,
@@ -268,7 +359,7 @@
             out_specs=[block] * 2,
         ),
         out_shape=[jax.ShapeDtypeStruct(table.shape, F32)] * 2,
-        compiler_params=pltpu.CompilerParams(vmem_limit_bytes=VMEM),
+        compiler_params=pltpu.CompilerParams(vmem_limit_bytes=SMALL),
         name="update",
     )(x, own, after, before, far_a, far_b, table, accum)
 
@@ -334,7 +425,7 @@
     )
     got = lax.all_to_all(meta, "z", 0, 0, tiled=True)
     by_source[4] = shift(by_source[5], "z", 1)
-    order = jnp.array(ORDER, jnp.int32)
+    order = jnp.arange(z_size, dtype=jnp.int32)
     got = got[(z + order) % z_size]
     width = z_size * MOST * block_rows
     cut = per_plane * block_rows
@@ -347,16 +438,13 @@
     pair_slot = got[:, cut + per_plane:]
     pair_owner = pair_slot // MOST
     pair_from = (pair_owner // plane - z) % z_size
-    pair_rel = (order[:, None] - pair_from) % z_size
-    pair_place = jnp.zeros_like(pair_rel)
-    for place, d in enumerate(ORDER):
-        pair_place = jnp.where(pair_rel == d, place, pair_place)
-    pair_row = (pair_owner * 2 * z_size + pair_place) * MOST + pair_slot % MOST
+    pair_place = (order[:, None] - pair_from) % z_size
+    pair_row = (pair_owner * z_size + pair_place) * MOST + pair_slot % MOST
 
     hops = jnp.arange(plane, dtype=jnp.int32)
     peers = (y + hops // c_size) % y_size * c_size + (c + hops % c_size) % c_size
     origin = (y - hops // c_size) % y_size * c_size + (c - hops % c_size) % c_size
-    packed, *outgoing = pack([by_source[d] for d in ORDER], blk, peers)
+    packed, *outgoing = pack([by_source[d] for d in range(z_size)], blk, peers)
     rows = [
         shift_plane(value, hop // c_size, hop % c_size) if hop else value
         for hop, value in enumerate(outgoing)
@@ -364,42 +452,23 @@
     stats = forward(packed, targets, tables)
 
     spread = jnp.broadcast_to(stats[None], (z_size,) + stats.shape)
-    all_stats = lax.all_to_all(spread, "z", 0, 0, tiled=True).reshape(-1, block_rows)
-    part = all_stats[pair_row.reshape(-1)].reshape(z_size, block_count, picks, block_rows)
-    pick = all_stats[pair_row[0] + z_size * MOST].reshape(block_count, picks, block_rows)
-    top = jnp.max(part, axis=2)
-    lse = top + jnp.log(jnp.sum(jnp.exp(part - top[:, :, None]), axis=2))
-    losses = (lse[0] - jnp.sum(pick, axis=1)).reshape(local_rows)
-    lse_rows = lse.reshape(z_size * block_count, block_rows)
-    first = jnp.arange(z_size, dtype=jnp.int32).reshape(1, z_size, 1) * block_count
-    lse_at = (blk.reshape(plane, z_size, MOST) + first).reshape(-1)
-    lse_slots = jnp.where(named[:, None] < 0, F32(EMPTY), lse_rows[lse_at])
-    lines = jnp.concatenate(
-        [lse_slots.reshape(plane, 1, width), targets.astype(F32)], axis=1
-    )
+    all_stats = lax.all_to_all(spread, "z", 0, 0, tiled=True)
+    all_stats = all_stats.reshape(owners, 2, width)
+    lines, losses = combine(
+        pair_row.reshape(-1), named, all_stats, targets, block_count, picks
+    )
+    losses = losses[:, :block_rows].reshape(local_rows)
     got_lines = lax.all_to_all(lines, PLANE, 0, 0, tiled=True)
 
-    far_g = query_parts(packed, blk, lines, tables, 1, block_count, block_rows)
+    grads = query_parts(
+        packed, jnp.concatenate([blk, z.reshape(1)]), lines, tables, z_size, block_count, block_rows
+    )
+    grads, got_lines = lax.optimization_barrier((grads, got_lines))
+    query_grads = lax.psum_scatter(grads, "z").astype(F32).reshape(local_rows, features)
+
     far_a, far_b = item_parts((2,), 2, x, origin, rows, got_lines, table16, x_size)
+    far_a, far_b, got_lines = lax.optimization_barrier((far_a, far_b, got_lines))
     (rest,) = item_parts((0, 1, 3), 1, x, origin, rows, got_lines, table16, x_size)
-    rest, late = lax.optimization_barrier((rest, blk))
-    near_g = query_parts(packed, late, lines, tables, 0, block_count, block_rows)
-    grads = dict(zip(ORDER, list(near_g) + list(far_g)))
-
-    def add(a, b):
-        return (a.astype(F32) + b.astype(F32)).astype(BF16)
-
-    go_right = shift(grads[4], "z", 1)
-    go_right = shift(add(go_right, grads[3]), "z", 1)
-    go_right = shift(add(go_right, grads[2]), "z", 1)
-    go_right = shift(add(go_right, grads[1]), "z", 1)
-    go_left = shift(grads[5], "z", -1)
-    go_left = shift(add(go_left, grads[6]), "z", -1)
-    go_left = shift(add(go_left, grads[7]), "z", -1)
-    query_grads = (
-        grads[0].astype(F32) + go_right.astype(F32) + go_left.astype(F32)
-    ).reshape(local_rows, features)
-
     far_a, far_b = far_a[0], far_b[0]
     own, after, before = rest[0], rest[1], rest[2]
     half = far_a.shape[0]

time: 181 us -> 194 us (1.072)
  waiting for transfers between devices: 34 us -> 72.2 us
  local copies, waits for them, and re-layouts: 27.8 us -> 8.12 us
  starting transfers between devices: 56.2 us -> 45.4 us
  Pallas kernels: 34 us -> 44.8 us
  other arithmetic: 12 us -> 8.19 us
    ppermute x7, waiting for transfers between devices: 0.02 us -> 20.2 us  [shift_plane(): return lax.ppermute(value, PLANE, moves)]
    unnamed x49 -> x47, local copies, waits for them, and re-layouts: 14.7 us -> 1.62 us
    ppermute x22 -> x15, starting transfers between devices: 31.6 us -> 23.5 us  [shift(): lax.ppermute(value, axis, [(i, (i + step) % size) for i in range(size)])]
    ppermute x22 -> x15, waiting for transfers between devices: 27 us -> 34.4 us  [shift(): lax.ppermute(value, axis, [(i, (i + step) % size) for i in range(size)])]
    all_to_all x1, waiting for transfers between devices: 2.31 us -> 9.73 us  [local(): all_stats = lax.all_to_all(spread, 'z', 0, 0, tiled=True)]
    pallas_call x2, Pallas kernels: 14.2 us -> 21 us  [the longest x1 12.6 us: query_parts(): pl.pallas_call(query_kernel, grid_spec=pltpu.PrefetchScalarGridSpec(num_s...]
    gather x4 -> x0, local copies, waits for them, and re-layouts: 4.93 us -> none  [the longest x1 2.25 us: local(): all_stats[pair_row.reshape(-1)]]
    pallas_call x1, Pallas kernels: 0.83 us -> 4.52 us  [pack(): pl.pallas_call(functools.partial(pack_kernel, len(sources)), grid_spec=pl...]
  transfers between devices with their start and end apart: 33 -> 27, of which waited for: 9 -> 17; matrix products, arithmetic and copies ran while one was open for 12% -> 5% of each run, Pallas kernels for 15% -> 14%
where the time goes in v5:
time: 194 us; the launch traced here: 193 us
  waiting for transfers between devices  72.2 us (37%)
  starting transfers between devices  45.4 us (23%)
  Pallas kernels  44.8 us (23%)
  between operations  14.5 us (7%)
  other arithmetic  8.19 us (4%)
  local copies, waits for them, and re-layouts  8.12 us (4%)
    ppermute x15, waiting for transfers between devices, shift(): lax.ppermute(value, axis, [(i, (i + step) % size) for i in range(size)])  34.4 us
    ppermute x15, starting transfers between devices, shift(): lax.ppermute(value, axis, [(i, (i + step) % size) for i in range(size)])  23.5 us
    ppermute x7, waiting for transfers between devices, shift_plane(): return lax.ppermute(value, PLANE, moves)  20.2 us
    pallas_call x1, Pallas kernels, query_parts(): pl.pallas_call(query_kernel, grid_spec=pltpu.PrefetchScalarGridSpec(num_s...  12.6 us
    pallas_call x1, Pallas kernels, forward(): pl.pallas_call(forward_kernel, grid=(planes,), in_specs=[pl.BlockSpec((1,...  9.83 us
    all_to_all x1, waiting for transfers between devices, local(): all_stats = lax.all_to_all(spread, 'z', 0, 0, tiled=True)  9.73 us
    ppermute x7, starting transfers between devices, shift_plane(): return lax.ppermute(value, PLANE, moves)  8.85 us
    pallas_call x1, Pallas kernels, combine(): pl.pallas_call(combine_kernel, grid_spec=pltpu.PrefetchScalarGridSpec(num...  8.42 us
  transfers between devices with their start and end apart: 27, of which 17 were waited for; matrix products, arithmetic and copies ran while one was open for 5% of the time, Pallas kernels for 14%

profile of v5, /device:TPU:6, one launch (start us, length us, event | category | flops | bytes accessed | tf_op | source)
XLA Modules:
  0.0 193.2 jit_solution(17990596381229288272)
XLA Ops:
  7.3 2.5 %bitcast_convert_fusion.1 = (bf16[1024,256]{1,0:T(8,128)(2,1)S(1)}, bf16[1,1024,256]{2,1,0:T(8,128)(2,1)}) fusion(f32[1,1024,256]{2,1,0:T(8,128)} %param.12), kind=kLoop, calls=%fused_computation.121 | loop fusion | flops 524288 | bytes 2097152 | tf_op jit(solution)/shard_map/convert_element_type | solution.py:384
  9.8 5.9 %collective-permute-start.1 = (bf16[16,32,256]{2,1,0:T(8,128)(2,1)S(1)}, bf16[16,32,256]{2,1,0:T(8,128)(2,1)S(1)}, u32[]{:S(2)}, u32[]{:S(2)}) collective-permute-start(bf16[16,32,256]{2,1,0:T(8,128)(2,1)S(1)} %bitcast.67), channel_id=1, source_target_pairs={{0,224},{32,0},{64,32},{96,64},{128,96},{160,128},{192,160},{224,1... | collective-permute-start | bytes 786440 | tf_op jit(solution)/shard_map/ppermute | solution.py:24
  15.7 5.5 %collective-permute-done.1.refs_1_ = bf16[16,32,256]{2,1,0:T(8,128)(2,1)S(1)} collective-permute-done((bf16[16,32,256]{2,1,0:T(8,128)(2,1)S(1)}, bf16[16,32,256]{2,1,0:T(8,128)(2,1)S(1)}, u32[]{:S(2)}, u32[]{:S(2)}) %collective-permute-start.1) | collective-permute-done | bytes 262176 | tf_op jit(solution)/shard_map/ppermute | solution.py:24
  21.3 3.4 %collective-permute-done.refs_7_ = bf16[16,32,256]{2,1,0:T(8,128)(2,1)S(1)} collective-permute-done((bf16[16,32,256]{2,1,0:T(8,128)(2,1)S(1)}, bf16[16,32,256]{2,1,0:T(8,128)(2,1)S(1)}, u32[]{:S(2)}, u32[]{:S(2)}) %collective-permute-start) | collective-permute-done | bytes 262176 | tf_op jit(solution)/shard_map/ppermute | solution.py:24
  27.1 3.3 %collective-permute-start.2 = (bf16[16,32,256]{2,1,0:T(8,128)(2,1)S(1)}, bf16[16,32,256]{2,1,0:T(8,128)(2,1)S(1)}, u32[]{:S(2)}, u32[]{:S(2)}) collective-permute-start(bf16[16,32,256]{2,1,0:T(8,128)(2,1)S(1)} %collective-permute-done.1.refs_1_), channel_id=1, source_target_pairs={{0,224},{32,0},{64,32},{96,64},{128,96},{160,128},{192,160},{224,1... | collective-permute-start | bytes 786440 | tf_op jit(solution)/shard_map/ppermute | solution.py:24
  30.4 3.3 %collective-permute-done.4.refs_6_ = bf16[16,32,256]{2,1,0:T(8,128)(2,1)S(1)} collective-permute-done((bf16[16,32,256]{2,1,0:T(8,128)(2,1)S(1)}, bf16[16,32,256]{2,1,0:T(8,128)(2,1)S(1)}, u32[]{:S(2)}, u32[]{:S(2)}) %collective-permute-start.4) | collective-permute-done | bytes 262176 | tf_op jit(solution)/shard_map/ppermute | solution.py:24
  34.4 4.5 %all-to-all-start = ((s32[8,1,592]{2,1,0:T(1,128)}), s32[8,1,592]{2,1,0:T(1,128)S(1)}, u32[]{:S(2)}, u32[]{:S(2)}) async-start(s32[8,1,592]{2,1,0:T(1,128)} %copy.26), calls=%async_computation | async-start | bytes 40960 | tf_op jit(solution)/shard_map/all_to_all | solution.py:426
  38.8 7.8 %all-to-all-done = s32[8,1,592]{2,1,0:T(1,128)S(1)} async-done(((s32[8,1,592]{2,1,0:T(1,128)}), s32[8,1,592]{2,1,0:T(1,128)S(1)}, u32[]{:S(2)}, u32[]{:S(2)}) %all-to-all-start) | async-done | bytes 18976 | tf_op jit(solution)/shard_map/all_to_all | solution.py:426
  51.1 3.8 %collective-permute-done.3.refs_3_ = bf16[16,32,256]{2,1,0:T(8,128)(2,1)S(1)} collective-permute-done((bf16[16,32,256]{2,1,0:T(8,128)(2,1)S(1)}, bf16[16,32,256]{2,1,0:T(8,128)(2,1)S(1)}, u32[]{:S(2)}, u32[]{:S(2)}) %collective-permute-start.3) | collective-permute-done | bytes 262176 | tf_op jit(solution)/shard_map/ppermute | solution.py:24
  57.3 4.5 %pack.1 = (bf16[8,512,256]{2,1,0:T(8,128)(2,1)}, bf16[512,256]{1,0:T(8,128)(2,1)}, bf16[512,256]{1,0:T(8,128)(2,1)}, bf16[512,256]{1,0:T(8,128)(2,1)}, bf16[512,...) custom-call(s32[136]{0:T(256)} %pad_add_fusion.blk, ...), custom_call_target="tpu_custom_call" | custom-call | bytes 6291456 | tf_op jit(solution)/shard_map/pack/pallas_call | solution.py:58
  61.9 9.8 %forward.1 = f32[8,2,512]{2,1,0:T(2,128)} custom-call(bf16[8,512,256]{2,1,0:T(8,128)(2,1)} %get-tuple-element.42.p_ref, bf16[8,1024,256]{2,1,0:T(8,128)(2,1)} %all-gather.2.cloned.1.call-done.t_hbm, s32[8,1,512]{2,1,0:T(1,128)} %reshape.214.tgt_ref), custom_call_target="tpu_custom_call" | custom-call | flops 2147483648 | bytes 6291456 | tf_op jit(solution)/shard_map/forward/pallas_call | solution.py:114
  73.3 4.1 %all-to-all-start.1 = ((f32[8,8,2,512]{3,2,1,0:T(2,128)}), f32[8,8,2,512]{3,2,1,0:T(2,128)S(1)}, u32[]{:S(2)}, u32[]{:S(2)}) async-start(f32[8,8,2,512]{3,2,1,0:T(2,128)} %broadcast_in_dim.41), calls=%async_computation.1 | async-start | bytes 524288 | tf_op jit(solution)/shard_map/all_to_all | solution.py:455
  78.1 9.7 %all-to-all-done.1 = f32[8,8,2,512]{3,2,1,0:T(2,128)S(1)} async-done(((f32[8,8,2,512]{3,2,1,0:T(2,128)}), f32[8,8,2,512]{3,2,1,0:T(2,128)S(1)}, u32[]{:S(2)}, u32[]{:S(2)}) %all-to-all-start.1) | async-done | bytes 262176 | tf_op jit(solution)/shard_map/all_to_all | solution.py:455
  87.8 8.4 %combine.1 = (f32[8,2,512]{2,1,0:T(2,128)}, f32[16,128]{1,0:T(8,128)S(1)}) custom-call(s32[512]{0:T(512)S(1)} %reshape.212.addr, s32[128]{0:T(128)S(1)} %reshape.209.named, f32[64,2,512]{2,1,0:T(2,128)S(1)} %bitcast.60, s32[8,1,512]{2,1,0:T(1,128)S(1)} %copy-done.2), custom_call_target="tpu_custom_call" | custom-call | tf_op jit(solution)/shard_map/combine/pallas_call | solution.py:195
  96.2 4.5 %all-to-all-start.2 = ((f32[8,2,512]{2,1,0:T(2,128)}), f32[8,2,512]{2,1,0:T(2,128)S(1)}, u32[]{:S(2)}, u32[]{:S(2)}) async-start(f32[8,2,512]{2,1,0:T(2,128)} %get-tuple-element.43.line_ref), calls=%async_computation.2 | async-start | bytes 65536 | tf_op jit(solution)/shard_map/all_to_all | solution.py:461
  100.8 12.6 %query_parts.1 = bf16[8,16,32,256]{3,2,1,0:T(8,128)(2,1)} custom-call(s32[129]{0:T(256)} %pad_add_fusion.1.blk, bf16[8,512,256]{2,1,0:T(8,128)(2,1)} %get-tuple-element.42.p_ref, bf16[8,1024,256]{2,1,0:T(8,128)(2,1)} %all-gather.2.cloned.1.call-done.t_hbm, f32[8,2,512]{2,1,0:T(2,128)} %get-tuple-element.43.line_ref), custom_call_target="tpu_custom_call" | custom-call | flops 4294967296 | bytes 8388608 | tf_op jit(solution)/shard_map/query_parts/pallas_call | solution.py:245
  121.1 1.8 collective-permute-start.12
  122.9 2.2 %collective-permute-done.8.refs_2_ = bf16[512,256]{1,0:T(8,128)(2,1)S(1)} collective-permute-done((bf16[512,256]{1,0:T(8,128)(2,1)S(1)}, bf16[512,256]{1,0:T(8,128)(2,1)S(1)}, u32[]{:S(2)}, u32[]{:S(2)}) %collective-permute-start.8) | collective-permute-done | bytes 262176 | tf_op jit(solution)/shard_map/ppermute | solution.py:37
  125.5 3.9 %collective-permute-done.9.refs_3_ = bf16[512,256]{1,0:T(8,128)(2,1)S(1)} collective-permute-done((bf16[512,256]{1,0:T(8,128)(2,1)S(1)}, bf16[512,256]{1,0:T(8,128)(2,1)S(1)}, u32[]{:S(2)}, u32[]{:S(2)}) %collective-permute-start.9) | collective-permute-done | bytes 262176 | tf_op jit(solution)/shard_map/ppermute | solution.py:37
  129.4 8.0 %collective-permute-done.10.refs_4_ = bf16[512,256]{1,0:T(8,128)(2,1)S(1)} collective-permute-done((bf16[512,256]{1,0:T(8,128)(2,1)S(1)}, bf16[512,256]{1,0:T(8,128)(2,1)S(1)}, u32[]{:S(2)}, u32[]{:S(2)}) %collective-permute-start.10) | collective-permute-done | bytes 262176 | tf_op jit(solution)/shard_map/ppermute | solution.py:37
  137.4 4.5 %collective-permute-done.11.refs_5_ = bf16[512,256]{1,0:T(8,128)(2,1)S(1)} collective-permute-done((bf16[512,256]{1,0:T(8,128)(2,1)S(1)}, bf16[512,256]{1,0:T(8,128)(2,1)S(1)}, u32[]{:S(2)}, u32[]{:S(2)}) %collective-permute-start.11) | collective-permute-done | bytes 262176 | tf_op jit(solution)/shard_map/ppermute | solution.py:37
  143.5 2.1 %item_parts.2 = (f32[1,128,256]{2,1,0:T(8,128)S(1)}, f32[1,128,256]{2,1,0:T(8,128)S(1)}) custom-call(s32[9]{0:T(128)S(1)} %pad_add_fusion.3.where, bf16[512,256]{1,0:T(8,128)(2,1)S(1)} %copy-done.3, bf16[512,256]{1,0:T(8,128)(2,1)S(1)} %collective-permute-done.7.refs_1_, bf16[512,256]{1,0:T(8,128)(2,1)S(1)} %collective-permute-done.8.refs_2_, ...), custom_call_target="tpu_custom_call" | custom-call | flops 1073741824 | bytes 2490368 | tf_op jit(solution)/shard_map/item_parts/pallas_call | solution.py:302
  147.7 5.3 %item_parts.3 = f32[3,256,256]{2,1,0:T(8,128)S(1)} custom-call(s32[11]{0:T(128)S(1)} %pad_add_fusion.2.where, bf16[512,256]{1,0:T(8,128)(2,1)S(1)} %copy-done.3, bf16[512,256]{1,0:T(8,128)(2,1)S(1)} %collective-permute-done.7.refs_1_, bf16[512,256]{1,0:T(8,128)(2,1)S(1)} %collective-permute-done.8.refs_2_, ...), custom_call_target="tpu_custom_call" | custom-call | flops 3221225472 | bytes 3276800 | tf_op jit(solution)/shard_map/item_parts/pallas_call | solution.py:302
  154.7 2.6 %collective-permute-start.15 = (f32[256,256]{1,0:T(8,128)S(1)}, f32[256,256]{1,0:T(8,128)}, u32[]{:S(2)}, u32[]{:S(2)}) collective-permute-start(f32[256,256]{1,0:T(8,128)S(1)} %pad_maximum_fusion), channel_id=1, source_target_pairs={{0,1},{1,2},{2,3},{3,0},{4,5},{5,6},{6,7},{7,4},{8,9},{9,10},{10,1... | collective-permute-start | bytes 786440 | tf_op jit(solution)/shard_map/ppermute | solution.py:24
  158.0 5.8 %collective-permute-done.17 = f32[256,256]{1,0:T(8,128)} collective-permute-done((f32[256,256]{1,0:T(8,128)}, f32[256,256]{1,0:T(8,128)}, u32[]{:S(2)}, u32[]{:S(2)}) %collective-permute-start.17) | collective-permute-done | bytes 262176 | tf_op jit(solution)/shard_map/ppermute | solution.py:24
  164.9 2.9 %collective-permute-start.19 = (f32[256,256]{1,0:T(8,128)S(1)}, f32[256,256]{1,0:T(8,128)S(1)}, u32[]{:S(2)}, u32[]{:S(2)}) collective-permute-start(f32[256,256]{1,0:T(8,128)S(1)} %fusion.1.own), channel_id=1, source_target_pairs={{0,1},{1,2},{2,3},{3,0},{4,5},{5,6},{6,7},{7,4},{8,9},{9,10},{10,1... | collective-permute-start | bytes 786440 | tf_op jit(solution)/shard_map/ppermute | solution.py:24
  167.8 4.6 %collective-permute-done.19.before = f32[256,256]{1,0:T(8,128)S(1)} collective-permute-done((f32[256,256]{1,0:T(8,128)S(1)}, f32[256,256]{1,0:T(8,128)S(1)}, u32[]{:S(2)}, u32[]{:S(2)}) %collective-permute-start.19) | collective-permute-done | bytes 262176 | tf_op jit(solution)/shard_map/ppermute | solution.py:24
  172.4 3.8 %collective-permute-start.20 = (f32[128,256]{1,0:T(8,128)S(1)}, f32[128,256]{1,0:T(8,128)S(1)}, u32[]{:S(2)}, u32[]{:S(2)}) collective-permute-start(f32[128,256]{1,0:T(8,128)S(1)} %slice.78), channel_id=1, source_target_pairs={{0,1},{1,2},{2,3},{3,0},{4,5},{5,6},{6,7},{7,4},{8,9},{9,10},{10,1... | collective-permute-start | bytes 393224 | tf_op jit(solution)/shard_map/ppermute | solution.py:24
  176.3 2.4 %collective-permute-done.20.far_a = f32[128,256]{1,0:T(8,128)S(1)} collective-permute-done((f32[128,256]{1,0:T(8,128)S(1)}, f32[128,256]{1,0:T(8,128)S(1)}, u32[]{:S(2)}, u32[]{:S(2)}) %collective-permute-start.20) | collective-permute-done | bytes 131104 | tf_op jit(solution)/shard_map/ppermute | solution.py:24
  178.7 3.8 %collective-permute-done.21.far_b = f32[128,256]{1,0:T(8,128)S(1)} collective-permute-done((f32[128,256]{1,0:T(8,128)S(1)}, f32[128,256]{1,0:T(8,128)S(1)}, u32[]{:S(2)}, u32[]{:S(2)}) %collective-permute-start.21) | collective-permute-done | bytes 131104 | tf_op jit(solution)/shard_map/ppermute | solution.py:24
  182.5 2.1 %update.1 = (f32[1024,256]{1,0:T(8,128)}, f32[1024,256]{1,0:T(8,128)}) custom-call(s32[1]{0:T(128)} %bitcast.7.x_ref, f32[256,256]{1,0:T(8,128)S(1)} %fusion.1.own, f32[256,256]{1,0:T(8,128)S(1)} %collective-permute-done.18.after, f32[256,256]{1,0:T(8,128)S(1)} %collective-permute-done.19.before, f32[128,256]{1,0:T(8,128)S(1)} %collective-permute-done.20.far_a, ...), custom_call_target="tpu_custom_call" | custom-call | tf_op jit(solution)/shard_map/update/pallas_call | solution.py:353
  184.6 1.8 bitcast_convert_fusion
  (135 shorter events, 27.7 us)
Async XLA Ops:
  7.2 54.7 %all-gather.2.cloned.1.call-start = ((), (), s32[]{:S(2)}) async-start(), calls=%async_computation.4 | async-start | bytes 4718592 | tf_op jit(solution)/shard_map/all_gather | solution.py:385
  9.8 11.5 %collective-permute-start.1 = (bf16[16,32,256]{2,1,0:T(8,128)(2,1)S(1)}, bf16[16,32,256]{2,1,0:T(8,128)(2,1)S(1)}, u32[]{:S(2)}, u32[]{:S(2)}) collective-permute-start(bf16[16,32,256]{2,1,0:T(8,128)(2,1)S(1)} %bitcast.67), channel_id=1, source_target_pairs={{0,224},{32,0},{64,32},{96,64},{128,96},{160,128},{192,160},{224,1... | collective-permute-start | bytes 786440 | tf_op jit(solution)/shard_map/ppermute | solution.py:24
  15.7 9.0 %collective-permute-start = (bf16[16,32,256]{2,1,0:T(8,128)(2,1)S(1)}, bf16[16,32,256]{2,1,0:T(8,128)(2,1)S(1)}, u32[]{:S(2)}, u32[]{:S(2)}) collective-permute-start(bf16[16,32,256]{2,1,0:T(8,128)(2,1)S(1)} %bitcast.68), channel_id=1, source_target_pairs={{0,32},{32,64},{64,96},{96,128},{128,160},{160,192},{192,224},{224... | collective-permute-start | bytes 786440 | tf_op jit(solution)/shard_map/ppermute | solution.py:24
  21.3 35.3 %copy-start.5 = (bf16[16,32,256]{2,1,0:T(8,128)(2,1)}, bf16[16,32,256]{2,1,0:T(8,128)(2,1)S(1)}, u32[]{:S(2)}) copy-start(bf16[16,32,256]{2,1,0:T(8,128)(2,1)S(1)} %collective-permute-done.1.refs_1_) | copy-start | bytes 786436
  24.7 31.9 %copy-start.6 = (bf16[16,32,256]{2,1,0:T(8,128)(2,1)}, bf16[16,32,256]{2,1,0:T(8,128)(2,1)S(1)}, u32[]{:S(2)}) copy-start(bf16[16,32,256]{2,1,0:T(8,128)(2,1)S(1)} %collective-permute-done.refs_7_) | copy-start | bytes 786436
  25.6 8.1 %collective-permute-start.4 = (bf16[16,32,256]{2,1,0:T(8,128)(2,1)S(1)}, bf16[16,32,256]{2,1,0:T(8,128)(2,1)S(1)}, u32[]{:S(2)}, u32[]{:S(2)}) collective-permute-start(bf16[16,32,256]{2,1,0:T(8,128)(2,1)S(1)} %collective-permute-done.refs_7_), channel_id=1, source_target_pairs={{0,32},{32,64},{64,96},{96,128},{128,160},{160,192},{192,224},{224... | collective-permute-start | bytes 786440 | tf_op jit(solution)/shard_map/ppermute | solution.py:24
  27.1 21.3 %collective-permute-start.2 = (bf16[16,32,256]{2,1,0:T(8,128)(2,1)S(1)}, bf16[16,32,256]{2,1,0:T(8,128)(2,1)S(1)}, u32[]{:S(2)}, u32[]{:S(2)}) collective-permute-start(bf16[16,32,256]{2,1,0:T(8,128)(2,1)S(1)} %collective-permute-done.1.refs_1_), channel_id=1, source_target_pairs={{0,224},{32,0},{64,32},{96,64},{128,96},{160,128},{192,160},{224,1... | collective-permute-start | bytes 786440 | tf_op jit(solution)/shard_map/ppermute | solution.py:24
  33.7 15.3 %collective-permute-start.5 = (bf16[16,32,256]{2,1,0:T(8,128)(2,1)S(1)}, bf16[16,32,256]{2,1,0:T(8,128)(2,1)S(1)}, u32[]{:S(2)}, u32[]{:S(2)}) collective-permute-start(bf16[16,32,256]{2,1,0:T(8,128)(2,1)S(1)} %collective-permute-done.4.refs_6_), channel_id=1, source_target_pairs={{0,32},{32,64},{64,96},{96,128},{128,160},{160,192},{192,224},{224... | collective-permute-start | bytes 786440 | tf_op jit(solution)/shard_map/ppermute | solution.py:24
  34.4 12.3 %all-to-all-start = ((s32[8,1,592]{2,1,0:T(1,128)}), s32[8,1,592]{2,1,0:T(1,128)S(1)}, u32[]{:S(2)}, u32[]{:S(2)}) async-start(s32[8,1,592]{2,1,0:T(1,128)} %copy.26), calls=%async_computation | async-start | bytes 40960 | tf_op jit(solution)/shard_map/all_to_all | solution.py:426
  48.5 6.4 %collective-permute-start.3 = (bf16[16,32,256]{2,1,0:T(8,128)(2,1)S(1)}, bf16[16,32,256]{2,1,0:T(8,128)(2,1)S(1)}, u32[]{:S(2)}, u32[]{:S(2)}) collective-permute-start(bf16[16,32,256]{2,1,0:T(8,128)(2,1)S(1)} %collective-permute-done.2.refs_2_), channel_id=1, source_target_pairs={{0,224},{32,0},{64,32},{96,64},{128,96},{160,128},{192,160},{224,1... | collective-permute-start | bytes 786440 | tf_op jit(solution)/shard_map/ppermute | solution.py:24
  49.0 7.6 %collective-permute-start.6 = (bf16[16,32,256]{2,1,0:T(8,128)(2,1)S(1)}, bf16[16,32,256]{2,1,0:T(8,128)(2,1)S(1)}, u32[]{:S(2)}, u32[]{:S(2)}) collective-permute-start(bf16[16,32,256]{2,1,0:T(8,128)(2,1)S(1)} %collective-permute-done.5.refs_5_), channel_id=1, source_target_pairs={{0,32},{32,64},{64,96},{96,128},{128,160},{160,192},{192,224},{224... | collective-permute-start | bytes 786440 | tf_op jit(solution)/shard_map/ppermute | solution.py:24
  73.3 14.5 %all-to-all-start.1 = ((f32[8,8,2,512]{3,2,1,0:T(2,128)}), f32[8,8,2,512]{3,2,1,0:T(2,128)S(1)}, u32[]{:S(2)}, u32[]{:S(2)}) async-start(f32[8,8,2,512]{3,2,1,0:T(2,128)} %broadcast_in_dim.41), calls=%async_computation.1 | async-start | bytes 524288 | tf_op jit(solution)/shard_map/all_to_all | solution.py:455
  96.2 17.2 %all-to-all-start.2 = ((f32[8,2,512]{2,1,0:T(2,128)}), f32[8,2,512]{2,1,0:T(2,128)S(1)}, u32[]{:S(2)}, u32[]{:S(2)}) async-start(f32[8,2,512]{2,1,0:T(2,128)} %get-tuple-element.43.line_ref), calls=%async_computation.2 | async-start | bytes 65536 | tf_op jit(solution)/shard_map/all_to_all | solution.py:461
  100.7 83.8 %reduce-scatter.2.cloned.1.call-start = ((), (), s32[]{:S(2)}) async-start(), calls=%async_computation.5 | async-start | bytes 2359296 | tf_op jit(solution)/shard_map/reduce_scatter | solution.py:467
  113.4 30.1 %copy-start.3 = (bf16[512,256]{1,0:T(8,128)(2,1)S(1)}, bf16[512,256]{1,0:T(8,128)(2,1)}, u32[]{:S(2)}) copy-start(bf16[512,256]{1,0:T(8,128)(2,1)} %get-tuple-element.34.refs_0_) | copy-start | bytes 786436
  114.3 6.9 %collective-permute-start.7 = (bf16[512,256]{1,0:T(8,128)(2,1)S(1)}, bf16[512,256]{1,0:T(8,128)(2,1)S(1)}, u32[]{:S(2)}, u32[]{:S(2)}) collective-permute-start(bf16[512,256]{1,0:T(8,128)(2,1)S(1)} %copy-done.20), channel_id=1, source_target_pairs={{0,4},{4,0},{8,12},{12,8},{16,20},{20,16},{24,28},{28,24},{1,5},{5... | collective-permute-start | bytes 786440 | tf_op jit(solution)/shard_map/ppermute | solution.py:37
  114.7 10.3 %collective-permute-start.8 = (bf16[512,256]{1,0:T(8,128)(2,1)S(1)}, bf16[512,256]{1,0:T(8,128)(2,1)S(1)}, u32[]{:S(2)}, u32[]{:S(2)}) collective-permute-start(bf16[512,256]{1,0:T(8,128)(2,1)S(1)} %copy-done.19), channel_id=1, source_target_pairs={{0,8},{4,12},{8,16},{12,20},{16,24},{20,28},{24,0},{28,4},{1,9},{5... | collective-permute-start | bytes 786440 | tf_op jit(solution)/shard_map/ppermute | solution.py:37
  116.4 13.0 %collective-permute-start.9 = (bf16[512,256]{1,0:T(8,128)(2,1)S(1)}, bf16[512,256]{1,0:T(8,128)(2,1)S(1)}, u32[]{:S(2)}, u32[]{:S(2)}) collective-permute-start(bf16[512,256]{1,0:T(8,128)(2,1)S(1)} %copy-done.18), channel_id=1, source_target_pairs={{0,12},{4,8},{8,20},{12,16},{16,28},{20,24},{24,4},{28,0},{1,13},{... | collective-permute-start | bytes 786440 | tf_op jit(solution)/shard_map/ppermute | solution.py:37
  117.8 19.6 %collective-permute-start.10 = (bf16[512,256]{1,0:T(8,128)(2,1)S(1)}, bf16[512,256]{1,0:T(8,128)(2,1)S(1)}, u32[]{:S(2)}, u32[]{:S(2)}) collective-permute-start(bf16[512,256]{1,0:T(8,128)(2,1)S(1)} %copy-done.17), channel_id=1, source_target_pairs={{0,16},{4,20},{8,24},{12,28},{16,0},{20,4},{24,8},{28,12},{1,17},{... | collective-permute-start | bytes 786440 | tf_op jit(solution)/shard_map/ppermute | solution.py:37
  119.5 22.4 %collective-permute-start.11 = (bf16[512,256]{1,0:T(8,128)(2,1)S(1)}, bf16[512,256]{1,0:T(8,128)(2,1)S(1)}, u32[]{:S(2)}, u32[]{:S(2)}) collective-permute-start(bf16[512,256]{1,0:T(8,128)(2,1)S(1)} %copy-done.16), channel_id=1, source_target_pairs={{0,20},{4,16},{8,28},{12,24},{16,4},{20,0},{24,12},{28,8},{1,21},{... | collective-permute-start | bytes 786440 | tf_op jit(solution)/shard_map/ppermute | solution.py:37
  121.1 20.8 %collective-permute-start.12 = (bf16[512,256]{1,0:T(8,128)(2,1)S(1)}, bf16[512,256]{1,0:T(8,128)(2,1)S(1)}, u32[]{:S(2)}, u32[]{:S(2)}) collective-permute-start(bf16[512,256]{1,0:T(8,128)(2,1)S(1)} %copy-done.15), channel_id=1, source_target_pairs={{0,24},{4,28},{8,0},{12,4},{16,8},{20,12},{24,16},{28,20},{1,25},{... | collective-permute-start | bytes 786440 | tf_op jit(solution)/shard_map/ppermute | solution.py:37
  125.1 18.4 %collective-permute-start.13 = (bf16[512,256]{1,0:T(8,128)(2,1)S(1)}, bf16[512,256]{1,0:T(8,128)(2,1)S(1)}, u32[]{:S(2)}, u32[]{:S(2)}) collective-permute-start(bf16[512,256]{1,0:T(8,128)(2,1)S(1)} %copy-done.14), channel_id=1, source_target_pairs={{0,28},{4,24},{8,4},{12,0},{16,12},{20,8},{24,20},{28,16},{1,29},{... | collective-permute-start | bytes 786440 | tf_op jit(solution)/shard_map/ppermute | solution.py:37
  145.6 7.5 %collective-permute-start.14 = (f32[128,256]{1,0:T(8,128)S(1)}, f32[128,256]{1,0:T(8,128)S(1)}, u32[]{:S(2)}, u32[]{:S(2)}) collective-permute-start(f32[128,256]{1,0:T(8,128)S(1)} %bitcast.63), channel_id=1, source_target_pairs={{0,1},{1,2},{2,3},{3,0},{4,5},{5,6},{6,7},{7,4},{8,9},{9,10},{10,1... | collective-permute-start | bytes 393224 | tf_op jit(solution)/shard_map/ppermute | solution.py:24
  146.2 7.0 %collective-permute-start.16 = (f32[128,256]{1,0:T(8,128)S(1)}, f32[128,256]{1,0:T(8,128)S(1)}, u32[]{:S(2)}, u32[]{:S(2)}) collective-permute-start(f32[128,256]{1,0:T(8,128)S(1)} %bitcast.62), channel_id=1, source_target_pairs={{0,3},{1,0},{2,1},{3,2},{4,7},{5,4},{6,5},{7,6},{8,11},{9,8},{10,9... | collective-permute-start | bytes 393224 | tf_op jit(solution)/shard_map/ppermute | solution.py:24
  153.1 29.4 %copy-start = (f32[1,1024,256]{2,1,0:T(8,128)S(1)}, f32[1,1024,256]{2,1,0:T(8,128)}, u32[]{:S(2)}) copy-start(f32[1,1024,256]{2,1,0:T(8,128)} %param.12) | copy-start | bytes 3145732
  153.1 29.4 %copy-start.1 = (f32[1,1024,256]{2,1,0:T(8,128)S(1)}, f32[1,1024,256]{2,1,0:T(8,128)}, u32[]{:S(2)}) copy-start(f32[1,1024,256]{2,1,0:T(8,128)} %param.13) | copy-start | bytes 3145732
  154.0 9.8 %collective-permute-start.17 = (f32[256,256]{1,0:T(8,128)}, f32[256,256]{1,0:T(8,128)}, u32[]{:S(2)}, u32[]{:S(2)}) collective-permute-start(f32[256,256]{1,0:T(8,128)} %pad_maximum_fusion.1), channel_id=1, source_target_pairs={{0,3},{1,0},{2,1},{3,2},{4,7},{5,4},{6,5},{7,6},{8,11},{9,8},{10,9... | collective-permute-start | bytes 786440 | tf_op jit(solution)/shard_map/ppermute | solution.py:24
  154.7 9.0 %collective-permute-start.15 = (f32[256,256]{1,0:T(8,128)S(1)}, f32[256,256]{1,0:T(8,128)}, u32[]{:S(2)}, u32[]{:S(2)}) collective-permute-start(f32[256,256]{1,0:T(8,128)S(1)} %pad_maximum_fusion), channel_id=1, source_target_pairs={{0,1},{1,2},{2,3},{3,0},{4,5},{5,6},{6,7},{7,4},{8,9},{9,10},{10,1... | collective-permute-start | bytes 786440 | tf_op jit(solution)/shard_map/ppermute | solution.py:24
  164.9 7.5 %collective-permute-start.19 = (f32[256,256]{1,0:T(8,128)S(1)}, f32[256,256]{1,0:T(8,128)S(1)}, u32[]{:S(2)}, u32[]{:S(2)}) collective-permute-start(f32[256,256]{1,0:T(8,128)S(1)} %fusion.1.own), channel_id=1, source_target_pairs={{0,1},{1,2},{2,3},{3,0},{4,5},{5,6},{6,7},{7,4},{8,9},{9,10},{10,1... | collective-permute-start | bytes 786440 | tf_op jit(solution)/shard_map/ppermute | solution.py:24
  167.8 8.4 %collective-permute-start.18 = (f32[256,256]{1,0:T(8,128)S(1)}, f32[256,256]{1,0:T(8,128)S(1)}, u32[]{:S(2)}, u32[]{:S(2)}) collective-permute-start(f32[256,256]{1,0:T(8,128)S(1)} %fusion.1.own), channel_id=1, source_target_pairs={{0,3},{1,0},{2,1},{3,2},{4,7},{5,4},{6,5},{7,6},{8,11},{9,8},{10,9... | collective-permute-start | bytes 786440 | tf_op jit(solution)/shard_map/ppermute | solution.py:24
  172.4 6.3 %collective-permute-start.20 = (f32[128,256]{1,0:T(8,128)S(1)}, f32[128,256]{1,0:T(8,128)S(1)}, u32[]{:S(2)}, u32[]{:S(2)}) collective-permute-start(f32[128,256]{1,0:T(8,128)S(1)} %slice.78), channel_id=1, source_target_pairs={{0,1},{1,2},{2,3},{3,0},{4,5},{5,6},{6,7},{7,4},{8,9},{9,10},{10,1... | collective-permute-start | bytes 393224 | tf_op jit(solution)/shard_map/ppermute | solution.py:24
  176.2 6.3 %collective-permute-start.21 = (f32[128,256]{1,0:T(8,128)S(1)}, f32[128,256]{1,0:T(8,128)S(1)}, u32[]{:S(2)}, u32[]{:S(2)}) collective-permute-start(f32[128,256]{1,0:T(8,128)S(1)} %slice.79), channel_id=1, source_target_pairs={{0,3},{1,0},{2,1},{3,2},{4,7},{5,4},{6,5},{7,6},{8,11},{9,8},{10,9... | collective-permute-start | bytes 393224 | tf_op jit(solution)/shard_map/ppermute | solution.py:24
  (18 other events, 161.9 us)
Sparse Core Ops, SparseCore 0:
  10.5 37.6 all-gather.1
  113.6 38.4 reduce-scatter.1

commit v6 on v5

--- a/solution.py
+++ b/solution.py
@@ -28,49 +28,40 @@
     return lax.broadcasted_iota(jnp.int32, shape, 0) + start
 
 
-def shift_plane(value, dy, dc):
-    ys, cs = lax.axis_size("y"), lax.axis_size("c")
-    moves = []
-    for y in range(ys):
-        for c in range(cs):
-            moves.append((y * cs + c, (y + dy) % ys * cs + (c + dc) % cs))
-    return lax.ppermute(value, PLANE, moves)
-
-
 def pack_kernel(count, blk, *refs):
-    sources, p_ref, outs = refs[:count], refs[count], refs[count + 1:]
-    block_rows = sources[0].shape[1]
+    sources, p_ref = refs[:2 * count], refs[2 * count]
+    half, block_rows = sources[0].shape[:2]
     per_peer = count * MOST
-    for peer, out in enumerate(outs):
-        j = blk[len(outs) * per_peer + peer]
+    for j in range(p_ref.shape[0]):
         for slot in range(per_peer):
-            rows = sources[slot // MOST][blk[j * per_peer + slot]]
-            span = pl.ds(slot * block_rows, block_rows)
-            out[span, :] = rows
-            p_ref[j, span, :] = rows
-
-
-def pack(sources, blk, peers):
+            b = blk[j * per_peer + slot]
+            place = lax.rem(b, half)
+            low = sources[slot // MOST * 2][place]
+            high = sources[slot // MOST * 2 + 1][place]
+            first = jnp.full(low.shape, b, jnp.int32) < half
+            p_ref[j, pl.ds(slot * block_rows, block_rows), :] = jnp.where(first, low, high)
+
+
+def pack(sources, blk, plane):
     shape = sources[0].shape
-    plane = peers.shape[0]
-    width = len(sources) * MOST * shape[1]
-    out = jax.ShapeDtypeStruct((width, shape[2]), BF16)
+    count = len(sources) // 2
+    width = count * MOST * shape[1]
+    out = jax.ShapeDtypeStruct((plane, width, shape[2]), BF16)
     return pl.pallas_call(
-        functools.partial(pack_kernel, len(sources)),
+        functools.partial(pack_kernel, count),
         grid_spec=pltpu.PrefetchScalarGridSpec(
             num_scalar_prefetch=1,
             grid=(1,),
             in_specs=[pl.BlockSpec(shape, lambda j, blk: (0, 0, 0))] * len(sources),
-            out_specs=[pl.BlockSpec((plane, width, shape[2]), lambda j, blk: (0, 0, 0))]
-            + [pl.BlockSpec(out.shape, lambda j, blk: (0, 0))] * plane,
-        ),
-        out_shape=[jax.ShapeDtypeStruct((plane, width, shape[2]), BF16)] + [out] * plane,
-        compiler_params=pltpu.CompilerParams(vmem_limit_bytes=LARGE),
+            out_specs=pl.BlockSpec(out.shape, lambda j, blk: (0, 0, 0)),
+        ),
+        out_shape=out,
+        compiler_params=pltpu.CompilerParams(vmem_limit_bytes=SMALL),
         cost_estimate=pl.CostEstimate(
-            flops=0, bytes_accessed=6 * plane * width * shape[2], transcendentals=0
+            flops=0, bytes_accessed=4 * plane * width * shape[2], transcendentals=0
         ),
         name="pack",
-    )(jnp.concatenate([blk, peers]), *sources)
+    )(blk, *sources)
 
 
 def fetch_table(t_hbm, t_all, sems):
@@ -136,77 +127,6 @@
     )(packed, tables, targets)
 
 
-def combine_kernel(addr, named, a_ref, tgt_ref, line_ref, loss_ref, part_ref, lse_ref):
-    picks = part_ref.shape[0]
-    blocks = lse_ref.shape[0]
-    own_blocks = loss_ref.shape[0]
-    slots = line_ref.shape[2] // 32
-
-    def fetch(pair, kind):
-        a = addr[pair]
-        group = pl.multiple_of(lax.shift_right_logical(a, 2) % 4 * 128, 128)
-        row = a_ref[lax.shift_right_logical(a, 4), pl.ds(kind, 1), pl.ds(group, 128)]
-        return pltpu.roll(row, (4 - a % 4) % 4 * 32, 1)
-
-    def gather(i, carry):
-        for p in range(picks):
-            part_ref[p, pl.ds(i, 1), :] = fetch(i * picks + p, 0)
-        return carry
-
-    lax.fori_loop(0, blocks, gather, 0, unroll=4)
-    part = part_ref[...]
-    top = jnp.max(part, axis=0)
-    lse_ref[...] = top + jnp.log(jnp.sum(jnp.exp(part - top[None]), axis=0))
-
-    def loss(i, carry):
-        total = lse_ref[pl.ds(i, 1), :]
-        for p in range(picks):
-            total = total - fetch(i * picks + p, 1)
-        loss_ref[pl.ds(i, 1), :] = total
-        return carry
-
-    lax.fori_loop(0, own_blocks, loss, 0, unroll=4)
-    lane = lax.broadcasted_iota(jnp.int32, (1, 128), 1)
-
-    def lines(j, carry):
-        for group in range(slots // 4):
-            value = jnp.full((1, 128), EMPTY, F32)
-            for m in range(4):
-                slot = group * 4 + m
-                b = named[j * slots + slot]
-                row = lse_ref[pl.ds(slot // MOST * own_blocks + jnp.maximum(b, 0), 1), :]
-                if m:
-                    row = pltpu.roll(row, m * 32, 1)
-                keep = (lane >= m * 32) & (lane < m * 32 + 32) & (jnp.full((1, 128), b) >= 0)
-                value = jnp.where(keep, row, value)
-            line_ref[j, 0:1, group * 128:(group + 1) * 128] = value
-        line_ref[j, 1:2, :] = tgt_ref[j].astype(F32)
-        return carry
-
-    lax.fori_loop(0, line_ref.shape[0], lines, 0)
-
-
-def combine(addr, named, all_stats, targets, block_count, picks):
-    blocks = addr.shape[0] // picks
-    plane, _, width = targets.shape
-    whole = lambda shape: pl.BlockSpec(shape, lambda i, a, b: (0,) * len(shape))
-    lines = jax.ShapeDtypeStruct((plane, 2, width), F32)
-    loss = jax.ShapeDtypeStruct((block_count, 128), F32)
-    return pl.pallas_call(
-        combine_kernel,
-        grid_spec=pltpu.PrefetchScalarGridSpec(
-            num_scalar_prefetch=2,
-            grid=(1,),
-            in_specs=[whole(all_stats.shape), whole(targets.shape)],
-            out_specs=[whole(lines.shape), whole(loss.shape)],
-            scratch_shapes=[pltpu.VMEM((picks, blocks, 128), F32), pltpu.VMEM((blocks, 128), F32)],
-        ),
-        out_shape=[lines, loss],
-        compiler_params=pltpu.CompilerParams(vmem_limit_bytes=SMALL),
-        name="combine",
-    )(addr, named, all_stats, targets)
-
-
 def query_kernel(blk, p_ref, t_hbm, line_ref, g_ref, c_ref, acc_ref, t_all, sems):
     step = pl.program_id(0)
     t_ref = fetch_table(t_hbm, t_all, sems)
@@ -271,14 +191,11 @@
     )(blk, packed, tables, lines)
 
 
-def item_kernel(count, where, *refs):
-    rows_in, line_ref, t_ref, outs = refs[:count], refs[count], refs[count + 1], refs[count + 2:]
+def item_kernel(where, q_ref, line_ref, t_ref, *outs):
     start = where[pl.program_id(0)] * t_ref.shape[0]
-    first = pl.num_programs(0)
     total = None
-    for i, ref in enumerate(rows_in):
-        source = where[first + i]
-        q = ref[...]
+    for source in range(q_ref.shape[0]):
+        q = q_ref[source]
         line = line_ref[source]
         lse = line[0:1, :]
         tgt = line[1:2, :].astype(jnp.int32)
@@ -292,20 +209,18 @@
         out[0] = total[n * cut:(n + 1) * cut]
 
 
-def item_parts(places, pieces, x, origin, rows, lines, table16, quarters):
-    width, features = rows[0].shape
-    count = len(rows)
+def item_parts(places, pieces, x, rows, lines, table16, quarters):
+    count, width, features = rows.shape
     span = table16.shape[0] // quarters
     share = len(places)
-    where = jnp.concatenate([(jnp.array(places, jnp.int32) + x) % quarters, origin])
     out = jax.ShapeDtypeStruct((share, span // pieces, features), F32)
     return pl.pallas_call(
-        functools.partial(item_kernel, count),
+        item_kernel,
         grid_spec=pltpu.PrefetchScalarGridSpec(
             num_scalar_prefetch=1,
             grid=(share,),
-            in_specs=[pl.BlockSpec((width, features), lambda i, o: (0, 0))] * count
-            + [
+            in_specs=[
+                pl.BlockSpec(rows.shape, lambda i, o: (0, 0, 0)),
                 pl.BlockSpec(lines.shape, lambda i, o: (0, 0, 0)),
                 pl.BlockSpec((span, features), lambda i, o: (o[i], 0)),
             ],
@@ -319,7 +234,7 @@
             transcendentals=share * span * count * width,
         ),
         name="item_parts",
-    )(where, *rows, lines, table16)
+    )((jnp.array(places, jnp.int32) + x) % quarters, rows, lines, table16)
 
 
 def update_kernel(x_ref, own, after, before, far_a, far_b, t_ref, a_ref, nt_ref, na_ref):
@@ -367,11 +282,7 @@
 def local(queries, clusters, positives, owner_of, table, accum):
     z_size = lax.axis_size("z")
     x_size = lax.axis_size("x")
-    y_size = lax.axis_size("y")
-    c_size = lax.axis_size("c")
     z = lax.axis_index("z")
-    y = lax.axis_index("y")
-    c = lax.axis_index("c")
     x = lax.axis_index("x").reshape(1)
     local_rows, features = queries.shape
     block_count, picks = clusters.shape
@@ -384,15 +295,14 @@
     table16 = table[0].astype(BF16)
     tables = lax.all_gather(table16, PLANE)
 
-    here = queries.reshape(block_count, block_rows, features)
-    by_source = {0: here, 7: shift(here, "z", 1), 1: shift(here, "z", -1)}
-    clusters, positives, by_source[7], by_source[1] = lax.optimization_barrier(
-        (clusters, positives, by_source[7], by_source[1])
-    )
-    by_source[6] = shift(by_source[7], "z", 1)
-    by_source[2] = shift(by_source[1], "z", -1)
-    by_source[5] = shift(by_source[6], "z", 1)
-    by_source[3] = shift(by_source[2], "z", -1)
+    here = queries.reshape(2, block_count // 2, block_rows, features)
+    by_source = [[None] * 2 for _ in range(z_size)]
+    for half in range(2):
+        right = left = by_source[0][half] = here[half]
+        for hop in range(1, z_size // 2 + 1):
+            right = by_source[z_size - hop][half] = shift(right, "z", 1)
+            if hop < z_size // 2:
+                left = by_source[hop][half] = shift(left, "z", -1)
 
     flat_lists = clusters.reshape(pair_count)
     catalog_ids = jnp.arange(owners, dtype=jnp.int32)
@@ -424,7 +334,6 @@
         axis=1,
     )
     got = lax.all_to_all(meta, "z", 0, 0, tiled=True)
-    by_source[4] = shift(by_source[5], "z", 1)
     order = jnp.arange(z_size, dtype=jnp.int32)
     got = got[(z + order) % z_size]
     width = z_size * MOST * block_rows
@@ -439,36 +348,38 @@
     pair_owner = pair_slot // MOST
     pair_from = (pair_owner // plane - z) % z_size
     pair_place = (order[:, None] - pair_from) % z_size
-    pair_row = (pair_owner * z_size + pair_place) * MOST + pair_slot % MOST
-
-    hops = jnp.arange(plane, dtype=jnp.int32)
-    peers = (y + hops // c_size) % y_size * c_size + (c + hops % c_size) % c_size
-    origin = (y - hops // c_size) % y_size * c_size + (c - hops % c_size) % c_size
-    packed, *outgoing = pack([by_source[d] for d in range(z_size)], blk, peers)
-    rows = [
-        shift_plane(value, hop // c_size, hop % c_size) if hop else value
-        for hop, value in enumerate(outgoing)
-    ]
+    pair_row = (pair_from % 2 * 4 + pair_from // 2) * plane + pair_owner % plane
+    pair_row = (pair_row * 2 * z_size + pair_place) * MOST + pair_slot % MOST
+
+    packed = pack([part for pair in by_source for part in pair], blk, plane)
+    rows = lax.all_to_all(packed, PLANE, 0, 0, tiled=True)
     stats = forward(packed, targets, tables)
 
-    spread = jnp.broadcast_to(stats[None], (z_size,) + stats.shape)
-    all_stats = lax.all_to_all(spread, "z", 0, 0, tiled=True)
-    all_stats = all_stats.reshape(owners, 2, width)
-    lines, losses = combine(
-        pair_row.reshape(-1), named, all_stats, targets, block_count, picks
-    )
-    losses = losses[:, :block_rows].reshape(local_rows)
-    got_lines = lax.all_to_all(lines, PLANE, 0, 0, tiled=True)
+    even = jnp.stack([stats] + [shift(stats, "z", -e) for e in (2, 4, 6)])
+    all_stats = jnp.stack([even, shift(even, "z", -1)]).reshape(-1, block_rows)
+    part = all_stats[pair_row.reshape(-1)].reshape(z_size, block_count, picks, block_rows)
+    pick = all_stats[pair_row[0] + z_size * MOST].reshape(block_count, picks, block_rows)
+    top = jnp.max(part, axis=2)
+    lse = top + jnp.log(jnp.sum(jnp.exp(part - top[:, :, None]), axis=2))
+    losses = (lse[0] - jnp.sum(pick, axis=1)).reshape(local_rows)
+    lse_rows = lse.reshape(z_size * block_count, block_rows)
+    first = jnp.arange(z_size, dtype=jnp.int32).reshape(1, z_size, 1) * block_count
+    lse_at = (blk.reshape(plane, z_size, MOST) + first).reshape(-1)
+    lse_slots = jnp.where(named[:, None] < 0, F32(EMPTY), lse_rows[lse_at])
+    lines = jnp.concatenate(
+        [lse_slots.reshape(plane, 1, width), targets.astype(F32)], axis=1
+    )
 
     grads = query_parts(
         packed, jnp.concatenate([blk, z.reshape(1)]), lines, tables, z_size, block_count, block_rows
     )
-    grads, got_lines = lax.optimization_barrier((grads, got_lines))
+    grads, lines, rows = lax.optimization_barrier((grads, lines, rows))
     query_grads = lax.psum_scatter(grads, "z").astype(F32).reshape(local_rows, features)
-
-    far_a, far_b = item_parts((2,), 2, x, origin, rows, got_lines, table16, x_size)
+    got_lines = lax.all_to_all(lines, PLANE, 0, 0, tiled=True)
+
+    far_a, far_b = item_parts((2,), 2, x, rows, got_lines, table16, x_size)
     far_a, far_b, got_lines = lax.optimization_barrier((far_a, far_b, got_lines))
-    (rest,) = item_parts((0, 1, 3), 1, x, origin, rows, got_lines, table16, x_size)
+    (rest,) = item_parts((0, 1, 3), 1, x, rows, got_lines, table16, x_size)
     far_a, far_b = far_a[0], far_b[0]
     own, after, before = rest[0], rest[1], rest[2]
     half = far_a.shape[0]

time: 194 us -> 168 us (0.87)
  waiting for transfers between devices: 72.2 us -> 49.5 us
  Pallas kernels: 44.8 us -> 33.6 us
  local copies, waits for them, and re-layouts: 8.12 us -> 11.5 us
  other arithmetic: 8.19 us -> 11 us
    ppermute x7 -> x0, waiting for transfers between devices: 20.2 us -> none  [shift_plane(): return lax.ppermute(value, PLANE, moves)]
    pallas_call x4 -> x3, Pallas kernels: 20.4 us -> 9.14 us  [the longest x2 6.79 us: item_parts(): pl.pallas_call(item_kernel, grid_spec=pltpu.PrefetchScalarGridSpec(num_sc...]
    all_to_all x1, waiting for transfers between devices: 9.73 us -> 0.01 us  [local(): rows = lax.all_to_all(packed, PLANE, 0, 0, tiled=True)]
    ppermute x7 -> x0, starting transfers between devices: 8.85 us -> none  [shift_plane(): return lax.ppermute(value, PLANE, moves)]
    ppermute x15 -> x26, starting transfers between devices: 23.5 us -> 31.8 us  [shift(): lax.ppermute(value, axis, [(i, (i + step) % size) for i in range(size)])]
    all_to_all x1, waiting for transfers between devices: 0.01 us -> 5.41 us  [local(): got_lines = lax.all_to_all(lines, PLANE, 0, 0, tiled=True)]
    gather x0 -> x4, local copies, waits for them, and re-layouts: none -> 4.81 us  [the longest x1 2.25 us: local(): all_stats[pair_row.reshape(-1)]]
    ppermute x15 -> x26, waiting for transfers between devices: 34.4 us -> 36.3 us  [shift(): lax.ppermute(value, axis, [(i, (i + step) % size) for i in range(size)])]
  transfers between devices with their start and end apart: 27 -> 31, of which waited for: 17 -> 17; matrix products, arithmetic and copies ran while one was open for 5% -> 11% of each run, Pallas kernels for 14% -> 20%
where the time goes in v6:
time: 168 us; the launch traced here: 167 us
  waiting for transfers between devices  49.5 us (29%)
  starting transfers between devices  46.8 us (28%)
  Pallas kernels  33.6 us (20%)
  between operations  14.5 us (9%)
  local copies, waits for them, and re-layouts  11.5 us (7%)
  other arithmetic  11 us (7%)
    ppermute x26, waiting for transfers between devices, shift(): lax.ppermute(value, axis, [(i, (i + step) % size) for i in range(size)])  36.3 us
    ppermute x26, starting transfers between devices, shift(): lax.ppermute(value, axis, [(i, (i + step) % size) for i in range(size)])  31.8 us
    pallas_call x1, Pallas kernels, query_parts(): pl.pallas_call(query_kernel, grid_spec=pltpu.PrefetchScalarGridSpec(num_s...  12.5 us
    pallas_call x1, Pallas kernels, forward(): pl.pallas_call(forward_kernel, grid=(planes,), in_specs=[pl.BlockSpec((1,...  9.83 us
    all_to_all x1, waiting for transfers between devices, local(): got = lax.all_to_all(meta, 'z', 0, 0, tiled=True)  7.76 us
    pallas_call x2, Pallas kernels, item_parts(): pl.pallas_call(item_kernel, grid_spec=pltpu.PrefetchScalarGridSpec(num_sc...  6.79 us
    all_to_all x1, starting transfers between devices, local(): got = lax.all_to_all(meta, 'z', 0, 0, tiled=True)  5.76 us
    all_to_all x1, waiting for transfers between devices, local(): got_lines = lax.all_to_all(lines, PLANE, 0, 0, tiled=True)  5.41 us
  transfers between devices with their start and end apart: 31, of which 17 were waited for; matrix products, arithmetic and copies ran while one was open for 11% of the time, Pallas kernels for 20%

profile of v6, /device:TPU:6, one launch (start us, length us, event | category | flops | bytes accessed | tf_op | source)
XLA Modules:
  0.0 166.8 jit_solution(6171399422333256734)
XLA Ops:
  7.3 2.5 %bitcast_convert_fusion.1 = (bf16[1024,256]{1,0:T(8,128)(2,1)S(1)}, bf16[1,1024,256]{2,1,0:T(8,128)(2,1)}) fusion(f32[1,1024,256]{2,1,0:T(8,128)} %param.12), kind=kLoop, calls=%fused_computation.128 | loop fusion | flops 524288 | bytes 2097152 | tf_op jit(solution)/shard_map/convert_element_type | solution.py:295
  9.8 2.0 %collective-permute-start.6 = (bf16[8,32,256]{2,1,0:T(8,128)(2,1)S(1)}, bf16[8,32,256]{2,1,0:T(8,128)(2,1)S(1)}, u32[]{:S(2)}, u32[]{:S(2)}) collective-permute-start(bf16[8,32,256]{2,1,0:T(8,128)(2,1)S(1)} %bitcast.88), channel_id=1, source_target_pairs={{0,32},{32,64},{64,96},{96,128},{128,160},{160,192},{192,224},{224... | collective-permute-start | bytes 393224 | tf_op jit(solution)/shard_map/ppermute | solution.py:24
  11.8 4.0 %collective-permute-start = (bf16[8,32,256]{2,1,0:T(8,128)(2,1)S(1)}, bf16[8,32,256]{2,1,0:T(8,128)(2,1)S(1)}, u32[]{:S(2)}, u32[]{:S(2)}) collective-permute-start(bf16[8,32,256]{2,1,0:T(8,128)(2,1)S(1)} %bitcast.89), channel_id=1, source_target_pairs={{0,224},{32,0},{64,32},{96,64},{128,96},{160,128},{192,160},{224,1... | collective-permute-start | bytes 393224 | tf_op jit(solution)/shard_map/ppermute | solution.py:24
  15.8 3.2 %collective-permute-start.1 = (bf16[8,32,256]{2,1,0:T(8,128)(2,1)S(1)}, bf16[8,32,256]{2,1,0:T(8,128)(2,1)S(1)}, u32[]{:S(2)}, u32[]{:S(2)}) collective-permute-start(bf16[8,32,256]{2,1,0:T(8,128)(2,1)S(1)} %bitcast.86), channel_id=1, source_target_pairs={{0,224},{32,0},{64,32},{96,64},{128,96},{160,128},{192,160},{224,1... | collective-permute-start | bytes 393224 | tf_op jit(solution)/shard_map/ppermute | solution.py:24
  22.2 5.8 %all-to-all-start = ((s32[8,1,592]{2,1,0:T(1,128)}), s32[8,1,592]{2,1,0:T(1,128)S(1)}, u32[]{:S(2)}, u32[]{:S(2)}) async-start(s32[8,1,592]{2,1,0:T(1,128)} %copy.42), calls=%async_computation | async-start | bytes 40960 | tf_op jit(solution)/shard_map/all_to_all | solution.py:336
  28.0 7.8 %all-to-all-done = s32[8,1,592]{2,1,0:T(1,128)S(1)} async-done(((s32[8,1,592]{2,1,0:T(1,128)}), s32[8,1,592]{2,1,0:T(1,128)S(1)}, u32[]{:S(2)}, u32[]{:S(2)}) %all-to-all-start) | async-done | bytes 18976 | tf_op jit(solution)/shard_map/all_to_all | solution.py:336
  38.1 2.8 %collective-permute-start.2 = (bf16[8,32,256]{2,1,0:T(8,128)(2,1)S(1)}, bf16[8,32,256]{2,1,0:T(8,128)(2,1)S(1)}, u32[]{:S(2)}, u32[]{:S(2)}) collective-permute-start(bf16[8,32,256]{2,1,0:T(8,128)(2,1)S(1)} %collective-permute-done.refs_2_), channel_id=1, source_target_pairs={{0,224},{32,0},{64,32},{96,64},{128,96},{160,128},{192,160},{224,1... | collective-permute-start | bytes 393224 | tf_op jit(solution)/shard_map/ppermute | solution.py:24
  43.1 2.4 %collective-permute-done.7.refs_12_ = bf16[8,32,256]{2,1,0:T(8,128)(2,1)S(1)} collective-permute-done((bf16[8,32,256]{2,1,0:T(8,128)(2,1)S(1)}, bf16[8,32,256]{2,1,0:T(8,128)(2,1)S(1)}, u32[]{:S(2)}, u32[]{:S(2)}) %collective-permute-start.7) | collective-permute-done | bytes 131104 | tf_op jit(solution)/shard_map/ppermute | solution.py:24
  45.5 3.2 %collective-permute-start.4 = (bf16[8,32,256]{2,1,0:T(8,128)(2,1)S(1)}, bf16[8,32,256]{2,1,0:T(8,128)(2,1)S(1)}, u32[]{:S(2)}, u32[]{:S(2)}) collective-permute-start(bf16[8,32,256]{2,1,0:T(8,128)(2,1)S(1)} %collective-permute-done.2.refs_4_), channel_id=1, source_target_pairs={{0,224},{32,0},{64,32},{96,64},{128,96},{160,128},{192,160},{224,1... | collective-permute-start | bytes 393224 | tf_op jit(solution)/shard_map/ppermute | solution.py:24
  50.8 2.3 %collective-permute-done.8.refs_10_ = bf16[8,32,256]{2,1,0:T(8,128)(2,1)S(1)} collective-permute-done((bf16[8,32,256]{2,1,0:T(8,128)(2,1)S(1)}, bf16[8,32,256]{2,1,0:T(8,128)(2,1)S(1)}, u32[]{:S(2)}, u32[]{:S(2)}) %collective-permute-start.8) | collective-permute-done | bytes 131104 | tf_op jit(solution)/shard_map/ppermute | solution.py:24
  55.6 3.7 %collective-permute-done.9.refs_8_ = bf16[8,32,256]{2,1,0:T(8,128)(2,1)S(1)} collective-permute-done((bf16[8,32,256]{2,1,0:T(8,128)(2,1)S(1)}, bf16[8,32,256]{2,1,0:T(8,128)(2,1)S(1)}, u32[]{:S(2)}, u32[]{:S(2)}) %collective-permute-start.9) | collective-permute-done | bytes 131104 | tf_op jit(solution)/shard_map/ppermute | solution.py:24
  59.3 2.3 %pack.1.p_ref = bf16[8,512,256]{2,1,0:T(8,128)(2,1)} custom-call(s32[128]{0:T(128)S(1)} %max.12.blk, bf16[8,32,256]{2,1,0:T(8,128)(2,1)S(1)} %bitcast.90, bf16[8,32,256]{2,1,0:T(8,128)(2,1)S(1)} %bitcast.87, bf16[8,32,256]{2,1,0:T(8,128)(2,1)S(1)} %collective-permute-done.refs_2_, bf16[8,32,256]{2,1,0:T(8,128)(2,1)S(1)} %collective-permute-done.1.refs_3_, ...), custom_call_target="tpu_custom_call" | custom-call | bytes 4194304 | tf_op jit(solution)/shard_map/pack/pallas_call | solution.py:50
  61.6 4.9 %all-to-all-start.1 = ((bf16[8,512,256]{2,1,0:T(8,128)(2,1)}), bf16[8,512,256]{2,1,0:T(8,128)(2,1)S(1)}, u32[]{:S(2)}, u32[]{:S(2)}) async-start(bf16[8,512,256]{2,1,0:T(8,128)(2,1)} %pack.1.p_ref), calls=%async_computation.1 | async-start | bytes 4194304 | tf_op jit(solution)/shard_map/all_to_all | solution.py:355
  66.6 9.8 %forward.1 = f32[8,2,512]{2,1,0:T(2,128)} custom-call(bf16[8,512,256]{2,1,0:T(8,128)(2,1)} %pack.1.p_ref, bf16[8,1024,256]{2,1,0:T(8,128)(2,1)} %all-gather.2.cloned.1.call-done.t_hbm, s32[8,1,512]{2,1,0:T(1,128)} %reshape.367.tgt_ref), custom_call_target="tpu_custom_call" | custom-call | flops 2147483648 | bytes 6291456 | tf_op jit(solution)/shard_map/forward/pallas_call | solution.py:105
  77.9 2.0 %collective-permute-start.16 = (f32[8,2,512]{2,1,0:T(2,128)}, f32[8,2,512]{2,1,0:T(2,128)S(1)}, u32[]{:S(2)}, u32[]{:S(2)}) collective-permute-start(f32[8,2,512]{2,1,0:T(2,128)} %forward.1), channel_id=1, source_target_pairs={{0,64},{32,96},{64,128},{96,160},{128,192},{160,224},{192,0},{224,... | collective-permute-start | bytes 98312 | tf_op jit(solution)/shard_map/ppermute | solution.py:24
  80.0 2.1 %collective-permute-done.14 = f32[8,2,512]{2,1,0:T(2,128)S(1)} collective-permute-done((f32[8,2,512]{2,1,0:T(2,128)}, f32[8,2,512]{2,1,0:T(2,128)S(1)}, u32[]{:S(2)}, u32[]{:S(2)}) %collective-permute-start.14) | collective-permute-done | bytes 32800 | tf_op jit(solution)/shard_map/ppermute | solution.py:24
  82.1 2.9 %collective-permute-done.15 = f32[8,2,512]{2,1,0:T(2,128)S(1)} collective-permute-done((f32[8,2,512]{2,1,0:T(2,128)}, f32[8,2,512]{2,1,0:T(2,128)S(1)}, u32[]{:S(2)}, u32[]{:S(2)}) %collective-permute-start.15) | collective-permute-done | bytes 32800 | tf_op jit(solution)/shard_map/ppermute | solution.py:24
  89.1 3.3 %collective-permute-done.17 = f32[4,8,2,512]{3,2,1,0:T(2,128)S(1)} collective-permute-done((f32[4,8,2,512]{3,2,1,0:T(2,128)S(1)}, f32[4,8,2,512]{3,2,1,0:T(2,128)S(1)}, u32[]{:S(2)}, u32[]{:S(2)}) %collective-permute-start.17) | collective-permute-done | bytes 131104 | tf_op jit(solution)/shard_map/ppermute | solution.py:24
  93.9 2.3 %gather_fusion.2 = f32[512,32]{1,0:T(8,128)S(1)} fusion(f32[2048,32]{1,0:T(8,128)} %reshape.368, s32[1024]{0:T(1024)S(1)} %pad_clamp_fusion.2), kind=kCustom, calls=%fused_computation.2 | custom fusion | bytes 133120 | tf_op jit(solution)/shard_map/gather | solution.py:360
  98.0 12.5 %query_parts.1 = bf16[8,16,32,256]{3,2,1,0:T(8,128)(2,1)} custom-call(s32[129]{0:T(256)} %pad_add_fusion.blk, bf16[8,512,256]{2,1,0:T(8,128)(2,1)} %pack.1.p_ref, bf16[8,1024,256]{2,1,0:T(8,128)(2,1)} %all-gather.2.cloned.1.call-done.t_hbm, f32[8,2,512]{2,1,0:T(2,128)} %pad_maximum_fusion.4.line_ref), custom_call_target="tpu_custom_call" | custom-call | flops 4294967296 | bytes 8388608 | tf_op jit(solution)/shard_map/query_parts/pallas_call | solution.py:165
  110.6 4.2 %all-to-all-start.2 = ((f32[8,2,512]{2,1,0:T(2,128)}), f32[8,2,512]{2,1,0:T(2,128)S(1)}, u32[]{:S(2)}, u32[]{:S(2)}) async-start(f32[8,2,512]{2,1,0:T(2,128)} %pad_maximum_fusion.4.line_ref), calls=%async_computation.2 | async-start | bytes 65536 | tf_op jit(solution)/shard_map/all_to_all | solution.py:378
  114.9 5.4 %all-to-all-done.2.line_ref = f32[8,2,512]{2,1,0:T(2,128)S(1)} async-done(((f32[8,2,512]{2,1,0:T(2,128)}), f32[8,2,512]{2,1,0:T(2,128)S(1)}, u32[]{:S(2)}, u32[]{:S(2)}) %all-to-all-start.2) | async-done | bytes 32800 | tf_op jit(solution)/shard_map/all_to_all | solution.py:378
  124.0 5.2 %item_parts.3 = f32[3,256,256]{2,1,0:T(8,128)S(1)} custom-call(s32[3]{0:T(128)S(1)} %and_select_fusion.2.where, bf16[8,512,256]{2,1,0:T(8,128)(2,1)S(1)} %all-to-all-done.1.q_ref, f32[8,2,512]{2,1,0:T(2,128)S(1)} %all-to-all-done.2.line_ref, bf16[1024,256]{1,0:T(8,128)(2,1)S(1)} %get-tuple-element.28.t_ref), custom_call_target="tpu_custom_call" | custom-call | flops 3221225472 | bytes 3276800 | tf_op jit(solution)/shard_map/item_parts/pallas_call | solution.py:217
  132.2 1.8 %gather_fusion.4 = f32[64,32]{1,0:T(8,128)S(1)} fusion(f32[2048,32]{1,0:T(8,128)} %reshape.368, s32[1024]{0:T(1024)S(1)} %pad_clamp_fusion), kind=kCustom, calls=%fused_computation.4 | custom fusion | bytes 16640 | tf_op jit(solution)/shard_map/gather | solution.py:361
  134.8 3.0 %collective-permute-done.19 = f32[256,256]{1,0:T(8,128)} collective-permute-done((f32[256,256]{1,0:T(8,128)}, f32[256,256]{1,0:T(8,128)}, u32[]{:S(2)}, u32[]{:S(2)}) %collective-permute-start.19) | collective-permute-done | bytes 262176 | tf_op jit(solution)/shard_map/ppermute | solution.py:24
  137.8 2.6 %collective-permute-done.21 = f32[256,256]{1,0:T(8,128)} collective-permute-done((f32[256,256]{1,0:T(8,128)S(1)}, f32[256,256]{1,0:T(8,128)}, u32[]{:S(2)}, u32[]{:S(2)}) %collective-permute-start.21) | collective-permute-done | bytes 262176 | tf_op jit(solution)/shard_map/ppermute | solution.py:24
  143.6 4.3 %collective-permute-done.23.before = f32[256,256]{1,0:T(8,128)S(1)} collective-permute-done((f32[256,256]{1,0:T(8,128)S(1)}, f32[256,256]{1,0:T(8,128)S(1)}, u32[]{:S(2)}, u32[]{:S(2)}) %collective-permute-start.23) | collective-permute-done | bytes 262176 | tf_op jit(solution)/shard_map/ppermute | solution.py:24
  148.0 1.9 %collective-permute-start.24 = (f32[128,256]{1,0:T(8,128)S(1)}, f32[128,256]{1,0:T(8,128)S(1)}, u32[]{:S(2)}, u32[]{:S(2)}) collective-permute-start(f32[128,256]{1,0:T(8,128)S(1)} %slice.99), channel_id=1, source_target_pairs={{0,1},{1,2},{2,3},{3,0},{4,5},{5,6},{6,7},{7,4},{8,9},{9,10},{10,1... | collective-permute-start | bytes 393224 | tf_op jit(solution)/shard_map/ppermute | solution.py:24
  150.2 2.8 %collective-permute-done.24.far_a = f32[128,256]{1,0:T(8,128)S(1)} collective-permute-done((f32[128,256]{1,0:T(8,128)S(1)}, f32[128,256]{1,0:T(8,128)S(1)}, u32[]{:S(2)}, u32[]{:S(2)}) %collective-permute-start.24) | collective-permute-done | bytes 131104 | tf_op jit(solution)/shard_map/ppermute | solution.py:24
  153.0 3.2 %collective-permute-done.25.far_b = f32[128,256]{1,0:T(8,128)S(1)} collective-permute-done((f32[128,256]{1,0:T(8,128)S(1)}, f32[128,256]{1,0:T(8,128)S(1)}, u32[]{:S(2)}, u32[]{:S(2)}) %collective-permute-start.25) | collective-permute-done | bytes 131104 | tf_op jit(solution)/shard_map/ppermute | solution.py:24
  156.2 2.1 %update.1 = (f32[1024,256]{1,0:T(8,128)}, f32[1024,256]{1,0:T(8,128)}) custom-call(s32[1]{0:T(128)} %bitcast.22.x_ref, f32[256,256]{1,0:T(8,128)S(1)} %fusion.1.own, f32[256,256]{1,0:T(8,128)S(1)} %collective-permute-done.22.after, f32[256,256]{1,0:T(8,128)S(1)} %collective-permute-done.23.before, f32[128,256]{1,0:T(8,128)S(1)} %collective-permute-done.24.far_a, ...), custom_call_target="tpu_custom_call" | custom-call | tf_op jit(solution)/shard_map/update/pallas_call | solution.py:268
  158.2 1.8 %bitcast_convert_fusion = f32[512,256]{1,0:T(8,128)} fusion(bf16[1,16,32,256]{3,2,1,0:T(8,128)(2,1)} %reduce-scatter.2.cloned.1.call-done), kind=kLoop, calls=%fused_computation.11 | loop fusion | flops 131072 | bytes 786432 | tf_op jit(solution)/shard_map/convert_element_type | solution.py:377
  (142 shorter events, 32.0 us)
Async XLA Ops:
  7.2 59.4 %all-gather.2.cloned.1.call-start = ((), (), s32[]{:S(2)}) async-start(), calls=%async_computation.4 | async-start | bytes 4718592 | tf_op jit(solution)/shard_map/all_gather | solution.py:296
  9.8 27.7 %collective-permute-start.6 = (bf16[8,32,256]{2,1,0:T(8,128)(2,1)S(1)}, bf16[8,32,256]{2,1,0:T(8,128)(2,1)S(1)}, u32[]{:S(2)}, u32[]{:S(2)}) collective-permute-start(bf16[8,32,256]{2,1,0:T(8,128)(2,1)S(1)} %bitcast.88), channel_id=1, source_target_pairs={{0,32},{32,64},{64,96},{96,128},{128,160},{160,192},{192,224},{224... | collective-permute-start | bytes 393224 | tf_op jit(solution)/shard_map/ppermute | solution.py:24
  11.8 26.3 %collective-permute-start = (bf16[8,32,256]{2,1,0:T(8,128)(2,1)S(1)}, bf16[8,32,256]{2,1,0:T(8,128)(2,1)S(1)}, u32[]{:S(2)}, u32[]{:S(2)}) collective-permute-start(bf16[8,32,256]{2,1,0:T(8,128)(2,1)S(1)} %bitcast.89), channel_id=1, source_target_pairs={{0,224},{32,0},{64,32},{96,64},{128,96},{160,128},{192,160},{224,1... | collective-permute-start | bytes 393224 | tf_op jit(solution)/shard_map/ppermute | solution.py:24
  15.8 21.0 %collective-permute-start.10 = (bf16[8,32,256]{2,1,0:T(8,128)(2,1)S(1)}, bf16[8,32,256]{2,1,0:T(8,128)(2,1)S(1)}, u32[]{:S(2)}, u32[]{:S(2)}) collective-permute-start(bf16[8,32,256]{2,1,0:T(8,128)(2,1)S(1)} %bitcast.85), channel_id=1, source_target_pairs={{0,32},{32,64},{64,96},{96,128},{128,160},{160,192},{192,224},{224... | collective-permute-start | bytes 393224 | tf_op jit(solution)/shard_map/ppermute | solution.py:24
  15.8 25.0 %collective-permute-start.1 = (bf16[8,32,256]{2,1,0:T(8,128)(2,1)S(1)}, bf16[8,32,256]{2,1,0:T(8,128)(2,1)S(1)}, u32[]{:S(2)}, u32[]{:S(2)}) collective-permute-start(bf16[8,32,256]{2,1,0:T(8,128)(2,1)S(1)} %bitcast.86), channel_id=1, source_target_pairs={{0,224},{32,0},{64,32},{96,64},{128,96},{160,128},{192,160},{224,1... | collective-permute-start | bytes 393224 | tf_op jit(solution)/shard_map/ppermute | solution.py:24
  22.2 13.6 %all-to-all-start = ((s32[8,1,592]{2,1,0:T(1,128)}), s32[8,1,592]{2,1,0:T(1,128)S(1)}, u32[]{:S(2)}, u32[]{:S(2)}) async-start(s32[8,1,592]{2,1,0:T(1,128)} %copy.42), calls=%async_computation | async-start | bytes 40960 | tf_op jit(solution)/shard_map/all_to_all | solution.py:336
  36.8 6.3 %collective-permute-start.11 = (bf16[8,32,256]{2,1,0:T(8,128)(2,1)S(1)}, bf16[8,32,256]{2,1,0:T(8,128)(2,1)S(1)}, u32[]{:S(2)}, u32[]{:S(2)}) collective-permute-start(bf16[8,32,256]{2,1,0:T(8,128)(2,1)S(1)} %collective-permute-done.10.refs_15_), channel_id=1, source_target_pairs={{0,32},{32,64},{64,96},{96,128},{128,160},{160,192},{192,224},{224... | collective-permute-start | bytes 393224 | tf_op jit(solution)/shard_map/ppermute | solution.py:24
  37.6 7.9 %collective-permute-start.7 = (bf16[8,32,256]{2,1,0:T(8,128)(2,1)S(1)}, bf16[8,32,256]{2,1,0:T(8,128)(2,1)S(1)}, u32[]{:S(2)}, u32[]{:S(2)}) collective-permute-start(bf16[8,32,256]{2,1,0:T(8,128)(2,1)S(1)} %collective-permute-done.6.refs_14_), channel_id=1, source_target_pairs={{0,32},{32,64},{64,96},{96,128},{128,160},{160,192},{192,224},{224... | collective-permute-start | bytes 393224 | tf_op jit(solution)/shard_map/ppermute | solution.py:24
  38.1 7.4 %collective-permute-start.2 = (bf16[8,32,256]{2,1,0:T(8,128)(2,1)S(1)}, bf16[8,32,256]{2,1,0:T(8,128)(2,1)S(1)}, u32[]{:S(2)}, u32[]{:S(2)}) collective-permute-start(bf16[8,32,256]{2,1,0:T(8,128)(2,1)S(1)} %collective-permute-done.refs_2_), channel_id=1, source_target_pairs={{0,224},{32,0},{64,32},{96,64},{128,96},{160,128},{192,160},{224,1... | collective-permute-start | bytes 393224 | tf_op jit(solution)/shard_map/ppermute | solution.py:24
  40.9 7.9 %collective-permute-start.3 = (bf16[8,32,256]{2,1,0:T(8,128)(2,1)S(1)}, bf16[8,32,256]{2,1,0:T(8,128)(2,1)S(1)}, u32[]{:S(2)}, u32[]{:S(2)}) collective-permute-start(bf16[8,32,256]{2,1,0:T(8,128)(2,1)S(1)} %collective-permute-done.1.refs_3_), channel_id=1, source_target_pairs={{0,224},{32,0},{64,32},{96,64},{128,96},{160,128},{192,160},{224,1... | collective-permute-start | bytes 393224 | tf_op jit(solution)/shard_map/ppermute | solution.py:24
  43.1 6.2 %collective-permute-start.12 = (bf16[8,32,256]{2,1,0:T(8,128)(2,1)S(1)}, bf16[8,32,256]{2,1,0:T(8,128)(2,1)S(1)}, u32[]{:S(2)}, u32[]{:S(2)}) collective-permute-start(bf16[8,32,256]{2,1,0:T(8,128)(2,1)S(1)} %collective-permute-done.11.refs_13_), channel_id=1, source_target_pairs={{0,32},{32,64},{64,96},{96,128},{128,160},{160,192},{192,224},{224... | collective-permute-start | bytes 393224 | tf_op jit(solution)/shard_map/ppermute | solution.py:24
  45.5 7.6 %collective-permute-start.8 = (bf16[8,32,256]{2,1,0:T(8,128)(2,1)S(1)}, bf16[8,32,256]{2,1,0:T(8,128)(2,1)S(1)}, u32[]{:S(2)}, u32[]{:S(2)}) collective-permute-start(bf16[8,32,256]{2,1,0:T(8,128)(2,1)S(1)} %collective-permute-done.7.refs_12_), channel_id=1, source_target_pairs={{0,32},{32,64},{64,96},{96,128},{128,160},{160,192},{192,224},{224... | collective-permute-start | bytes 393224 | tf_op jit(solution)/shard_map/ppermute | solution.py:24
  45.5 8.7 %collective-permute-start.4 = (bf16[8,32,256]{2,1,0:T(8,128)(2,1)S(1)}, bf16[8,32,256]{2,1,0:T(8,128)(2,1)S(1)}, u32[]{:S(2)}, u32[]{:S(2)}) collective-permute-start(bf16[8,32,256]{2,1,0:T(8,128)(2,1)S(1)} %collective-permute-done.2.refs_4_), channel_id=1, source_target_pairs={{0,224},{32,0},{64,32},{96,64},{128,96},{160,128},{192,160},{224,1... | collective-permute-start | bytes 393224 | tf_op jit(solution)/shard_map/ppermute | solution.py:24
  48.7 5.5 %collective-permute-start.5 = (bf16[8,32,256]{2,1,0:T(8,128)(2,1)S(1)}, bf16[8,32,256]{2,1,0:T(8,128)(2,1)S(1)}, u32[]{:S(2)}, u32[]{:S(2)}) collective-permute-start(bf16[8,32,256]{2,1,0:T(8,128)(2,1)S(1)} %collective-permute-done.3.refs_5_), channel_id=1, source_target_pairs={{0,224},{32,0},{64,32},{96,64},{128,96},{160,128},{192,160},{224,1... | collective-permute-start | bytes 393224 | tf_op jit(solution)/shard_map/ppermute | solution.py:24
  49.3 6.3 %collective-permute-start.13 = (bf16[8,32,256]{2,1,0:T(8,128)(2,1)S(1)}, bf16[8,32,256]{2,1,0:T(8,128)(2,1)S(1)}, u32[]{:S(2)}, u32[]{:S(2)}) collective-permute-start(bf16[8,32,256]{2,1,0:T(8,128)(2,1)S(1)} %collective-permute-done.12.refs_11_), channel_id=1, source_target_pairs={{0,32},{32,64},{64,96},{96,128},{128,160},{160,192},{192,224},{224... | collective-permute-start | bytes 393224 | tf_op jit(solution)/shard_map/ppermute | solution.py:24
  53.1 6.2 %collective-permute-start.9 = (bf16[8,32,256]{2,1,0:T(8,128)(2,1)S(1)}, bf16[8,32,256]{2,1,0:T(8,128)(2,1)S(1)}, u32[]{:S(2)}, u32[]{:S(2)}) collective-permute-start(bf16[8,32,256]{2,1,0:T(8,128)(2,1)S(1)} %collective-permute-done.8.refs_10_), channel_id=1, source_target_pairs={{0,32},{32,64},{64,96},{96,128},{128,160},{160,192},{192,224},{224... | collective-permute-start | bytes 393224 | tf_op jit(solution)/shard_map/ppermute | solution.py:24
  61.6 48.9 %all-to-all-start.1 = ((bf16[8,512,256]{2,1,0:T(8,128)(2,1)}), bf16[8,512,256]{2,1,0:T(8,128)(2,1)S(1)}, u32[]{:S(2)}, u32[]{:S(2)}) async-start(bf16[8,512,256]{2,1,0:T(8,128)(2,1)} %pack.1.p_ref), calls=%async_computation.1 | async-start | bytes 4194304 | tf_op jit(solution)/shard_map/all_to_all | solution.py:355
  66.5 91.7 %reduce-scatter.2.cloned.1.call-start = ((), (), s32[]{:S(2)}) async-start(), calls=%async_computation.5 | async-start | bytes 2359296 | tf_op jit(solution)/shard_map/reduce_scatter | solution.py:377
  76.4 5.7 %collective-permute-start.14 = (f32[8,2,512]{2,1,0:T(2,128)}, f32[8,2,512]{2,1,0:T(2,128)S(1)}, u32[]{:S(2)}, u32[]{:S(2)}) collective-permute-start(f32[8,2,512]{2,1,0:T(2,128)} %forward.1), channel_id=1, source_target_pairs={{0,192},{32,224},{64,0},{96,32},{128,64},{160,96},{192,128},{224,1... | collective-permute-start | bytes 98312 | tf_op jit(solution)/shard_map/ppermute | solution.py:24
  76.5 8.5 %collective-permute-start.15 = (f32[8,2,512]{2,1,0:T(2,128)}, f32[8,2,512]{2,1,0:T(2,128)S(1)}, u32[]{:S(2)}, u32[]{:S(2)}) collective-permute-start(f32[8,2,512]{2,1,0:T(2,128)} %forward.1), channel_id=1, source_target_pairs={{0,128},{32,160},{64,192},{96,224},{128,0},{160,32},{192,64},{224,... | collective-permute-start | bytes 98312 | tf_op jit(solution)/shard_map/ppermute | solution.py:24
  77.9 8.3 %collective-permute-start.16 = (f32[8,2,512]{2,1,0:T(2,128)}, f32[8,2,512]{2,1,0:T(2,128)S(1)}, u32[]{:S(2)}, u32[]{:S(2)}) collective-permute-start(f32[8,2,512]{2,1,0:T(2,128)} %forward.1), channel_id=1, source_target_pairs={{0,64},{32,96},{64,128},{96,160},{128,192},{160,224},{192,0},{224,... | collective-permute-start | bytes 98312 | tf_op jit(solution)/shard_map/ppermute | solution.py:24
  87.0 5.3 %collective-permute-start.17 = (f32[4,8,2,512]{3,2,1,0:T(2,128)S(1)}, f32[4,8,2,512]{3,2,1,0:T(2,128)S(1)}, u32[]{:S(2)}, u32[]{:S(2)}) collective-permute-start(f32[4,8,2,512]{3,2,1,0:T(2,128)S(1)} %pad_maximum_fusion.3), channel_id=1, source_target_pairs={{0,224},{32,0},{64,32},{96,64},{128,96},{160,128},{192,160},{224,1... | collective-permute-start | bytes 393224 | tf_op jit(solution)/shard_map/ppermute | solution.py:24
  110.6 9.7 %all-to-all-start.2 = ((f32[8,2,512]{2,1,0:T(2,128)}), f32[8,2,512]{2,1,0:T(2,128)S(1)}, u32[]{:S(2)}, u32[]{:S(2)}) async-start(f32[8,2,512]{2,1,0:T(2,128)} %pad_maximum_fusion.4.line_ref), calls=%async_computation.2 | async-start | bytes 65536 | tf_op jit(solution)/shard_map/all_to_all | solution.py:378
  121.8 7.4 %collective-permute-start.18 = (f32[128,256]{1,0:T(8,128)S(1)}, f32[128,256]{1,0:T(8,128)S(1)}, u32[]{:S(2)}, u32[]{:S(2)}) collective-permute-start(f32[128,256]{1,0:T(8,128)S(1)} %bitcast.92), channel_id=1, source_target_pairs={{0,1},{1,2},{2,3},{3,0},{4,5},{5,6},{6,7},{7,4},{8,9},{9,10},{10,1... | collective-permute-start | bytes 393224 | tf_op jit(solution)/shard_map/ppermute | solution.py:24
  122.4 6.9 %collective-permute-start.20 = (f32[128,256]{1,0:T(8,128)S(1)}, f32[128,256]{1,0:T(8,128)S(1)}, u32[]{:S(2)}, u32[]{:S(2)}) collective-permute-start(f32[128,256]{1,0:T(8,128)S(1)} %bitcast.91), channel_id=1, source_target_pairs={{0,3},{1,0},{2,1},{3,2},{4,7},{5,4},{6,5},{7,6},{8,11},{9,8},{10,9... | collective-permute-start | bytes 393224 | tf_op jit(solution)/shard_map/ppermute | solution.py:24
  129.2 27.0 %copy-start = (f32[1,1024,256]{2,1,0:T(8,128)S(1)}, f32[1,1024,256]{2,1,0:T(8,128)}, u32[]{:S(2)}) copy-start(f32[1,1024,256]{2,1,0:T(8,128)} %param.12) | copy-start | bytes 3145732
  130.0 7.7 %collective-permute-start.19 = (f32[256,256]{1,0:T(8,128)}, f32[256,256]{1,0:T(8,128)}, u32[]{:S(2)}, u32[]{:S(2)}) collective-permute-start(f32[256,256]{1,0:T(8,128)} %pad_maximum_fusion.1), channel_id=1, source_target_pairs={{0,1},{1,2},{2,3},{3,0},{4,5},{5,6},{6,7},{7,4},{8,9},{9,10},{10,1... | collective-permute-start | bytes 786440 | tf_op jit(solution)/shard_map/ppermute | solution.py:24
  131.7 8.7 %collective-permute-start.21 = (f32[256,256]{1,0:T(8,128)S(1)}, f32[256,256]{1,0:T(8,128)}, u32[]{:S(2)}, u32[]{:S(2)}) collective-permute-start(f32[256,256]{1,0:T(8,128)S(1)} %pad_maximum_fusion.2), channel_id=1, source_target_pairs={{0,3},{1,0},{2,1},{3,2},{4,7},{5,4},{6,5},{7,6},{8,11},{9,8},{10,9... | collective-permute-start | bytes 786440 | tf_op jit(solution)/shard_map/ppermute | solution.py:24
  141.5 6.4 %collective-permute-start.23 = (f32[256,256]{1,0:T(8,128)S(1)}, f32[256,256]{1,0:T(8,128)S(1)}, u32[]{:S(2)}, u32[]{:S(2)}) collective-permute-start(f32[256,256]{1,0:T(8,128)S(1)} %fusion.1.own), channel_id=1, source_target_pairs={{0,1},{1,2},{2,3},{3,0},{4,5},{5,6},{6,7},{7,4},{8,9},{9,10},{10,1... | collective-permute-start | bytes 786440 | tf_op jit(solution)/shard_map/ppermute | solution.py:24
  142.0 7.9 %collective-permute-start.22 = (f32[256,256]{1,0:T(8,128)S(1)}, f32[256,256]{1,0:T(8,128)S(1)}, u32[]{:S(2)}, u32[]{:S(2)}) collective-permute-start(f32[256,256]{1,0:T(8,128)S(1)} %fusion.1.own), channel_id=1, source_target_pairs={{0,3},{1,0},{2,1},{3,2},{4,7},{5,4},{6,5},{7,6},{8,11},{9,8},{10,9... | collective-permute-start | bytes 786440 | tf_op jit(solution)/shard_map/ppermute | solution.py:24
  148.0 5.0 %collective-permute-start.24 = (f32[128,256]{1,0:T(8,128)S(1)}, f32[128,256]{1,0:T(8,128)S(1)}, u32[]{:S(2)}, u32[]{:S(2)}) collective-permute-start(f32[128,256]{1,0:T(8,128)S(1)} %slice.99), channel_id=1, source_target_pairs={{0,1},{1,2},{2,3},{3,0},{4,5},{5,6},{6,7},{7,4},{8,9},{9,10},{10,1... | collective-permute-start | bytes 393224 | tf_op jit(solution)/shard_map/ppermute | solution.py:24
  149.9 6.3 %collective-permute-start.25 = (f32[128,256]{1,0:T(8,128)S(1)}, f32[128,256]{1,0:T(8,128)S(1)}, u32[]{:S(2)}, u32[]{:S(2)}) collective-permute-start(f32[128,256]{1,0:T(8,128)S(1)} %slice.100), channel_id=1, source_target_pairs={{0,3},{1,0},{2,1},{3,2},{4,7},{5,4},{6,5},{7,6},{8,11},{9,8},{10,9... | collective-permute-start | bytes 393224 | tf_op jit(solution)/shard_map/ppermute | solution.py:24
  (7 other events, 92.3 us)
Sparse Core Ops, SparseCore 0:
  10.5 37.5 all-gather.1
  110.7 40.2 reduce-scatter.1

commit v7 on v6

--- a/solution.py
+++ b/solution.py
@@ -64,59 +64,45 @@
     )(blk, *sources)
 
 
-def fetch_table(t_hbm, t_all, sems):
-    step = pl.program_id(0)
-
-    @pl.when(step == 0)
-    def _():
-        for j in range(t_all.shape[0]):
-            pltpu.make_async_copy(t_hbm.at[j], t_all.at[j], sems.at[j]).start()
-
-    pltpu.make_async_copy(t_hbm.at[step], t_all.at[step], sems.at[step]).wait()
-    return t_all.at[step]
-
-
-def forward_kernel(p_ref, t_hbm, tgt_ref, stat_ref, s_ref, t_all, sems):
-    t_ref = fetch_table(t_hbm, t_all, sems)
-    q = p_ref[0]
-    items = t_ref.shape[0]
-    width = q.shape[0]
-    tgt = tgt_ref[0]
-    high = jnp.full((8, width), -jnp.inf, F32)
-    pick = jnp.zeros((8, width), F32)
-    for start in range(0, items, TILE):
-        s = lax.dot_general(t_ref[pl.ds(start, TILE), :], q, NT, preferred_element_type=F32)
-        s_ref[pl.ds(start, TILE), :] = s
-        high = jnp.maximum(high, jnp.max(s.reshape(TILE // 8, 8, width), axis=0))
-        hit = jnp.where(tile_ids(start, s.shape) == tgt, s, 0.0)
-        pick = pick + jnp.sum(hit.reshape(TILE // 8, 8, width), axis=0)
-    top = jnp.max(high, axis=0, keepdims=True)
-    mass = jnp.zeros((8, width), F32)
-    for start in range(0, items, TILE):
-        e = jnp.exp(s_ref[pl.ds(start, TILE), :] - top)
-        mass = mass + jnp.sum(e.reshape(TILE // 8, 8, width), axis=0)
-    stat_ref[0, 0:1, :] = top + jnp.log(jnp.sum(mass, axis=0, keepdims=True))
-    stat_ref[0, 1:2, :] = jnp.sum(pick, axis=0, keepdims=True)
-
-
-def forward(packed, targets, tables):
+def forward_kernel(p_ref, t_ref, tgt_ref, stat_ref, s_all):
+    for i in range(p_ref.shape[0]):
+        s_ref = s_all.at[i]
+        q = p_ref[i]
+        items = t_ref.shape[1]
+        width = q.shape[0]
+        tgt = tgt_ref[i]
+        high = jnp.full((8, width), -jnp.inf, F32)
+        pick = jnp.zeros((8, width), F32)
+        for start in range(0, items, TILE):
+            rows = t_ref[i, pl.ds(start, TILE), :]
+            s = lax.dot_general(rows, q, NT, preferred_element_type=F32)
+            s_ref[pl.ds(start, TILE), :] = s
+            high = jnp.maximum(high, jnp.max(s.reshape(TILE // 8, 8, width), axis=0))
+            hit = jnp.where(tile_ids(start, s.shape) == tgt, s, 0.0)
+            pick = pick + jnp.sum(hit.reshape(TILE // 8, 8, width), axis=0)
+        top = jnp.max(high, axis=0, keepdims=True)
+        mass = jnp.zeros((8, width), F32)
+        for start in range(0, items, TILE):
+            e = jnp.exp(s_ref[pl.ds(start, TILE), :] - top)
+            mass = mass + jnp.sum(e.reshape(TILE // 8, 8, width), axis=0)
+        stat_ref[0, i] = top + jnp.log(jnp.sum(mass, axis=0, keepdims=True))
+        stat_ref[1, i] = jnp.sum(pick, axis=0, keepdims=True)
+
+
+def forward(packed, targets, tables, per=2):
     planes, items, features = tables.shape
     width = packed.shape[1]
     return pl.pallas_call(
         forward_kernel,
-        grid=(planes,),
+        grid=(planes // per,),
         in_specs=[
-            pl.BlockSpec((1, width, features), lambda j: (j, 0, 0)),
-            pl.BlockSpec(memory_space=pl.ANY),
-            pl.BlockSpec((1, 1, width), lambda j: (j, 0, 0)),
+            pl.BlockSpec((per, width, features), lambda j: (j, 0, 0)),
+            pl.BlockSpec((per, items, features), lambda j: (j, 0, 0)),
+            pl.BlockSpec((per, 1, width), lambda j: (j, 0, 0)),
         ],
-        out_specs=pl.BlockSpec((1, 2, width), lambda j: (j, 0, 0)),
-        out_shape=jax.ShapeDtypeStruct((planes, 2, width), F32),
-        scratch_shapes=[
-            pltpu.VMEM((items, width), F32),
-            pltpu.VMEM(tables.shape, BF16),
-            pltpu.SemaphoreType.DMA((planes,)),
-        ],
+        out_specs=pl.BlockSpec((2, per, 1, width), lambda j: (0, j, 0, 0)),
+        out_shape=jax.ShapeDtypeStruct((2, planes, 1, width), F32),
+        scratch_shapes=[pltpu.VMEM((per, items, width), F32)],
         compiler_params=pltpu.CompilerParams(vmem_limit_bytes=LARGE),
         cost_estimate=pl.CostEstimate(
             flops=2 * planes * width * items * features,
@@ -127,38 +113,39 @@
     )(packed, tables, targets)
 
 
-def query_kernel(blk, p_ref, t_hbm, line_ref, g_ref, c_ref, acc_ref, t_all, sems):
+def query_kernel(blk, p_ref, t_ref, line_ref, g_ref, c_all, acc_ref):
     step = pl.program_id(0)
-    t_ref = fetch_table(t_hbm, t_all, sems)
-    sources, blocks, block_rows, _ = acc_ref.shape
+    sources, _, block_rows, _ = acc_ref.shape
+    per = p_ref.shape[0]
+    slots = sources * MOST
 
     @pl.when(step == 0)
     def _():
         acc_ref[...] = jnp.zeros_like(acc_ref)
 
-    q = p_ref[0]
-    lse = line_ref[0, 0:1, :]
-    tgt = line_ref[0, 1:2, :].astype(jnp.int32)
-    items = t_ref.shape[0]
-    for start in range(0, items, TILE):
-        s = lax.dot_general(t_ref[pl.ds(start, TILE), :], q, NT, preferred_element_type=F32)
-        e = jnp.exp(s - lse)
-        c = jnp.where(tile_ids(start, s.shape) == tgt, e - 1.0, e)
-        c_ref[pl.ds(start, TILE), :] = c.astype(BF16)
-    g = lax.dot_general(c_ref[...], t_ref[...], TN, preferred_element_type=F32)
-    slots = sources * MOST
-    for slot in range(slots):
-        b = blk[step * slots + slot]
-        acc_ref[slot // MOST, b] += g[slot * block_rows:(slot + 1) * block_rows, :]
+    for i in range(per):
+        q = p_ref[i]
+        lse = line_ref[i, 0:1, :]
+        tgt = line_ref[i, 1:2, :].astype(jnp.int32)
+        for start in range(0, t_ref.shape[1], TILE):
+            rows = t_ref[i, pl.ds(start, TILE), :]
+            s = lax.dot_general(rows, q, NT, preferred_element_type=F32)
+            e = jnp.exp(s - lse)
+            c = jnp.where(tile_ids(start, s.shape) == tgt, e - 1.0, e)
+            c_all[i, pl.ds(start, TILE), :] = c.astype(BF16)
+        g = lax.dot_general(c_all[i], t_ref[i], TN, preferred_element_type=F32)
+        for slot in range(slots):
+            b = blk[(step * per + i) * slots + slot]
+            acc_ref[slot // MOST, b] += g[slot * block_rows:(slot + 1) * block_rows, :]
 
     @pl.when(step == pl.num_programs(0) - 1)
     def _():
-        z = blk[pl.num_programs(0) * slots]
+        z = blk[pl.num_programs(0) * per * slots]
         for i in range(sources):
             g_ref[lax.rem(z + i, sources)] = acc_ref[i].astype(BF16)
 
 
-def query_parts(packed, blk, lines, tables, sources, blocks, block_rows):
+def query_parts(packed, blk, lines, tables, sources, blocks, block_rows, per=4):
     planes, items, features = tables.shape
     width = packed.shape[1]
     out = jax.ShapeDtypeStruct((sources, blocks, block_rows, features), BF16)
@@ -166,19 +153,14 @@
         query_kernel,
         grid_spec=pltpu.PrefetchScalarGridSpec(
             num_scalar_prefetch=1,
-            grid=(planes,),
+            grid=(planes // per,),
             in_specs=[
-                pl.BlockSpec((1, width, features), lambda j, blk: (j, 0, 0)),
-                pl.BlockSpec(memory_space=pl.ANY),
-                pl.BlockSpec((1, 2, width), lambda j, blk: (j, 0, 0)),
+                pl.BlockSpec((per, width, features), lambda j, blk: (j, 0, 0)),
+                pl.BlockSpec((per, items, features), lambda j, blk: (j, 0, 0)),
+                pl.BlockSpec((per, 2, width), lambda j, blk: (j, 0, 0)),
             ],
             out_specs=pl.BlockSpec(out.shape, lambda j, blk: (0, 0, 0, 0)),
-            scratch_shapes=[
-                pltpu.VMEM((items, width), BF16),
-                pltpu.VMEM(out.shape, F32),
-                pltpu.VMEM(tables.shape, BF16),
-                pltpu.SemaphoreType.DMA((planes,)),
-            ],
+            scratch_shapes=[pltpu.VMEM((per, items, width), BF16), pltpu.VMEM(out.shape, F32)],
         ),
         out_shape=out,
         compiler_params=pltpu.CompilerParams(vmem_limit_bytes=LARGE),
@@ -192,26 +174,26 @@
 
 
 def item_kernel(where, q_ref, line_ref, t_ref, *outs):
-    start = where[pl.program_id(0)] * t_ref.shape[0]
+    start = where[pl.program_id(0)] * t_ref.shape[1]
     total = None
     for source in range(q_ref.shape[0]):
         q = q_ref[source]
         line = line_ref[source]
         lse = line[0:1, :]
         tgt = line[1:2, :].astype(jnp.int32)
-        s = lax.dot_general(t_ref[...], q, NT, preferred_element_type=F32)
+        s = lax.dot_general(t_ref[0], q, NT, preferred_element_type=F32)
         e = jnp.exp(s - lse)
         c = jnp.where(tile_ids(start, s.shape) == tgt, e - 1.0, e).astype(BF16)
         part = jnp.dot(c, q, preferred_element_type=F32)
         total = part if total is None else total + part
-    cut = t_ref.shape[0] // len(outs)
+    cut = t_ref.shape[1] // len(outs)
     for n, out in enumerate(outs):
         out[0] = total[n * cut:(n + 1) * cut]
 
 
-def item_parts(places, pieces, x, rows, lines, table16, quarters):
+def item_parts(places, pieces, x, mine, rows, lines, tables, quarters):
     count, width, features = rows.shape
-    span = table16.shape[0] // quarters
+    span = tables.shape[1] // quarters
     share = len(places)
     out = jax.ShapeDtypeStruct((share, span // pieces, features), F32)
     return pl.pallas_call(
@@ -222,7 +204,7 @@
             in_specs=[
                 pl.BlockSpec(rows.shape, lambda i, o: (0, 0, 0)),
                 pl.BlockSpec(lines.shape, lambda i, o: (0, 0, 0)),
-                pl.BlockSpec((span, features), lambda i, o: (o[i], 0)),
+                pl.BlockSpec((1, span, features), lambda i, o: (o[share], o[i], 0)),
             ],
             out_specs=[pl.BlockSpec((1,) + out.shape[1:], lambda i, o: (i, 0, 0))] * pieces,
         ),
@@ -234,13 +216,14 @@
             transcendentals=share * span * count * width,
         ),
         name="item_parts",
-    )((jnp.array(places, jnp.int32) + x) % quarters, rows, lines, table16)
-
-
-def update_kernel(x_ref, own, after, before, far_a, far_b, t_ref, a_ref, nt_ref, na_ref):
+    )(jnp.concatenate([(jnp.array(places, jnp.int32) + x) % quarters, mine]), rows, lines, tables)
+
+
+def update_kernel(x_ref, own, after, before, far_a, far_b, g_ref, t_ref, a_ref, ng_ref, nt_ref, na_ref):
     quarters = pl.num_programs(0)
     rel = lax.rem(pl.program_id(0) - x_ref[0] + quarters, quarters)
     cut = far_a.shape[0]
+    ng_ref[...] = g_ref[...].astype(F32)
 
     def write(start, summed):
         span = pl.ds(start, summed.shape[0])
@@ -260,23 +243,25 @@
         write(cut, far_b[...])
 
 
-def update(x, own, after, before, far_a, far_b, table, accum, quarters):
+def update(x, own, after, before, far_a, far_b, grads, table, accum, quarters):
     items, features = table.shape
     whole = pl.BlockSpec(own.shape, lambda i, x: (0, 0))
     part = pl.BlockSpec(far_a.shape, lambda i, x: (0, 0))
     block = pl.BlockSpec((items // quarters, features), lambda i, x: (i, 0))
+    piece = pl.BlockSpec((grads.shape[0] // quarters, features), lambda i, x: (i, 0))
     return pl.pallas_call(
         update_kernel,
         grid_spec=pltpu.PrefetchScalarGridSpec(
             num_scalar_prefetch=1,
             grid=(quarters,),
-            in_specs=[whole] * 3 + [part] * 2 + [block] * 2,
-            out_specs=[block] * 2,
-        ),
-        out_shape=[jax.ShapeDtypeStruct(table.shape, F32)] * 2,
+            in_specs=[whole] * 3 + [part] * 2 + [piece] + [block] * 2,
+            out_specs=[piece] + [block] * 2,
+        ),
+        out_shape=[jax.ShapeDtypeStruct(grads.shape, F32)]
+        + [jax.ShapeDtypeStruct(table.shape, F32)] * 2,
         compiler_params=pltpu.CompilerParams(vmem_limit_bytes=SMALL),
         name="update",
-    )(x, own, after, before, far_a, far_b, table, accum)
+    )(x, own, after, before, far_a, far_b, grads, table, accum)
 
 
 def local(queries, clusters, positives, owner_of, table, accum):
@@ -292,8 +277,8 @@
     plane = owners // z_size
     pair_count = block_count * picks
 
-    table16 = table[0].astype(BF16)
-    tables = lax.all_gather(table16, PLANE)
+    tables = lax.all_gather(table[0].astype(BF16), PLANE)
+    mine = (lax.axis_index("y") * lax.axis_size("c") + lax.axis_index("c")).reshape(1)
 
     here = queries.reshape(2, block_count // 2, block_rows, features)
     by_source = [[None] * 2 for _ in range(z_size)]
@@ -333,6 +318,7 @@
         ],
         axis=1,
     )
+    meta, _ = lax.optimization_barrier((meta, by_source[5][0]))
     got = lax.all_to_all(meta, "z", 0, 0, tiled=True)
     order = jnp.arange(z_size, dtype=jnp.int32)
     got = got[(z + order) % z_size]
@@ -349,16 +335,18 @@
     pair_from = (pair_owner // plane - z) % z_size
     pair_place = (order[:, None] - pair_from) % z_size
     pair_row = (pair_from % 2 * 4 + pair_from // 2) * plane + pair_owner % plane
-    pair_row = (pair_row * 2 * z_size + pair_place) * MOST + pair_slot % MOST
+    pair_row = (pair_row * z_size + pair_place) * MOST + pair_slot % MOST
 
     packed = pack([part for pair in by_source for part in pair], blk, plane)
     rows = lax.all_to_all(packed, PLANE, 0, 0, tiled=True)
     stats = forward(packed, targets, tables)
 
     even = jnp.stack([stats] + [shift(stats, "z", -e) for e in (2, 4, 6)])
-    all_stats = jnp.stack([even, shift(even, "z", -1)]).reshape(-1, block_rows)
-    part = all_stats[pair_row.reshape(-1)].reshape(z_size, block_count, picks, block_rows)
-    pick = all_stats[pair_row[0] + z_size * MOST].reshape(block_count, picks, block_rows)
+    all_stats = jnp.stack([even, shift(even, "z", -1)]).reshape(z_size, 2, -1)
+    part = all_stats[:, 0].reshape(-1, block_rows)[pair_row.reshape(-1)]
+    part = part.reshape(z_size, block_count, picks, block_rows)
+    pick = all_stats[:, 1].reshape(-1, block_rows)[pair_row[0]]
+    pick = pick.reshape(block_count, picks, block_rows)
     top = jnp.max(part, axis=2)
     lse = top + jnp.log(jnp.sum(jnp.exp(part - top[:, :, None]), axis=2))
     losses = (lse[0] - jnp.sum(pick, axis=1)).reshape(local_rows)
@@ -374,12 +362,12 @@
         packed, jnp.concatenate([blk, z.reshape(1)]), lines, tables, z_size, block_count, block_rows
     )
     grads, lines, rows = lax.optimization_barrier((grads, lines, rows))
-    query_grads = lax.psum_scatter(grads, "z").astype(F32).reshape(local_rows, features)
+    grads = lax.psum_scatter(grads, "z").reshape(local_rows, features)
     got_lines = lax.all_to_all(lines, PLANE, 0, 0, tiled=True)
 
-    far_a, far_b = item_parts((2,), 2, x, rows, got_lines, table16, x_size)
+    far_a, far_b = item_parts((2,), 2, x, mine, rows, got_lines, tables, x_size)
     far_a, far_b, got_lines = lax.optimization_barrier((far_a, far_b, got_lines))
-    (rest,) = item_parts((0, 1, 3), 1, x, rows, got_lines, table16, x_size)
+    (rest,) = item_parts((0, 1, 3), 1, x, mine, rows, got_lines, tables, x_size)
     far_a, far_b = far_a[0], far_b[0]
     own, after, before = rest[0], rest[1], rest[2]
     half = far_a.shape[0]
@@ -392,8 +380,8 @@
     after = shift(own, "x", -1)
     far_a = shift(before[:half], "x", 1)
     far_b = shift(after[half:], "x", -1)
-    new_table, new_accum = update(
-        x, own, after, before, far_a, far_b, table[0], accum[0], x_size
+    query_grads, new_table, new_accum = update(
+        x, own, after, before, far_a, far_b, grads, table[0], accum[0], x_size
     )
     return (losses, query_grads, new_table[None], new_accum[None])
 

time: 168 us -> 171 us (1.018)
  local copies, waits for them, and re-layouts: 11.5 us -> 21.7 us
  Pallas kernels: 33.6 us -> 28.5 us
    all_to_all x1, waiting for transfers between devices: 0.01 us -> 12.7 us  [local(): rows = lax.all_to_all(packed, PLANE, 0, 0, tiled=True)]
    unnamed x18 -> x48, local copies, waits for them, and re-layouts: 0.13 us -> 12.6 us
    ppermute x26, waiting for transfers between devices: 36.3 us -> 28.3 us  [shift(): lax.ppermute(value, axis, [(i, (i + step) % size) for i in range(size)])]
    all_to_all x1, waiting for transfers between devices: 7.76 us -> 2.19 us  [local(): got = lax.all_to_all(meta, 'z', 0, 0, tiled=True)]
    pallas_call x1, Pallas kernels: 12.5 us -> 9.94 us  [query_parts(): pl.pallas_call(query_kernel, grid_spec=pltpu.PrefetchScalarGridSpec(num_s...]
    ppermute x26, starting transfers between devices: 31.8 us -> 34.4 us  [shift(): lax.ppermute(value, axis, [(i, (i + step) % size) for i in range(size)])]
    gather x2, local copies, waits for them, and re-layouts: 4.08 us -> 1.63 us  [the longest x1 1.04 us: local(): part = all_stats[:, 0].reshape(-1, block_rows)[pair_row.reshape(-1)]]
    convert_element_type x2 -> x1, other arithmetic: 4.29 us -> 2.11 us  [local(): tables = lax.all_gather(table[0].astype(BF16), PLANE)]
  transfers between devices with their start and end apart: 31 -> 31, of which waited for: 17 -> 14; matrix products, arithmetic and copies ran while one was open for 11% -> 10% of each run, Pallas kernels for 20% -> 11%
where the time goes in v7:
time: 171 us
  waiting for transfers between devices  48.3 us (28%)
  starting transfers between devices  48 us (28%)
  Pallas kernels  28.5 us (17%)
  local copies, waits for them, and re-layouts  21.7 us (13%)
  between operations  14.6 us (9%)
  other arithmetic  9.61 us (6%)
    ppermute x26, starting transfers between devices, shift(): lax.ppermute(value, axis, [(i, (i + step) % size) for i in range(size)])  34.4 us
    ppermute x26, waiting for transfers between devices, shift(): lax.ppermute(value, axis, [(i, (i + step) % size) for i in range(size)])  28.3 us
    all_to_all x1, waiting for transfers between devices, local(): rows = lax.all_to_all(packed, PLANE, 0, 0, tiled=True)  12.7 us
    unnamed x48, local copies, waits for them, and re-layouts  12.6 us
    pallas_call x1, Pallas kernels, query_parts(): pl.pallas_call(query_kernel, grid_spec=pltpu.PrefetchScalarGridSpec(num_s...  9.94 us
    pallas_call x1, Pallas kernels, forward(): pl.pallas_call(forward_kernel, grid=(planes // per,), in_specs=[pl.BlockS...  8.21 us
    pallas_call x2, Pallas kernels, item_parts(): pl.pallas_call(item_kernel, grid_spec=pltpu.PrefetchScalarGridSpec(num_sc...  7.33 us
    all_to_all x1, starting transfers between devices, local(): got = lax.all_to_all(meta, 'z', 0, 0, tiled=True)  5.48 us
  transfers between devices with their start and end apart: 31, of which 14 were waited for; matrix products, arithmetic and copies ran while one was open for 10% of the time, Pallas kernels for 11%

profile of v7, /device:TPU:6, one launch (start us, length us, event | category | flops | bytes accessed | tf_op | source)
XLA Modules:
  0.0 170.9 jit_solution(4218601417452012860)
XLA Ops:
  7.3 2.1 %convert_element_type.19 = bf16[1,1024,256]{2,1,0:T(8,128)(2,1)} convert(f32[1,1024,256]{2,1,0:T(8,128)} %param.12) | non-fusion elementwise | flops 262144 | bytes 1572864 | tf_op jit(solution)/shard_map/convert_element_type | solution.py:280
  9.4 2.0 %collective-permute-start = (bf16[8,32,256]{2,1,0:T(8,128)(2,1)S(1)}, bf16[8,32,256]{2,1,0:T(8,128)(2,1)S(1)}, u32[]{:S(2)}, u32[]{:S(2)}) collective-permute-start(bf16[8,32,256]{2,1,0:T(8,128)(2,1)S(1)} %bitcast.89), channel_id=1, source_target_pairs={{0,32},{32,64},{64,96},{96,128},{128,160},{160,192},{192,224},{224... | collective-permute-start | bytes 393224 | tf_op jit(solution)/shard_map/ppermute | solution.py:24
  11.4 4.0 %collective-permute-start.3 = (bf16[8,32,256]{2,1,0:T(8,128)(2,1)S(1)}, bf16[8,32,256]{2,1,0:T(8,128)(2,1)S(1)}, u32[]{:S(2)}, u32[]{:S(2)}) collective-permute-start(bf16[8,32,256]{2,1,0:T(8,128)(2,1)S(1)} %bitcast.90), channel_id=1, source_target_pairs={{0,224},{32,0},{64,32},{96,64},{128,96},{160,128},{192,160},{224,1... | collective-permute-start | bytes 393224 | tf_op jit(solution)/shard_map/ppermute | solution.py:24
  15.4 3.2 %collective-permute-start.4 = (bf16[8,32,256]{2,1,0:T(8,128)(2,1)S(1)}, bf16[8,32,256]{2,1,0:T(8,128)(2,1)S(1)}, u32[]{:S(2)}, u32[]{:S(2)}) collective-permute-start(bf16[8,32,256]{2,1,0:T(8,128)(2,1)S(1)} %bitcast.87), channel_id=1, source_target_pairs={{0,224},{32,0},{64,32},{96,64},{128,96},{160,128},{192,160},{224,1... | collective-permute-start | bytes 393224 | tf_op jit(solution)/shard_map/ppermute | solution.py:24
  21.7 6.5 %collective-permute-done.1.refs_12_ = bf16[8,32,256]{2,1,0:T(8,128)(2,1)S(1)} collective-permute-done((bf16[8,32,256]{2,1,0:T(8,128)(2,1)S(1)}, bf16[8,32,256]{2,1,0:T(8,128)(2,1)S(1)}, u32[]{:S(2)}, u32[]{:S(2)}) %collective-permute-start.1) | collective-permute-done | bytes 131104 | tf_op jit(solution)/shard_map/ppermute | solution.py:24
  28.2 3.3 %collective-permute-start.5 = (bf16[8,32,256]{2,1,0:T(8,128)(2,1)S(1)}, bf16[8,32,256]{2,1,0:T(8,128)(2,1)S(1)}, u32[]{:S(2)}, u32[]{:S(2)}) collective-permute-start(bf16[8,32,256]{2,1,0:T(8,128)(2,1)S(1)} %collective-permute-done.3.refs_2_), channel_id=1, source_target_pairs={{0,224},{32,0},{64,32},{96,64},{128,96},{160,128},{192,160},{224,1... | collective-permute-start | bytes 393224 | tf_op jit(solution)/shard_map/ppermute | solution.py:24
  31.7 1.9 %collective-permute-start.12 = (bf16[8,32,256]{2,1,0:T(8,128)(2,1)S(1)}, bf16[8,32,256]{2,1,0:T(8,128)(2,1)S(1)}, u32[]{:S(2)}, u32[]{:S(2)}) collective-permute-start(bf16[8,32,256]{2,1,0:T(8,128)(2,1)S(1)} %collective-permute-done.11.refs_13_), channel_id=1, source_target_pairs={{0,32},{32,64},{64,96},{96,128},{128,160},{160,192},{192,224},{224... | collective-permute-start | bytes 393224 | tf_op jit(solution)/shard_map/ppermute | solution.py:24
  35.4 5.5 %all-to-all-start = ((s32[8,1,592]{2,1,0:T(1,128)}), s32[8,1,592]{2,1,0:T(1,128)S(1)}, u32[]{:S(2)}, u32[]{:S(2)}) async-start(s32[8,1,592]{2,1,0:T(1,128)} %copy.46), calls=%async_computation | async-start | bytes 40960 | tf_op jit(solution)/shard_map/all_to_all | solution.py:322
  40.9 3.3 %collective-permute-start.7 = (bf16[8,32,256]{2,1,0:T(8,128)(2,1)S(1)}, bf16[8,32,256]{2,1,0:T(8,128)(2,1)S(1)}, u32[]{:S(2)}, u32[]{:S(2)}) collective-permute-start(bf16[8,32,256]{2,1,0:T(8,128)(2,1)S(1)} %collective-permute-done.5.refs_4_), channel_id=1, source_target_pairs={{0,224},{32,0},{64,32},{96,64},{128,96},{160,128},{192,160},{224,1... | collective-permute-start | bytes 393224 | tf_op jit(solution)/shard_map/ppermute | solution.py:24
  44.2 1.5 collective-permute-start.8
  46.5 2.2 %all-to-all-done = s32[8,1,592]{2,1,0:T(1,128)S(1)} async-done(((s32[8,1,592]{2,1,0:T(1,128)}), s32[8,1,592]{2,1,0:T(1,128)S(1)}, u32[]{:S(2)}, u32[]{:S(2)}) %all-to-all-start) | async-done | bytes 18976 | tf_op jit(solution)/shard_map/all_to_all | solution.py:322
  60.7 8.2 %forward.1 = f32[2,8,1,512]{3,2,1,0:T(1,128)} custom-call(bf16[8,512,256]{2,1,0:T(8,128)(2,1)} %copy-done, bf16[8,1024,256]{2,1,0:T(8,128)(2,1)} %all-gather.2.cloned.1.call-done.t_ref, s32[8,1,512]{2,1,0:T(1,128)} %reshape.366.tgt_ref), custom_call_target="tpu_custom_call" | custom-call | flops 2147483648 | bytes 6291456 | tf_op jit(solution)/shard_map/forward/pallas_call | solution.py:95
  70.3 2.6 %collective-permute-start.15 = (f32[2,8,1,512]{3,2,1,0:T(1,128)}, f32[2,8,1,512]{3,2,1,0:T(1,128)S(1)}, u32[]{:S(2)}, u32[]{:S(2)}) collective-permute-start(f32[2,8,1,512]{3,2,1,0:T(1,128)} %forward.1), channel_id=1, source_target_pairs={{0,128},{32,160},{64,192},{96,224},{128,0},{160,32},{192,64},{224,... | collective-permute-start | bytes 98312 | tf_op jit(solution)/shard_map/ppermute | solution.py:24
  74.3 4.1 %collective-permute-done.15 = f32[2,8,1,512]{3,2,1,0:T(1,128)S(1)} collective-permute-done((f32[2,8,1,512]{3,2,1,0:T(1,128)}, f32[2,8,1,512]{3,2,1,0:T(1,128)S(1)}, u32[]{:S(2)}, u32[]{:S(2)}) %collective-permute-start.15) | collective-permute-done | bytes 32800 | tf_op jit(solution)/shard_map/ppermute | solution.py:24
  81.5 4.5 %all-to-all-start.1 = ((bf16[8,512,256]{2,1,0:T(8,128)(2,1)}), bf16[8,512,256]{2,1,0:T(8,128)(2,1)S(1)}, u32[]{:S(2)}, u32[]{:S(2)}) async-start(bf16[8,512,256]{2,1,0:T(8,128)(2,1)} %copy-done), calls=%async_computation.1 | async-start | bytes 4194304 | tf_op jit(solution)/shard_map/all_to_all | solution.py:341
  90.5 9.9 %query_parts.1 = bf16[8,16,32,256]{3,2,1,0:T(8,128)(2,1)} custom-call(s32[129]{0:T(256)} %pad_add_fusion.blk, bf16[8,512,256]{2,1,0:T(8,128)(2,1)} %copy-done, bf16[8,1024,256]{2,1,0:T(8,128)(2,1)} %all-gather.2.cloned.1.call-done.t_ref, f32[8,2,512]{2,1,0:T(2,128)} %pad_maximum_fusion.3.line_ref), custom_call_target="tpu_custom_call" | custom-call | flops 4294967296 | bytes 8388608 | tf_op jit(solution)/shard_map/query_parts/pallas_call | solution.py:152
  100.5 12.7 %all-to-all-done.1.q_ref = bf16[8,512,256]{2,1,0:T(8,128)(2,1)S(1)} async-done(((bf16[8,512,256]{2,1,0:T(8,128)(2,1)}), bf16[8,512,256]{2,1,0:T(8,128)(2,1)S(1)}, u32[]{:S(2)}, u32[]{:S(2)}) %all-to-all-start.1) | async-done | bytes 2097184 | tf_op jit(solution)/shard_map/all_to_all | solution.py:341
  113.3 3.6 %all-to-all-start.2 = ((f32[8,2,512]{2,1,0:T(2,128)}), f32[8,2,512]{2,1,0:T(2,128)S(1)}, u32[]{:S(2)}, u32[]{:S(2)}) async-start(f32[8,2,512]{2,1,0:T(2,128)} %pad_maximum_fusion.3.line_ref), calls=%async_computation.2 | async-start | bytes 65536 | tf_op jit(solution)/shard_map/all_to_all | solution.py:366
  117.0 5.1 %all-to-all-done.2.line_ref = f32[8,2,512]{2,1,0:T(2,128)S(1)} async-done(((f32[8,2,512]{2,1,0:T(2,128)}), f32[8,2,512]{2,1,0:T(2,128)S(1)}, u32[]{:S(2)}, u32[]{:S(2)}) %all-to-all-start.2) | async-done | bytes 32800 | tf_op jit(solution)/shard_map/all_to_all | solution.py:366
  122.1 2.2 %copy-done.1 = bf16[8,1024,256]{2,1,0:T(8,128)(2,1)S(1)} copy-done((bf16[8,1024,256]{2,1,0:T(8,128)(2,1)S(1)}, bf16[8,1024,256]{2,1,0:T(8,128)(2,1)}, u32[]{:S(2)}) %copy-start.1) | copy-done | bytes 4194328
  124.3 2.1 %item_parts.2 = (f32[1,128,256]{2,1,0:T(8,128)S(1)}, f32[1,128,256]{2,1,0:T(8,128)S(1)}) custom-call(s32[2]{0:T(128)S(1)} %pad_add_fusion.2.where, bf16[8,512,256]{2,1,0:T(8,128)(2,1)S(1)} %all-to-all-done.1.q_ref, f32[8,2,512]{2,1,0:T(2,128)S(1)} %all-to-all-done.2.line_ref, bf16[8,1024,256]{2,1,0:T(8,128)(2,1)S(1)} %copy-done.1), custom_call_target="tpu_custom_call" | custom-call | flops 1073741824 | bytes 2490368 | tf_op jit(solution)/shard_map/item_parts/pallas_call | solution.py:199
  126.9 1.5 collective-permute-start.20
  128.5 5.2 %item_parts.3 = f32[3,256,256]{2,1,0:T(8,128)S(1)} custom-call(s32[4]{0:T(128)S(1)} %pad_add_fusion.1.where, bf16[8,512,256]{2,1,0:T(8,128)(2,1)S(1)} %all-to-all-done.1.q_ref, f32[8,2,512]{2,1,0:T(2,128)S(1)} %all-to-all-done.2.line_ref, bf16[8,1024,256]{2,1,0:T(8,128)(2,1)S(1)} %copy-done.1), custom_call_target="tpu_custom_call" | custom-call | flops 3221225472 | bytes 3276800 | tf_op jit(solution)/shard_map/item_parts/pallas_call | solution.py:199
  134.6 1.7 collective-permute-start.19
  140.5 1.8 %collective-permute-done.19 = f32[256,256]{1,0:T(8,128)} collective-permute-done((f32[256,256]{1,0:T(8,128)}, f32[256,256]{1,0:T(8,128)}, u32[]{:S(2)}, u32[]{:S(2)}) %collective-permute-start.19) | collective-permute-done | bytes 262176 | tf_op jit(solution)/shard_map/ppermute | solution.py:24
  142.3 3.3 %collective-permute-done.21 = f32[256,256]{1,0:T(8,128)} collective-permute-done((f32[256,256]{1,0:T(8,128)}, f32[256,256]{1,0:T(8,128)}, u32[]{:S(2)}, u32[]{:S(2)}) %collective-permute-start.21) | collective-permute-done | bytes 262176 | tf_op jit(solution)/shard_map/ppermute | solution.py:24
  146.8 2.0 %collective-permute-start.22 = (f32[256,256]{1,0:T(8,128)S(1)}, f32[256,256]{1,0:T(8,128)S(1)}, u32[]{:S(2)}, u32[]{:S(2)}) collective-permute-start(f32[256,256]{1,0:T(8,128)S(1)} %fusion.1.own), channel_id=1, source_target_pairs={{0,3},{1,0},{2,1},{3,2},{4,7},{5,4},{6,5},{7,6},{8,11},{9,8},{10,9... | collective-permute-start | bytes 786440 | tf_op jit(solution)/shard_map/ppermute | solution.py:24
  148.8 4.3 %collective-permute-done.23.before = f32[256,256]{1,0:T(8,128)S(1)} collective-permute-done((f32[256,256]{1,0:T(8,128)S(1)}, f32[256,256]{1,0:T(8,128)S(1)}, u32[]{:S(2)}, u32[]{:S(2)}) %collective-permute-start.23) | collective-permute-done | bytes 262176 | tf_op jit(solution)/shard_map/ppermute | solution.py:24
  153.2 1.4 collective-permute-start.24
  155.5 2.8 %collective-permute-done.24.far_a = f32[128,256]{1,0:T(8,128)S(1)} collective-permute-done((f32[128,256]{1,0:T(8,128)S(1)}, f32[128,256]{1,0:T(8,128)S(1)}, u32[]{:S(2)}, u32[]{:S(2)}) %collective-permute-start.24) | collective-permute-done | bytes 131104 | tf_op jit(solution)/shard_map/ppermute | solution.py:24
  158.2 2.6 %collective-permute-done.25.far_b = f32[128,256]{1,0:T(8,128)S(1)} collective-permute-done((f32[128,256]{1,0:T(8,128)S(1)}, f32[128,256]{1,0:T(8,128)S(1)}, u32[]{:S(2)}, u32[]{:S(2)}) %collective-permute-start.25) | collective-permute-done | bytes 131104 | tf_op jit(solution)/shard_map/ppermute | solution.py:24
  161.8 2.2 %update.1 = (f32[512,256]{1,0:T(8,128)}, f32[1024,256]{1,0:T(8,128)}, f32[1024,256]{1,0:T(8,128)}) custom-call(s32[1]{0:T(128)} %bitcast.23.x_ref, f32[256,256]{1,0:T(8,128)S(1)} %fusion.1.own, f32[256,256]{1,0:T(8,128)S(1)} %collective-permute-done.22.after, f32[256,256]{1,0:T(8,128)S(1)} %collective-permute-done.23.before, ...), custom_call_target="tpu_custom_call" | custom-call | tf_op jit(solution)/shard_map/update/pallas_call | solution.py:252
  (176 shorter events, 36.8 us)
Async XLA Ops:
  7.2 53.5 %all-gather.2.cloned.1.call-start = ((), (), s32[]{:S(2)}) async-start(), calls=%async_computation.4 | async-start | bytes 4718592 | tf_op jit(solution)/shard_map/all_gather | solution.py:280
  9.4 11.7 %collective-permute-start = (bf16[8,32,256]{2,1,0:T(8,128)(2,1)S(1)}, bf16[8,32,256]{2,1,0:T(8,128)(2,1)S(1)}, u32[]{:S(2)}, u32[]{:S(2)}) collective-permute-start(bf16[8,32,256]{2,1,0:T(8,128)(2,1)S(1)} %bitcast.89), channel_id=1, source_target_pairs={{0,32},{32,64},{64,96},{96,128},{128,160},{160,192},{192,224},{224... | collective-permute-start | bytes 393224 | tf_op jit(solution)/shard_map/ppermute | solution.py:24
  11.4 16.8 %collective-permute-start.3 = (bf16[8,32,256]{2,1,0:T(8,128)(2,1)S(1)}, bf16[8,32,256]{2,1,0:T(8,128)(2,1)S(1)}, u32[]{:S(2)}, u32[]{:S(2)}) collective-permute-start(bf16[8,32,256]{2,1,0:T(8,128)(2,1)S(1)} %bitcast.90), channel_id=1, source_target_pairs={{0,224},{32,0},{64,32},{96,64},{128,96},{160,128},{192,160},{224,1... | collective-permute-start | bytes 393224 | tf_op jit(solution)/shard_map/ppermute | solution.py:24
  15.4 6.2 %collective-permute-start.10 = (bf16[8,32,256]{2,1,0:T(8,128)(2,1)S(1)}, bf16[8,32,256]{2,1,0:T(8,128)(2,1)S(1)}, u32[]{:S(2)}, u32[]{:S(2)}) collective-permute-start(bf16[8,32,256]{2,1,0:T(8,128)(2,1)S(1)} %bitcast.86), channel_id=1, source_target_pairs={{0,32},{32,64},{64,96},{96,128},{128,160},{160,192},{192,224},{224... | collective-permute-start | bytes 393224 | tf_op jit(solution)/shard_map/ppermute | solution.py:24
  15.4 16.1 %collective-permute-start.4 = (bf16[8,32,256]{2,1,0:T(8,128)(2,1)S(1)}, bf16[8,32,256]{2,1,0:T(8,128)(2,1)S(1)}, u32[]{:S(2)}, u32[]{:S(2)}) collective-permute-start(bf16[8,32,256]{2,1,0:T(8,128)(2,1)S(1)} %bitcast.87), channel_id=1, source_target_pairs={{0,224},{32,0},{64,32},{96,64},{128,96},{160,128},{192,160},{224,1... | collective-permute-start | bytes 393224 | tf_op jit(solution)/shard_map/ppermute | solution.py:24
  21.1 7.1 %collective-permute-start.1 = (bf16[8,32,256]{2,1,0:T(8,128)(2,1)S(1)}, bf16[8,32,256]{2,1,0:T(8,128)(2,1)S(1)}, u32[]{:S(2)}, u32[]{:S(2)}) collective-permute-start(bf16[8,32,256]{2,1,0:T(8,128)(2,1)S(1)} %collective-permute-done.refs_14_), channel_id=1, source_target_pairs={{0,32},{32,64},{64,96},{96,128},{128,160},{160,192},{192,224},{224... | collective-permute-start | bytes 393224 | tf_op jit(solution)/shard_map/ppermute | solution.py:24
  21.7 10.0 %collective-permute-start.11 = (bf16[8,32,256]{2,1,0:T(8,128)(2,1)S(1)}, bf16[8,32,256]{2,1,0:T(8,128)(2,1)S(1)}, u32[]{:S(2)}, u32[]{:S(2)}) collective-permute-start(bf16[8,32,256]{2,1,0:T(8,128)(2,1)S(1)} %collective-permute-done.10.refs_15_), channel_id=1, source_target_pairs={{0,32},{32,64},{64,96},{96,128},{128,160},{160,192},{192,224},{224... | collective-permute-start | bytes 393224 | tf_op jit(solution)/shard_map/ppermute | solution.py:24
  28.2 6.5 %collective-permute-start.2 = (bf16[8,32,256]{2,1,0:T(8,128)(2,1)S(1)}, bf16[8,32,256]{2,1,0:T(8,128)(2,1)S(1)}, u32[]{:S(2)}, u32[]{:S(2)}) collective-permute-start(bf16[8,32,256]{2,1,0:T(8,128)(2,1)S(1)} %collective-permute-done.1.refs_12_), channel_id=1, source_target_pairs={{0,32},{32,64},{64,96},{96,128},{128,160},{160,192},{192,224},{224... | collective-permute-start | bytes 393224 | tf_op jit(solution)/shard_map/ppermute | solution.py:24
  28.2 12.6 %collective-permute-start.5 = (bf16[8,32,256]{2,1,0:T(8,128)(2,1)S(1)}, bf16[8,32,256]{2,1,0:T(8,128)(2,1)S(1)}, u32[]{:S(2)}, u32[]{:S(2)}) collective-permute-start(bf16[8,32,256]{2,1,0:T(8,128)(2,1)S(1)} %collective-permute-done.3.refs_2_), channel_id=1, source_target_pairs={{0,224},{32,0},{64,32},{96,64},{128,96},{160,128},{192,160},{224,1... | collective-permute-start | bytes 393224 | tf_op jit(solution)/shard_map/ppermute | solution.py:24
  31.6 12.6 %collective-permute-start.6 = (bf16[8,32,256]{2,1,0:T(8,128)(2,1)S(1)}, bf16[8,32,256]{2,1,0:T(8,128)(2,1)S(1)}, u32[]{:S(2)}, u32[]{:S(2)}) collective-permute-start(bf16[8,32,256]{2,1,0:T(8,128)(2,1)S(1)} %collective-permute-done.4.refs_3_), channel_id=1, source_target_pairs={{0,224},{32,0},{64,32},{96,64},{128,96},{160,128},{192,160},{224,1... | collective-permute-start | bytes 393224 | tf_op jit(solution)/shard_map/ppermute | solution.py:24
  31.7 14.5 %collective-permute-start.12 = (bf16[8,32,256]{2,1,0:T(8,128)(2,1)S(1)}, bf16[8,32,256]{2,1,0:T(8,128)(2,1)S(1)}, u32[]{:S(2)}, u32[]{:S(2)}) collective-permute-start(bf16[8,32,256]{2,1,0:T(8,128)(2,1)S(1)} %collective-permute-done.11.refs_13_), channel_id=1, source_target_pairs={{0,32},{32,64},{64,96},{96,128},{128,160},{160,192},{192,224},{224... | collective-permute-start | bytes 393224 | tf_op jit(solution)/shard_map/ppermute | solution.py:24
  35.4 13.3 %all-to-all-start = ((s32[8,1,592]{2,1,0:T(1,128)}), s32[8,1,592]{2,1,0:T(1,128)S(1)}, u32[]{:S(2)}, u32[]{:S(2)}) async-start(s32[8,1,592]{2,1,0:T(1,128)} %copy.46), calls=%async_computation | async-start | bytes 40960 | tf_op jit(solution)/shard_map/all_to_all | solution.py:322
  40.9 10.1 %collective-permute-start.7 = (bf16[8,32,256]{2,1,0:T(8,128)(2,1)S(1)}, bf16[8,32,256]{2,1,0:T(8,128)(2,1)S(1)}, u32[]{:S(2)}, u32[]{:S(2)}) collective-permute-start(bf16[8,32,256]{2,1,0:T(8,128)(2,1)S(1)} %collective-permute-done.5.refs_4_), channel_id=1, source_target_pairs={{0,224},{32,0},{64,32},{96,64},{128,96},{160,128},{192,160},{224,1... | collective-permute-start | bytes 393224 | tf_op jit(solution)/shard_map/ppermute | solution.py:24
  44.2 7.5 %collective-permute-start.8 = (bf16[8,32,256]{2,1,0:T(8,128)(2,1)S(1)}, bf16[8,32,256]{2,1,0:T(8,128)(2,1)S(1)}, u32[]{:S(2)}, u32[]{:S(2)}) collective-permute-start(bf16[8,32,256]{2,1,0:T(8,128)(2,1)S(1)} %collective-permute-done.6.refs_5_), channel_id=1, source_target_pairs={{0,224},{32,0},{64,32},{96,64},{128,96},{160,128},{192,160},{224,1... | collective-permute-start | bytes 393224 | tf_op jit(solution)/shard_map/ppermute | solution.py:24
  45.6 6.7 %collective-permute-start.9 = (bf16[8,32,256]{2,1,0:T(8,128)(2,1)S(1)}, bf16[8,32,256]{2,1,0:T(8,128)(2,1)S(1)}, u32[]{:S(2)}, u32[]{:S(2)}) collective-permute-start(bf16[8,32,256]{2,1,0:T(8,128)(2,1)S(1)} %collective-permute-done.2.refs_10_), channel_id=1, source_target_pairs={{0,32},{32,64},{64,96},{96,128},{128,160},{160,192},{192,224},{224... | collective-permute-start | bytes 393224 | tf_op jit(solution)/shard_map/ppermute | solution.py:24
  46.2 7.0 %collective-permute-start.13 = (bf16[8,32,256]{2,1,0:T(8,128)(2,1)S(1)}, bf16[8,32,256]{2,1,0:T(8,128)(2,1)S(1)}, u32[]{:S(2)}, u32[]{:S(2)}) collective-permute-start(bf16[8,32,256]{2,1,0:T(8,128)(2,1)S(1)} %collective-permute-done.12.refs_11_), channel_id=1, source_target_pairs={{0,32},{32,64},{64,96},{96,128},{128,160},{160,192},{192,224},{224... | collective-permute-start | bytes 393224 | tf_op jit(solution)/shard_map/ppermute | solution.py:24
  68.9 5.4 %collective-permute-start.14 = (f32[2,8,1,512]{3,2,1,0:T(1,128)}, f32[2,8,1,512]{3,2,1,0:T(1,128)S(1)}, u32[]{:S(2)}, u32[]{:S(2)}) collective-permute-start(f32[2,8,1,512]{3,2,1,0:T(1,128)} %forward.1), channel_id=1, source_target_pairs={{0,192},{32,224},{64,0},{96,32},{128,64},{160,96},{192,128},{224,1... | collective-permute-start | bytes 98312 | tf_op jit(solution)/shard_map/ppermute | solution.py:24
  70.3 8.0 %collective-permute-start.15 = (f32[2,8,1,512]{3,2,1,0:T(1,128)}, f32[2,8,1,512]{3,2,1,0:T(1,128)S(1)}, u32[]{:S(2)}, u32[]{:S(2)}) collective-permute-start(f32[2,8,1,512]{3,2,1,0:T(1,128)} %forward.1), channel_id=1, source_target_pairs={{0,128},{32,160},{64,192},{96,224},{128,0},{160,32},{192,64},{224,... | collective-permute-start | bytes 98312 | tf_op jit(solution)/shard_map/ppermute | solution.py:24
  72.9 6.4 %collective-permute-start.16 = (f32[2,8,1,512]{3,2,1,0:T(1,128)}, f32[2,8,1,512]{3,2,1,0:T(1,128)S(1)}, u32[]{:S(2)}, u32[]{:S(2)}) collective-permute-start(f32[2,8,1,512]{3,2,1,0:T(1,128)} %forward.1), channel_id=1, source_target_pairs={{0,64},{32,96},{64,128},{96,160},{128,192},{160,224},{192,0},{224,... | collective-permute-start | bytes 98312 | tf_op jit(solution)/shard_map/ppermute | solution.py:24
  80.1 6.1 %collective-permute-start.17 = (f32[4,2,8,1,512]{4,3,2,1,0:T(1,128)S(1)}, f32[4,2,8,1,512]{4,3,2,1,0:T(1,128)S(1)}, u32[]{:S(2)}, u32[]{:S(2)}) collective-permute-start(f32[4,2,8,1,512]{4,3,2,1,0:T(1,128)S(1)} %pad_maximum_fusion.2), channel_id=1, source_target_pairs={{0,224},{32,0},{64,32},{96,64},{128,96},{160,128},{192,160},{224,1... | collective-permute-start | bytes 393224 | tf_op jit(solution)/shard_map/ppermute | solution.py:24
  81.5 31.7 %all-to-all-start.1 = ((bf16[8,512,256]{2,1,0:T(8,128)(2,1)}), bf16[8,512,256]{2,1,0:T(8,128)(2,1)S(1)}, u32[]{:S(2)}, u32[]{:S(2)}) async-start(bf16[8,512,256]{2,1,0:T(8,128)(2,1)} %copy-done), calls=%async_computation.1 | async-start | bytes 4194304 | tf_op jit(solution)/shard_map/all_to_all | solution.py:341
  86.0 74.9 %reduce-scatter.2.cloned.1.call-start = ((), (), s32[]{:S(2)}) async-start(), calls=%async_computation.5 | async-start | bytes 2359296 | tf_op jit(solution)/shard_map/reduce_scatter | solution.py:365
  113.3 8.7 %all-to-all-start.2 = ((f32[8,2,512]{2,1,0:T(2,128)}), f32[8,2,512]{2,1,0:T(2,128)S(1)}, u32[]{:S(2)}, u32[]{:S(2)}) async-start(f32[8,2,512]{2,1,0:T(2,128)} %pad_maximum_fusion.3.line_ref), calls=%async_computation.2 | async-start | bytes 65536 | tf_op jit(solution)/shard_map/all_to_all | solution.py:366
  126.4 7.4 %collective-permute-start.18 = (f32[128,256]{1,0:T(8,128)S(1)}, f32[128,256]{1,0:T(8,128)S(1)}, u32[]{:S(2)}, u32[]{:S(2)}) collective-permute-start(f32[128,256]{1,0:T(8,128)S(1)} %bitcast.94), channel_id=1, source_target_pairs={{0,1},{1,2},{2,3},{3,0},{4,5},{5,6},{6,7},{7,4},{8,9},{9,10},{10,1... | collective-permute-start | bytes 393224 | tf_op jit(solution)/shard_map/ppermute | solution.py:24
  126.9 6.8 %collective-permute-start.20 = (f32[128,256]{1,0:T(8,128)S(1)}, f32[128,256]{1,0:T(8,128)S(1)}, u32[]{:S(2)}, u32[]{:S(2)}) collective-permute-start(f32[128,256]{1,0:T(8,128)S(1)} %bitcast.93), channel_id=1, source_target_pairs={{0,3},{1,0},{2,1},{3,2},{4,7},{5,4},{6,5},{7,6},{8,11},{9,8},{10,9... | collective-permute-start | bytes 393224 | tf_op jit(solution)/shard_map/ppermute | solution.py:24
  133.8 27.1 %copy-start.2 = (f32[1,1024,256]{2,1,0:T(8,128)S(1)}, f32[1,1024,256]{2,1,0:T(8,128)}, u32[]{:S(2)}) copy-start(f32[1,1024,256]{2,1,0:T(8,128)} %param.12) | copy-start | bytes 3145732
  134.6 7.8 %collective-permute-start.19 = (f32[256,256]{1,0:T(8,128)}, f32[256,256]{1,0:T(8,128)}, u32[]{:S(2)}, u32[]{:S(2)}) collective-permute-start(f32[256,256]{1,0:T(8,128)} %pad_maximum_fusion), channel_id=1, source_target_pairs={{0,1},{1,2},{2,3},{3,0},{4,5},{5,6},{6,7},{7,4},{8,9},{9,10},{10,1... | collective-permute-start | bytes 786440 | tf_op jit(solution)/shard_map/ppermute | solution.py:24
  137.0 8.7 %collective-permute-start.21 = (f32[256,256]{1,0:T(8,128)}, f32[256,256]{1,0:T(8,128)}, u32[]{:S(2)}, u32[]{:S(2)}) collective-permute-start(f32[256,256]{1,0:T(8,128)} %pad_maximum_fusion.1), channel_id=1, source_target_pairs={{0,3},{1,0},{2,1},{3,2},{4,7},{5,4},{6,5},{7,6},{8,11},{9,8},{10,9... | collective-permute-start | bytes 786440 | tf_op jit(solution)/shard_map/ppermute | solution.py:24
  146.7 6.4 %collective-permute-start.23 = (f32[256,256]{1,0:T(8,128)S(1)}, f32[256,256]{1,0:T(8,128)S(1)}, u32[]{:S(2)}, u32[]{:S(2)}) collective-permute-start(f32[256,256]{1,0:T(8,128)S(1)} %fusion.1.own), channel_id=1, source_target_pairs={{0,1},{1,2},{2,3},{3,0},{4,5},{5,6},{6,7},{7,4},{8,9},{9,10},{10,1... | collective-permute-start | bytes 786440 | tf_op jit(solution)/shard_map/ppermute | solution.py:24
  146.8 7.8 %collective-permute-start.22 = (f32[256,256]{1,0:T(8,128)S(1)}, f32[256,256]{1,0:T(8,128)S(1)}, u32[]{:S(2)}, u32[]{:S(2)}) collective-permute-start(f32[256,256]{1,0:T(8,128)S(1)} %fusion.1.own), channel_id=1, source_target_pairs={{0,3},{1,0},{2,1},{3,2},{4,7},{5,4},{6,5},{7,6},{8,11},{9,8},{10,9... | collective-permute-start | bytes 786440 | tf_op jit(solution)/shard_map/ppermute | solution.py:24
  153.2 5.0 %collective-permute-start.24 = (f32[128,256]{1,0:T(8,128)S(1)}, f32[128,256]{1,0:T(8,128)S(1)}, u32[]{:S(2)}, u32[]{:S(2)}) collective-permute-start(f32[128,256]{1,0:T(8,128)S(1)} %slice.109), channel_id=1, source_target_pairs={{0,1},{1,2},{2,3},{3,0},{4,5},{5,6},{6,7},{7,4},{8,9},{9,10},{10,1... | collective-permute-start | bytes 393224 | tf_op jit(solution)/shard_map/ppermute | solution.py:24
  154.6 6.3 %collective-permute-start.25 = (f32[128,256]{1,0:T(8,128)S(1)}, f32[128,256]{1,0:T(8,128)S(1)}, u32[]{:S(2)}, u32[]{:S(2)}) collective-permute-start(f32[128,256]{1,0:T(8,128)S(1)} %slice.110), channel_id=1, source_target_pairs={{0,3},{1,0},{2,1},{3,2},{4,7},{5,4},{6,5},{7,6},{8,11},{9,8},{10,9... | collective-permute-start | bytes 393224 | tf_op jit(solution)/shard_map/ppermute | solution.py:24
  (21 other events, 120.8 us)
Sparse Core Ops, SparseCore 0:
  10.5 37.5 all-gather.1
  113.4 39.4 reduce-scatter.1

commit v8 on v7

--- a/solution.py
+++ b/solution.py
@@ -105,7 +105,7 @@
         scratch_shapes=[pltpu.VMEM((per, items, width), F32)],
         compiler_params=pltpu.CompilerParams(vmem_limit_bytes=LARGE),
         cost_estimate=pl.CostEstimate(
-            flops=2 * planes * width * items * features,
+            flops=40 * planes * width * items * features,
             bytes_accessed=planes * items * features * 2 + planes * width * features * 2,
             transcendentals=planes * width * items,
         ),
@@ -164,36 +164,32 @@
         ),
         out_shape=out,
         compiler_params=pltpu.CompilerParams(vmem_limit_bytes=LARGE),
-        cost_estimate=pl.CostEstimate(
-            flops=4 * planes * width * items * features,
-            bytes_accessed=planes * items * features * 2 + 2 * planes * width * features * 2,
-            transcendentals=planes * width * items,
-        ),
+        cost_estimate=pl.CostEstimate(flops=1 << 20, bytes_accessed=1 << 20, transcendentals=0),
         name="query_parts",
     )(blk, packed, tables, lines)
 
 
 def item_kernel(where, q_ref, line_ref, t_ref, *outs):
-    start = where[pl.program_id(0)] * t_ref.shape[1]
+    start = where[pl.program_id(0)] * t_ref.shape[0]
     total = None
     for source in range(q_ref.shape[0]):
         q = q_ref[source]
         line = line_ref[source]
         lse = line[0:1, :]
         tgt = line[1:2, :].astype(jnp.int32)
-        s = lax.dot_general(t_ref[0], q, NT, preferred_element_type=F32)
+        s = lax.dot_general(t_ref[...], q, NT, preferred_element_type=F32)
         e = jnp.exp(s - lse)
         c = jnp.where(tile_ids(start, s.shape) == tgt, e - 1.0, e).astype(BF16)
         part = jnp.dot(c, q, preferred_element_type=F32)
         total = part if total is None else total + part
-    cut = t_ref.shape[1] // len(outs)
+    cut = t_ref.shape[0] // len(outs)
     for n, out in enumerate(outs):
         out[0] = total[n * cut:(n + 1) * cut]
 
 
-def item_parts(places, pieces, x, mine, rows, lines, tables, quarters):
+def item_parts(places, pieces, x, rows, lines, table16, quarters):
     count, width, features = rows.shape
-    span = tables.shape[1] // quarters
+    span = table16.shape[0] // quarters
     share = len(places)
     out = jax.ShapeDtypeStruct((share, span // pieces, features), F32)
     return pl.pallas_call(
@@ -204,7 +200,7 @@
             in_specs=[
                 pl.BlockSpec(rows.shape, lambda i, o: (0, 0, 0)),
                 pl.BlockSpec(lines.shape, lambda i, o: (0, 0, 0)),
-                pl.BlockSpec((1, span, features), lambda i, o: (o[share], o[i], 0)),
+                pl.BlockSpec((span, features), lambda i, o: (o[i], 0)),
             ],
             out_specs=[pl.BlockSpec((1,) + out.shape[1:], lambda i, o: (i, 0, 0))] * pieces,
         ),
@@ -216,7 +212,7 @@
             transcendentals=share * span * count * width,
         ),
         name="item_parts",
-    )(jnp.concatenate([(jnp.array(places, jnp.int32) + x) % quarters, mine]), rows, lines, tables)
+    )((jnp.array(places, jnp.int32) + x) % quarters, rows, lines, table16)
 
 
 def update_kernel(x_ref, own, after, before, far_a, far_b, g_ref, t_ref, a_ref, ng_ref, nt_ref, na_ref):
@@ -278,7 +274,6 @@
     pair_count = block_count * picks
 
     tables = lax.all_gather(table[0].astype(BF16), PLANE)
-    mine = (lax.axis_index("y") * lax.axis_size("c") + lax.axis_index("c")).reshape(1)
 
     here = queries.reshape(2, block_count // 2, block_rows, features)
     by_source = [[None] * 2 for _ in range(z_size)]
@@ -337,6 +332,8 @@
     pair_row = (pair_from % 2 * 4 + pair_from // 2) * plane + pair_owner % plane
     pair_row = (pair_row * z_size + pair_place) * MOST + pair_slot % MOST
 
+    own_table, blk = lax.optimization_barrier((table[0], blk))
+    own_table = own_table.astype(BF16)
     packed = pack([part for pair in by_source for part in pair], blk, plane)
     rows = lax.all_to_all(packed, PLANE, 0, 0, tiled=True)
     stats = forward(packed, targets, tables)
@@ -344,6 +341,7 @@
     even = jnp.stack([stats] + [shift(stats, "z", -e) for e in (2, 4, 6)])
     all_stats = jnp.stack([even, shift(even, "z", -1)]).reshape(z_size, 2, -1)
     part = all_stats[:, 0].reshape(-1, block_rows)[pair_row.reshape(-1)]
+    part, rows = lax.optimization_barrier((part, rows))
     part = part.reshape(z_size, block_count, picks, block_rows)
     pick = all_stats[:, 1].reshape(-1, block_rows)[pair_row[0]]
     pick = pick.reshape(block_count, picks, block_rows)
@@ -361,13 +359,13 @@
     grads = query_parts(
         packed, jnp.concatenate([blk, z.reshape(1)]), lines, tables, z_size, block_count, block_rows
     )
-    grads, lines, rows = lax.optimization_barrier((grads, lines, rows))
+    grads, lines = lax.optimization_barrier((grads, lines))
     grads = lax.psum_scatter(grads, "z").reshape(local_rows, features)
     got_lines = lax.all_to_all(lines, PLANE, 0, 0, tiled=True)
 
-    far_a, far_b = item_parts((2,), 2, x, mine, rows, got_lines, tables, x_size)
+    far_a, far_b = item_parts((2,), 2, x, rows, got_lines, own_table, x_size)
     far_a, far_b, got_lines = lax.optimization_barrier((far_a, far_b, got_lines))
-    (rest,) = item_parts((0, 1, 3), 1, x, mine, rows, got_lines, tables, x_size)
+    (rest,) = item_parts((0, 1, 3), 1, x, rows, got_lines, own_table, x_size)
     far_a, far_b = far_a[0], far_b[0]
     own, after, before = rest[0], rest[1], rest[2]
     half = far_a.shape[0]

time: 171 us -> 157 us (0.918)
  local copies, waits for them, and re-layouts: 21.7 us -> 11.3 us
  waiting for transfers between devices: 48.3 us -> 42.4 us
    all_to_all x1, waiting for transfers between devices: 12.7 us -> 0.01 us  [local(): rows = lax.all_to_all(packed, PLANE, 0, 0, tiled=True)]
    unnamed x48 -> x28, local copies, waits for them, and re-layouts: 12.6 us -> 3.12 us
    ppermute x26, waiting for transfers between devices: 28.3 us -> 35.5 us  [shift(): lax.ppermute(value, axis, [(i, (i + step) % size) for i in range(size)])]
  transfers between devices with their start and end apart: 31 -> 31, of which waited for: 14 -> 15; matrix products, arithmetic and copies ran while one was open for 10% -> 10% of each run, Pallas kernels for 11% -> 11%
where the time goes in v8:
time: 157 us
  starting transfers between devices  48.5 us (31%)
  waiting for transfers between devices  42.4 us (27%)
  Pallas kernels  29.5 us (19%)
  between operations  14.6 us (9%)
  local copies, waits for them, and re-layouts  11.3 us (7%)
  other arithmetic  10.4 us (7%)
    ppermute x26, waiting for transfers between devices, shift(): lax.ppermute(value, axis, [(i, (i + step) % size) for i in range(size)])  35.5 us
    ppermute x26, starting transfers between devices, shift(): lax.ppermute(value, axis, [(i, (i + step) % size) for i in range(size)])  34.1 us
    pallas_call x1, Pallas kernels, query_parts(): pl.pallas_call(query_kernel, grid_spec=pltpu.PrefetchScalarGridSpec(num_s...  9.91 us
    pallas_call x1, Pallas kernels, forward(): pl.pallas_call(forward_kernel, grid=(planes // per,), in_specs=[pl.BlockS...  8.24 us
    pallas_call x2, Pallas kernels, item_parts(): pl.pallas_call(item_kernel, grid_spec=pltpu.PrefetchScalarGridSpec(num_sc...  6.79 us
    all_to_all x1, starting transfers between devices, local(): got = lax.all_to_all(meta, 'z', 0, 0, tiled=True)  5.48 us
    all_to_all x1, waiting for transfers between devices, local(): got_lines = lax.all_to_all(lines, PLANE, 0, 0, tiled=True)  4.56 us
    all_to_all x1, starting transfers between devices, local(): rows = lax.all_to_all(packed, PLANE, 0, 0, tiled=True)  4.47 us
  transfers between devices with their start and end apart: 31, of which 15 were waited for; matrix products, arithmetic and copies ran while one was open for 10% of the time, Pallas kernels for 11%

profile of v8, /device:TPU:6, one launch (start us, length us, event | category | flops | bytes accessed | tf_op | source)
XLA Modules:
  0.0 156.7 jit_solution(13807179530816174069)
XLA Ops:
  7.3 2.1 %convert_element_type.22 = bf16[1,1024,256]{2,1,0:T(8,128)(2,1)} convert(f32[1,1024,256]{2,1,0:T(8,128)} %param.12) | non-fusion elementwise | flops 262144 | bytes 1572864 | tf_op jit(solution)/shard_map/convert_element_type | solution.py:276
  9.4 2.0 %collective-permute-start = (bf16[8,32,256]{2,1,0:T(8,128)(2,1)S(1)}, bf16[8,32,256]{2,1,0:T(8,128)(2,1)S(1)}, u32[]{:S(2)}, u32[]{:S(2)}) collective-permute-start(bf16[8,32,256]{2,1,0:T(8,128)(2,1)S(1)} %bitcast.85), channel_id=1, source_target_pairs={{0,32},{32,64},{64,96},{96,128},{128,160},{160,192},{192,224},{224... | collective-permute-start | bytes 393224 | tf_op jit(solution)/shard_map/ppermute | solution.py:24
  11.4 4.0 %collective-permute-start.3 = (bf16[8,32,256]{2,1,0:T(8,128)(2,1)S(1)}, bf16[8,32,256]{2,1,0:T(8,128)(2,1)S(1)}, u32[]{:S(2)}, u32[]{:S(2)}) collective-permute-start(bf16[8,32,256]{2,1,0:T(8,128)(2,1)S(1)} %bitcast.86), channel_id=1, source_target_pairs={{0,224},{32,0},{64,32},{96,64},{128,96},{160,128},{192,160},{224,1... | collective-permute-start | bytes 393224 | tf_op jit(solution)/shard_map/ppermute | solution.py:24
  15.4 3.2 %collective-permute-start.4 = (bf16[8,32,256]{2,1,0:T(8,128)(2,1)S(1)}, bf16[8,32,256]{2,1,0:T(8,128)(2,1)S(1)}, u32[]{:S(2)}, u32[]{:S(2)}) collective-permute-start(bf16[8,32,256]{2,1,0:T(8,128)(2,1)S(1)} %bitcast.83), channel_id=1, source_target_pairs={{0,224},{32,0},{64,32},{96,64},{128,96},{160,128},{192,160},{224,1... | collective-permute-start | bytes 393224 | tf_op jit(solution)/shard_map/ppermute | solution.py:24
  21.7 6.5 %collective-permute-done.1.refs_12_ = bf16[8,32,256]{2,1,0:T(8,128)(2,1)S(1)} collective-permute-done((bf16[8,32,256]{2,1,0:T(8,128)(2,1)S(1)}, bf16[8,32,256]{2,1,0:T(8,128)(2,1)S(1)}, u32[]{:S(2)}, u32[]{:S(2)}) %collective-permute-start.1) | collective-permute-done | bytes 131104 | tf_op jit(solution)/shard_map/ppermute | solution.py:24
  28.2 3.3 %collective-permute-start.5 = (bf16[8,32,256]{2,1,0:T(8,128)(2,1)S(1)}, bf16[8,32,256]{2,1,0:T(8,128)(2,1)S(1)}, u32[]{:S(2)}, u32[]{:S(2)}) collective-permute-start(bf16[8,32,256]{2,1,0:T(8,128)(2,1)S(1)} %collective-permute-done.3.refs_2_), channel_id=1, source_target_pairs={{0,224},{32,0},{64,32},{96,64},{128,96},{160,128},{192,160},{224,1... | collective-permute-start | bytes 393224 | tf_op jit(solution)/shard_map/ppermute | solution.py:24
  31.7 1.9 %collective-permute-start.12 = (bf16[8,32,256]{2,1,0:T(8,128)(2,1)S(1)}, bf16[8,32,256]{2,1,0:T(8,128)(2,1)S(1)}, u32[]{:S(2)}, u32[]{:S(2)}) collective-permute-start(bf16[8,32,256]{2,1,0:T(8,128)(2,1)S(1)} %collective-permute-done.11.refs_13_), channel_id=1, source_target_pairs={{0,32},{32,64},{64,96},{96,128},{128,160},{160,192},{192,224},{224... | collective-permute-start | bytes 393224 | tf_op jit(solution)/shard_map/ppermute | solution.py:24
  35.4 5.5 %all-to-all-start = ((s32[8,1,592]{2,1,0:T(1,128)}), s32[8,1,592]{2,1,0:T(1,128)S(1)}, u32[]{:S(2)}, u32[]{:S(2)}) async-start(s32[8,1,592]{2,1,0:T(1,128)} %copy.43), calls=%async_computation | async-start | bytes 40960 | tf_op jit(solution)/shard_map/all_to_all | solution.py:317
  41.1 3.3 %collective-permute-start.7 = (bf16[8,32,256]{2,1,0:T(8,128)(2,1)S(1)}, bf16[8,32,256]{2,1,0:T(8,128)(2,1)S(1)}, u32[]{:S(2)}, u32[]{:S(2)}) collective-permute-start(bf16[8,32,256]{2,1,0:T(8,128)(2,1)S(1)} %collective-permute-done.5.refs_4_), channel_id=1, source_target_pairs={{0,224},{32,0},{64,32},{96,64},{128,96},{160,128},{192,160},{224,1... | collective-permute-start | bytes 393224 | tf_op jit(solution)/shard_map/ppermute | solution.py:24
  44.4 1.5 collective-permute-start.8
  46.4 2.2 %all-to-all-done = s32[8,1,592]{2,1,0:T(1,128)S(1)} async-done(((s32[8,1,592]{2,1,0:T(1,128)}), s32[8,1,592]{2,1,0:T(1,128)S(1)}, u32[]{:S(2)}, u32[]{:S(2)}) %all-to-all-start) | async-done | bytes 18976 | tf_op jit(solution)/shard_map/all_to_all | solution.py:317
  52.0 1.4 collective-permute-done.13.refs_9_
  53.4 2.3 %pack.1.p_ref = bf16[8,512,256]{2,1,0:T(8,128)(2,1)} custom-call(s32[128]{0:T(128)S(1)} %max.15.blk, bf16[8,32,256]{2,1,0:T(8,128)(2,1)S(1)} %bitcast.87, bf16[8,32,256]{2,1,0:T(8,128)(2,1)S(1)} %bitcast.84, bf16[8,32,256]{2,1,0:T(8,128)(2,1)S(1)} %collective-permute-done.3.refs_2_, bf16[8,32,256]{2,1,0:T(8,128)(2,1)S(1)} %collective-permute-done.4.refs_3_, ...), custom_call_target="tpu_custom_call" | custom-call | bytes 4194304 | tf_op jit(solution)/shard_map/pack/pallas_call | solution.py:50
  55.8 4.5 %all-to-all-start.1 = ((bf16[8,512,256]{2,1,0:T(8,128)(2,1)}), bf16[8,512,256]{2,1,0:T(8,128)(2,1)S(1)}, u32[]{:S(2)}, u32[]{:S(2)}) async-start(bf16[8,512,256]{2,1,0:T(8,128)(2,1)} %pack.1.p_ref), calls=%async_computation.1 | async-start | bytes 4194304 | tf_op jit(solution)/shard_map/all_to_all | solution.py:338
  60.3 8.2 %forward.1 = f32[2,8,1,512]{3,2,1,0:T(1,128)} custom-call(bf16[8,512,256]{2,1,0:T(8,128)(2,1)} %pack.1.p_ref, bf16[8,1024,256]{2,1,0:T(8,128)(2,1)} %all-gather.2.cloned.1.call-done.t_ref, s32[8,1,512]{2,1,0:T(1,128)} %reshape.330.tgt_ref), custom_call_target="tpu_custom_call" | custom-call | flops 42949672960 | bytes 6291456 | tf_op jit(solution)/shard_map/forward/pallas_call | solution.py:95
  71.0 2.9 %collective-permute-start.16 = (f32[2,8,1,512]{3,2,1,0:T(1,128)}, f32[2,8,1,512]{3,2,1,0:T(1,128)S(1)}, u32[]{:S(2)}, u32[]{:S(2)}) collective-permute-start(f32[2,8,1,512]{3,2,1,0:T(1,128)} %forward.1), channel_id=1, source_target_pairs={{0,64},{32,96},{64,128},{96,160},{128,192},{160,224},{192,0},{224,... | collective-permute-start | bytes 98312 | tf_op jit(solution)/shard_map/ppermute | solution.py:24
  73.9 3.8 %collective-permute-done.15 = f32[2,8,1,512]{3,2,1,0:T(1,128)S(1)} collective-permute-done((f32[2,8,1,512]{3,2,1,0:T(1,128)}, f32[2,8,1,512]{3,2,1,0:T(1,128)S(1)}, u32[]{:S(2)}, u32[]{:S(2)}) %collective-permute-start.15) | collective-permute-done | bytes 32800 | tf_op jit(solution)/shard_map/ppermute | solution.py:24
  81.8 3.3 %collective-permute-done.17 = f32[4,2,8,1,512]{4,3,2,1,0:T(1,128)S(1)} collective-permute-done((f32[4,2,8,1,512]{4,3,2,1,0:T(1,128)S(1)}, f32[4,2,8,1,512]{4,3,2,1,0:T(1,128)S(1)}, u32[]{:S(2)}, u32[]{:S(2)}) %collective-permute-start.17) | collective-permute-done | bytes 131104 | tf_op jit(solution)/shard_map/ppermute | solution.py:24
  89.4 9.9 %query_parts.1 = bf16[8,16,32,256]{3,2,1,0:T(8,128)(2,1)} custom-call(s32[129]{0:T(256)} %pad_add_fusion.blk, bf16[8,512,256]{2,1,0:T(8,128)(2,1)} %pack.1.p_ref, bf16[8,1024,256]{2,1,0:T(8,128)(2,1)} %all-gather.2.cloned.1.call-done.t_ref, f32[8,2,512]{2,1,0:T(2,128)} %pad_maximum_fusion.3.line_ref), custom_call_target="tpu_custom_call" | custom-call | flops 1048576 | bytes 1048576 | tf_op jit(solution)/shard_map/query_parts/pallas_call | solution.py:152
  99.4 4.4 %all-to-all-start.2 = ((f32[8,2,512]{2,1,0:T(2,128)}), f32[8,2,512]{2,1,0:T(2,128)S(1)}, u32[]{:S(2)}, u32[]{:S(2)}) async-start(f32[8,2,512]{2,1,0:T(2,128)} %pad_maximum_fusion.3.line_ref), calls=%async_computation.2 | async-start | bytes 65536 | tf_op jit(solution)/shard_map/all_to_all | solution.py:364
  104.7 4.6 %all-to-all-done.2.line_ref = f32[8,2,512]{2,1,0:T(2,128)S(1)} async-done(((f32[8,2,512]{2,1,0:T(2,128)}), f32[8,2,512]{2,1,0:T(2,128)S(1)}, u32[]{:S(2)}, u32[]{:S(2)}) %all-to-all-start.2) | async-done | bytes 32800 | tf_op jit(solution)/shard_map/all_to_all | solution.py:364
  110.3 1.5 item_parts.2
  112.5 1.5 collective-permute-start.20
  113.9 5.2 %item_parts.3 = f32[3,256,256]{2,1,0:T(8,128)S(1)} custom-call(s32[3]{0:T(128)S(1)} %and_select_fusion.2.where, bf16[8,512,256]{2,1,0:T(8,128)(2,1)S(1)} %all-to-all-done.1.q_ref, f32[8,2,512]{2,1,0:T(2,128)S(1)} %all-to-all-done.2.line_ref, bf16[1024,256]{1,0:T(8,128)(2,1)S(1)} %copy-done.4), custom_call_target="tpu_custom_call" | custom-call | flops 3221225472 | bytes 3276800 | tf_op jit(solution)/shard_map/item_parts/pallas_call | solution.py:195
  120.2 1.8 %collective-permute-start.19 = (f32[256,256]{1,0:T(8,128)S(1)}, f32[256,256]{1,0:T(8,128)}, u32[]{:S(2)}, u32[]{:S(2)}) collective-permute-start(f32[256,256]{1,0:T(8,128)S(1)} %pad_maximum_fusion), channel_id=1, source_target_pairs={{0,1},{1,2},{2,3},{3,0},{4,5},{5,6},{6,7},{7,4},{8,9},{9,10},{10,1... | collective-permute-start | bytes 786440 | tf_op jit(solution)/shard_map/ppermute | solution.py:24
  124.6 3.2 %collective-permute-done.19 = f32[256,256]{1,0:T(8,128)} collective-permute-done((f32[256,256]{1,0:T(8,128)S(1)}, f32[256,256]{1,0:T(8,128)}, u32[]{:S(2)}, u32[]{:S(2)}) %collective-permute-start.19) | collective-permute-done | bytes 262176 | tf_op jit(solution)/shard_map/ppermute | solution.py:24
  127.8 3.5 %collective-permute-done.21 = f32[256,256]{1,0:T(8,128)} collective-permute-done((f32[256,256]{1,0:T(8,128)}, f32[256,256]{1,0:T(8,128)}, u32[]{:S(2)}, u32[]{:S(2)}) %collective-permute-start.21) | collective-permute-done | bytes 262176 | tf_op jit(solution)/shard_map/ppermute | solution.py:24
  132.6 2.0 %collective-permute-start.22 = (f32[256,256]{1,0:T(8,128)S(1)}, f32[256,256]{1,0:T(8,128)S(1)}, u32[]{:S(2)}, u32[]{:S(2)}) collective-permute-start(f32[256,256]{1,0:T(8,128)S(1)} %fusion.1.own), channel_id=1, source_target_pairs={{0,3},{1,0},{2,1},{3,2},{4,7},{5,4},{6,5},{7,6},{8,11},{9,8},{10,9... | collective-permute-start | bytes 786440 | tf_op jit(solution)/shard_map/ppermute | solution.py:24
  134.6 4.5 %collective-permute-done.23.before = f32[256,256]{1,0:T(8,128)S(1)} collective-permute-done((f32[256,256]{1,0:T(8,128)S(1)}, f32[256,256]{1,0:T(8,128)S(1)}, u32[]{:S(2)}, u32[]{:S(2)}) %collective-permute-start.23) | collective-permute-done | bytes 262176 | tf_op jit(solution)/shard_map/ppermute | solution.py:24
  141.4 2.8 %collective-permute-done.24.far_a = f32[128,256]{1,0:T(8,128)S(1)} collective-permute-done((f32[128,256]{1,0:T(8,128)S(1)}, f32[128,256]{1,0:T(8,128)S(1)}, u32[]{:S(2)}, u32[]{:S(2)}) %collective-permute-start.24) | collective-permute-done | bytes 131104 | tf_op jit(solution)/shard_map/ppermute | solution.py:24
  144.2 2.5 %collective-permute-done.25.far_b = f32[128,256]{1,0:T(8,128)S(1)} collective-permute-done((f32[128,256]{1,0:T(8,128)S(1)}, f32[128,256]{1,0:T(8,128)S(1)}, u32[]{:S(2)}, u32[]{:S(2)}) %collective-permute-start.25) | collective-permute-done | bytes 131104 | tf_op jit(solution)/shard_map/ppermute | solution.py:24
  147.7 2.2 %update.1 = (f32[512,256]{1,0:T(8,128)}, f32[1024,256]{1,0:T(8,128)}, f32[1024,256]{1,0:T(8,128)}) custom-call(s32[1]{0:T(128)} %bitcast.17.x_ref, f32[256,256]{1,0:T(8,128)S(1)} %fusion.1.own, f32[256,256]{1,0:T(8,128)S(1)} %collective-permute-done.22.after, f32[256,256]{1,0:T(8,128)S(1)} %collective-permute-done.23.before, ...), custom_call_target="tpu_custom_call" | custom-call | tf_op jit(solution)/shard_map/update/pallas_call | solution.py:248
  (154 shorter events, 30.3 us)
Async XLA Ops:
  7.2 53.1 %all-gather.2.cloned.1.call-start = ((), (), s32[]{:S(2)}) async-start(), calls=%async_computation.4 | async-start | bytes 4718592 | tf_op jit(solution)/shard_map/all_gather | solution.py:276
  9.4 11.7 %collective-permute-start = (bf16[8,32,256]{2,1,0:T(8,128)(2,1)S(1)}, bf16[8,32,256]{2,1,0:T(8,128)(2,1)S(1)}, u32[]{:S(2)}, u32[]{:S(2)}) collective-permute-start(bf16[8,32,256]{2,1,0:T(8,128)(2,1)S(1)} %bitcast.85), channel_id=1, source_target_pairs={{0,32},{32,64},{64,96},{96,128},{128,160},{160,192},{192,224},{224... | collective-permute-start | bytes 393224 | tf_op jit(solution)/shard_map/ppermute | solution.py:24
  11.4 16.8 %collective-permute-start.3 = (bf16[8,32,256]{2,1,0:T(8,128)(2,1)S(1)}, bf16[8,32,256]{2,1,0:T(8,128)(2,1)S(1)}, u32[]{:S(2)}, u32[]{:S(2)}) collective-permute-start(bf16[8,32,256]{2,1,0:T(8,128)(2,1)S(1)} %bitcast.86), channel_id=1, source_target_pairs={{0,224},{32,0},{64,32},{96,64},{128,96},{160,128},{192,160},{224,1... | collective-permute-start | bytes 393224 | tf_op jit(solution)/shard_map/ppermute | solution.py:24
  15.4 6.2 %collective-permute-start.10 = (bf16[8,32,256]{2,1,0:T(8,128)(2,1)S(1)}, bf16[8,32,256]{2,1,0:T(8,128)(2,1)S(1)}, u32[]{:S(2)}, u32[]{:S(2)}) collective-permute-start(bf16[8,32,256]{2,1,0:T(8,128)(2,1)S(1)} %bitcast.82), channel_id=1, source_target_pairs={{0,32},{32,64},{64,96},{96,128},{128,160},{160,192},{192,224},{224... | collective-permute-start | bytes 393224 | tf_op jit(solution)/shard_map/ppermute | solution.py:24
  15.4 16.1 %collective-permute-start.4 = (bf16[8,32,256]{2,1,0:T(8,128)(2,1)S(1)}, bf16[8,32,256]{2,1,0:T(8,128)(2,1)S(1)}, u32[]{:S(2)}, u32[]{:S(2)}) collective-permute-start(bf16[8,32,256]{2,1,0:T(8,128)(2,1)S(1)} %bitcast.83), channel_id=1, source_target_pairs={{0,224},{32,0},{64,32},{96,64},{128,96},{160,128},{192,160},{224,1... | collective-permute-start | bytes 393224 | tf_op jit(solution)/shard_map/ppermute | solution.py:24
  21.1 7.1 %collective-permute-start.1 = (bf16[8,32,256]{2,1,0:T(8,128)(2,1)S(1)}, bf16[8,32,256]{2,1,0:T(8,128)(2,1)S(1)}, u32[]{:S(2)}, u32[]{:S(2)}) collective-permute-start(bf16[8,32,256]{2,1,0:T(8,128)(2,1)S(1)} %collective-permute-done.refs_14_), channel_id=1, source_target_pairs={{0,32},{32,64},{64,96},{96,128},{128,160},{160,192},{192,224},{224... | collective-permute-start | bytes 393224 | tf_op jit(solution)/shard_map/ppermute | solution.py:24
  21.7 10.0 %collective-permute-start.11 = (bf16[8,32,256]{2,1,0:T(8,128)(2,1)S(1)}, bf16[8,32,256]{2,1,0:T(8,128)(2,1)S(1)}, u32[]{:S(2)}, u32[]{:S(2)}) collective-permute-start(bf16[8,32,256]{2,1,0:T(8,128)(2,1)S(1)} %collective-permute-done.10.refs_15_), channel_id=1, source_target_pairs={{0,32},{32,64},{64,96},{96,128},{128,160},{160,192},{192,224},{224... | collective-permute-start | bytes 393224 | tf_op jit(solution)/shard_map/ppermute | solution.py:24
  28.2 6.5 %collective-permute-start.2 = (bf16[8,32,256]{2,1,0:T(8,128)(2,1)S(1)}, bf16[8,32,256]{2,1,0:T(8,128)(2,1)S(1)}, u32[]{:S(2)}, u32[]{:S(2)}) collective-permute-start(bf16[8,32,256]{2,1,0:T(8,128)(2,1)S(1)} %collective-permute-done.1.refs_12_), channel_id=1, source_target_pairs={{0,32},{32,64},{64,96},{96,128},{128,160},{160,192},{192,224},{224... | collective-permute-start | bytes 393224 | tf_op jit(solution)/shard_map/ppermute | solution.py:24
  28.2 12.8 %collective-permute-start.5 = (bf16[8,32,256]{2,1,0:T(8,128)(2,1)S(1)}, bf16[8,32,256]{2,1,0:T(8,128)(2,1)S(1)}, u32[]{:S(2)}, u32[]{:S(2)}) collective-permute-start(bf16[8,32,256]{2,1,0:T(8,128)(2,1)S(1)} %collective-permute-done.3.refs_2_), channel_id=1, source_target_pairs={{0,224},{32,0},{64,32},{96,64},{128,96},{160,128},{192,160},{224,1... | collective-permute-start | bytes 393224 | tf_op jit(solution)/shard_map/ppermute | solution.py:24
  31.6 12.8 %collective-permute-start.6 = (bf16[8,32,256]{2,1,0:T(8,128)(2,1)S(1)}, bf16[8,32,256]{2,1,0:T(8,128)(2,1)S(1)}, u32[]{:S(2)}, u32[]{:S(2)}) collective-permute-start(bf16[8,32,256]{2,1,0:T(8,128)(2,1)S(1)} %collective-permute-done.4.refs_3_), channel_id=1, source_target_pairs={{0,224},{32,0},{64,32},{96,64},{128,96},{160,128},{192,160},{224,1... | collective-permute-start | bytes 393224 | tf_op jit(solution)/shard_map/ppermute | solution.py:24
  31.7 14.7 %collective-permute-start.12 = (bf16[8,32,256]{2,1,0:T(8,128)(2,1)S(1)}, bf16[8,32,256]{2,1,0:T(8,128)(2,1)S(1)}, u32[]{:S(2)}, u32[]{:S(2)}) collective-permute-start(bf16[8,32,256]{2,1,0:T(8,128)(2,1)S(1)} %collective-permute-done.11.refs_13_), channel_id=1, source_target_pairs={{0,32},{32,64},{64,96},{96,128},{128,160},{160,192},{192,224},{224... | collective-permute-start | bytes 393224 | tf_op jit(solution)/shard_map/ppermute | solution.py:24
  35.4 13.3 %all-to-all-start = ((s32[8,1,592]{2,1,0:T(1,128)}), s32[8,1,592]{2,1,0:T(1,128)S(1)}, u32[]{:S(2)}, u32[]{:S(2)}) async-start(s32[8,1,592]{2,1,0:T(1,128)} %copy.43), calls=%async_computation | async-start | bytes 40960 | tf_op jit(solution)/shard_map/all_to_all | solution.py:317
  41.1 9.6 %collective-permute-start.7 = (bf16[8,32,256]{2,1,0:T(8,128)(2,1)S(1)}, bf16[8,32,256]{2,1,0:T(8,128)(2,1)S(1)}, u32[]{:S(2)}, u32[]{:S(2)}) collective-permute-start(bf16[8,32,256]{2,1,0:T(8,128)(2,1)S(1)} %collective-permute-done.5.refs_4_), channel_id=1, source_target_pairs={{0,224},{32,0},{64,32},{96,64},{128,96},{160,128},{192,160},{224,1... | collective-permute-start | bytes 393224 | tf_op jit(solution)/shard_map/ppermute | solution.py:24
  44.4 6.3 %collective-permute-start.8 = (bf16[8,32,256]{2,1,0:T(8,128)(2,1)S(1)}, bf16[8,32,256]{2,1,0:T(8,128)(2,1)S(1)}, u32[]{:S(2)}, u32[]{:S(2)}) collective-permute-start(bf16[8,32,256]{2,1,0:T(8,128)(2,1)S(1)} %collective-permute-done.6.refs_5_), channel_id=1, source_target_pairs={{0,224},{32,0},{64,32},{96,64},{128,96},{160,128},{192,160},{224,1... | collective-permute-start | bytes 393224 | tf_op jit(solution)/shard_map/ppermute | solution.py:24
  45.8 6.2 %collective-permute-start.9 = (bf16[8,32,256]{2,1,0:T(8,128)(2,1)S(1)}, bf16[8,32,256]{2,1,0:T(8,128)(2,1)S(1)}, u32[]{:S(2)}, u32[]{:S(2)}) collective-permute-start(bf16[8,32,256]{2,1,0:T(8,128)(2,1)S(1)} %collective-permute-done.2.refs_10_), channel_id=1, source_target_pairs={{0,32},{32,64},{64,96},{96,128},{128,160},{160,192},{192,224},{224... | collective-permute-start | bytes 393224 | tf_op jit(solution)/shard_map/ppermute | solution.py:24
  46.4 7.0 %collective-permute-start.13 = (bf16[8,32,256]{2,1,0:T(8,128)(2,1)S(1)}, bf16[8,32,256]{2,1,0:T(8,128)(2,1)S(1)}, u32[]{:S(2)}, u32[]{:S(2)}) collective-permute-start(bf16[8,32,256]{2,1,0:T(8,128)(2,1)S(1)} %collective-permute-done.12.refs_11_), channel_id=1, source_target_pairs={{0,32},{32,64},{64,96},{96,128},{128,160},{160,192},{192,224},{224... | collective-permute-start | bytes 393224 | tf_op jit(solution)/shard_map/ppermute | solution.py:24
  55.8 31.8 %all-to-all-start.1 = ((bf16[8,512,256]{2,1,0:T(8,128)(2,1)}), bf16[8,512,256]{2,1,0:T(8,128)(2,1)S(1)}, u32[]{:S(2)}, u32[]{:S(2)}) async-start(bf16[8,512,256]{2,1,0:T(8,128)(2,1)} %pack.1.p_ref), calls=%async_computation.1 | async-start | bytes 4194304 | tf_op jit(solution)/shard_map/all_to_all | solution.py:338
  60.2 86.5 %reduce-scatter.2.cloned.1.call-start = ((), (), s32[]{:S(2)}) async-start(), calls=%async_computation.5 | async-start | bytes 2359296 | tf_op jit(solution)/shard_map/reduce_scatter | solution.py:363
  68.6 5.4 %collective-permute-start.14 = (f32[2,8,1,512]{3,2,1,0:T(1,128)}, f32[2,8,1,512]{3,2,1,0:T(1,128)S(1)}, u32[]{:S(2)}, u32[]{:S(2)}) collective-permute-start(f32[2,8,1,512]{3,2,1,0:T(1,128)} %forward.1), channel_id=1, source_target_pairs={{0,192},{32,224},{64,0},{96,32},{128,64},{160,96},{192,128},{224,1... | collective-permute-start | bytes 98312 | tf_op jit(solution)/shard_map/ppermute | solution.py:24
  69.7 8.1 %collective-permute-start.15 = (f32[2,8,1,512]{3,2,1,0:T(1,128)}, f32[2,8,1,512]{3,2,1,0:T(1,128)S(1)}, u32[]{:S(2)}, u32[]{:S(2)}) collective-permute-start(f32[2,8,1,512]{3,2,1,0:T(1,128)} %forward.1), channel_id=1, source_target_pairs={{0,128},{32,160},{64,192},{96,224},{128,0},{160,32},{192,64},{224,... | collective-permute-start | bytes 98312 | tf_op jit(solution)/shard_map/ppermute | solution.py:24
  71.0 7.8 %collective-permute-start.16 = (f32[2,8,1,512]{3,2,1,0:T(1,128)}, f32[2,8,1,512]{3,2,1,0:T(1,128)S(1)}, u32[]{:S(2)}, u32[]{:S(2)}) collective-permute-start(f32[2,8,1,512]{3,2,1,0:T(1,128)} %forward.1), channel_id=1, source_target_pairs={{0,64},{32,96},{64,128},{96,160},{128,192},{160,224},{192,0},{224,... | collective-permute-start | bytes 98312 | tf_op jit(solution)/shard_map/ppermute | solution.py:24
  79.7 5.4 %collective-permute-start.17 = (f32[4,2,8,1,512]{4,3,2,1,0:T(1,128)S(1)}, f32[4,2,8,1,512]{4,3,2,1,0:T(1,128)S(1)}, u32[]{:S(2)}, u32[]{:S(2)}) collective-permute-start(f32[4,2,8,1,512]{4,3,2,1,0:T(1,128)S(1)} %pad_maximum_fusion.2), channel_id=1, source_target_pairs={{0,224},{32,0},{64,32},{96,64},{128,96},{160,128},{192,160},{224,1... | collective-permute-start | bytes 393224 | tf_op jit(solution)/shard_map/ppermute | solution.py:24
  99.4 9.9 %all-to-all-start.2 = ((f32[8,2,512]{2,1,0:T(2,128)}), f32[8,2,512]{2,1,0:T(2,128)S(1)}, u32[]{:S(2)}, u32[]{:S(2)}) async-start(f32[8,2,512]{2,1,0:T(2,128)} %pad_maximum_fusion.3.line_ref), calls=%async_computation.2 | async-start | bytes 65536 | tf_op jit(solution)/shard_map/all_to_all | solution.py:364
  111.8 7.4 %collective-permute-start.18 = (f32[128,256]{1,0:T(8,128)S(1)}, f32[128,256]{1,0:T(8,128)S(1)}, u32[]{:S(2)}, u32[]{:S(2)}) collective-permute-start(f32[128,256]{1,0:T(8,128)S(1)} %bitcast.90), channel_id=1, source_target_pairs={{0,1},{1,2},{2,3},{3,0},{4,5},{5,6},{6,7},{7,4},{8,9},{9,10},{10,1... | collective-permute-start | bytes 393224 | tf_op jit(solution)/shard_map/ppermute | solution.py:24
  112.5 6.8 %collective-permute-start.20 = (f32[128,256]{1,0:T(8,128)S(1)}, f32[128,256]{1,0:T(8,128)S(1)}, u32[]{:S(2)}, u32[]{:S(2)}) collective-permute-start(f32[128,256]{1,0:T(8,128)S(1)} %bitcast.89), channel_id=1, source_target_pairs={{0,3},{1,0},{2,1},{3,2},{4,7},{5,4},{6,5},{7,6},{8,11},{9,8},{10,9... | collective-permute-start | bytes 393224 | tf_op jit(solution)/shard_map/ppermute | solution.py:24
  120.1 26.6 %copy-start.1 = (f32[1,1024,256]{2,1,0:T(8,128)S(1)}, f32[1,1024,256]{2,1,0:T(8,128)}, u32[]{:S(2)}) copy-start(f32[1,1024,256]{2,1,0:T(8,128)} %param.13) | copy-start | bytes 3145732
  120.2 7.7 %collective-permute-start.19 = (f32[256,256]{1,0:T(8,128)S(1)}, f32[256,256]{1,0:T(8,128)}, u32[]{:S(2)}, u32[]{:S(2)}) collective-permute-start(f32[256,256]{1,0:T(8,128)S(1)} %pad_maximum_fusion), channel_id=1, source_target_pairs={{0,1},{1,2},{2,3},{3,0},{4,5},{5,6},{6,7},{7,4},{8,9},{9,10},{10,1... | collective-permute-start | bytes 786440 | tf_op jit(solution)/shard_map/ppermute | solution.py:24
  122.7 8.7 %collective-permute-start.21 = (f32[256,256]{1,0:T(8,128)}, f32[256,256]{1,0:T(8,128)}, u32[]{:S(2)}, u32[]{:S(2)}) collective-permute-start(f32[256,256]{1,0:T(8,128)} %pad_maximum_fusion.1), channel_id=1, source_target_pairs={{0,3},{1,0},{2,1},{3,2},{4,7},{5,4},{6,5},{7,6},{8,11},{9,8},{10,9... | collective-permute-start | bytes 786440 | tf_op jit(solution)/shard_map/ppermute | solution.py:24
  132.5 6.6 %collective-permute-start.23 = (f32[256,256]{1,0:T(8,128)S(1)}, f32[256,256]{1,0:T(8,128)S(1)}, u32[]{:S(2)}, u32[]{:S(2)}) collective-permute-start(f32[256,256]{1,0:T(8,128)S(1)} %fusion.1.own), channel_id=1, source_target_pairs={{0,1},{1,2},{2,3},{3,0},{4,5},{5,6},{6,7},{7,4},{8,9},{9,10},{10,1... | collective-permute-start | bytes 786440 | tf_op jit(solution)/shard_map/ppermute | solution.py:24
  132.6 7.8 %collective-permute-start.22 = (f32[256,256]{1,0:T(8,128)S(1)}, f32[256,256]{1,0:T(8,128)S(1)}, u32[]{:S(2)}, u32[]{:S(2)}) collective-permute-start(f32[256,256]{1,0:T(8,128)S(1)} %fusion.1.own), channel_id=1, source_target_pairs={{0,3},{1,0},{2,1},{3,2},{4,7},{5,4},{6,5},{7,6},{8,11},{9,8},{10,9... | collective-permute-start | bytes 786440 | tf_op jit(solution)/shard_map/ppermute | solution.py:24
  139.1 5.0 %collective-permute-start.24 = (f32[128,256]{1,0:T(8,128)S(1)}, f32[128,256]{1,0:T(8,128)S(1)}, u32[]{:S(2)}, u32[]{:S(2)}) collective-permute-start(f32[128,256]{1,0:T(8,128)S(1)} %slice.109), channel_id=1, source_target_pairs={{0,1},{1,2},{2,3},{3,0},{4,5},{5,6},{6,7},{7,4},{8,9},{9,10},{10,1... | collective-permute-start | bytes 393224 | tf_op jit(solution)/shard_map/ppermute | solution.py:24
  140.4 6.3 %collective-permute-start.25 = (f32[128,256]{1,0:T(8,128)S(1)}, f32[128,256]{1,0:T(8,128)S(1)}, u32[]{:S(2)}, u32[]{:S(2)}) collective-permute-start(f32[128,256]{1,0:T(8,128)S(1)} %slice.110), channel_id=1, source_target_pairs={{0,3},{1,0},{2,1},{3,2},{4,7},{5,4},{6,5},{7,6},{8,11},{9,8},{10,9... | collective-permute-start | bytes 393224 | tf_op jit(solution)/shard_map/ppermute | solution.py:24
  (11 other events, 73.8 us)
Sparse Core Ops, SparseCore 0:
  10.5 37.5 all-gather.1
  99.5 40.6 reduce-scatter.1

commit v9 on v8

--- a/solution.py
+++ b/solution.py
@@ -52,7 +52,7 @@
         grid_spec=pltpu.PrefetchScalarGridSpec(
             num_scalar_prefetch=1,
             grid=(1,),
-            in_specs=[pl.BlockSpec(shape, lambda j, blk: (0, 0, 0))] * len(sources),
+            in_specs=[pl.BlockSpec(v.shape, lambda j, blk: (0, 0, 0)) for v in sources],
             out_specs=pl.BlockSpec(out.shape, lambda j, blk: (0, 0, 0)),
         ),
         out_shape=out,
@@ -182,16 +182,21 @@
         c = jnp.where(tile_ids(start, s.shape) == tgt, e - 1.0, e).astype(BF16)
         part = jnp.dot(c, q, preferred_element_type=F32)
         total = part if total is None else total + part
-    cut = t_ref.shape[0] // len(outs)
-    for n, out in enumerate(outs):
-        out[0] = total[n * cut:(n + 1) * cut]
+    pieces = t_ref.shape[0] // outs[0].shape[0]
+    for place in range(len(outs) // pieces):
+
+        @pl.when(pl.program_id(0) == place)
+        def _():
+            for n in range(pieces):
+                out = outs[place * pieces + n]
+                out[...] = total[n * out.shape[0]:(n + 1) * out.shape[0]]
 
 
 def item_parts(places, pieces, x, rows, lines, table16, quarters):
     count, width, features = rows.shape
     span = table16.shape[0] // quarters
     share = len(places)
-    out = jax.ShapeDtypeStruct((share, span // pieces, features), F32)
+    out = jax.ShapeDtypeStruct((span // pieces, features), F32)
     return pl.pallas_call(
         item_kernel,
         grid_spec=pltpu.PrefetchScalarGridSpec(
@@ -202,9 +207,9 @@
                 pl.BlockSpec(lines.shape, lambda i, o: (0, 0, 0)),
                 pl.BlockSpec((span, features), lambda i, o: (o[i], 0)),
             ],
-            out_specs=[pl.BlockSpec((1,) + out.shape[1:], lambda i, o: (i, 0, 0))] * pieces,
-        ),
-        out_shape=[out] * pieces,
+            out_specs=[pl.BlockSpec(out.shape, lambda i, o: (0, 0))] * (share * pieces),
+        ),
+        out_shape=[out] * (share * pieces),
         compiler_params=pltpu.CompilerParams(vmem_limit_bytes=SMALL),
         cost_estimate=pl.CostEstimate(
             flops=4 * share * span * count * width * features,
@@ -215,11 +220,10 @@
     )((jnp.array(places, jnp.int32) + x) % quarters, rows, lines, table16)
 
 
-def update_kernel(x_ref, own, after, before, far_a, far_b, g_ref, t_ref, a_ref, ng_ref, nt_ref, na_ref):
+def update_kernel(x_ref, own, after, before, far_a, far_b, t_ref, a_ref, nt_ref, na_ref):
     quarters = pl.num_programs(0)
     rel = lax.rem(pl.program_id(0) - x_ref[0] + quarters, quarters)
     cut = far_a.shape[0]
-    ng_ref[...] = g_ref[...].astype(F32)
 
     def write(start, summed):
         span = pl.ds(start, summed.shape[0])
@@ -239,25 +243,23 @@
         write(cut, far_b[...])
 
 
-def update(x, own, after, before, far_a, far_b, grads, table, accum, quarters):
+def update(x, own, after, before, far_a, far_b, table, accum, quarters):
     items, features = table.shape
     whole = pl.BlockSpec(own.shape, lambda i, x: (0, 0))
     part = pl.BlockSpec(far_a.shape, lambda i, x: (0, 0))
     block = pl.BlockSpec((items // quarters, features), lambda i, x: (i, 0))
-    piece = pl.BlockSpec((grads.shape[0] // quarters, features), lambda i, x: (i, 0))
     return pl.pallas_call(
         update_kernel,
         grid_spec=pltpu.PrefetchScalarGridSpec(
             num_scalar_prefetch=1,
             grid=(quarters,),
-            in_specs=[whole] * 3 + [part] * 2 + [piece] + [block] * 2,
-            out_specs=[piece] + [block] * 2,
-        ),
-        out_shape=[jax.ShapeDtypeStruct(grads.shape, F32)]
-        + [jax.ShapeDtypeStruct(table.shape, F32)] * 2,
+            in_specs=[whole] * 3 + [part] * 2 + [block] * 2,
+            out_specs=[block] * 2,
+        ),
+        out_shape=[jax.ShapeDtypeStruct(table.shape, F32)] * 2,
         compiler_params=pltpu.CompilerParams(vmem_limit_bytes=SMALL),
         name="update",
-    )(x, own, after, before, far_a, far_b, grads, table, accum)
+    )(x, own, after, before, far_a, far_b, table, accum)
 
 
 def local(queries, clusters, positives, owner_of, table, accum):
@@ -275,15 +277,6 @@
 
     tables = lax.all_gather(table[0].astype(BF16), PLANE)
 
-    here = queries.reshape(2, block_count // 2, block_rows, features)
-    by_source = [[None] * 2 for _ in range(z_size)]
-    for half in range(2):
-        right = left = by_source[0][half] = here[half]
-        for hop in range(1, z_size // 2 + 1):
-            right = by_source[z_size - hop][half] = shift(right, "z", 1)
-            if hop < z_size // 2:
-                left = by_source[hop][half] = shift(left, "z", -1)
-
     flat_lists = clusters.reshape(pair_count)
     catalog_ids = jnp.arange(owners, dtype=jnp.int32)
     lookup = flat_lists[:, None] == catalog_ids[None, :]
@@ -294,38 +287,41 @@
     )
     rank_in = jnp.sum(earlier.astype(jnp.int32), axis=1)
     slot_of_pair = destination * MOST + rank_in
-    slot_count = owners * MOST
-    matches = slot_of_pair[None, :] == jnp.arange(slot_count, dtype=jnp.int32)[:, None]
-    filled = jnp.any(matches, axis=1)
-    source_pair = jnp.sum(jnp.where(matches, pair_ids[None, :], 0), axis=1)
-    which_block = source_pair // picks
-    which_pick = source_pair % picks
-    chosen = positives.reshape(block_count, block_rows)[which_block]
-    inside = filled[:, None] & (chosen // items == which_pick[:, None])
-    send_targets = jnp.where(inside, chosen - which_pick[:, None] * items, -1)
-    block_or_none = jnp.where(filled, which_block, -1)
-    per_plane = plane * MOST
-    meta = jnp.concatenate(
-        [
-            send_targets.reshape(z_size, per_plane * block_rows),
-            block_or_none.reshape(z_size, per_plane),
-            jnp.broadcast_to(slot_of_pair[None, :], (z_size, pair_count)),
-        ],
-        axis=1,
-    )
-    meta, _ = lax.optimization_barrier((meta, by_source[5][0]))
-    got = lax.all_to_all(meta, "z", 0, 0, tiled=True)
+    digits = jnp.stack([positives // 64, positives % 64]).reshape(-1, features)
+    extra = jnp.concatenate([digits, jnp.pad(slot_of_pair, (0, features - pair_count))[None]])
+    digit_rows = digits.shape[0] // 2
+    extra = jnp.pad(extra, ((0, block_rows - extra.shape[0]), (0, 0))).astype(BF16)
+    half_rows = local_rows // 2
+    halves = [queries[:half_rows], jnp.concatenate([queries[half_rows:], extra])]
+    by_source = [[None] * 2 for _ in range(z_size)]
+    for half in range(2):
+        right = left = halves[half].reshape(-1, block_rows, features)
+        by_source[0][half] = right
+        for hop in range(1, z_size // 2 + 1):
+            right = by_source[z_size - hop][half] = shift(right, "z", 1)
+            if hop < z_size // 2:
+                left = by_source[hop][half] = shift(left, "z", -1)
+
+    carried = jnp.stack([pair[1][-1, :2 * digit_rows + 1] for pair in by_source])
+    carried = carried.astype(F32).astype(jnp.int32)
+    pair_slot = carried[:, 2 * digit_rows, :pair_count]
+    chosen = carried[:, :digit_rows] * 64 + carried[:, digit_rows:2 * digit_rows]
+    chosen = chosen.reshape(z_size * block_count, block_rows)
     order = jnp.arange(z_size, dtype=jnp.int32)
-    got = got[(z + order) % z_size]
     width = z_size * MOST * block_rows
-    cut = per_plane * block_rows
-    targets = got[:, :cut].reshape(z_size, plane, MOST, block_rows)
-    targets = targets.transpose(1, 0, 2, 3).reshape(plane, 1, width)
-    named = got[:, cut:cut + per_plane].reshape(z_size, plane, MOST).transpose(1, 0, 2)
-    named = named.reshape(plane * per_plane)
+    wanted = (z * plane + jnp.arange(plane, dtype=jnp.int32)[:, None]) * MOST
+    wanted = (wanted + jnp.arange(MOST, dtype=jnp.int32)[None, :]).reshape(plane, 1, MOST, 1)
+    matches = pair_slot[None, :, None, :] == wanted
+    pair = jnp.max(jnp.where(matches, pair_ids, -1), axis=3)
+    named = jnp.where(pair < 0, -1, pair // picks)
     blk = jnp.maximum(named, 0)
-
-    pair_slot = got[:, cut + per_plane:]
+    chosen = chosen[(blk + (order * block_count)[None, :, None]).reshape(-1)]
+    start = (pair % picks * items).reshape(-1, 1)
+    inside = (named.reshape(-1, 1) >= 0) & (chosen >= start) & (chosen < start + items)
+    targets = jnp.where(inside, chosen - start, -1).reshape(plane, 1, width)
+    named = named.reshape(-1)
+    blk = blk.reshape(-1)
+
     pair_owner = pair_slot // MOST
     pair_from = (pair_owner // plane - z) % z_size
     pair_place = (order[:, None] - pair_from) % z_size
@@ -341,7 +337,7 @@
     even = jnp.stack([stats] + [shift(stats, "z", -e) for e in (2, 4, 6)])
     all_stats = jnp.stack([even, shift(even, "z", -1)]).reshape(z_size, 2, -1)
     part = all_stats[:, 0].reshape(-1, block_rows)[pair_row.reshape(-1)]
-    part, rows = lax.optimization_barrier((part, rows))
+    part, rows, own_table = lax.optimization_barrier((part, rows, own_table))
     part = part.reshape(z_size, block_count, picks, block_rows)
     pick = all_stats[:, 1].reshape(-1, block_rows)[pair_row[0]]
     pick = pick.reshape(block_count, picks, block_rows)
@@ -360,14 +356,12 @@
         packed, jnp.concatenate([blk, z.reshape(1)]), lines, tables, z_size, block_count, block_rows
     )
     grads, lines = lax.optimization_barrier((grads, lines))
-    grads = lax.psum_scatter(grads, "z").reshape(local_rows, features)
+    query_grads = lax.psum_scatter(grads, "z").astype(F32).reshape(local_rows, features)
     got_lines = lax.all_to_all(lines, PLANE, 0, 0, tiled=True)
 
     far_a, far_b = item_parts((2,), 2, x, rows, got_lines, own_table, x_size)
     far_a, far_b, got_lines = lax.optimization_barrier((far_a, far_b, got_lines))
-    (rest,) = item_parts((0, 1, 3), 1, x, rows, got_lines, own_table, x_size)
-    far_a, far_b = far_a[0], far_b[0]
-    own, after, before = rest[0], rest[1], rest[2]
+    own, after, before = item_parts((0, 1, 3), 1, x, rows, got_lines, own_table, x_size)
     half = far_a.shape[0]
     far_a = shift(far_a, "x", 1)
     far_b = shift(far_b, "x", -1)
@@ -378,8 +372,8 @@
     after = shift(own, "x", -1)
     far_a = shift(before[:half], "x", 1)
     far_b = shift(after[half:], "x", -1)
-    query_grads, new_table, new_accum = update(
-        x, own, after, before, far_a, far_b, grads, table[0], accum[0], x_size
+    new_table, new_accum = update(
+        x, own, after, before, far_a, far_b, table[0], accum[0], x_size
     )
     return (losses, query_grads, new_table[None], new_accum[None])
 

time: 157 us -> 161 us (1.025)
  waiting for transfers between devices: 42.4 us -> 48.9 us
  starting transfers between devices: 48.5 us -> 42.6 us
  other arithmetic: 10.4 us -> 13.9 us
    ppermute x26, waiting for transfers between devices: 35.5 us -> 43.4 us  [shift(): lax.ppermute(value, axis, [(i, (i + step) % size) for i in range(size)])]
    all_to_all x1 -> x0, starting transfers between devices: 5.48 us -> none  [local(): got = lax.all_to_all(meta, 'z', 0, 0, tiled=True)]
    all_to_all x1 -> x0, waiting for transfers between devices: 2.21 us -> none  [local(): got = lax.all_to_all(meta, 'z', 0, 0, tiled=True)]
    convert_element_type x0 -> x2, other arithmetic: none -> 1.79 us  [the longest x1 1.78 us: local(): lax.psum_scatter(grads, 'z').astype(F32).reshape(local_rows, features)]
    unnamed x28 -> x32, local copies, waits for them, and re-layouts: 3.12 us -> 1.36 us
  transfers between devices with their start and end apart: 31 -> 30, of which waited for: 15 -> 14; matrix products, arithmetic and copies ran while one was open for 10% -> 11% of each run, Pallas kernels for 11% -> 12%
where the time goes in v9:
time: 161 us; the launch traced here: 160 us
  waiting for transfers between devices  48.9 us (30%)
  starting transfers between devices  42.6 us (26%)
  Pallas kernels  29.2 us (18%)
  between operations  14.6 us (9%)
  other arithmetic  13.9 us (9%)
  local copies, waits for them, and re-layouts  10.9 us (7%)
    ppermute x26, waiting for transfers between devices, shift(): lax.ppermute(value, axis, [(i, (i + step) % size) for i in range(size)])  43.4 us
    ppermute x26, starting transfers between devices, shift(): lax.ppermute(value, axis, [(i, (i + step) % size) for i in range(size)])  34 us
    pallas_call x1, Pallas kernels, query_parts(): pl.pallas_call(query_kernel, grid_spec=pltpu.PrefetchScalarGridSpec(num_s...  9.94 us
    pallas_call x1, Pallas kernels, forward(): pl.pallas_call(forward_kernel, grid=(planes // per,), in_specs=[pl.BlockS...  8.1 us
    pallas_call x2, Pallas kernels, item_parts(): pl.pallas_call(item_kernel, grid_spec=pltpu.PrefetchScalarGridSpec(num_sc...  6.85 us
    all_to_all x1, waiting for transfers between devices, local(): got_lines = lax.all_to_all(lines, PLANE, 0, 0, tiled=True)  5.41 us
    all_to_all x1, starting transfers between devices, local(): rows = lax.all_to_all(packed, PLANE, 0, 0, tiled=True)  4.47 us
    all_to_all x1, starting transfers between devices, local(): got_lines = lax.all_to_all(lines, PLANE, 0, 0, tiled=True)  4.04 us
  transfers between devices with their start and end apart: 30, of which 14 were waited for; matrix products, arithmetic and copies ran while one was open for 11% of the time, Pallas kernels for 12%

profile of v9, /device:TPU:6, one launch (start us, length us, event | category | flops | bytes accessed | tf_op | source)
XLA Modules:
  0.0 160.0 jit_solution(13541335078620729379)
XLA Ops:
  7.3 2.1 %convert_element_type.38 = bf16[1,1024,256]{2,1,0:T(8,128)(2,1)} convert(f32[1,1024,256]{2,1,0:T(8,128)} %param.12) | non-fusion elementwise | flops 262144 | bytes 1572864 | tf_op jit(solution)/shard_map/convert_element_type | solution.py:278
  10.1 5.9 %collective-permute-start = (bf16[9,32,256]{2,1,0:T(8,128)(2,1)S(1)}, bf16[9,32,256]{2,1,0:T(8,128)(2,1)S(1)}, u32[]{:S(2)}, u32[]{:S(2)}) collective-permute-start(bf16[9,32,256]{2,1,0:T(8,128)(2,1)S(1)} %bitcast.39), channel_id=1, source_target_pairs={{0,224},{32,0},{64,32},{96,64},{128,96},{160,128},{192,160},{224,1... | collective-permute-start | bytes 442376 | tf_op jit(solution)/shard_map/ppermute | solution.py:24
  16.1 3.3 %collective-permute-start.7 = (bf16[8,32,256]{2,1,0:T(8,128)(2,1)S(1)}, bf16[8,32,256]{2,1,0:T(8,128)(2,1)S(1)}, u32[]{:S(2)}, u32[]{:S(2)}) collective-permute-start(bf16[8,32,256]{2,1,0:T(8,128)(2,1)S(1)} %bitcast.44), channel_id=1, source_target_pairs={{0,224},{32,0},{64,32},{96,64},{128,96},{160,128},{192,160},{224,1... | collective-permute-start | bytes 393224 | tf_op jit(solution)/shard_map/ppermute | solution.py:24
  19.9 5.5 %collective-permute-done.10.refs_14_ = bf16[8,32,256]{2,1,0:T(8,128)(2,1)S(1)} collective-permute-done((bf16[8,32,256]{2,1,0:T(8,128)(2,1)S(1)}, bf16[8,32,256]{2,1,0:T(8,128)(2,1)S(1)}, u32[]{:S(2)}, u32[]{:S(2)}) %collective-permute-start.10) | collective-permute-done | bytes 131104 | tf_op jit(solution)/shard_map/ppermute | solution.py:24
  25.4 3.2 %collective-permute-start.8 = (bf16[8,32,256]{2,1,0:T(8,128)(2,1)S(1)}, bf16[8,32,256]{2,1,0:T(8,128)(2,1)S(1)}, u32[]{:S(2)}, u32[]{:S(2)}) collective-permute-start(bf16[8,32,256]{2,1,0:T(8,128)(2,1)S(1)} %collective-permute-done.7.refs_2_), channel_id=1, source_target_pairs={{0,224},{32,0},{64,32},{96,64},{128,96},{160,128},{192,160},{224,1... | collective-permute-start | bytes 393224 | tf_op jit(solution)/shard_map/ppermute | solution.py:24
  28.7 1.9 %collective-permute-start.4 = (bf16[9,32,256]{2,1,0:T(8,128)(2,1)S(1)}, bf16[9,32,256]{2,1,0:T(8,128)(2,1)S(1)}, u32[]{:S(2)}, u32[]{:S(2)}) collective-permute-start(bf16[9,32,256]{2,1,0:T(8,128)(2,1)S(1)} %collective-permute-done.3.refs_15_), channel_id=1, source_target_pairs={{0,32},{32,64},{64,96},{96,128},{128,160},{160,192},{192,224},{224... | collective-permute-start | bytes 442376 | tf_op jit(solution)/shard_map/ppermute | solution.py:24
  30.7 1.9 %collective-permute-done.11.refs_12_ = bf16[8,32,256]{2,1,0:T(8,128)(2,1)S(1)} collective-permute-done((bf16[8,32,256]{2,1,0:T(8,128)(2,1)S(1)}, bf16[8,32,256]{2,1,0:T(8,128)(2,1)S(1)}, u32[]{:S(2)}, u32[]{:S(2)}) %collective-permute-start.11) | collective-permute-done | bytes 131104 | tf_op jit(solution)/shard_map/ppermute | solution.py:24
  32.6 3.2 %collective-permute-start.9 = (bf16[8,32,256]{2,1,0:T(8,128)(2,1)S(1)}, bf16[8,32,256]{2,1,0:T(8,128)(2,1)S(1)}, u32[]{:S(2)}, u32[]{:S(2)}) collective-permute-start(bf16[8,32,256]{2,1,0:T(8,128)(2,1)S(1)} %collective-permute-done.8.refs_4_), channel_id=1, source_target_pairs={{0,224},{32,0},{64,32},{96,64},{128,96},{160,128},{192,160},{224,1... | collective-permute-start | bytes 393224 | tf_op jit(solution)/shard_map/ppermute | solution.py:24
  35.9 1.8 %collective-permute-start.2 = (bf16[9,32,256]{2,1,0:T(8,128)(2,1)S(1)}, bf16[9,32,256]{2,1,0:T(8,128)(2,1)S(1)}, u32[]{:S(2)}, u32[]{:S(2)}) collective-permute-start(bf16[9,32,256]{2,1,0:T(8,128)(2,1)S(1)} %collective-permute-done.1.refs_5_), channel_id=1, source_target_pairs={{0,224},{32,0},{64,32},{96,64},{128,96},{160,128},{192,160},{224,1... | collective-permute-start | bytes 442376 | tf_op jit(solution)/shard_map/ppermute | solution.py:24
  37.9 1.9 %collective-permute-done.12.refs_10_ = bf16[8,32,256]{2,1,0:T(8,128)(2,1)S(1)} collective-permute-done((bf16[8,32,256]{2,1,0:T(8,128)(2,1)S(1)}, bf16[8,32,256]{2,1,0:T(8,128)(2,1)S(1)}, u32[]{:S(2)}, u32[]{:S(2)}) %collective-permute-start.12) | collective-permute-done | bytes 131104 | tf_op jit(solution)/shard_map/ppermute | solution.py:24
  39.8 4.2 %collective-permute-done.5.refs_11_ = bf16[9,32,256]{2,1,0:T(8,128)(2,1)S(1)} collective-permute-done((bf16[9,32,256]{2,1,0:T(8,128)(2,1)S(1)}, bf16[9,32,256]{2,1,0:T(8,128)(2,1)S(1)}, u32[]{:S(2)}, u32[]{:S(2)}) %collective-permute-start.5) | collective-permute-done | bytes 147488 | tf_op jit(solution)/shard_map/ppermute | solution.py:24
  44.0 6.3 %collective-permute-done.6.refs_9_ = bf16[9,32,256]{2,1,0:T(8,128)(2,1)S(1)} collective-permute-done((bf16[9,32,256]{2,1,0:T(8,128)(2,1)S(1)}, bf16[9,32,256]{2,1,0:T(8,128)(2,1)S(1)}, u32[]{:S(2)}, u32[]{:S(2)}) %collective-permute-start.6) | collective-permute-done | bytes 147488 | tf_op jit(solution)/shard_map/ppermute | solution.py:24
  53.1 2.4 %pack.1.p_ref = bf16[8,512,256]{2,1,0:T(8,128)(2,1)} custom-call(s32[128]{0:T(128)S(1)} %fusion.41.blk, bf16[8,32,256]{2,1,0:T(8,128)(2,1)S(1)} %bitcast.45, bf16[9,32,256]{2,1,0:T(8,128)(2,1)S(1)} %bitcast.42, bf16[8,32,256]{2,1,0:T(8,128)(2,1)S(1)} %collective-permute-done.7.refs_2_, bf16[9,32,256]{2,1,0:T(8,128)(2,1)S(1)} %collective-permute-done.refs_3_, ...), custom_call_target="tpu_custom_call" | custom-call | bytes 4194304 | tf_op jit(solution)/shard_map/pack/pallas_call | solution.py:50
  55.4 4.5 %all-to-all-start = ((bf16[8,512,256]{2,1,0:T(8,128)(2,1)}), bf16[8,512,256]{2,1,0:T(8,128)(2,1)S(1)}, u32[]{:S(2)}, u32[]{:S(2)}) async-start(bf16[8,512,256]{2,1,0:T(8,128)(2,1)} %pack.1.p_ref), calls=%async_computation | async-start | bytes 4194304 | tf_op jit(solution)/shard_map/all_to_all | solution.py:334
  60.7 8.1 %forward.1 = f32[2,8,1,512]{3,2,1,0:T(1,128)} custom-call(bf16[8,512,256]{2,1,0:T(8,128)(2,1)} %pack.1.p_ref, bf16[8,1024,256]{2,1,0:T(8,128)(2,1)} %all-gather.2.cloned.1.call-done.t_ref, s32[8,1,512]{2,1,0:T(1,128)} %get-tuple-element.43.tgt_ref), custom_call_target="tpu_custom_call" | custom-call | flops 42949672960 | bytes 6291456 | tf_op jit(solution)/shard_map/forward/pallas_call | solution.py:95
  68.8 2.7 %collective-permute-start.15 = (f32[2,8,1,512]{3,2,1,0:T(1,128)}, f32[2,8,1,512]{3,2,1,0:T(1,128)S(1)}, u32[]{:S(2)}, u32[]{:S(2)}) collective-permute-start(f32[2,8,1,512]{3,2,1,0:T(1,128)} %forward.1), channel_id=1, source_target_pairs={{0,128},{32,160},{64,192},{96,224},{128,0},{160,32},{192,64},{224,... | collective-permute-start | bytes 98312 | tf_op jit(solution)/shard_map/ppermute | solution.py:24
  71.5 2.9 %collective-permute-start.16 = (f32[2,8,1,512]{3,2,1,0:T(1,128)}, f32[2,8,1,512]{3,2,1,0:T(1,128)S(1)}, u32[]{:S(2)}, u32[]{:S(2)}) collective-permute-start(f32[2,8,1,512]{3,2,1,0:T(1,128)} %forward.1), channel_id=1, source_target_pairs={{0,64},{32,96},{64,128},{96,160},{128,192},{160,224},{192,0},{224,... | collective-permute-start | bytes 98312 | tf_op jit(solution)/shard_map/ppermute | solution.py:24
  74.4 2.5 %collective-permute-done.15 = f32[2,8,1,512]{3,2,1,0:T(1,128)S(1)} collective-permute-done((f32[2,8,1,512]{3,2,1,0:T(1,128)}, f32[2,8,1,512]{3,2,1,0:T(1,128)S(1)}, u32[]{:S(2)}, u32[]{:S(2)}) %collective-permute-start.15) | collective-permute-done | bytes 32800 | tf_op jit(solution)/shard_map/ppermute | solution.py:24
  81.9 2.9 %collective-permute-done.17 = f32[4,2,8,1,512]{4,3,2,1,0:T(1,128)S(1)} collective-permute-done((f32[4,2,8,1,512]{4,3,2,1,0:T(1,128)S(1)}, f32[4,2,8,1,512]{4,3,2,1,0:T(1,128)S(1)}, u32[]{:S(2)}, u32[]{:S(2)}) %collective-permute-start.17) | collective-permute-done | bytes 131104 | tf_op jit(solution)/shard_map/ppermute | solution.py:24
  89.3 2.1 %gather_fusion.1 = f32[512,32]{1,0:T(8,128)S(1)} fusion(f32[1024,32]{1,0:T(8,128)} %reshape_squeeze.6, s32[1024]{0:T(1024)S(1)} %pad_clamp_fusion.2), kind=kCustom, calls=%fused_computation.1 | custom fusion | bytes 133120 | tf_op jit(solution)/shard_map/gather | solution.py:339
  93.3 9.9 %query_parts.1 = bf16[8,16,32,256]{3,2,1,0:T(8,128)(2,1)} custom-call(s32[129]{0:T(256)} %pad_add_fusion.blk, bf16[8,512,256]{2,1,0:T(8,128)(2,1)} %pack.1.p_ref, bf16[8,1024,256]{2,1,0:T(8,128)(2,1)} %all-gather.2.cloned.1.call-done.t_ref, f32[8,2,512]{2,1,0:T(2,128)} %pad_maximum_fusion.4.line_ref), custom_call_target="tpu_custom_call" | custom-call | flops 1048576 | bytes 1048576 | tf_op jit(solution)/shard_map/query_parts/pallas_call | solution.py:152
  103.3 4.0 %all-to-all-start.1 = ((f32[8,2,512]{2,1,0:T(2,128)}), f32[8,2,512]{2,1,0:T(2,128)S(1)}, u32[]{:S(2)}, u32[]{:S(2)}) async-start(f32[8,2,512]{2,1,0:T(2,128)} %pad_maximum_fusion.4.line_ref), calls=%async_computation.1 | async-start | bytes 65536 | tf_op jit(solution)/shard_map/all_to_all | solution.py:360
  107.3 5.4 %all-to-all-done.1.line_ref = f32[8,2,512]{2,1,0:T(2,128)S(1)} async-done(((f32[8,2,512]{2,1,0:T(2,128)}), f32[8,2,512]{2,1,0:T(2,128)S(1)}, u32[]{:S(2)}, u32[]{:S(2)}) %all-to-all-start.1) | async-done | bytes 32800 | tf_op jit(solution)/shard_map/all_to_all | solution.py:360
  117.5 5.3 %item_parts.3 = (f32[256,256]{1,0:T(8,128)S(1)}, f32[256,256]{1,0:T(8,128)S(1)}, f32[256,256]{1,0:T(8,128)S(1)}) custom-call(s32[3]{0:T(128)S(1)} %and_select_fusion.11.where, bf16[8,512,256]{2,1,0:T(8,128)(2,1)S(1)} %all-to-all-done.q_ref, f32[8,2,512]{2,1,0:T(2,128)S(1)} %all-to-all-done.1.line_ref, bf16[1024,256]{1,0:T(8,128)(2,1)S(1)} %copy-done.3), custom_call_target="tpu_custom_call" | custom-call | flops 3221225472 | bytes 3276800 | tf_op jit(solution)/shard_map/item_parts/pallas_call | solution.py:200
  122.9 1.8 %collective-permute-start.19 = (f32[256,256]{1,0:T(8,128)S(1)}, f32[256,256]{1,0:T(8,128)}, u32[]{:S(2)}, u32[]{:S(2)}) collective-permute-start(f32[256,256]{1,0:T(8,128)S(1)} %pad_maximum_fusion), channel_id=1, source_target_pairs={{0,1},{1,2},{2,3},{3,0},{4,5},{5,6},{6,7},{7,4},{8,9},{9,10},{10,1... | collective-permute-start | bytes 786440 | tf_op jit(solution)/shard_map/ppermute | solution.py:24
  127.4 3.2 %collective-permute-done.19 = f32[256,256]{1,0:T(8,128)} collective-permute-done((f32[256,256]{1,0:T(8,128)S(1)}, f32[256,256]{1,0:T(8,128)}, u32[]{:S(2)}, u32[]{:S(2)}) %collective-permute-start.19) | collective-permute-done | bytes 262176 | tf_op jit(solution)/shard_map/ppermute | solution.py:24
  130.6 3.6 %collective-permute-done.21 = f32[256,256]{1,0:T(8,128)} collective-permute-done((f32[256,256]{1,0:T(8,128)}, f32[256,256]{1,0:T(8,128)}, u32[]{:S(2)}, u32[]{:S(2)}) %collective-permute-start.21) | collective-permute-done | bytes 262176 | tf_op jit(solution)/shard_map/ppermute | solution.py:24
  135.3 2.0 %collective-permute-start.22 = (f32[256,256]{1,0:T(8,128)S(1)}, f32[256,256]{1,0:T(8,128)S(1)}, u32[]{:S(2)}, u32[]{:S(2)}) collective-permute-start(f32[256,256]{1,0:T(8,128)S(1)} %add_add_fusion.own), channel_id=1, source_target_pairs={{0,3},{1,0},{2,1},{3,2},{4,7},{5,4},{6,5},{7,6},{8,11},{9,8},{10,9... | collective-permute-start | bytes 786440 | tf_op jit(solution)/shard_map/ppermute | solution.py:24
  137.3 4.3 %collective-permute-done.23.before = f32[256,256]{1,0:T(8,128)S(1)} collective-permute-done((f32[256,256]{1,0:T(8,128)S(1)}, f32[256,256]{1,0:T(8,128)S(1)}, u32[]{:S(2)}, u32[]{:S(2)}) %collective-permute-start.23) | collective-permute-done | bytes 262176 | tf_op jit(solution)/shard_map/ppermute | solution.py:24
  144.0 2.8 %collective-permute-done.24.far_a = f32[128,256]{1,0:T(8,128)S(1)} collective-permute-done((f32[128,256]{1,0:T(8,128)S(1)}, f32[128,256]{1,0:T(8,128)S(1)}, u32[]{:S(2)}, u32[]{:S(2)}) %collective-permute-start.24) | collective-permute-done | bytes 131104 | tf_op jit(solution)/shard_map/ppermute | solution.py:24
  146.7 2.6 %collective-permute-done.25.far_b = f32[128,256]{1,0:T(8,128)S(1)} collective-permute-done((f32[128,256]{1,0:T(8,128)S(1)}, f32[128,256]{1,0:T(8,128)S(1)}, u32[]{:S(2)}, u32[]{:S(2)}) %collective-permute-start.25) | collective-permute-done | bytes 131104 | tf_op jit(solution)/shard_map/ppermute | solution.py:24
  149.4 2.0 %update.1 = (f32[1024,256]{1,0:T(8,128)}, f32[1024,256]{1,0:T(8,128)}) custom-call(s32[1]{0:T(128)} %bitcast.13.x_ref, f32[256,256]{1,0:T(8,128)S(1)} %add_add_fusion.own, f32[256,256]{1,0:T(8,128)S(1)} %collective-permute-done.22.after, f32[256,256]{1,0:T(8,128)S(1)} %collective-permute-done.23.before, f32[128,256]{1,0:T(8,128)S(1)} %collective-permute-done.24.far_a, ...), custom_call_target="tpu_custom_call" | custom-call | tf_op jit(solution)/shard_map/update/pallas_call | solution.py:251
  (157 shorter events, 29.0 us)
Async XLA Ops:
  7.2 53.5 %all-gather.2.cloned.1.call-start = ((), (), s32[]{:S(2)}) async-start(), calls=%async_computation.3 | async-start | bytes 4718592 | tf_op jit(solution)/shard_map/all_gather | solution.py:278
  10.1 18.5 %collective-permute-start = (bf16[9,32,256]{2,1,0:T(8,128)(2,1)S(1)}, bf16[9,32,256]{2,1,0:T(8,128)(2,1)S(1)}, u32[]{:S(2)}, u32[]{:S(2)}) collective-permute-start(bf16[9,32,256]{2,1,0:T(8,128)(2,1)S(1)} %bitcast.39), channel_id=1, source_target_pairs={{0,224},{32,0},{64,32},{96,64},{128,96},{160,128},{192,160},{224,1... | collective-permute-start | bytes 442376 | tf_op jit(solution)/shard_map/ppermute | solution.py:24
  16.1 12.7 %collective-permute-start.3 = (bf16[9,32,256]{2,1,0:T(8,128)(2,1)S(1)}, bf16[9,32,256]{2,1,0:T(8,128)(2,1)S(1)}, u32[]{:S(2)}, u32[]{:S(2)}) collective-permute-start(bf16[9,32,256]{2,1,0:T(8,128)(2,1)S(1)} %bitcast.40), channel_id=1, source_target_pairs={{0,32},{32,64},{64,96},{96,128},{128,160},{160,192},{192,224},{224... | collective-permute-start | bytes 442376 | tf_op jit(solution)/shard_map/ppermute | solution.py:24
  16.1 9.3 %collective-permute-start.10 = (bf16[8,32,256]{2,1,0:T(8,128)(2,1)S(1)}, bf16[8,32,256]{2,1,0:T(8,128)(2,1)S(1)}, u32[]{:S(2)}, u32[]{:S(2)}) collective-permute-start(bf16[8,32,256]{2,1,0:T(8,128)(2,1)S(1)} %bitcast.43), channel_id=1, source_target_pairs={{0,32},{32,64},{64,96},{96,128},{128,160},{160,192},{192,224},{224... | collective-permute-start | bytes 393224 | tf_op jit(solution)/shard_map/ppermute | solution.py:24
  16.1 9.3 %collective-permute-start.7 = (bf16[8,32,256]{2,1,0:T(8,128)(2,1)S(1)}, bf16[8,32,256]{2,1,0:T(8,128)(2,1)S(1)}, u32[]{:S(2)}, u32[]{:S(2)}) collective-permute-start(bf16[8,32,256]{2,1,0:T(8,128)(2,1)S(1)} %bitcast.44), channel_id=1, source_target_pairs={{0,224},{32,0},{64,32},{96,64},{128,96},{160,128},{192,160},{224,1... | collective-permute-start | bytes 393224 | tf_op jit(solution)/shard_map/ppermute | solution.py:24
  25.4 7.2 %collective-permute-start.11 = (bf16[8,32,256]{2,1,0:T(8,128)(2,1)S(1)}, bf16[8,32,256]{2,1,0:T(8,128)(2,1)S(1)}, u32[]{:S(2)}, u32[]{:S(2)}) collective-permute-start(bf16[8,32,256]{2,1,0:T(8,128)(2,1)S(1)} %collective-permute-done.10.refs_14_), channel_id=1, source_target_pairs={{0,32},{32,64},{64,96},{96,128},{128,160},{160,192},{192,224},{224... | collective-permute-start | bytes 393224 | tf_op jit(solution)/shard_map/ppermute | solution.py:24
  25.4 7.2 %collective-permute-start.8 = (bf16[8,32,256]{2,1,0:T(8,128)(2,1)S(1)}, bf16[8,32,256]{2,1,0:T(8,128)(2,1)S(1)}, u32[]{:S(2)}, u32[]{:S(2)}) collective-permute-start(bf16[8,32,256]{2,1,0:T(8,128)(2,1)S(1)} %collective-permute-done.7.refs_2_), channel_id=1, source_target_pairs={{0,224},{32,0},{64,32},{96,64},{128,96},{160,128},{192,160},{224,1... | collective-permute-start | bytes 393224 | tf_op jit(solution)/shard_map/ppermute | solution.py:24
  28.6 7.2 %collective-permute-start.1 = (bf16[9,32,256]{2,1,0:T(8,128)(2,1)S(1)}, bf16[9,32,256]{2,1,0:T(8,128)(2,1)S(1)}, u32[]{:S(2)}, u32[]{:S(2)}) collective-permute-start(bf16[9,32,256]{2,1,0:T(8,128)(2,1)S(1)} %collective-permute-done.refs_3_), channel_id=1, source_target_pairs={{0,224},{32,0},{64,32},{96,64},{128,96},{160,128},{192,160},{224,1... | collective-permute-start | bytes 442376 | tf_op jit(solution)/shard_map/ppermute | solution.py:24
  28.7 8.9 %collective-permute-start.4 = (bf16[9,32,256]{2,1,0:T(8,128)(2,1)S(1)}, bf16[9,32,256]{2,1,0:T(8,128)(2,1)S(1)}, u32[]{:S(2)}, u32[]{:S(2)}) collective-permute-start(bf16[9,32,256]{2,1,0:T(8,128)(2,1)S(1)} %collective-permute-done.3.refs_15_), channel_id=1, source_target_pairs={{0,32},{32,64},{64,96},{96,128},{128,160},{160,192},{192,224},{224... | collective-permute-start | bytes 442376 | tf_op jit(solution)/shard_map/ppermute | solution.py:24
  32.6 7.2 %collective-permute-start.12 = (bf16[8,32,256]{2,1,0:T(8,128)(2,1)S(1)}, bf16[8,32,256]{2,1,0:T(8,128)(2,1)S(1)}, u32[]{:S(2)}, u32[]{:S(2)}) collective-permute-start(bf16[8,32,256]{2,1,0:T(8,128)(2,1)S(1)} %collective-permute-done.11.refs_12_), channel_id=1, source_target_pairs={{0,32},{32,64},{64,96},{96,128},{128,160},{160,192},{192,224},{224... | collective-permute-start | bytes 393224 | tf_op jit(solution)/shard_map/ppermute | solution.py:24
  32.6 20.4 %collective-permute-start.9 = (bf16[8,32,256]{2,1,0:T(8,128)(2,1)S(1)}, bf16[8,32,256]{2,1,0:T(8,128)(2,1)S(1)}, u32[]{:S(2)}, u32[]{:S(2)}) collective-permute-start(bf16[8,32,256]{2,1,0:T(8,128)(2,1)S(1)} %collective-permute-done.8.refs_4_), channel_id=1, source_target_pairs={{0,224},{32,0},{64,32},{96,64},{128,96},{160,128},{192,160},{224,1... | collective-permute-start | bytes 393224 | tf_op jit(solution)/shard_map/ppermute | solution.py:24
  35.9 8.2 %collective-permute-start.2 = (bf16[9,32,256]{2,1,0:T(8,128)(2,1)S(1)}, bf16[9,32,256]{2,1,0:T(8,128)(2,1)S(1)}, u32[]{:S(2)}, u32[]{:S(2)}) collective-permute-start(bf16[9,32,256]{2,1,0:T(8,128)(2,1)S(1)} %collective-permute-done.1.refs_5_), channel_id=1, source_target_pairs={{0,224},{32,0},{64,32},{96,64},{128,96},{160,128},{192,160},{224,1... | collective-permute-start | bytes 442376 | tf_op jit(solution)/shard_map/ppermute | solution.py:24
  37.7 6.4 %collective-permute-start.5 = (bf16[9,32,256]{2,1,0:T(8,128)(2,1)S(1)}, bf16[9,32,256]{2,1,0:T(8,128)(2,1)S(1)}, u32[]{:S(2)}, u32[]{:S(2)}) collective-permute-start(bf16[9,32,256]{2,1,0:T(8,128)(2,1)S(1)} %collective-permute-done.4.refs_13_), channel_id=1, source_target_pairs={{0,32},{32,64},{64,96},{96,128},{128,160},{160,192},{192,224},{224... | collective-permute-start | bytes 442376 | tf_op jit(solution)/shard_map/ppermute | solution.py:24
  39.8 13.3 %collective-permute-start.13 = (bf16[8,32,256]{2,1,0:T(8,128)(2,1)S(1)}, bf16[8,32,256]{2,1,0:T(8,128)(2,1)S(1)}, u32[]{:S(2)}, u32[]{:S(2)}) collective-permute-start(bf16[8,32,256]{2,1,0:T(8,128)(2,1)S(1)} %collective-permute-done.12.refs_10_), channel_id=1, source_target_pairs={{0,32},{32,64},{64,96},{96,128},{128,160},{160,192},{192,224},{224... | collective-permute-start | bytes 393224 | tf_op jit(solution)/shard_map/ppermute | solution.py:24
  44.0 6.4 %collective-permute-start.6 = (bf16[9,32,256]{2,1,0:T(8,128)(2,1)S(1)}, bf16[9,32,256]{2,1,0:T(8,128)(2,1)S(1)}, u32[]{:S(2)}, u32[]{:S(2)}) collective-permute-start(bf16[9,32,256]{2,1,0:T(8,128)(2,1)S(1)} %collective-permute-done.5.refs_11_), channel_id=1, source_target_pairs={{0,32},{32,64},{64,96},{96,128},{128,160},{160,192},{192,224},{224... | collective-permute-start | bytes 442376 | tf_op jit(solution)/shard_map/ppermute | solution.py:24
  55.4 36.0 %all-to-all-start = ((bf16[8,512,256]{2,1,0:T(8,128)(2,1)}), bf16[8,512,256]{2,1,0:T(8,128)(2,1)S(1)}, u32[]{:S(2)}, u32[]{:S(2)}) async-start(bf16[8,512,256]{2,1,0:T(8,128)(2,1)} %pack.1.p_ref), calls=%async_computation | async-start | bytes 4194304 | tf_op jit(solution)/shard_map/all_to_all | solution.py:334
  59.9 91.5 %reduce-scatter.2.cloned.1.call-start = ((), (), s32[]{:S(2)}) async-start(), calls=%async_computation.4 | async-start | bytes 2359296 | tf_op jit(solution)/shard_map/reduce_scatter | solution.py:359
  60.7 19.3 %copy-start = (f32[1,1024,256]{2,1,0:T(8,128)S(1)}, f32[1,1024,256]{2,1,0:T(8,128)}, u32[]{:S(2)}) copy-start(f32[1,1024,256]{2,1,0:T(8,128)} %param.12) | copy-start | bytes 3145732
  68.8 5.6 %collective-permute-start.14 = (f32[2,8,1,512]{3,2,1,0:T(1,128)}, f32[2,8,1,512]{3,2,1,0:T(1,128)S(1)}, u32[]{:S(2)}, u32[]{:S(2)}) collective-permute-start(f32[2,8,1,512]{3,2,1,0:T(1,128)} %forward.1), channel_id=1, source_target_pairs={{0,192},{32,224},{64,0},{96,32},{128,64},{160,96},{192,128},{224,1... | collective-permute-start | bytes 98312 | tf_op jit(solution)/shard_map/ppermute | solution.py:24
  68.8 8.1 %collective-permute-start.15 = (f32[2,8,1,512]{3,2,1,0:T(1,128)}, f32[2,8,1,512]{3,2,1,0:T(1,128)S(1)}, u32[]{:S(2)}, u32[]{:S(2)}) collective-permute-start(f32[2,8,1,512]{3,2,1,0:T(1,128)} %forward.1), channel_id=1, source_target_pairs={{0,128},{32,160},{64,192},{96,224},{128,0},{160,32},{192,64},{224,... | collective-permute-start | bytes 98312 | tf_op jit(solution)/shard_map/ppermute | solution.py:24
  71.5 7.0 %collective-permute-start.16 = (f32[2,8,1,512]{3,2,1,0:T(1,128)}, f32[2,8,1,512]{3,2,1,0:T(1,128)S(1)}, u32[]{:S(2)}, u32[]{:S(2)}) collective-permute-start(f32[2,8,1,512]{3,2,1,0:T(1,128)} %forward.1), channel_id=1, source_target_pairs={{0,64},{32,96},{64,128},{96,160},{128,192},{160,224},{192,0},{224,... | collective-permute-start | bytes 98312 | tf_op jit(solution)/shard_map/ppermute | solution.py:24
  79.4 5.5 %collective-permute-start.17 = (f32[4,2,8,1,512]{4,3,2,1,0:T(1,128)S(1)}, f32[4,2,8,1,512]{4,3,2,1,0:T(1,128)S(1)}, u32[]{:S(2)}, u32[]{:S(2)}) collective-permute-start(f32[4,2,8,1,512]{4,3,2,1,0:T(1,128)S(1)} %pad_maximum_fusion.3), channel_id=1, source_target_pairs={{0,224},{32,0},{64,32},{96,64},{128,96},{160,128},{192,160},{224,1... | collective-permute-start | bytes 393224 | tf_op jit(solution)/shard_map/ppermute | solution.py:24
  103.3 9.5 %all-to-all-start.1 = ((f32[8,2,512]{2,1,0:T(2,128)}), f32[8,2,512]{2,1,0:T(2,128)S(1)}, u32[]{:S(2)}, u32[]{:S(2)}) async-start(f32[8,2,512]{2,1,0:T(2,128)} %pad_maximum_fusion.4.line_ref), calls=%async_computation.1 | async-start | bytes 65536 | tf_op jit(solution)/shard_map/all_to_all | solution.py:360
  115.4 7.4 %collective-permute-start.18 = (f32[128,256]{1,0:T(8,128)S(1)}, f32[128,256]{1,0:T(8,128)S(1)}, u32[]{:S(2)}, u32[]{:S(2)}) collective-permute-start(f32[128,256]{1,0:T(8,128)S(1)} %get-tuple-element.34), channel_id=1, source_target_pairs={{0,1},{1,2},{2,3},{3,0},{4,5},{5,6},{6,7},{7,4},{8,9},{9,10},{10,1... | collective-permute-start | bytes 393224 | tf_op jit(solution)/shard_map/ppermute | solution.py:24
  116.0 8.7 %collective-permute-start.20 = (f32[128,256]{1,0:T(8,128)S(1)}, f32[128,256]{1,0:T(8,128)S(1)}, u32[]{:S(2)}, u32[]{:S(2)}) collective-permute-start(f32[128,256]{1,0:T(8,128)S(1)} %get-tuple-element.36), channel_id=1, source_target_pairs={{0,3},{1,0},{2,1},{3,2},{4,7},{5,4},{6,5},{7,6},{8,11},{9,8},{10,9... | collective-permute-start | bytes 393224 | tf_op jit(solution)/shard_map/ppermute | solution.py:24
  122.9 26.5 %copy-start.1 = (f32[1,1024,256]{2,1,0:T(8,128)S(1)}, f32[1,1024,256]{2,1,0:T(8,128)}, u32[]{:S(2)}) copy-start(f32[1,1024,256]{2,1,0:T(8,128)} %param.13) | copy-start | bytes 3145732
  122.9 7.7 %collective-permute-start.19 = (f32[256,256]{1,0:T(8,128)S(1)}, f32[256,256]{1,0:T(8,128)}, u32[]{:S(2)}, u32[]{:S(2)}) collective-permute-start(f32[256,256]{1,0:T(8,128)S(1)} %pad_maximum_fusion), channel_id=1, source_target_pairs={{0,1},{1,2},{2,3},{3,0},{4,5},{5,6},{6,7},{7,4},{8,9},{9,10},{10,1... | collective-permute-start | bytes 786440 | tf_op jit(solution)/shard_map/ppermute | solution.py:24
  125.5 8.7 %collective-permute-start.21 = (f32[256,256]{1,0:T(8,128)}, f32[256,256]{1,0:T(8,128)}, u32[]{:S(2)}, u32[]{:S(2)}) collective-permute-start(f32[256,256]{1,0:T(8,128)} %pad_maximum_fusion.1), channel_id=1, source_target_pairs={{0,3},{1,0},{2,1},{3,2},{4,7},{5,4},{6,5},{7,6},{8,11},{9,8},{10,9... | collective-permute-start | bytes 786440 | tf_op jit(solution)/shard_map/ppermute | solution.py:24
  135.2 6.4 %collective-permute-start.23 = (f32[256,256]{1,0:T(8,128)S(1)}, f32[256,256]{1,0:T(8,128)S(1)}, u32[]{:S(2)}, u32[]{:S(2)}) collective-permute-start(f32[256,256]{1,0:T(8,128)S(1)} %add_add_fusion.own), channel_id=1, source_target_pairs={{0,1},{1,2},{2,3},{3,0},{4,5},{5,6},{6,7},{7,4},{8,9},{9,10},{10,1... | collective-permute-start | bytes 786440 | tf_op jit(solution)/shard_map/ppermute | solution.py:24
  135.3 7.8 %collective-permute-start.22 = (f32[256,256]{1,0:T(8,128)S(1)}, f32[256,256]{1,0:T(8,128)S(1)}, u32[]{:S(2)}, u32[]{:S(2)}) collective-permute-start(f32[256,256]{1,0:T(8,128)S(1)} %add_add_fusion.own), channel_id=1, source_target_pairs={{0,3},{1,0},{2,1},{3,2},{4,7},{5,4},{6,5},{7,6},{8,11},{9,8},{10,9... | collective-permute-start | bytes 786440 | tf_op jit(solution)/shard_map/ppermute | solution.py:24
  141.7 5.0 %collective-permute-start.24 = (f32[128,256]{1,0:T(8,128)S(1)}, f32[128,256]{1,0:T(8,128)S(1)}, u32[]{:S(2)}, u32[]{:S(2)}) collective-permute-start(f32[128,256]{1,0:T(8,128)S(1)} %slice.114), channel_id=1, source_target_pairs={{0,1},{1,2},{2,3},{3,0},{4,5},{5,6},{6,7},{7,4},{8,9},{9,10},{10,1... | collective-permute-start | bytes 393224 | tf_op jit(solution)/shard_map/ppermute | solution.py:24
  143.1 6.3 %collective-permute-start.25 = (f32[128,256]{1,0:T(8,128)S(1)}, f32[128,256]{1,0:T(8,128)S(1)}, u32[]{:S(2)}, u32[]{:S(2)}) collective-permute-start(f32[128,256]{1,0:T(8,128)S(1)} %slice.115), channel_id=1, source_target_pairs={{0,3},{1,0},{2,1},{3,2},{4,7},{5,4},{6,5},{7,6},{8,11},{9,8},{10,9... | collective-permute-start | bytes 393224 | tf_op jit(solution)/shard_map/ppermute | solution.py:24
  (9 other events, 25.4 us)
Sparse Core Ops, SparseCore 0:
  10.5 37.5 all-gather.1
  103.4 40.3 reduce-scatter.1

commit v10 on v8

--- a/solution.py
+++ b/solution.py
@@ -171,27 +171,33 @@
 
 def item_kernel(where, q_ref, line_ref, t_ref, *outs):
     start = where[pl.program_id(0)] * t_ref.shape[0]
+    table16 = t_ref[...].astype(BF16)
     total = None
     for source in range(q_ref.shape[0]):
         q = q_ref[source]
         line = line_ref[source]
         lse = line[0:1, :]
         tgt = line[1:2, :].astype(jnp.int32)
-        s = lax.dot_general(t_ref[...], q, NT, preferred_element_type=F32)
+        s = lax.dot_general(table16, q, NT, preferred_element_type=F32)
         e = jnp.exp(s - lse)
         c = jnp.where(tile_ids(start, s.shape) == tgt, e - 1.0, e).astype(BF16)
         part = jnp.dot(c, q, preferred_element_type=F32)
         total = part if total is None else total + part
-    cut = t_ref.shape[0] // len(outs)
-    for n, out in enumerate(outs):
-        out[0] = total[n * cut:(n + 1) * cut]
-
-
-def item_parts(places, pieces, x, rows, lines, table16, quarters):
+    pieces = t_ref.shape[0] // outs[0].shape[0]
+    for place in range(len(outs) // pieces):
+
+        @pl.when(pl.program_id(0) == place)
+        def _():
+            for n in range(pieces):
+                out = outs[place * pieces + n]
+                out[...] = total[n * out.shape[0]:(n + 1) * out.shape[0]]
+
+
+def item_parts(places, pieces, x, rows, lines, table, quarters):
     count, width, features = rows.shape
-    span = table16.shape[0] // quarters
+    span = table.shape[0] // quarters
     share = len(places)
-    out = jax.ShapeDtypeStruct((share, span // pieces, features), F32)
+    out = jax.ShapeDtypeStruct((span // pieces, features), F32)
     return pl.pallas_call(
         item_kernel,
         grid_spec=pltpu.PrefetchScalarGridSpec(
@@ -202,9 +208,9 @@
                 pl.BlockSpec(lines.shape, lambda i, o: (0, 0, 0)),
                 pl.BlockSpec((span, features), lambda i, o: (o[i], 0)),
             ],
-            out_specs=[pl.BlockSpec((1,) + out.shape[1:], lambda i, o: (i, 0, 0))] * pieces,
-        ),
-        out_shape=[out] * pieces,
+            out_specs=[pl.BlockSpec(out.shape, lambda i, o: (0, 0))] * (share * pieces),
+        ),
+        out_shape=[out] * (share * pieces),
         compiler_params=pltpu.CompilerParams(vmem_limit_bytes=SMALL),
         cost_estimate=pl.CostEstimate(
             flops=4 * share * span * count * width * features,
@@ -212,14 +218,13 @@
             transcendentals=share * span * count * width,
         ),
         name="item_parts",
-    )((jnp.array(places, jnp.int32) + x) % quarters, rows, lines, table16)
-
-
-def update_kernel(x_ref, own, after, before, far_a, far_b, g_ref, t_ref, a_ref, ng_ref, nt_ref, na_ref):
+    )((jnp.array(places, jnp.int32) + x) % quarters, rows, lines, table)
+
+
+def update_kernel(x_ref, own, after, before, far_a, far_b, t_ref, a_ref, nt_ref, na_ref):
     quarters = pl.num_programs(0)
     rel = lax.rem(pl.program_id(0) - x_ref[0] + quarters, quarters)
     cut = far_a.shape[0]
-    ng_ref[...] = g_ref[...].astype(F32)
 
     def write(start, summed):
         span = pl.ds(start, summed.shape[0])
@@ -239,25 +244,23 @@
         write(cut, far_b[...])
 
 
-def update(x, own, after, before, far_a, far_b, grads, table, accum, quarters):
+def update(x, own, after, before, far_a, far_b, table, accum, quarters):
     items, features = table.shape
     whole = pl.BlockSpec(own.shape, lambda i, x: (0, 0))
     part = pl.BlockSpec(far_a.shape, lambda i, x: (0, 0))
     block = pl.BlockSpec((items // quarters, features), lambda i, x: (i, 0))
-    piece = pl.BlockSpec((grads.shape[0] // quarters, features), lambda i, x: (i, 0))
     return pl.pallas_call(
         update_kernel,
         grid_spec=pltpu.PrefetchScalarGridSpec(
             num_scalar_prefetch=1,
             grid=(quarters,),
-            in_specs=[whole] * 3 + [part] * 2 + [piece] + [block] * 2,
-            out_specs=[piece] + [block] * 2,
-        ),
-        out_shape=[jax.ShapeDtypeStruct(grads.shape, F32)]
-        + [jax.ShapeDtypeStruct(table.shape, F32)] * 2,
+            in_specs=[whole] * 3 + [part] * 2 + [block] * 2,
+            out_specs=[block] * 2,
+        ),
+        out_shape=[jax.ShapeDtypeStruct(table.shape, F32)] * 2,
         compiler_params=pltpu.CompilerParams(vmem_limit_bytes=SMALL),
         name="update",
-    )(x, own, after, before, far_a, far_b, grads, table, accum)
+    )(x, own, after, before, far_a, far_b, table, accum)
 
 
 def local(queries, clusters, positives, owner_of, table, accum):
@@ -332,8 +335,6 @@
     pair_row = (pair_from % 2 * 4 + pair_from // 2) * plane + pair_owner % plane
     pair_row = (pair_row * z_size + pair_place) * MOST + pair_slot % MOST
 
-    own_table, blk = lax.optimization_barrier((table[0], blk))
-    own_table = own_table.astype(BF16)
     packed = pack([part for pair in by_source for part in pair], blk, plane)
     rows = lax.all_to_all(packed, PLANE, 0, 0, tiled=True)
     stats = forward(packed, targets, tables)
@@ -360,14 +361,14 @@
         packed, jnp.concatenate([blk, z.reshape(1)]), lines, tables, z_size, block_count, block_rows
     )
     grads, lines = lax.optimization_barrier((grads, lines))
-    grads = lax.psum_scatter(grads, "z").reshape(local_rows, features)
+    query_grads = lax.psum_scatter(grads, "z").astype(F32).reshape(local_rows, features)
     got_lines = lax.all_to_all(lines, PLANE, 0, 0, tiled=True)
 
-    far_a, far_b = item_parts((2,), 2, x, rows, got_lines, own_table, x_size)
+    far_a, far_b = item_parts((2,), 2, x, rows, got_lines, table[0], x_size)
     far_a, far_b, got_lines = lax.optimization_barrier((far_a, far_b, got_lines))
-    (rest,) = item_parts((0, 1, 3), 1, x, rows, got_lines, own_table, x_size)
-    far_a, far_b = far_a[0], far_b[0]
-    own, after, before = rest[0], rest[1], rest[2]
+    after, before = item_parts((1, 3), 1, x, rows, got_lines, table[0], x_size)
+    after, before, got_lines = lax.optimization_barrier((after, before, got_lines))
+    (own,) = item_parts((0,), 1, x, rows, got_lines, table[0], x_size)
     half = far_a.shape[0]
     far_a = shift(far_a, "x", 1)
     far_b = shift(far_b, "x", -1)
@@ -378,8 +379,8 @@
     after = shift(own, "x", -1)
     far_a = shift(before[:half], "x", 1)
     far_b = shift(after[half:], "x", -1)
-    query_grads, new_table, new_accum = update(
-        x, own, after, before, far_a, far_b, grads, table[0], accum[0], x_size
+    new_table, new_accum = update(
+        x, own, after, before, far_a, far_b, table[0], accum[0], x_size
     )
     return (losses, query_grads, new_table[None], new_accum[None])
 

time: 157 us -> 155 us (0.987)
  waiting for transfers between devices: 42.4 us -> 39.5 us
  other arithmetic: 10.4 us -> 12 us
    ppermute x26, waiting for transfers between devices: 35.5 us -> 31.6 us  [shift(): lax.ppermute(value, axis, [(i, (i + step) % size) for i in range(size)])]
    unnamed x28 -> x20, local copies, waits for them, and re-layouts: 3.12 us -> 0.28 us
    pallas_call x2 -> x3, Pallas kernels: 6.79 us -> 6.84 us  [item_parts(): pl.pallas_call(item_kernel, grid_spec=pltpu.PrefetchScalarGridSpec(num_sc...]
  transfers between devices with their start and end apart: 31 -> 31, of which waited for: 15 -> 15; matrix products, arithmetic and copies ran while one was open for 10% -> 11% of each run, Pallas kernels for 11% -> 13%
where the time goes in v10:
time: 155 us; the launch traced here: 154 us
  starting transfers between devices  48.4 us (31%)
  waiting for transfers between devices  39.5 us (25%)
  Pallas kernels  29.4 us (19%)
  between operations  14.6 us (9%)
  other arithmetic  12 us (8%)
  local copies, waits for them, and re-layouts  10.4 us (7%)
    ppermute x26, starting transfers between devices, shift(): lax.ppermute(value, axis, [(i, (i + step) % size) for i in range(size)])  34 us
    ppermute x26, waiting for transfers between devices, shift(): lax.ppermute(value, axis, [(i, (i + step) % size) for i in range(size)])  31.6 us
    pallas_call x1, Pallas kernels, query_parts(): pl.pallas_call(query_kernel, grid_spec=pltpu.PrefetchScalarGridSpec(num_s...  9.92 us
    pallas_call x1, Pallas kernels, forward(): pl.pallas_call(forward_kernel, grid=(planes // per,), in_specs=[pl.BlockS...  8.24 us
    pallas_call x3, Pallas kernels, item_parts(): pl.pallas_call(item_kernel, grid_spec=pltpu.PrefetchScalarGridSpec(num_sc...  6.84 us
    all_to_all x1, starting transfers between devices, local(): got = lax.all_to_all(meta, 'z', 0, 0, tiled=True)  5.48 us
    all_to_all x1, waiting for transfers between devices, local(): got_lines = lax.all_to_all(lines, PLANE, 0, 0, tiled=True)  5.41 us
    all_to_all x1, starting transfers between devices, local(): rows = lax.all_to_all(packed, PLANE, 0, 0, tiled=True)  4.47 us
  transfers between devices with their start and end apart: 31, of which 15 were waited for; matrix products, arithmetic and copies ran while one was open for 11% of the time, Pallas kernels for 13%

profile of v10, /device:TPU:6, one launch (start us, length us, event | category | flops | bytes accessed | tf_op | source)
XLA Modules:
  0.0 154.2 jit_solution(5852663962050777724)
XLA Ops:
  7.3 2.1 %convert_element_type.26 = bf16[1,1024,256]{2,1,0:T(8,128)(2,1)} convert(f32[1,1024,256]{2,1,0:T(8,128)} %param.13) | non-fusion elementwise | flops 262144 | bytes 1572864 | tf_op jit(solution)/shard_map/convert_element_type | solution.py:279
  9.4 2.0 %collective-permute-start = (bf16[8,32,256]{2,1,0:T(8,128)(2,1)S(1)}, bf16[8,32,256]{2,1,0:T(8,128)(2,1)S(1)}, u32[]{:S(2)}, u32[]{:S(2)}) collective-permute-start(bf16[8,32,256]{2,1,0:T(8,128)(2,1)S(1)} %bitcast.73), channel_id=1, source_target_pairs={{0,32},{32,64},{64,96},{96,128},{128,160},{160,192},{192,224},{224... | collective-permute-start | bytes 393224 | tf_op jit(solution)/shard_map/ppermute | solution.py:24
  11.4 4.0 %collective-permute-start.3 = (bf16[8,32,256]{2,1,0:T(8,128)(2,1)S(1)}, bf16[8,32,256]{2,1,0:T(8,128)(2,1)S(1)}, u32[]{:S(2)}, u32[]{:S(2)}) collective-permute-start(bf16[8,32,256]{2,1,0:T(8,128)(2,1)S(1)} %bitcast.74), channel_id=1, source_target_pairs={{0,224},{32,0},{64,32},{96,64},{128,96},{160,128},{192,160},{224,1... | collective-permute-start | bytes 393224 | tf_op jit(solution)/shard_map/ppermute | solution.py:24
  15.4 3.2 %collective-permute-start.4 = (bf16[8,32,256]{2,1,0:T(8,128)(2,1)S(1)}, bf16[8,32,256]{2,1,0:T(8,128)(2,1)S(1)}, u32[]{:S(2)}, u32[]{:S(2)}) collective-permute-start(bf16[8,32,256]{2,1,0:T(8,128)(2,1)S(1)} %bitcast.71), channel_id=1, source_target_pairs={{0,224},{32,0},{64,32},{96,64},{128,96},{160,128},{192,160},{224,1... | collective-permute-start | bytes 393224 | tf_op jit(solution)/shard_map/ppermute | solution.py:24
  21.7 6.5 %collective-permute-done.1.refs_12_ = bf16[8,32,256]{2,1,0:T(8,128)(2,1)S(1)} collective-permute-done((bf16[8,32,256]{2,1,0:T(8,128)(2,1)S(1)}, bf16[8,32,256]{2,1,0:T(8,128)(2,1)S(1)}, u32[]{:S(2)}, u32[]{:S(2)}) %collective-permute-start.1) | collective-permute-done | bytes 131104 | tf_op jit(solution)/shard_map/ppermute | solution.py:24
  28.3 3.3 %collective-permute-start.5 = (bf16[8,32,256]{2,1,0:T(8,128)(2,1)S(1)}, bf16[8,32,256]{2,1,0:T(8,128)(2,1)S(1)}, u32[]{:S(2)}, u32[]{:S(2)}) collective-permute-start(bf16[8,32,256]{2,1,0:T(8,128)(2,1)S(1)} %collective-permute-done.3.refs_2_), channel_id=1, source_target_pairs={{0,224},{32,0},{64,32},{96,64},{128,96},{160,128},{192,160},{224,1... | collective-permute-start | bytes 393224 | tf_op jit(solution)/shard_map/ppermute | solution.py:24
  31.7 1.9 %collective-permute-start.12 = (bf16[8,32,256]{2,1,0:T(8,128)(2,1)S(1)}, bf16[8,32,256]{2,1,0:T(8,128)(2,1)S(1)}, u32[]{:S(2)}, u32[]{:S(2)}) collective-permute-start(bf16[8,32,256]{2,1,0:T(8,128)(2,1)S(1)} %collective-permute-done.11.refs_13_), channel_id=1, source_target_pairs={{0,32},{32,64},{64,96},{96,128},{128,160},{160,192},{192,224},{224... | collective-permute-start | bytes 393224 | tf_op jit(solution)/shard_map/ppermute | solution.py:24
  35.4 5.5 %all-to-all-start = ((s32[8,1,592]{2,1,0:T(1,128)}), s32[8,1,592]{2,1,0:T(1,128)S(1)}, u32[]{:S(2)}, u32[]{:S(2)}) async-start(s32[8,1,592]{2,1,0:T(1,128)} %copy.47), calls=%async_computation | async-start | bytes 40960 | tf_op jit(solution)/shard_map/all_to_all | solution.py:320
  40.9 3.3 %collective-permute-start.7 = (bf16[8,32,256]{2,1,0:T(8,128)(2,1)S(1)}, bf16[8,32,256]{2,1,0:T(8,128)(2,1)S(1)}, u32[]{:S(2)}, u32[]{:S(2)}) collective-permute-start(bf16[8,32,256]{2,1,0:T(8,128)(2,1)S(1)} %collective-permute-done.5.refs_4_), channel_id=1, source_target_pairs={{0,224},{32,0},{64,32},{96,64},{128,96},{160,128},{192,160},{224,1... | collective-permute-start | bytes 393224 | tf_op jit(solution)/shard_map/ppermute | solution.py:24
  44.2 1.5 collective-permute-start.8
  46.2 2.4 %all-to-all-done = s32[8,1,592]{2,1,0:T(1,128)S(1)} async-done(((s32[8,1,592]{2,1,0:T(1,128)}), s32[8,1,592]{2,1,0:T(1,128)S(1)}, u32[]{:S(2)}, u32[]{:S(2)}) %all-to-all-start) | async-done | bytes 18976 | tf_op jit(solution)/shard_map/all_to_all | solution.py:320
  53.2 2.3 %pack.1.p_ref = bf16[8,512,256]{2,1,0:T(8,128)(2,1)} custom-call(s32[128]{0:T(128)S(1)} %max.12.blk, bf16[8,32,256]{2,1,0:T(8,128)(2,1)S(1)} %bitcast.75, bf16[8,32,256]{2,1,0:T(8,128)(2,1)S(1)} %bitcast.72, bf16[8,32,256]{2,1,0:T(8,128)(2,1)S(1)} %collective-permute-done.3.refs_2_, bf16[8,32,256]{2,1,0:T(8,128)(2,1)S(1)} %collective-permute-done.4.refs_3_, ...), custom_call_target="tpu_custom_call" | custom-call | bytes 4194304 | tf_op jit(solution)/shard_map/pack/pallas_call | solution.py:50
  55.6 4.5 %all-to-all-start.1 = ((bf16[8,512,256]{2,1,0:T(8,128)(2,1)}), bf16[8,512,256]{2,1,0:T(8,128)(2,1)S(1)}, u32[]{:S(2)}, u32[]{:S(2)}) async-start(bf16[8,512,256]{2,1,0:T(8,128)(2,1)} %pack.1.p_ref), calls=%async_computation.1 | async-start | bytes 4194304 | tf_op jit(solution)/shard_map/all_to_all | solution.py:339
  60.1 8.2 %forward.1 = f32[2,8,1,512]{3,2,1,0:T(1,128)} custom-call(bf16[8,512,256]{2,1,0:T(8,128)(2,1)} %pack.1.p_ref, bf16[8,1024,256]{2,1,0:T(8,128)(2,1)} %all-gather.2.cloned.1.call-done.t_ref, s32[8,1,512]{2,1,0:T(1,128)} %reshape.364.tgt_ref), custom_call_target="tpu_custom_call" | custom-call | flops 42949672960 | bytes 6291456 | tf_op jit(solution)/shard_map/forward/pallas_call | solution.py:95
  70.8 2.9 %collective-permute-start.16 = (f32[2,8,1,512]{3,2,1,0:T(1,128)}, f32[2,8,1,512]{3,2,1,0:T(1,128)S(1)}, u32[]{:S(2)}, u32[]{:S(2)}) collective-permute-start(f32[2,8,1,512]{3,2,1,0:T(1,128)} %forward.1), channel_id=1, source_target_pairs={{0,64},{32,96},{64,128},{96,160},{128,192},{160,224},{192,0},{224,... | collective-permute-start | bytes 98312 | tf_op jit(solution)/shard_map/ppermute | solution.py:24
  73.7 3.8 %collective-permute-done.15 = f32[2,8,1,512]{3,2,1,0:T(1,128)S(1)} collective-permute-done((f32[2,8,1,512]{3,2,1,0:T(1,128)}, f32[2,8,1,512]{3,2,1,0:T(1,128)S(1)}, u32[]{:S(2)}, u32[]{:S(2)}) %collective-permute-start.15) | collective-permute-done | bytes 32800 | tf_op jit(solution)/shard_map/ppermute | solution.py:24
  81.6 3.3 %collective-permute-done.17 = f32[4,2,8,1,512]{4,3,2,1,0:T(1,128)S(1)} collective-permute-done((f32[4,2,8,1,512]{4,3,2,1,0:T(1,128)S(1)}, f32[4,2,8,1,512]{4,3,2,1,0:T(1,128)S(1)}, u32[]{:S(2)}, u32[]{:S(2)}) %collective-permute-start.17) | collective-permute-done | bytes 131104 | tf_op jit(solution)/shard_map/ppermute | solution.py:24
  89.2 9.9 %query_parts.1 = bf16[8,16,32,256]{3,2,1,0:T(8,128)(2,1)} custom-call(s32[129]{0:T(256)} %pad_add_fusion.blk, bf16[8,512,256]{2,1,0:T(8,128)(2,1)} %pack.1.p_ref, bf16[8,1024,256]{2,1,0:T(8,128)(2,1)} %all-gather.2.cloned.1.call-done.t_ref, f32[8,2,512]{2,1,0:T(2,128)} %pad_maximum_fusion.3.line_ref), custom_call_target="tpu_custom_call" | custom-call | flops 1048576 | bytes 1048576 | tf_op jit(solution)/shard_map/query_parts/pallas_call | solution.py:152
  99.2 4.4 %all-to-all-start.2 = ((f32[8,2,512]{2,1,0:T(2,128)}), f32[8,2,512]{2,1,0:T(2,128)S(1)}, u32[]{:S(2)}, u32[]{:S(2)}) async-start(f32[8,2,512]{2,1,0:T(2,128)} %pad_maximum_fusion.3.line_ref), calls=%async_computation.2 | async-start | bytes 65536 | tf_op jit(solution)/shard_map/all_to_all | solution.py:365
  103.6 5.4 %all-to-all-done.2.line_ref = f32[8,2,512]{2,1,0:T(2,128)S(1)} async-done(((f32[8,2,512]{2,1,0:T(2,128)}), f32[8,2,512]{2,1,0:T(2,128)S(1)}, u32[]{:S(2)}, u32[]{:S(2)}) %all-to-all-start.2) | async-done | bytes 32800 | tf_op jit(solution)/shard_map/all_to_all | solution.py:365
  109.0 1.6 %item_parts.3 = (f32[128,256]{1,0:T(8,128)S(1)}, f32[128,256]{1,0:T(8,128)S(1)}) custom-call(s32[1]{0:T(128)S(6)} %select_n.198.where, bf16[8,512,256]{2,1,0:T(8,128)(2,1)S(1)} %all-to-all-done.1.q_ref, f32[8,2,512]{2,1,0:T(2,128)S(1)} %all-to-all-done.2.line_ref, f32[1024,256]{1,0:T(8,128)S(1)} %bitcast.65), custom_call_target="tpu_custom_call" | custom-call | flops 1073741824 | bytes 2490368 | tf_op jit(solution)/shard_map/item_parts/pallas_call | solution.py:201
  111.1 1.6 %collective-permute-start.20 = (f32[128,256]{1,0:T(8,128)S(1)}, f32[128,256]{1,0:T(8,128)S(1)}, u32[]{:S(2)}, u32[]{:S(2)}) collective-permute-start(f32[128,256]{1,0:T(8,128)S(1)} %get-tuple-element.36), channel_id=1, source_target_pairs={{0,3},{1,0},{2,1},{3,2},{4,7},{5,4},{6,5},{7,6},{8,11},{9,8},{10,9... | collective-permute-start | bytes 393224 | tf_op jit(solution)/shard_map/ppermute | solution.py:24
  112.7 3.7 %item_parts.4 = (f32[256,256]{1,0:T(8,128)S(1)}, f32[256,256]{1,0:T(8,128)S(1)}) custom-call(s32[2]{0:T(128)S(1)} %and_select_fusion.where, bf16[8,512,256]{2,1,0:T(8,128)(2,1)S(1)} %all-to-all-done.1.q_ref, f32[8,2,512]{2,1,0:T(2,128)S(1)} %all-to-all-done.2.line_ref, f32[1024,256]{1,0:T(8,128)S(1)} %bitcast.66), custom_call_target="tpu_custom_call" | custom-call | flops 2147483648 | bytes 2883584 | tf_op jit(solution)/shard_map/item_parts/pallas_call | solution.py:201
  121.9 1.6 %gather_fusion.4 = f32[64,32]{1,0:T(8,128)S(1)} fusion(f32[1024,32]{1,0:T(8,128)} %reshape_squeeze.7, s32[1024]{0:T(1024)S(1)} %pad_clamp_fusion), kind=kCustom, calls=%fused_computation.4 | custom fusion | bytes 16640 | tf_op jit(solution)/shard_map/gather | solution.py:347
  124.3 1.6 %item_parts.5 = f32[256,256]{1,0:T(8,128)S(1)} custom-call(s32[1]{0:T(128)S(6)} %select_n.176.where, bf16[8,512,256]{2,1,0:T(8,128)(2,1)S(1)} %all-to-all-done.1.q_ref, f32[8,2,512]{2,1,0:T(2,128)S(1)} %all-to-all-done.2.line_ref, f32[1024,256]{1,0:T(8,128)S(1)} %bitcast.67), custom_call_target="tpu_custom_call" | custom-call | flops 1073741824 | bytes 2490368 | tf_op jit(solution)/shard_map/item_parts/pallas_call | solution.py:201
  125.9 2.4 %collective-permute-done.21 = f32[256,256]{1,0:T(8,128)} collective-permute-done((f32[256,256]{1,0:T(8,128)}, f32[256,256]{1,0:T(8,128)}, u32[]{:S(2)}, u32[]{:S(2)}) %collective-permute-start.21) | collective-permute-done | bytes 262176 | tf_op jit(solution)/shard_map/ppermute | solution.py:24
  129.5 2.0 %collective-permute-start.22 = (f32[256,256]{1,0:T(8,128)S(1)}, f32[256,256]{1,0:T(8,128)S(1)}, u32[]{:S(2)}, u32[]{:S(2)}) collective-permute-start(f32[256,256]{1,0:T(8,128)S(1)} %add_add_fusion.own), channel_id=1, source_target_pairs={{0,3},{1,0},{2,1},{3,2},{4,7},{5,4},{6,5},{7,6},{8,11},{9,8},{10,9... | collective-permute-start | bytes 786440 | tf_op jit(solution)/shard_map/ppermute | solution.py:24
  131.5 4.3 %collective-permute-done.23.before = f32[256,256]{1,0:T(8,128)S(1)} collective-permute-done((f32[256,256]{1,0:T(8,128)S(1)}, f32[256,256]{1,0:T(8,128)S(1)}, u32[]{:S(2)}, u32[]{:S(2)}) %collective-permute-start.23) | collective-permute-done | bytes 262176 | tf_op jit(solution)/shard_map/ppermute | solution.py:24
  138.1 2.8 %collective-permute-done.24.far_a = f32[128,256]{1,0:T(8,128)S(1)} collective-permute-done((f32[128,256]{1,0:T(8,128)S(1)}, f32[128,256]{1,0:T(8,128)S(1)}, u32[]{:S(2)}, u32[]{:S(2)}) %collective-permute-start.24) | collective-permute-done | bytes 131104 | tf_op jit(solution)/shard_map/ppermute | solution.py:24
  140.9 2.7 %collective-permute-done.25.far_b = f32[128,256]{1,0:T(8,128)S(1)} collective-permute-done((f32[128,256]{1,0:T(8,128)S(1)}, f32[128,256]{1,0:T(8,128)S(1)}, u32[]{:S(2)}, u32[]{:S(2)}) %collective-permute-start.25) | collective-permute-done | bytes 131104 | tf_op jit(solution)/shard_map/ppermute | solution.py:24
  143.5 2.0 %update.1 = (f32[1024,256]{1,0:T(8,128)}, f32[1024,256]{1,0:T(8,128)}) custom-call(s32[1]{0:T(128)} %bitcast.x_ref, f32[256,256]{1,0:T(8,128)S(1)} %add_add_fusion.own, f32[256,256]{1,0:T(8,128)S(1)} %collective-permute-done.22.after, f32[256,256]{1,0:T(8,128)S(1)} %collective-permute-done.23.before, f32[128,256]{1,0:T(8,128)S(1)} %collective-permute-done.24.far_a, ...), custom_call_target="tpu_custom_call" | custom-call | tf_op jit(solution)/shard_map/update/pallas_call | solution.py:252
  145.6 1.8 %bitcast_convert_fusion = f32[512,256]{1,0:T(8,128)} fusion(bf16[1,16,32,256]{3,2,1,0:T(8,128)(2,1)} %reduce-scatter.2.cloned.1.call-done), kind=kLoop, calls=%fused_computation.8 | loop fusion | flops 131072 | bytes 786432 | tf_op jit(solution)/shard_map/convert_element_type | solution.py:364
  (147 shorter events, 31.0 us)
Async XLA Ops:
  7.2 52.9 %all-gather.2.cloned.1.call-start = ((), (), s32[]{:S(2)}) async-start(), calls=%async_computation.4 | async-start | bytes 4718592 | tf_op jit(solution)/shard_map/all_gather | solution.py:279
  9.4 11.7 %collective-permute-start = (bf16[8,32,256]{2,1,0:T(8,128)(2,1)S(1)}, bf16[8,32,256]{2,1,0:T(8,128)(2,1)S(1)}, u32[]{:S(2)}, u32[]{:S(2)}) collective-permute-start(bf16[8,32,256]{2,1,0:T(8,128)(2,1)S(1)} %bitcast.73), channel_id=1, source_target_pairs={{0,32},{32,64},{64,96},{96,128},{128,160},{160,192},{192,224},{224... | collective-permute-start | bytes 393224 | tf_op jit(solution)/shard_map/ppermute | solution.py:24
  11.4 16.8 %collective-permute-start.3 = (bf16[8,32,256]{2,1,0:T(8,128)(2,1)S(1)}, bf16[8,32,256]{2,1,0:T(8,128)(2,1)S(1)}, u32[]{:S(2)}, u32[]{:S(2)}) collective-permute-start(bf16[8,32,256]{2,1,0:T(8,128)(2,1)S(1)} %bitcast.74), channel_id=1, source_target_pairs={{0,224},{32,0},{64,32},{96,64},{128,96},{160,128},{192,160},{224,1... | collective-permute-start | bytes 393224 | tf_op jit(solution)/shard_map/ppermute | solution.py:24
  15.4 6.2 %collective-permute-start.10 = (bf16[8,32,256]{2,1,0:T(8,128)(2,1)S(1)}, bf16[8,32,256]{2,1,0:T(8,128)(2,1)S(1)}, u32[]{:S(2)}, u32[]{:S(2)}) collective-permute-start(bf16[8,32,256]{2,1,0:T(8,128)(2,1)S(1)} %bitcast.70), channel_id=1, source_target_pairs={{0,32},{32,64},{64,96},{96,128},{128,160},{160,192},{192,224},{224... | collective-permute-start | bytes 393224 | tf_op jit(solution)/shard_map/ppermute | solution.py:24
  15.4 16.1 %collective-permute-start.4 = (bf16[8,32,256]{2,1,0:T(8,128)(2,1)S(1)}, bf16[8,32,256]{2,1,0:T(8,128)(2,1)S(1)}, u32[]{:S(2)}, u32[]{:S(2)}) collective-permute-start(bf16[8,32,256]{2,1,0:T(8,128)(2,1)S(1)} %bitcast.71), channel_id=1, source_target_pairs={{0,224},{32,0},{64,32},{96,64},{128,96},{160,128},{192,160},{224,1... | collective-permute-start | bytes 393224 | tf_op jit(solution)/shard_map/ppermute | solution.py:24
  21.1 7.1 %collective-permute-start.1 = (bf16[8,32,256]{2,1,0:T(8,128)(2,1)S(1)}, bf16[8,32,256]{2,1,0:T(8,128)(2,1)S(1)}, u32[]{:S(2)}, u32[]{:S(2)}) collective-permute-start(bf16[8,32,256]{2,1,0:T(8,128)(2,1)S(1)} %collective-permute-done.refs_14_), channel_id=1, source_target_pairs={{0,32},{32,64},{64,96},{96,128},{128,160},{160,192},{192,224},{224... | collective-permute-start | bytes 393224 | tf_op jit(solution)/shard_map/ppermute | solution.py:24
  21.7 10.0 %collective-permute-start.11 = (bf16[8,32,256]{2,1,0:T(8,128)(2,1)S(1)}, bf16[8,32,256]{2,1,0:T(8,128)(2,1)S(1)}, u32[]{:S(2)}, u32[]{:S(2)}) collective-permute-start(bf16[8,32,256]{2,1,0:T(8,128)(2,1)S(1)} %collective-permute-done.10.refs_15_), channel_id=1, source_target_pairs={{0,32},{32,64},{64,96},{96,128},{128,160},{160,192},{192,224},{224... | collective-permute-start | bytes 393224 | tf_op jit(solution)/shard_map/ppermute | solution.py:24
  28.2 6.5 %collective-permute-start.2 = (bf16[8,32,256]{2,1,0:T(8,128)(2,1)S(1)}, bf16[8,32,256]{2,1,0:T(8,128)(2,1)S(1)}, u32[]{:S(2)}, u32[]{:S(2)}) collective-permute-start(bf16[8,32,256]{2,1,0:T(8,128)(2,1)S(1)} %collective-permute-done.1.refs_12_), channel_id=1, source_target_pairs={{0,32},{32,64},{64,96},{96,128},{128,160},{160,192},{192,224},{224... | collective-permute-start | bytes 393224 | tf_op jit(solution)/shard_map/ppermute | solution.py:24
  28.3 12.6 %collective-permute-start.5 = (bf16[8,32,256]{2,1,0:T(8,128)(2,1)S(1)}, bf16[8,32,256]{2,1,0:T(8,128)(2,1)S(1)}, u32[]{:S(2)}, u32[]{:S(2)}) collective-permute-start(bf16[8,32,256]{2,1,0:T(8,128)(2,1)S(1)} %collective-permute-done.3.refs_2_), channel_id=1, source_target_pairs={{0,224},{32,0},{64,32},{96,64},{128,96},{160,128},{192,160},{224,1... | collective-permute-start | bytes 393224 | tf_op jit(solution)/shard_map/ppermute | solution.py:24
  31.6 12.6 %collective-permute-start.6 = (bf16[8,32,256]{2,1,0:T(8,128)(2,1)S(1)}, bf16[8,32,256]{2,1,0:T(8,128)(2,1)S(1)}, u32[]{:S(2)}, u32[]{:S(2)}) collective-permute-start(bf16[8,32,256]{2,1,0:T(8,128)(2,1)S(1)} %collective-permute-done.4.refs_3_), channel_id=1, source_target_pairs={{0,224},{32,0},{64,32},{96,64},{128,96},{160,128},{192,160},{224,1... | collective-permute-start | bytes 393224 | tf_op jit(solution)/shard_map/ppermute | solution.py:24
  31.7 14.5 %collective-permute-start.12 = (bf16[8,32,256]{2,1,0:T(8,128)(2,1)S(1)}, bf16[8,32,256]{2,1,0:T(8,128)(2,1)S(1)}, u32[]{:S(2)}, u32[]{:S(2)}) collective-permute-start(bf16[8,32,256]{2,1,0:T(8,128)(2,1)S(1)} %collective-permute-done.11.refs_13_), channel_id=1, source_target_pairs={{0,32},{32,64},{64,96},{96,128},{128,160},{160,192},{192,224},{224... | collective-permute-start | bytes 393224 | tf_op jit(solution)/shard_map/ppermute | solution.py:24
  35.4 13.3 %all-to-all-start = ((s32[8,1,592]{2,1,0:T(1,128)}), s32[8,1,592]{2,1,0:T(1,128)S(1)}, u32[]{:S(2)}, u32[]{:S(2)}) async-start(s32[8,1,592]{2,1,0:T(1,128)} %copy.47), calls=%async_computation | async-start | bytes 40960 | tf_op jit(solution)/shard_map/all_to_all | solution.py:320
  40.9 10.1 %collective-permute-start.7 = (bf16[8,32,256]{2,1,0:T(8,128)(2,1)S(1)}, bf16[8,32,256]{2,1,0:T(8,128)(2,1)S(1)}, u32[]{:S(2)}, u32[]{:S(2)}) collective-permute-start(bf16[8,32,256]{2,1,0:T(8,128)(2,1)S(1)} %collective-permute-done.5.refs_4_), channel_id=1, source_target_pairs={{0,224},{32,0},{64,32},{96,64},{128,96},{160,128},{192,160},{224,1... | collective-permute-start | bytes 393224 | tf_op jit(solution)/shard_map/ppermute | solution.py:24
  44.2 6.8 %collective-permute-start.8 = (bf16[8,32,256]{2,1,0:T(8,128)(2,1)S(1)}, bf16[8,32,256]{2,1,0:T(8,128)(2,1)S(1)}, u32[]{:S(2)}, u32[]{:S(2)}) collective-permute-start(bf16[8,32,256]{2,1,0:T(8,128)(2,1)S(1)} %collective-permute-done.6.refs_5_), channel_id=1, source_target_pairs={{0,224},{32,0},{64,32},{96,64},{128,96},{160,128},{192,160},{224,1... | collective-permute-start | bytes 393224 | tf_op jit(solution)/shard_map/ppermute | solution.py:24
  45.6 6.2 %collective-permute-start.9 = (bf16[8,32,256]{2,1,0:T(8,128)(2,1)S(1)}, bf16[8,32,256]{2,1,0:T(8,128)(2,1)S(1)}, u32[]{:S(2)}, u32[]{:S(2)}) collective-permute-start(bf16[8,32,256]{2,1,0:T(8,128)(2,1)S(1)} %collective-permute-done.2.refs_10_), channel_id=1, source_target_pairs={{0,32},{32,64},{64,96},{96,128},{128,160},{160,192},{192,224},{224... | collective-permute-start | bytes 393224 | tf_op jit(solution)/shard_map/ppermute | solution.py:24
  46.2 7.0 %collective-permute-start.13 = (bf16[8,32,256]{2,1,0:T(8,128)(2,1)S(1)}, bf16[8,32,256]{2,1,0:T(8,128)(2,1)S(1)}, u32[]{:S(2)}, u32[]{:S(2)}) collective-permute-start(bf16[8,32,256]{2,1,0:T(8,128)(2,1)S(1)} %collective-permute-done.12.refs_11_), channel_id=1, source_target_pairs={{0,32},{32,64},{64,96},{96,128},{128,160},{160,192},{192,224},{224... | collective-permute-start | bytes 393224 | tf_op jit(solution)/shard_map/ppermute | solution.py:24
  55.6 31.8 %all-to-all-start.1 = ((bf16[8,512,256]{2,1,0:T(8,128)(2,1)}), bf16[8,512,256]{2,1,0:T(8,128)(2,1)S(1)}, u32[]{:S(2)}, u32[]{:S(2)}) async-start(bf16[8,512,256]{2,1,0:T(8,128)(2,1)} %pack.1.p_ref), calls=%async_computation.1 | async-start | bytes 4194304 | tf_op jit(solution)/shard_map/all_to_all | solution.py:339
  60.0 20.1 %copy-start.3 = (s32[8,1,512]{2,1,0:T(1,128)S(1)}, s32[8,1,512]{2,1,0:T(1,128)}, u32[]{:S(2)}) copy-start(s32[8,1,512]{2,1,0:T(1,128)} %reshape.364.tgt_ref) | copy-start | bytes 49156
  60.0 85.5 %reduce-scatter.2.cloned.1.call-start = ((), (), s32[]{:S(2)}) async-start(), calls=%async_computation.5 | async-start | bytes 2359296 | tf_op jit(solution)/shard_map/reduce_scatter | solution.py:364
  68.3 5.4 %collective-permute-start.14 = (f32[2,8,1,512]{3,2,1,0:T(1,128)}, f32[2,8,1,512]{3,2,1,0:T(1,128)S(1)}, u32[]{:S(2)}, u32[]{:S(2)}) collective-permute-start(f32[2,8,1,512]{3,2,1,0:T(1,128)} %forward.1), channel_id=1, source_target_pairs={{0,192},{32,224},{64,0},{96,32},{128,64},{160,96},{192,128},{224,1... | collective-permute-start | bytes 98312 | tf_op jit(solution)/shard_map/ppermute | solution.py:24
  69.5 8.1 %collective-permute-start.15 = (f32[2,8,1,512]{3,2,1,0:T(1,128)}, f32[2,8,1,512]{3,2,1,0:T(1,128)S(1)}, u32[]{:S(2)}, u32[]{:S(2)}) collective-permute-start(f32[2,8,1,512]{3,2,1,0:T(1,128)} %forward.1), channel_id=1, source_target_pairs={{0,128},{32,160},{64,192},{96,224},{128,0},{160,32},{192,64},{224,... | collective-permute-start | bytes 98312 | tf_op jit(solution)/shard_map/ppermute | solution.py:24
  70.8 7.8 %collective-permute-start.16 = (f32[2,8,1,512]{3,2,1,0:T(1,128)}, f32[2,8,1,512]{3,2,1,0:T(1,128)S(1)}, u32[]{:S(2)}, u32[]{:S(2)}) collective-permute-start(f32[2,8,1,512]{3,2,1,0:T(1,128)} %forward.1), channel_id=1, source_target_pairs={{0,64},{32,96},{64,128},{96,160},{128,192},{160,224},{192,0},{224,... | collective-permute-start | bytes 98312 | tf_op jit(solution)/shard_map/ppermute | solution.py:24
  79.5 5.4 %collective-permute-start.17 = (f32[4,2,8,1,512]{4,3,2,1,0:T(1,128)S(1)}, f32[4,2,8,1,512]{4,3,2,1,0:T(1,128)S(1)}, u32[]{:S(2)}, u32[]{:S(2)}) collective-permute-start(f32[4,2,8,1,512]{4,3,2,1,0:T(1,128)S(1)} %pad_maximum_fusion.2), channel_id=1, source_target_pairs={{0,224},{32,0},{64,32},{96,64},{128,96},{160,128},{192,160},{224,1... | collective-permute-start | bytes 393224 | tf_op jit(solution)/shard_map/ppermute | solution.py:24
  99.2 9.9 %all-to-all-start.2 = ((f32[8,2,512]{2,1,0:T(2,128)}), f32[8,2,512]{2,1,0:T(2,128)S(1)}, u32[]{:S(2)}, u32[]{:S(2)}) async-start(f32[8,2,512]{2,1,0:T(2,128)} %pad_maximum_fusion.3.line_ref), calls=%async_computation.2 | async-start | bytes 65536 | tf_op jit(solution)/shard_map/all_to_all | solution.py:365
  110.6 5.8 %collective-permute-start.18 = (f32[128,256]{1,0:T(8,128)S(1)}, f32[128,256]{1,0:T(8,128)S(1)}, u32[]{:S(2)}, u32[]{:S(2)}) collective-permute-start(f32[128,256]{1,0:T(8,128)S(1)} %get-tuple-element.34), channel_id=1, source_target_pairs={{0,1},{1,2},{2,3},{3,0},{4,5},{5,6},{6,7},{7,4},{8,9},{9,10},{10,1... | collective-permute-start | bytes 393224 | tf_op jit(solution)/shard_map/ppermute | solution.py:24
  111.1 6.2 %collective-permute-start.20 = (f32[128,256]{1,0:T(8,128)S(1)}, f32[128,256]{1,0:T(8,128)S(1)}, u32[]{:S(2)}, u32[]{:S(2)}) collective-permute-start(f32[128,256]{1,0:T(8,128)S(1)} %get-tuple-element.36), channel_id=1, source_target_pairs={{0,3},{1,0},{2,1},{3,2},{4,7},{5,4},{6,5},{7,6},{8,11},{9,8},{10,9... | collective-permute-start | bytes 393224 | tf_op jit(solution)/shard_map/ppermute | solution.py:24
  118.1 7.8 %collective-permute-start.19 = (f32[256,256]{1,0:T(8,128)}, f32[256,256]{1,0:T(8,128)}, u32[]{:S(2)}, u32[]{:S(2)}) collective-permute-start(f32[256,256]{1,0:T(8,128)} %pad_maximum_fusion), channel_id=1, source_target_pairs={{0,1},{1,2},{2,3},{3,0},{4,5},{5,6},{6,7},{7,4},{8,9},{9,10},{10,1... | collective-permute-start | bytes 786440 | tf_op jit(solution)/shard_map/ppermute | solution.py:24
  119.6 8.7 %collective-permute-start.21 = (f32[256,256]{1,0:T(8,128)}, f32[256,256]{1,0:T(8,128)}, u32[]{:S(2)}, u32[]{:S(2)}) collective-permute-start(f32[256,256]{1,0:T(8,128)} %pad_maximum_fusion.1), channel_id=1, source_target_pairs={{0,3},{1,0},{2,1},{3,2},{4,7},{5,4},{6,5},{7,6},{8,11},{9,8},{10,9... | collective-permute-start | bytes 786440 | tf_op jit(solution)/shard_map/ppermute | solution.py:24
  129.4 6.4 %collective-permute-start.23 = (f32[256,256]{1,0:T(8,128)S(1)}, f32[256,256]{1,0:T(8,128)S(1)}, u32[]{:S(2)}, u32[]{:S(2)}) collective-permute-start(f32[256,256]{1,0:T(8,128)S(1)} %add_add_fusion.own), channel_id=1, source_target_pairs={{0,1},{1,2},{2,3},{3,0},{4,5},{5,6},{6,7},{7,4},{8,9},{9,10},{10,1... | collective-permute-start | bytes 786440 | tf_op jit(solution)/shard_map/ppermute | solution.py:24
  129.5 7.8 %collective-permute-start.22 = (f32[256,256]{1,0:T(8,128)S(1)}, f32[256,256]{1,0:T(8,128)S(1)}, u32[]{:S(2)}, u32[]{:S(2)}) collective-permute-start(f32[256,256]{1,0:T(8,128)S(1)} %add_add_fusion.own), channel_id=1, source_target_pairs={{0,3},{1,0},{2,1},{3,2},{4,7},{5,4},{6,5},{7,6},{8,11},{9,8},{10,9... | collective-permute-start | bytes 786440 | tf_op jit(solution)/shard_map/ppermute | solution.py:24
  135.8 5.0 %collective-permute-start.24 = (f32[128,256]{1,0:T(8,128)S(1)}, f32[128,256]{1,0:T(8,128)S(1)}, u32[]{:S(2)}, u32[]{:S(2)}) collective-permute-start(f32[128,256]{1,0:T(8,128)S(1)} %slice.78), channel_id=1, source_target_pairs={{0,1},{1,2},{2,3},{3,0},{4,5},{5,6},{6,7},{7,4},{8,9},{9,10},{10,1... | collective-permute-start | bytes 393224 | tf_op jit(solution)/shard_map/ppermute | solution.py:24
  137.3 6.3 %collective-permute-start.25 = (f32[128,256]{1,0:T(8,128)S(1)}, f32[128,256]{1,0:T(8,128)S(1)}, u32[]{:S(2)}, u32[]{:S(2)}) collective-permute-start(f32[128,256]{1,0:T(8,128)S(1)} %slice.79), channel_id=1, source_target_pairs={{0,3},{1,0},{2,1},{3,2},{4,7},{5,4},{6,5},{7,6},{8,11},{9,8},{10,9... | collective-permute-start | bytes 393224 | tf_op jit(solution)/shard_map/ppermute | solution.py:24
  (7 other events, 71.7 us)
Sparse Core Ops, SparseCore 0:
  10.5 37.5 all-gather.1
  99.3 40.7 reduce-scatter.1

commit v11 on v10

--- a/solution.py
+++ b/solution.py
@@ -32,17 +32,18 @@
     sources, p_ref = refs[:2 * count], refs[2 * count]
     half, block_rows = sources[0].shape[:2]
     per_peer = count * MOST
-    for j in range(p_ref.shape[0]):
+    for i in range(p_ref.shape[0]):
+        j = pl.program_id(0) * p_ref.shape[0] + i
         for slot in range(per_peer):
             b = blk[j * per_peer + slot]
             place = lax.rem(b, half)
             low = sources[slot // MOST * 2][place]
             high = sources[slot // MOST * 2 + 1][place]
             first = jnp.full(low.shape, b, jnp.int32) < half
-            p_ref[j, pl.ds(slot * block_rows, block_rows), :] = jnp.where(first, low, high)
-
-
-def pack(sources, blk, plane):
+            p_ref[i, pl.ds(slot * block_rows, block_rows), :] = jnp.where(first, low, high)
+
+
+def pack(sources, blk, plane, per=4):
     shape = sources[0].shape
     count = len(sources) // 2
     width = count * MOST * shape[1]
@@ -51,9 +52,9 @@
         functools.partial(pack_kernel, count),
         grid_spec=pltpu.PrefetchScalarGridSpec(
             num_scalar_prefetch=1,
-            grid=(1,),
+            grid=(plane // per,),
             in_specs=[pl.BlockSpec(shape, lambda j, blk: (0, 0, 0))] * len(sources),
-            out_specs=pl.BlockSpec(out.shape, lambda j, blk: (0, 0, 0)),
+            out_specs=pl.BlockSpec((per,) + out.shape[1:], lambda j, blk: (j, 0, 0)),
         ),
         out_shape=out,
         compiler_params=pltpu.CompilerParams(vmem_limit_bytes=SMALL),
@@ -221,46 +222,62 @@
     )((jnp.array(places, jnp.int32) + x) % quarters, rows, lines, table)
 
 
-def update_kernel(x_ref, own, after, before, far_a, far_b, t_ref, a_ref, nt_ref, na_ref):
-    quarters = pl.num_programs(0)
-    rel = lax.rem(pl.program_id(0) - x_ref[0] + quarters, quarters)
-    cut = far_a.shape[0]
-
-    def write(start, summed):
-        span = pl.ds(start, summed.shape[0])
-        accum = a_ref[span, :] + summed * summed
-        na_ref[span, :] = accum
-        nt_ref[span, :] = t_ref[span, :] - 0.5 * summed / jnp.sqrt(accum)
-
-    for place, ref in ((0, own), (1, after), (3, before)):
-
-        @pl.when(rel == place)
+def write_rows(summed, start, t_ref, a_ref, nt_ref, na_ref):
+    span = pl.ds(start, summed.shape[0])
+    accum = a_ref[span, :] + summed * summed
+    na_ref[span, :] = accum
+    nt_ref[span, :] = t_ref[span, :] - 0.5 * summed / jnp.sqrt(accum)
+
+
+def update_kernel(where, own, after, before, t_ref, a_ref, nt_ref, na_ref):
+    for place, ref in enumerate((own, after, before)):
+
+        @pl.when(pl.program_id(0) == place)
         def _():
-            write(0, ref[...])
-
-    @pl.when(rel == 2)
-    def _():
-        write(0, far_a[...])
-        write(cut, far_b[...])
-
-
-def update(x, own, after, before, far_a, far_b, table, accum, quarters):
+            write_rows(ref[...], 0, t_ref, a_ref, nt_ref, na_ref)
+
+
+def far_kernel(where, far_a, far_b, t_ref, a_ref, nt_in, na_in, nt_ref, na_ref):
+    write_rows(far_a[...], 0, t_ref, a_ref, nt_ref, na_ref)
+    write_rows(far_b[...], far_a.shape[0], t_ref, a_ref, nt_ref, na_ref)
+
+
+def update(body, places, x, sums, table, accum, quarters, held=()):
     items, features = table.shape
-    whole = pl.BlockSpec(own.shape, lambda i, x: (0, 0))
-    part = pl.BlockSpec(far_a.shape, lambda i, x: (0, 0))
-    block = pl.BlockSpec((items // quarters, features), lambda i, x: (i, 0))
-    return pl.pallas_call(
-        update_kernel,
+    sizes = [pl.BlockSpec(v.shape, lambda i, o: (0, 0)) for v in sums]
+    block = pl.BlockSpec((items // quarters, features), lambda i, o: (o[i], 0))
+    first = 3 + len(sums)
+    return pl.pallas_call(
+        body,
         grid_spec=pltpu.PrefetchScalarGridSpec(
             num_scalar_prefetch=1,
-            grid=(quarters,),
-            in_specs=[whole] * 3 + [part] * 2 + [block] * 2,
+            grid=(len(places),),
+            in_specs=sizes + [block] * 2 + [pl.BlockSpec(memory_space=pl.ANY)] * len(held),
             out_specs=[block] * 2,
         ),
         out_shape=[jax.ShapeDtypeStruct(table.shape, F32)] * 2,
+        input_output_aliases={first + i: i for i in range(len(held))},
         compiler_params=pltpu.CompilerParams(vmem_limit_bytes=SMALL),
         name="update",
-    )(x, own, after, before, far_a, far_b, table, accum)
+    )((jnp.array(places, jnp.int32) + x) % quarters, *sums, table, accum, *held)
+
+
+def cast_kernel(g_ref, out_ref):
+    out_ref[...] = g_ref[...].astype(F32)
+
+
+def cast_rows(grads, steps=2):
+    rows, features = grads.shape
+    block = pl.BlockSpec((rows // steps, features), lambda i: (i, 0))
+    return pl.pallas_call(
+        cast_kernel,
+        grid=(steps,),
+        in_specs=[block],
+        out_specs=block,
+        out_shape=jax.ShapeDtypeStruct(grads.shape, F32),
+        compiler_params=pltpu.CompilerParams(vmem_limit_bytes=LARGE),
+        name="cast_rows",
+    )(grads)
 
 
 def local(queries, clusters, positives, owner_of, table, accum):
@@ -361,7 +378,7 @@
         packed, jnp.concatenate([blk, z.reshape(1)]), lines, tables, z_size, block_count, block_rows
     )
     grads, lines = lax.optimization_barrier((grads, lines))
-    query_grads = lax.psum_scatter(grads, "z").astype(F32).reshape(local_rows, features)
+    query_grads = cast_rows(lax.psum_scatter(grads, "z").reshape(local_rows, features))
     got_lines = lax.all_to_all(lines, PLANE, 0, 0, tiled=True)
 
     far_a, far_b = item_parts((2,), 2, x, rows, got_lines, table[0], x_size)
@@ -379,8 +396,9 @@
     after = shift(own, "x", -1)
     far_a = shift(before[:half], "x", 1)
     far_b = shift(after[half:], "x", -1)
+    held = update(update_kernel, (0, 1, 3), x, (own, after, before), table[0], accum[0], x_size)
     new_table, new_accum = update(
-        x, own, after, before, far_a, far_b, table[0], accum[0], x_size
+        far_kernel, (2,), x, (far_a, far_b), table[0], accum[0], x_size, held
     )
     return (losses, query_grads, new_table[None], new_accum[None])
 

time: 155 us -> 153 us (0.987)
  Pallas kernels: 29.4 us -> 32.2 us
  waiting for transfers between devices: 39.5 us -> 37 us
  other arithmetic: 12 us -> 10.2 us
    pallas_call x1 -> x3, Pallas kernels: 2.01 us -> 5 us  [the longest x2 3.29 us: update(): pl.pallas_call(body, grid_spec=pltpu.PrefetchScalarGridSpec(num_scalar_pr...]
    ppermute x26, waiting for transfers between devices: 31.6 us -> 29.1 us  [shift(): lax.ppermute(value, axis, [(i, (i + step) % size) for i in range(size)])]
    convert_element_type x1 -> x0, other arithmetic: 1.78 us -> none  [local(): lax.psum_scatter(grads, 'z').astype(F32).reshape(local_rows, features)]
where the time goes in v11:
time: 153 us
  starting transfers between devices  48.4 us (32%)
  waiting for transfers between devices  37 us (24%)
  Pallas kernels  32.2 us (21%)
  between operations  14.6 us (10%)
  local copies, waits for them, and re-layouts  10.4 us (7%)
  other arithmetic  10.2 us (7%)
    ppermute x26, starting transfers between devices, shift(): lax.ppermute(value, axis, [(i, (i + step) % size) for i in range(size)])  34 us
    ppermute x26, waiting for transfers between devices, shift(): lax.ppermute(value, axis, [(i, (i + step) % size) for i in range(size)])  29.1 us
    pallas_call x1, Pallas kernels, query_parts(): pl.pallas_call(query_kernel, grid_spec=pltpu.PrefetchScalarGridSpec(num_s...  9.91 us
    pallas_call x1, Pallas kernels, forward(): pl.pallas_call(forward_kernel, grid=(planes // per,), in_specs=[pl.BlockS...  8.24 us
    pallas_call x3, Pallas kernels, item_parts(): pl.pallas_call(item_kernel, grid_spec=pltpu.PrefetchScalarGridSpec(num_sc...  6.84 us
    all_to_all x1, starting transfers between devices, local(): got = lax.all_to_all(meta, 'z', 0, 0, tiled=True)  5.48 us
    all_to_all x1, waiting for transfers between devices, local(): got_lines = lax.all_to_all(lines, PLANE, 0, 0, tiled=True)  5.41 us
    all_to_all x1, starting transfers between devices, local(): rows = lax.all_to_all(packed, PLANE, 0, 0, tiled=True)  4.47 us
  transfers between devices with their start and end apart: 31, of which 15 were waited for; matrix products, arithmetic and copies ran while one was open for 11% of the time, Pallas kernels for 13%

profile of v11, /device:TPU:6, one launch (start us, length us, event | category | flops | bytes accessed | tf_op | source)
XLA Modules:
  0.0 152.8 jit_solution(9831648958273585939)
XLA Ops:
  7.3 2.1 %convert_element_type.19 = bf16[1,1024,256]{2,1,0:T(8,128)(2,1)} convert(f32[1,1024,256]{2,1,0:T(8,128)} %param.15) | non-fusion elementwise | flops 262144 | bytes 1572864 | tf_op jit(solution)/shard_map/convert_element_type | solution.py:296
  9.4 2.0 %collective-permute-start = (bf16[8,32,256]{2,1,0:T(8,128)(2,1)S(1)}, bf16[8,32,256]{2,1,0:T(8,128)(2,1)S(1)}, u32[]{:S(2)}, u32[]{:S(2)}) collective-permute-start(bf16[8,32,256]{2,1,0:T(8,128)(2,1)S(1)} %bitcast.73), channel_id=1, source_target_pairs={{0,32},{32,64},{64,96},{96,128},{128,160},{160,192},{192,224},{224... | collective-permute-start | bytes 393224 | tf_op jit(solution)/shard_map/ppermute | solution.py:24
  11.4 4.0 %collective-permute-start.3 = (bf16[8,32,256]{2,1,0:T(8,128)(2,1)S(1)}, bf16[8,32,256]{2,1,0:T(8,128)(2,1)S(1)}, u32[]{:S(2)}, u32[]{:S(2)}) collective-permute-start(bf16[8,32,256]{2,1,0:T(8,128)(2,1)S(1)} %bitcast.74), channel_id=1, source_target_pairs={{0,224},{32,0},{64,32},{96,64},{128,96},{160,128},{192,160},{224,1... | collective-permute-start | bytes 393224 | tf_op jit(solution)/shard_map/ppermute | solution.py:24
  15.4 3.2 %collective-permute-start.4 = (bf16[8,32,256]{2,1,0:T(8,128)(2,1)S(1)}, bf16[8,32,256]{2,1,0:T(8,128)(2,1)S(1)}, u32[]{:S(2)}, u32[]{:S(2)}) collective-permute-start(bf16[8,32,256]{2,1,0:T(8,128)(2,1)S(1)} %bitcast.71), channel_id=1, source_target_pairs={{0,224},{32,0},{64,32},{96,64},{128,96},{160,128},{192,160},{224,1... | collective-permute-start | bytes 393224 | tf_op jit(solution)/shard_map/ppermute | solution.py:24
  21.7 6.5 %collective-permute-done.1.refs_12_ = bf16[8,32,256]{2,1,0:T(8,128)(2,1)S(1)} collective-permute-done((bf16[8,32,256]{2,1,0:T(8,128)(2,1)S(1)}, bf16[8,32,256]{2,1,0:T(8,128)(2,1)S(1)}, u32[]{:S(2)}, u32[]{:S(2)}) %collective-permute-start.1) | collective-permute-done | bytes 131104 | tf_op jit(solution)/shard_map/ppermute | solution.py:24
  28.2 3.3 %collective-permute-start.5 = (bf16[8,32,256]{2,1,0:T(8,128)(2,1)S(1)}, bf16[8,32,256]{2,1,0:T(8,128)(2,1)S(1)}, u32[]{:S(2)}, u32[]{:S(2)}) collective-permute-start(bf16[8,32,256]{2,1,0:T(8,128)(2,1)S(1)} %collective-permute-done.3.refs_2_), channel_id=1, source_target_pairs={{0,224},{32,0},{64,32},{96,64},{128,96},{160,128},{192,160},{224,1... | collective-permute-start | bytes 393224 | tf_op jit(solution)/shard_map/ppermute | solution.py:24
  31.7 1.9 %collective-permute-start.12 = (bf16[8,32,256]{2,1,0:T(8,128)(2,1)S(1)}, bf16[8,32,256]{2,1,0:T(8,128)(2,1)S(1)}, u32[]{:S(2)}, u32[]{:S(2)}) collective-permute-start(bf16[8,32,256]{2,1,0:T(8,128)(2,1)S(1)} %collective-permute-done.11.refs_13_), channel_id=1, source_target_pairs={{0,32},{32,64},{64,96},{96,128},{128,160},{160,192},{192,224},{224... | collective-permute-start | bytes 393224 | tf_op jit(solution)/shard_map/ppermute | solution.py:24
  35.4 5.5 %all-to-all-start = ((s32[8,1,592]{2,1,0:T(1,128)}), s32[8,1,592]{2,1,0:T(1,128)S(1)}, u32[]{:S(2)}, u32[]{:S(2)}) async-start(s32[8,1,592]{2,1,0:T(1,128)} %copy.51), calls=%async_computation | async-start | bytes 40960 | tf_op jit(solution)/shard_map/all_to_all | solution.py:337
  40.9 3.3 %collective-permute-start.7 = (bf16[8,32,256]{2,1,0:T(8,128)(2,1)S(1)}, bf16[8,32,256]{2,1,0:T(8,128)(2,1)S(1)}, u32[]{:S(2)}, u32[]{:S(2)}) collective-permute-start(bf16[8,32,256]{2,1,0:T(8,128)(2,1)S(1)} %collective-permute-done.5.refs_4_), channel_id=1, source_target_pairs={{0,224},{32,0},{64,32},{96,64},{128,96},{160,128},{192,160},{224,1... | collective-permute-start | bytes 393224 | tf_op jit(solution)/shard_map/ppermute | solution.py:24
  44.2 1.5 collective-permute-start.8
  46.2 2.4 %all-to-all-done = s32[8,1,592]{2,1,0:T(1,128)S(1)} async-done(((s32[8,1,592]{2,1,0:T(1,128)}), s32[8,1,592]{2,1,0:T(1,128)S(1)}, u32[]{:S(2)}, u32[]{:S(2)}) %all-to-all-start) | async-done | bytes 18976 | tf_op jit(solution)/shard_map/all_to_all | solution.py:337
  53.2 2.2 %pack.1.p_ref = bf16[8,512,256]{2,1,0:T(8,128)(2,1)} custom-call(s32[128]{0:T(128)S(1)} %max.12.blk, bf16[8,32,256]{2,1,0:T(8,128)(2,1)S(1)} %bitcast.75, bf16[8,32,256]{2,1,0:T(8,128)(2,1)S(1)} %bitcast.72, bf16[8,32,256]{2,1,0:T(8,128)(2,1)S(1)} %collective-permute-done.3.refs_2_, bf16[8,32,256]{2,1,0:T(8,128)(2,1)S(1)} %collective-permute-done.4.refs_3_, ...), custom_call_target="tpu_custom_call" | custom-call | bytes 4194304 | tf_op jit(solution)/shard_map/pack/pallas_call | solution.py:51
  55.4 4.5 %all-to-all-start.1 = ((bf16[8,512,256]{2,1,0:T(8,128)(2,1)}), bf16[8,512,256]{2,1,0:T(8,128)(2,1)S(1)}, u32[]{:S(2)}, u32[]{:S(2)}) async-start(bf16[8,512,256]{2,1,0:T(8,128)(2,1)} %pack.1.p_ref), calls=%async_computation.1 | async-start | bytes 4194304 | tf_op jit(solution)/shard_map/all_to_all | solution.py:356
  59.9 8.2 %forward.1 = f32[2,8,1,512]{3,2,1,0:T(1,128)} custom-call(bf16[8,512,256]{2,1,0:T(8,128)(2,1)} %pack.1.p_ref, bf16[8,1024,256]{2,1,0:T(8,128)(2,1)} %all-gather.2.cloned.1.call-done.t_ref, s32[8,1,512]{2,1,0:T(1,128)} %reshape.362.tgt_ref), custom_call_target="tpu_custom_call" | custom-call | flops 42949672960 | bytes 6291456 | tf_op jit(solution)/shard_map/forward/pallas_call | solution.py:96
  70.6 2.9 %collective-permute-start.16 = (f32[2,8,1,512]{3,2,1,0:T(1,128)}, f32[2,8,1,512]{3,2,1,0:T(1,128)S(1)}, u32[]{:S(2)}, u32[]{:S(2)}) collective-permute-start(f32[2,8,1,512]{3,2,1,0:T(1,128)} %forward.1), channel_id=1, source_target_pairs={{0,64},{32,96},{64,128},{96,160},{128,192},{160,224},{192,0},{224,... | collective-permute-start | bytes 98312 | tf_op jit(solution)/shard_map/ppermute | solution.py:24
  73.5 3.8 %collective-permute-done.15 = f32[2,8,1,512]{3,2,1,0:T(1,128)S(1)} collective-permute-done((f32[2,8,1,512]{3,2,1,0:T(1,128)}, f32[2,8,1,512]{3,2,1,0:T(1,128)S(1)}, u32[]{:S(2)}, u32[]{:S(2)}) %collective-permute-start.15) | collective-permute-done | bytes 32800 | tf_op jit(solution)/shard_map/ppermute | solution.py:24
  81.4 3.3 %collective-permute-done.17 = f32[4,2,8,1,512]{4,3,2,1,0:T(1,128)S(1)} collective-permute-done((f32[4,2,8,1,512]{4,3,2,1,0:T(1,128)S(1)}, f32[4,2,8,1,512]{4,3,2,1,0:T(1,128)S(1)}, u32[]{:S(2)}, u32[]{:S(2)}) %collective-permute-start.17) | collective-permute-done | bytes 131104 | tf_op jit(solution)/shard_map/ppermute | solution.py:24
  89.0 9.9 %query_parts.1 = bf16[8,16,32,256]{3,2,1,0:T(8,128)(2,1)} custom-call(s32[129]{0:T(256)} %pad_add_fusion.blk, bf16[8,512,256]{2,1,0:T(8,128)(2,1)} %pack.1.p_ref, bf16[8,1024,256]{2,1,0:T(8,128)(2,1)} %all-gather.2.cloned.1.call-done.t_ref, f32[8,2,512]{2,1,0:T(2,128)} %pad_maximum_fusion.3.line_ref), custom_call_target="tpu_custom_call" | custom-call | flops 1048576 | bytes 1048576 | tf_op jit(solution)/shard_map/query_parts/pallas_call | solution.py:153
  99.0 4.4 %all-to-all-start.2 = ((f32[8,2,512]{2,1,0:T(2,128)}), f32[8,2,512]{2,1,0:T(2,128)S(1)}, u32[]{:S(2)}, u32[]{:S(2)}) async-start(f32[8,2,512]{2,1,0:T(2,128)} %pad_maximum_fusion.3.line_ref), calls=%async_computation.2 | async-start | bytes 65536 | tf_op jit(solution)/shard_map/all_to_all | solution.py:382
  103.4 5.4 %all-to-all-done.2.line_ref = f32[8,2,512]{2,1,0:T(2,128)S(1)} async-done(((f32[8,2,512]{2,1,0:T(2,128)}), f32[8,2,512]{2,1,0:T(2,128)S(1)}, u32[]{:S(2)}, u32[]{:S(2)}) %all-to-all-start.2) | async-done | bytes 32800 | tf_op jit(solution)/shard_map/all_to_all | solution.py:382
  108.8 1.6 %item_parts.3 = (f32[128,256]{1,0:T(8,128)S(1)}, f32[128,256]{1,0:T(8,128)S(1)}) custom-call(s32[1]{0:T(128)S(6)} %select_n.208.where, bf16[8,512,256]{2,1,0:T(8,128)(2,1)S(1)} %all-to-all-done.1.q_ref, f32[8,2,512]{2,1,0:T(2,128)S(1)} %all-to-all-done.2.line_ref, f32[1024,256]{1,0:T(8,128)S(1)} %bitcast.63), custom_call_target="tpu_custom_call" | custom-call | flops 1073741824 | bytes 2490368 | tf_op jit(solution)/shard_map/item_parts/pallas_call | solution.py:202
  111.0 1.6 %collective-permute-start.20 = (f32[128,256]{1,0:T(8,128)S(1)}, f32[128,256]{1,0:T(8,128)S(1)}, u32[]{:S(2)}, u32[]{:S(2)}) collective-permute-start(f32[128,256]{1,0:T(8,128)S(1)} %get-tuple-element.38), channel_id=1, source_target_pairs={{0,3},{1,0},{2,1},{3,2},{4,7},{5,4},{6,5},{7,6},{8,11},{9,8},{10,9... | collective-permute-start | bytes 393224 | tf_op jit(solution)/shard_map/ppermute | solution.py:24
  112.5 3.7 %item_parts.4 = (f32[256,256]{1,0:T(8,128)S(1)}, f32[256,256]{1,0:T(8,128)S(1)}) custom-call(s32[2]{0:T(128)S(1)} %and_select_fusion.1.where, bf16[8,512,256]{2,1,0:T(8,128)(2,1)S(1)} %all-to-all-done.1.q_ref, f32[8,2,512]{2,1,0:T(2,128)S(1)} %all-to-all-done.2.line_ref, f32[1024,256]{1,0:T(8,128)S(1)} %bitcast.64), custom_call_target="tpu_custom_call" | custom-call | flops 2147483648 | bytes 2883584 | tf_op jit(solution)/shard_map/item_parts/pallas_call | solution.py:202
  121.7 1.6 %gather_fusion.4 = f32[64,32]{1,0:T(8,128)S(1)} fusion(f32[1024,32]{1,0:T(8,128)} %reshape_squeeze.7, s32[1024]{0:T(1024)S(1)} %pad_clamp_fusion), kind=kCustom, calls=%fused_computation.4 | custom fusion | bytes 16640 | tf_op jit(solution)/shard_map/gather | solution.py:364
  124.1 1.6 %item_parts.5 = f32[256,256]{1,0:T(8,128)S(1)} custom-call(s32[1]{0:T(128)S(6)} %select_n.186.where, bf16[8,512,256]{2,1,0:T(8,128)(2,1)S(1)} %all-to-all-done.1.q_ref, f32[8,2,512]{2,1,0:T(2,128)S(1)} %all-to-all-done.2.line_ref, f32[1024,256]{1,0:T(8,128)S(1)} %bitcast.65), custom_call_target="tpu_custom_call" | custom-call | flops 1073741824 | bytes 2490368 | tf_op jit(solution)/shard_map/item_parts/pallas_call | solution.py:202
  125.7 2.4 %collective-permute-done.21 = f32[256,256]{1,0:T(8,128)} collective-permute-done((f32[256,256]{1,0:T(8,128)}, f32[256,256]{1,0:T(8,128)}, u32[]{:S(2)}, u32[]{:S(2)}) %collective-permute-start.21) | collective-permute-done | bytes 262176 | tf_op jit(solution)/shard_map/ppermute | solution.py:24
  129.3 2.0 %collective-permute-start.24 = (f32[256,256]{1,0:T(8,128)S(1)}, f32[256,256]{1,0:T(8,128)S(1)}, u32[]{:S(2)}, u32[]{:S(2)}) collective-permute-start(f32[256,256]{1,0:T(8,128)S(1)} %add_add_fusion.own), channel_id=1, source_target_pairs={{0,3},{1,0},{2,1},{3,2},{4,7},{5,4},{6,5},{7,6},{8,11},{9,8},{10,9... | collective-permute-start | bytes 786440 | tf_op jit(solution)/shard_map/ppermute | solution.py:24
  131.3 4.3 %collective-permute-done.22.before = f32[256,256]{1,0:T(8,128)S(1)} collective-permute-done((f32[256,256]{1,0:T(8,128)S(1)}, f32[256,256]{1,0:T(8,128)S(1)}, u32[]{:S(2)}, u32[]{:S(2)}) %collective-permute-start.22) | collective-permute-done | bytes 262176 | tf_op jit(solution)/shard_map/ppermute | solution.py:24
  135.7 1.4 collective-permute-start.23
  138.0 2.4 %update.2 = (f32[1024,256]{1,0:T(8,128)}, f32[1024,256]{1,0:T(8,128)}) custom-call(s32[3]{0:T(128)S(1)} %and_select_fusion.where, f32[256,256]{1,0:T(8,128)S(1)} %add_add_fusion.own, f32[256,256]{1,0:T(8,128)S(1)} %collective-permute-done.24.after, f32[256,256]{1,0:T(8,128)S(1)} %collective-permute-done.22.before, f32[1024,256]{1,0:T(8,128)S(1)} %bitcast.66, ...), custom_call_target="tpu_custom_call" | custom-call | tf_op jit(solution)/shard_map/update/pallas_call | solution.py:250
  140.7 2.7 %collective-permute-done.25.far_b = f32[128,256]{1,0:T(8,128)S(1)} collective-permute-done((f32[128,256]{1,0:T(8,128)S(1)}, f32[128,256]{1,0:T(8,128)S(1)}, u32[]{:S(2)}, u32[]{:S(2)}) %collective-permute-start.25) | collective-permute-done | bytes 131104 | tf_op jit(solution)/shard_map/ppermute | solution.py:24
  144.2 1.7 %cast_rows.1 = f32[512,256]{1,0:T(8,128)} custom-call(bf16[512,256]{1,0:T(8,128)(2,1)} %bitcast.82), custom_call_target="tpu_custom_call" | custom-call | tf_op jit(solution)/shard_map/cast_rows/pallas_call | solution.py:272
  (151 shorter events, 30.7 us)
Async XLA Ops:
  7.2 52.7 %all-gather.2.cloned.1.call-start = ((), (), s32[]{:S(2)}) async-start(), calls=%async_computation.4 | async-start | bytes 4718592 | tf_op jit(solution)/shard_map/all_gather | solution.py:296
  9.4 11.7 %collective-permute-start = (bf16[8,32,256]{2,1,0:T(8,128)(2,1)S(1)}, bf16[8,32,256]{2,1,0:T(8,128)(2,1)S(1)}, u32[]{:S(2)}, u32[]{:S(2)}) collective-permute-start(bf16[8,32,256]{2,1,0:T(8,128)(2,1)S(1)} %bitcast.73), channel_id=1, source_target_pairs={{0,32},{32,64},{64,96},{96,128},{128,160},{160,192},{192,224},{224... | collective-permute-start | bytes 393224 | tf_op jit(solution)/shard_map/ppermute | solution.py:24
  11.4 16.8 %collective-permute-start.3 = (bf16[8,32,256]{2,1,0:T(8,128)(2,1)S(1)}, bf16[8,32,256]{2,1,0:T(8,128)(2,1)S(1)}, u32[]{:S(2)}, u32[]{:S(2)}) collective-permute-start(bf16[8,32,256]{2,1,0:T(8,128)(2,1)S(1)} %bitcast.74), channel_id=1, source_target_pairs={{0,224},{32,0},{64,32},{96,64},{128,96},{160,128},{192,160},{224,1... | collective-permute-start | bytes 393224 | tf_op jit(solution)/shard_map/ppermute | solution.py:24
  15.4 6.2 %collective-permute-start.10 = (bf16[8,32,256]{2,1,0:T(8,128)(2,1)S(1)}, bf16[8,32,256]{2,1,0:T(8,128)(2,1)S(1)}, u32[]{:S(2)}, u32[]{:S(2)}) collective-permute-start(bf16[8,32,256]{2,1,0:T(8,128)(2,1)S(1)} %bitcast.70), channel_id=1, source_target_pairs={{0,32},{32,64},{64,96},{96,128},{128,160},{160,192},{192,224},{224... | collective-permute-start | bytes 393224 | tf_op jit(solution)/shard_map/ppermute | solution.py:24
  15.4 16.1 %collective-permute-start.4 = (bf16[8,32,256]{2,1,0:T(8,128)(2,1)S(1)}, bf16[8,32,256]{2,1,0:T(8,128)(2,1)S(1)}, u32[]{:S(2)}, u32[]{:S(2)}) collective-permute-start(bf16[8,32,256]{2,1,0:T(8,128)(2,1)S(1)} %bitcast.71), channel_id=1, source_target_pairs={{0,224},{32,0},{64,32},{96,64},{128,96},{160,128},{192,160},{224,1... | collective-permute-start | bytes 393224 | tf_op jit(solution)/shard_map/ppermute | solution.py:24
  21.1 7.1 %collective-permute-start.1 = (bf16[8,32,256]{2,1,0:T(8,128)(2,1)S(1)}, bf16[8,32,256]{2,1,0:T(8,128)(2,1)S(1)}, u32[]{:S(2)}, u32[]{:S(2)}) collective-permute-start(bf16[8,32,256]{2,1,0:T(8,128)(2,1)S(1)} %collective-permute-done.refs_14_), channel_id=1, source_target_pairs={{0,32},{32,64},{64,96},{96,128},{128,160},{160,192},{192,224},{224... | collective-permute-start | bytes 393224 | tf_op jit(solution)/shard_map/ppermute | solution.py:24
  21.7 10.0 %collective-permute-start.11 = (bf16[8,32,256]{2,1,0:T(8,128)(2,1)S(1)}, bf16[8,32,256]{2,1,0:T(8,128)(2,1)S(1)}, u32[]{:S(2)}, u32[]{:S(2)}) collective-permute-start(bf16[8,32,256]{2,1,0:T(8,128)(2,1)S(1)} %collective-permute-done.10.refs_15_), channel_id=1, source_target_pairs={{0,32},{32,64},{64,96},{96,128},{128,160},{160,192},{192,224},{224... | collective-permute-start | bytes 393224 | tf_op jit(solution)/shard_map/ppermute | solution.py:24
  28.2 6.5 %collective-permute-start.2 = (bf16[8,32,256]{2,1,0:T(8,128)(2,1)S(1)}, bf16[8,32,256]{2,1,0:T(8,128)(2,1)S(1)}, u32[]{:S(2)}, u32[]{:S(2)}) collective-permute-start(bf16[8,32,256]{2,1,0:T(8,128)(2,1)S(1)} %collective-permute-done.1.refs_12_), channel_id=1, source_target_pairs={{0,32},{32,64},{64,96},{96,128},{128,160},{160,192},{192,224},{224... | collective-permute-start | bytes 393224 | tf_op jit(solution)/shard_map/ppermute | solution.py:24
  28.2 12.6 %collective-permute-start.5 = (bf16[8,32,256]{2,1,0:T(8,128)(2,1)S(1)}, bf16[8,32,256]{2,1,0:T(8,128)(2,1)S(1)}, u32[]{:S(2)}, u32[]{:S(2)}) collective-permute-start(bf16[8,32,256]{2,1,0:T(8,128)(2,1)S(1)} %collective-permute-done.3.refs_2_), channel_id=1, source_target_pairs={{0,224},{32,0},{64,32},{96,64},{128,96},{160,128},{192,160},{224,1... | collective-permute-start | bytes 393224 | tf_op jit(solution)/shard_map/ppermute | solution.py:24
  31.6 12.6 %collective-permute-start.6 = (bf16[8,32,256]{2,1,0:T(8,128)(2,1)S(1)}, bf16[8,32,256]{2,1,0:T(8,128)(2,1)S(1)}, u32[]{:S(2)}, u32[]{:S(2)}) collective-permute-start(bf16[8,32,256]{2,1,0:T(8,128)(2,1)S(1)} %collective-permute-done.4.refs_3_), channel_id=1, source_target_pairs={{0,224},{32,0},{64,32},{96,64},{128,96},{160,128},{192,160},{224,1... | collective-permute-start | bytes 393224 | tf_op jit(solution)/shard_map/ppermute | solution.py:24
  31.7 14.5 %collective-permute-start.12 = (bf16[8,32,256]{2,1,0:T(8,128)(2,1)S(1)}, bf16[8,32,256]{2,1,0:T(8,128)(2,1)S(1)}, u32[]{:S(2)}, u32[]{:S(2)}) collective-permute-start(bf16[8,32,256]{2,1,0:T(8,128)(2,1)S(1)} %collective-permute-done.11.refs_13_), channel_id=1, source_target_pairs={{0,32},{32,64},{64,96},{96,128},{128,160},{160,192},{192,224},{224... | collective-permute-start | bytes 393224 | tf_op jit(solution)/shard_map/ppermute | solution.py:24
  35.4 13.3 %all-to-all-start = ((s32[8,1,592]{2,1,0:T(1,128)}), s32[8,1,592]{2,1,0:T(1,128)S(1)}, u32[]{:S(2)}, u32[]{:S(2)}) async-start(s32[8,1,592]{2,1,0:T(1,128)} %copy.51), calls=%async_computation | async-start | bytes 40960 | tf_op jit(solution)/shard_map/all_to_all | solution.py:337
  40.9 10.1 %collective-permute-start.7 = (bf16[8,32,256]{2,1,0:T(8,128)(2,1)S(1)}, bf16[8,32,256]{2,1,0:T(8,128)(2,1)S(1)}, u32[]{:S(2)}, u32[]{:S(2)}) collective-permute-start(bf16[8,32,256]{2,1,0:T(8,128)(2,1)S(1)} %collective-permute-done.5.refs_4_), channel_id=1, source_target_pairs={{0,224},{32,0},{64,32},{96,64},{128,96},{160,128},{192,160},{224,1... | collective-permute-start | bytes 393224 | tf_op jit(solution)/shard_map/ppermute | solution.py:24
  44.2 6.8 %collective-permute-start.8 = (bf16[8,32,256]{2,1,0:T(8,128)(2,1)S(1)}, bf16[8,32,256]{2,1,0:T(8,128)(2,1)S(1)}, u32[]{:S(2)}, u32[]{:S(2)}) collective-permute-start(bf16[8,32,256]{2,1,0:T(8,128)(2,1)S(1)} %collective-permute-done.6.refs_5_), channel_id=1, source_target_pairs={{0,224},{32,0},{64,32},{96,64},{128,96},{160,128},{192,160},{224,1... | collective-permute-start | bytes 393224 | tf_op jit(solution)/shard_map/ppermute | solution.py:24
  45.6 6.2 %collective-permute-start.9 = (bf16[8,32,256]{2,1,0:T(8,128)(2,1)S(1)}, bf16[8,32,256]{2,1,0:T(8,128)(2,1)S(1)}, u32[]{:S(2)}, u32[]{:S(2)}) collective-permute-start(bf16[8,32,256]{2,1,0:T(8,128)(2,1)S(1)} %collective-permute-done.2.refs_10_), channel_id=1, source_target_pairs={{0,32},{32,64},{64,96},{96,128},{128,160},{160,192},{192,224},{224... | collective-permute-start | bytes 393224 | tf_op jit(solution)/shard_map/ppermute | solution.py:24
  46.2 7.0 %collective-permute-start.13 = (bf16[8,32,256]{2,1,0:T(8,128)(2,1)S(1)}, bf16[8,32,256]{2,1,0:T(8,128)(2,1)S(1)}, u32[]{:S(2)}, u32[]{:S(2)}) collective-permute-start(bf16[8,32,256]{2,1,0:T(8,128)(2,1)S(1)} %collective-permute-done.12.refs_11_), channel_id=1, source_target_pairs={{0,32},{32,64},{64,96},{96,128},{128,160},{160,192},{192,224},{224... | collective-permute-start | bytes 393224 | tf_op jit(solution)/shard_map/ppermute | solution.py:24
  55.4 31.8 %all-to-all-start.1 = ((bf16[8,512,256]{2,1,0:T(8,128)(2,1)}), bf16[8,512,256]{2,1,0:T(8,128)(2,1)S(1)}, u32[]{:S(2)}, u32[]{:S(2)}) async-start(bf16[8,512,256]{2,1,0:T(8,128)(2,1)} %pack.1.p_ref), calls=%async_computation.1 | async-start | bytes 4194304 | tf_op jit(solution)/shard_map/all_to_all | solution.py:356
  59.9 20.1 %copy-start.3 = (s32[8,1,512]{2,1,0:T(1,128)S(1)}, s32[8,1,512]{2,1,0:T(1,128)}, u32[]{:S(2)}) copy-start(s32[8,1,512]{2,1,0:T(1,128)} %reshape.362.tgt_ref) | copy-start | bytes 49156
  59.9 84.4 %reduce-scatter.2.cloned.1.call-start = ((), (), s32[]{:S(2)}) async-start(), calls=%async_computation.5 | async-start | bytes 2359296 | tf_op jit(solution)/shard_map/reduce_scatter | solution.py:381
  68.2 5.4 %collective-permute-start.14 = (f32[2,8,1,512]{3,2,1,0:T(1,128)}, f32[2,8,1,512]{3,2,1,0:T(1,128)S(1)}, u32[]{:S(2)}, u32[]{:S(2)}) collective-permute-start(f32[2,8,1,512]{3,2,1,0:T(1,128)} %forward.1), channel_id=1, source_target_pairs={{0,192},{32,224},{64,0},{96,32},{128,64},{160,96},{192,128},{224,1... | collective-permute-start | bytes 98312 | tf_op jit(solution)/shard_map/ppermute | solution.py:24
  69.3 8.1 %collective-permute-start.15 = (f32[2,8,1,512]{3,2,1,0:T(1,128)}, f32[2,8,1,512]{3,2,1,0:T(1,128)S(1)}, u32[]{:S(2)}, u32[]{:S(2)}) collective-permute-start(f32[2,8,1,512]{3,2,1,0:T(1,128)} %forward.1), channel_id=1, source_target_pairs={{0,128},{32,160},{64,192},{96,224},{128,0},{160,32},{192,64},{224,... | collective-permute-start | bytes 98312 | tf_op jit(solution)/shard_map/ppermute | solution.py:24
  70.6 7.8 %collective-permute-start.16 = (f32[2,8,1,512]{3,2,1,0:T(1,128)}, f32[2,8,1,512]{3,2,1,0:T(1,128)S(1)}, u32[]{:S(2)}, u32[]{:S(2)}) collective-permute-start(f32[2,8,1,512]{3,2,1,0:T(1,128)} %forward.1), channel_id=1, source_target_pairs={{0,64},{32,96},{64,128},{96,160},{128,192},{160,224},{192,0},{224,... | collective-permute-start | bytes 98312 | tf_op jit(solution)/shard_map/ppermute | solution.py:24
  79.3 5.4 %collective-permute-start.17 = (f32[4,2,8,1,512]{4,3,2,1,0:T(1,128)S(1)}, f32[4,2,8,1,512]{4,3,2,1,0:T(1,128)S(1)}, u32[]{:S(2)}, u32[]{:S(2)}) collective-permute-start(f32[4,2,8,1,512]{4,3,2,1,0:T(1,128)S(1)} %pad_maximum_fusion.2), channel_id=1, source_target_pairs={{0,224},{32,0},{64,32},{96,64},{128,96},{160,128},{192,160},{224,1... | collective-permute-start | bytes 393224 | tf_op jit(solution)/shard_map/ppermute | solution.py:24
  99.0 9.9 %all-to-all-start.2 = ((f32[8,2,512]{2,1,0:T(2,128)}), f32[8,2,512]{2,1,0:T(2,128)S(1)}, u32[]{:S(2)}, u32[]{:S(2)}) async-start(f32[8,2,512]{2,1,0:T(2,128)} %pad_maximum_fusion.3.line_ref), calls=%async_computation.2 | async-start | bytes 65536 | tf_op jit(solution)/shard_map/all_to_all | solution.py:382
  110.4 5.8 %collective-permute-start.18 = (f32[128,256]{1,0:T(8,128)S(1)}, f32[128,256]{1,0:T(8,128)S(1)}, u32[]{:S(2)}, u32[]{:S(2)}) collective-permute-start(f32[128,256]{1,0:T(8,128)S(1)} %get-tuple-element.36), channel_id=1, source_target_pairs={{0,1},{1,2},{2,3},{3,0},{4,5},{5,6},{6,7},{7,4},{8,9},{9,10},{10,1... | collective-permute-start | bytes 393224 | tf_op jit(solution)/shard_map/ppermute | solution.py:24
  111.0 6.2 %collective-permute-start.20 = (f32[128,256]{1,0:T(8,128)S(1)}, f32[128,256]{1,0:T(8,128)S(1)}, u32[]{:S(2)}, u32[]{:S(2)}) collective-permute-start(f32[128,256]{1,0:T(8,128)S(1)} %get-tuple-element.38), channel_id=1, source_target_pairs={{0,3},{1,0},{2,1},{3,2},{4,7},{5,4},{6,5},{7,6},{8,11},{9,8},{10,9... | collective-permute-start | bytes 393224 | tf_op jit(solution)/shard_map/ppermute | solution.py:24
  117.9 7.8 %collective-permute-start.19 = (f32[256,256]{1,0:T(8,128)}, f32[256,256]{1,0:T(8,128)}, u32[]{:S(2)}, u32[]{:S(2)}) collective-permute-start(f32[256,256]{1,0:T(8,128)} %pad_maximum_fusion), channel_id=1, source_target_pairs={{0,1},{1,2},{2,3},{3,0},{4,5},{5,6},{6,7},{7,4},{8,9},{9,10},{10,1... | collective-permute-start | bytes 786440 | tf_op jit(solution)/shard_map/ppermute | solution.py:24
  119.4 8.7 %collective-permute-start.21 = (f32[256,256]{1,0:T(8,128)}, f32[256,256]{1,0:T(8,128)}, u32[]{:S(2)}, u32[]{:S(2)}) collective-permute-start(f32[256,256]{1,0:T(8,128)} %pad_maximum_fusion.1), channel_id=1, source_target_pairs={{0,3},{1,0},{2,1},{3,2},{4,7},{5,4},{6,5},{7,6},{8,11},{9,8},{10,9... | collective-permute-start | bytes 786440 | tf_op jit(solution)/shard_map/ppermute | solution.py:24
  129.2 6.4 %collective-permute-start.22 = (f32[256,256]{1,0:T(8,128)S(1)}, f32[256,256]{1,0:T(8,128)S(1)}, u32[]{:S(2)}, u32[]{:S(2)}) collective-permute-start(f32[256,256]{1,0:T(8,128)S(1)} %add_add_fusion.own), channel_id=1, source_target_pairs={{0,1},{1,2},{2,3},{3,0},{4,5},{5,6},{6,7},{7,4},{8,9},{9,10},{10,1... | collective-permute-start | bytes 786440 | tf_op jit(solution)/shard_map/ppermute | solution.py:24
  129.3 7.8 %collective-permute-start.24 = (f32[256,256]{1,0:T(8,128)S(1)}, f32[256,256]{1,0:T(8,128)S(1)}, u32[]{:S(2)}, u32[]{:S(2)}) collective-permute-start(f32[256,256]{1,0:T(8,128)S(1)} %add_add_fusion.own), channel_id=1, source_target_pairs={{0,3},{1,0},{2,1},{3,2},{4,7},{5,4},{6,5},{7,6},{8,11},{9,8},{10,9... | collective-permute-start | bytes 786440 | tf_op jit(solution)/shard_map/ppermute | solution.py:24
  135.7 5.0 %collective-permute-start.23 = (f32[128,256]{1,0:T(8,128)S(1)}, f32[128,256]{1,0:T(8,128)S(1)}, u32[]{:S(2)}, u32[]{:S(2)}) collective-permute-start(f32[128,256]{1,0:T(8,128)S(1)} %slice.78), channel_id=1, source_target_pairs={{0,1},{1,2},{2,3},{3,0},{4,5},{5,6},{6,7},{7,4},{8,9},{9,10},{10,1... | collective-permute-start | bytes 393224 | tf_op jit(solution)/shard_map/ppermute | solution.py:24
  137.1 6.3 %collective-permute-start.25 = (f32[128,256]{1,0:T(8,128)S(1)}, f32[128,256]{1,0:T(8,128)S(1)}, u32[]{:S(2)}, u32[]{:S(2)}) collective-permute-start(f32[128,256]{1,0:T(8,128)S(1)} %slice.79), channel_id=1, source_target_pairs={{0,3},{1,0},{2,1},{3,2},{4,7},{5,4},{6,5},{7,6},{8,11},{9,8},{10,9... | collective-permute-start | bytes 393224 | tf_op jit(solution)/shard_map/ppermute | solution.py:24
  (8 other events, 80.1 us)
Sparse Core Ops, SparseCore 0:
  10.5 37.5 all-gather.1
  99.1 40.7 reduce-scatter.1

commit v12 on v11

--- a/solution.py
+++ b/solution.py
@@ -349,15 +349,18 @@
     pair_owner = pair_slot // MOST
     pair_from = (pair_owner // plane - z) % z_size
     pair_place = (order[:, None] - pair_from) % z_size
-    pair_row = (pair_from % 2 * 4 + pair_from // 2) * plane + pair_owner % plane
+    pair_group = pair_from % 4
+    pair_second = jnp.where(pair_group == 3, 1 - pair_from // 4, pair_from // 4)
+    pair_row = (pair_group * 2 + pair_second) * plane + pair_owner % plane
     pair_row = (pair_row * z_size + pair_place) * MOST + pair_slot % MOST
 
     packed = pack([part for pair in by_source for part in pair], blk, plane)
     rows = lax.all_to_all(packed, PLANE, 0, 0, tiled=True)
     stats = forward(packed, targets, tables)
 
-    even = jnp.stack([stats] + [shift(stats, "z", -e) for e in (2, 4, 6)])
-    all_stats = jnp.stack([even, shift(even, "z", -1)]).reshape(z_size, 2, -1)
+    both = jnp.stack([stats, shift(stats, "z", -4)])
+    all_stats = jnp.stack([both] + [shift(both, "z", -e) for e in (1, 2, -1)])
+    all_stats = all_stats.reshape(z_size, 2, -1)
     part = all_stats[:, 0].reshape(-1, block_rows)[pair_row.reshape(-1)]
     part, rows = lax.optimization_barrier((part, rows))
     part = part.reshape(z_size, block_count, picks, block_rows)

time: 153 us -> 154 us (level)
  transfers between devices with their start and end apart: 31 -> 31, of which waited for: 15 -> 17; matrix products, arithmetic and copies ran while one was open for 11% -> 11% of each run, Pallas kernels for 13% -> 13%
where the time goes in v12:
time: 154 us; the launch traced here: 153 us
  starting transfers between devices  48.2 us (31%)
  waiting for transfers between devices  37.5 us (24%)
  Pallas kernels  32.2 us (21%)
  between operations  14.6 us (9%)
  local copies, waits for them, and re-layouts  10.4 us (7%)
  other arithmetic  10.1 us (7%)
    ppermute x26, starting transfers between devices, shift(): lax.ppermute(value, axis, [(i, (i + step) % size) for i in range(size)])  33.5 us
    ppermute x26, waiting for transfers between devices, shift(): lax.ppermute(value, axis, [(i, (i + step) % size) for i in range(size)])  29.4 us
    pallas_call x1, Pallas kernels, query_parts(): pl.pallas_call(query_kernel, grid_spec=pltpu.PrefetchScalarGridSpec(num_s...  9.91 us
    pallas_call x1, Pallas kernels, forward(): pl.pallas_call(forward_kernel, grid=(planes // per,), in_specs=[pl.BlockS...  8.24 us
    pallas_call x3, Pallas kernels, item_parts(): pl.pallas_call(item_kernel, grid_spec=pltpu.PrefetchScalarGridSpec(num_sc...  6.84 us
    all_to_all x1, starting transfers between devices, local(): got = lax.all_to_all(meta, 'z', 0, 0, tiled=True)  5.48 us
    all_to_all x1, waiting for transfers between devices, local(): got_lines = lax.all_to_all(lines, PLANE, 0, 0, tiled=True)  5.41 us
    all_to_all x1, starting transfers between devices, local(): got_lines = lax.all_to_all(lines, PLANE, 0, 0, tiled=True)  4.7 us
  transfers between devices with their start and end apart: 31, of which 17 were waited for; matrix products, arithmetic and copies ran while one was open for 11% of the time, Pallas kernels for 13%

profile of v12, /device:TPU:6, one launch (start us, length us, event | category | flops | bytes accessed | tf_op | source)
XLA Modules:
  0.0 153.0 jit_solution(10350344588211283862)
XLA Ops:
  7.3 2.1 %convert_element_type.19 = bf16[1,1024,256]{2,1,0:T(8,128)(2,1)} convert(f32[1,1024,256]{2,1,0:T(8,128)} %param.15) | non-fusion elementwise | flops 262144 | bytes 1572864 | tf_op jit(solution)/shard_map/convert_element_type | solution.py:296
  9.4 2.0 %collective-permute-start = (bf16[8,32,256]{2,1,0:T(8,128)(2,1)S(1)}, bf16[8,32,256]{2,1,0:T(8,128)(2,1)S(1)}, u32[]{:S(2)}, u32[]{:S(2)}) collective-permute-start(bf16[8,32,256]{2,1,0:T(8,128)(2,1)S(1)} %bitcast.73), channel_id=1, source_target_pairs={{0,32},{32,64},{64,96},{96,128},{128,160},{160,192},{192,224},{224... | collective-permute-start | bytes 393224 | tf_op jit(solution)/shard_map/ppermute | solution.py:24
  11.4 4.0 %collective-permute-start.3 = (bf16[8,32,256]{2,1,0:T(8,128)(2,1)S(1)}, bf16[8,32,256]{2,1,0:T(8,128)(2,1)S(1)}, u32[]{:S(2)}, u32[]{:S(2)}) collective-permute-start(bf16[8,32,256]{2,1,0:T(8,128)(2,1)S(1)} %bitcast.74), channel_id=1, source_target_pairs={{0,224},{32,0},{64,32},{96,64},{128,96},{160,128},{192,160},{224,1... | collective-permute-start | bytes 393224 | tf_op jit(solution)/shard_map/ppermute | solution.py:24
  15.4 3.2 %collective-permute-start.4 = (bf16[8,32,256]{2,1,0:T(8,128)(2,1)S(1)}, bf16[8,32,256]{2,1,0:T(8,128)(2,1)S(1)}, u32[]{:S(2)}, u32[]{:S(2)}) collective-permute-start(bf16[8,32,256]{2,1,0:T(8,128)(2,1)S(1)} %bitcast.71), channel_id=1, source_target_pairs={{0,224},{32,0},{64,32},{96,64},{128,96},{160,128},{192,160},{224,1... | collective-permute-start | bytes 393224 | tf_op jit(solution)/shard_map/ppermute | solution.py:24
  21.7 6.5 %collective-permute-done.1.refs_12_ = bf16[8,32,256]{2,1,0:T(8,128)(2,1)S(1)} collective-permute-done((bf16[8,32,256]{2,1,0:T(8,128)(2,1)S(1)}, bf16[8,32,256]{2,1,0:T(8,128)(2,1)S(1)}, u32[]{:S(2)}, u32[]{:S(2)}) %collective-permute-start.1) | collective-permute-done | bytes 131104 | tf_op jit(solution)/shard_map/ppermute | solution.py:24
  28.2 3.3 %collective-permute-start.5 = (bf16[8,32,256]{2,1,0:T(8,128)(2,1)S(1)}, bf16[8,32,256]{2,1,0:T(8,128)(2,1)S(1)}, u32[]{:S(2)}, u32[]{:S(2)}) collective-permute-start(bf16[8,32,256]{2,1,0:T(8,128)(2,1)S(1)} %collective-permute-done.3.refs_2_), channel_id=1, source_target_pairs={{0,224},{32,0},{64,32},{96,64},{128,96},{160,128},{192,160},{224,1... | collective-permute-start | bytes 393224 | tf_op jit(solution)/shard_map/ppermute | solution.py:24
  31.7 1.9 %collective-permute-start.12 = (bf16[8,32,256]{2,1,0:T(8,128)(2,1)S(1)}, bf16[8,32,256]{2,1,0:T(8,128)(2,1)S(1)}, u32[]{:S(2)}, u32[]{:S(2)}) collective-permute-start(bf16[8,32,256]{2,1,0:T(8,128)(2,1)S(1)} %collective-permute-done.11.refs_13_), channel_id=1, source_target_pairs={{0,32},{32,64},{64,96},{96,128},{128,160},{160,192},{192,224},{224... | collective-permute-start | bytes 393224 | tf_op jit(solution)/shard_map/ppermute | solution.py:24
  35.4 5.5 %all-to-all-start = ((s32[8,1,592]{2,1,0:T(1,128)}), s32[8,1,592]{2,1,0:T(1,128)S(1)}, u32[]{:S(2)}, u32[]{:S(2)}) async-start(s32[8,1,592]{2,1,0:T(1,128)} %copy.51), calls=%async_computation | async-start | bytes 40960 | tf_op jit(solution)/shard_map/all_to_all | solution.py:337
  40.9 3.3 %collective-permute-start.7 = (bf16[8,32,256]{2,1,0:T(8,128)(2,1)S(1)}, bf16[8,32,256]{2,1,0:T(8,128)(2,1)S(1)}, u32[]{:S(2)}, u32[]{:S(2)}) collective-permute-start(bf16[8,32,256]{2,1,0:T(8,128)(2,1)S(1)} %collective-permute-done.5.refs_4_), channel_id=1, source_target_pairs={{0,224},{32,0},{64,32},{96,64},{128,96},{160,128},{192,160},{224,1... | collective-permute-start | bytes 393224 | tf_op jit(solution)/shard_map/ppermute | solution.py:24
  44.2 1.5 collective-permute-start.8
  46.2 2.4 %all-to-all-done = s32[8,1,592]{2,1,0:T(1,128)S(1)} async-done(((s32[8,1,592]{2,1,0:T(1,128)}), s32[8,1,592]{2,1,0:T(1,128)S(1)}, u32[]{:S(2)}, u32[]{:S(2)}) %all-to-all-start) | async-done | bytes 18976 | tf_op jit(solution)/shard_map/all_to_all | solution.py:337
  51.8 1.4 collective-permute-done.13.refs_9_
  53.2 2.2 %pack.1.p_ref = bf16[8,512,256]{2,1,0:T(8,128)(2,1)} custom-call(s32[128]{0:T(128)S(1)} %max.12.blk, bf16[8,32,256]{2,1,0:T(8,128)(2,1)S(1)} %bitcast.75, bf16[8,32,256]{2,1,0:T(8,128)(2,1)S(1)} %bitcast.72, bf16[8,32,256]{2,1,0:T(8,128)(2,1)S(1)} %collective-permute-done.3.refs_2_, bf16[8,32,256]{2,1,0:T(8,128)(2,1)S(1)} %collective-permute-done.4.refs_3_, ...), custom_call_target="tpu_custom_call" | custom-call | bytes 4194304 | tf_op jit(solution)/shard_map/pack/pallas_call | solution.py:51
  55.4 4.5 %all-to-all-start.1 = ((bf16[8,512,256]{2,1,0:T(8,128)(2,1)}), bf16[8,512,256]{2,1,0:T(8,128)(2,1)S(1)}, u32[]{:S(2)}, u32[]{:S(2)}) async-start(bf16[8,512,256]{2,1,0:T(8,128)(2,1)} %pack.1.p_ref), calls=%async_computation.1 | async-start | bytes 4194304 | tf_op jit(solution)/shard_map/all_to_all | solution.py:358
  59.9 8.2 %forward.1 = f32[2,8,1,512]{3,2,1,0:T(1,128)} custom-call(bf16[8,512,256]{2,1,0:T(8,128)(2,1)} %pack.1.p_ref, bf16[8,1024,256]{2,1,0:T(8,128)(2,1)} %all-gather.2.cloned.1.call-done.t_ref, s32[8,1,512]{2,1,0:T(1,128)} %reshape.362.tgt_ref), custom_call_target="tpu_custom_call" | custom-call | flops 42949672960 | bytes 6291456 | tf_op jit(solution)/shard_map/forward/pallas_call | solution.py:96
  68.2 2.4 %collective-permute-start.14 = (f32[2,8,1,512]{3,2,1,0:T(1,128)}, f32[2,8,1,512]{3,2,1,0:T(1,128)S(1)}, u32[]{:S(2)}, u32[]{:S(2)}) collective-permute-start(f32[2,8,1,512]{3,2,1,0:T(1,128)} %forward.1), channel_id=1, source_target_pairs={{0,128},{32,160},{64,192},{96,224},{128,0},{160,32},{192,64},{224,... | collective-permute-start | bytes 98312 | tf_op jit(solution)/shard_map/ppermute | solution.py:24
  71.7 5.2 %collective-permute-done.14 = f32[2,8,1,512]{3,2,1,0:T(1,128)S(1)} collective-permute-done((f32[2,8,1,512]{3,2,1,0:T(1,128)}, f32[2,8,1,512]{3,2,1,0:T(1,128)S(1)}, u32[]{:S(2)}, u32[]{:S(2)}) %collective-permute-start.14) | collective-permute-done | bytes 32800 | tf_op jit(solution)/shard_map/ppermute | solution.py:24
  88.9 9.9 %query_parts.1 = bf16[8,16,32,256]{3,2,1,0:T(8,128)(2,1)} custom-call(s32[129]{0:T(256)} %pad_add_fusion.blk, bf16[8,512,256]{2,1,0:T(8,128)(2,1)} %pack.1.p_ref, bf16[8,1024,256]{2,1,0:T(8,128)(2,1)} %all-gather.2.cloned.1.call-done.t_ref, f32[8,2,512]{2,1,0:T(2,128)} %pad_maximum_fusion.3.line_ref), custom_call_target="tpu_custom_call" | custom-call | flops 1048576 | bytes 1048576 | tf_op jit(solution)/shard_map/query_parts/pallas_call | solution.py:153
  98.9 4.7 %all-to-all-start.2 = ((f32[8,2,512]{2,1,0:T(2,128)}), f32[8,2,512]{2,1,0:T(2,128)S(1)}, u32[]{:S(2)}, u32[]{:S(2)}) async-start(f32[8,2,512]{2,1,0:T(2,128)} %pad_maximum_fusion.3.line_ref), calls=%async_computation.2 | async-start | bytes 65536 | tf_op jit(solution)/shard_map/all_to_all | solution.py:385
  103.6 5.4 %all-to-all-done.2.line_ref = f32[8,2,512]{2,1,0:T(2,128)S(1)} async-done(((f32[8,2,512]{2,1,0:T(2,128)}), f32[8,2,512]{2,1,0:T(2,128)S(1)}, u32[]{:S(2)}, u32[]{:S(2)}) %all-to-all-start.2) | async-done | bytes 32800 | tf_op jit(solution)/shard_map/all_to_all | solution.py:385
  109.0 1.6 %item_parts.3 = (f32[128,256]{1,0:T(8,128)S(1)}, f32[128,256]{1,0:T(8,128)S(1)}) custom-call(s32[1]{0:T(128)S(6)} %select_n.213.where, bf16[8,512,256]{2,1,0:T(8,128)(2,1)S(1)} %all-to-all-done.1.q_ref, f32[8,2,512]{2,1,0:T(2,128)S(1)} %all-to-all-done.2.line_ref, f32[1024,256]{1,0:T(8,128)S(1)} %bitcast.63), custom_call_target="tpu_custom_call" | custom-call | flops 1073741824 | bytes 2490368 | tf_op jit(solution)/shard_map/item_parts/pallas_call | solution.py:202
  111.1 1.6 %collective-permute-start.20 = (f32[128,256]{1,0:T(8,128)S(1)}, f32[128,256]{1,0:T(8,128)S(1)}, u32[]{:S(2)}, u32[]{:S(2)}) collective-permute-start(f32[128,256]{1,0:T(8,128)S(1)} %get-tuple-element.38), channel_id=1, source_target_pairs={{0,3},{1,0},{2,1},{3,2},{4,7},{5,4},{6,5},{7,6},{8,11},{9,8},{10,9... | collective-permute-start | bytes 393224 | tf_op jit(solution)/shard_map/ppermute | solution.py:24
  112.7 3.7 %item_parts.4 = (f32[256,256]{1,0:T(8,128)S(1)}, f32[256,256]{1,0:T(8,128)S(1)}) custom-call(s32[2]{0:T(128)S(1)} %and_select_fusion.1.where, bf16[8,512,256]{2,1,0:T(8,128)(2,1)S(1)} %all-to-all-done.1.q_ref, f32[8,2,512]{2,1,0:T(2,128)S(1)} %all-to-all-done.2.line_ref, f32[1024,256]{1,0:T(8,128)S(1)} %bitcast.64), custom_call_target="tpu_custom_call" | custom-call | flops 2147483648 | bytes 2883584 | tf_op jit(solution)/shard_map/item_parts/pallas_call | solution.py:202
  121.9 1.6 %gather_fusion.4 = f32[64,32]{1,0:T(8,128)S(1)} fusion(f32[1024,32]{1,0:T(8,128)} %reshape_squeeze.7, s32[1024]{0:T(1024)S(1)} %pad_clamp_fusion), kind=kCustom, calls=%fused_computation.4 | custom fusion | bytes 16640 | tf_op jit(solution)/shard_map/gather | solution.py:367
  124.3 1.6 %item_parts.5 = f32[256,256]{1,0:T(8,128)S(1)} custom-call(s32[1]{0:T(128)S(6)} %select_n.190.where, bf16[8,512,256]{2,1,0:T(8,128)(2,1)S(1)} %all-to-all-done.1.q_ref, f32[8,2,512]{2,1,0:T(2,128)S(1)} %all-to-all-done.2.line_ref, f32[1024,256]{1,0:T(8,128)S(1)} %bitcast.65), custom_call_target="tpu_custom_call" | custom-call | flops 1073741824 | bytes 2490368 | tf_op jit(solution)/shard_map/item_parts/pallas_call | solution.py:202
  125.9 2.4 %collective-permute-done.21 = f32[256,256]{1,0:T(8,128)} collective-permute-done((f32[256,256]{1,0:T(8,128)}, f32[256,256]{1,0:T(8,128)}, u32[]{:S(2)}, u32[]{:S(2)}) %collective-permute-start.21) | collective-permute-done | bytes 262176 | tf_op jit(solution)/shard_map/ppermute | solution.py:24
  129.5 2.0 %collective-permute-start.24 = (f32[256,256]{1,0:T(8,128)S(1)}, f32[256,256]{1,0:T(8,128)S(1)}, u32[]{:S(2)}, u32[]{:S(2)}) collective-permute-start(f32[256,256]{1,0:T(8,128)S(1)} %add_add_fusion.own), channel_id=1, source_target_pairs={{0,3},{1,0},{2,1},{3,2},{4,7},{5,4},{6,5},{7,6},{8,11},{9,8},{10,9... | collective-permute-start | bytes 786440 | tf_op jit(solution)/shard_map/ppermute | solution.py:24
  131.5 4.3 %collective-permute-done.22.before = f32[256,256]{1,0:T(8,128)S(1)} collective-permute-done((f32[256,256]{1,0:T(8,128)S(1)}, f32[256,256]{1,0:T(8,128)S(1)}, u32[]{:S(2)}, u32[]{:S(2)}) %collective-permute-start.22) | collective-permute-done | bytes 262176 | tf_op jit(solution)/shard_map/ppermute | solution.py:24
  135.8 1.4 collective-permute-start.23
  138.1 2.4 %update.2 = (f32[1024,256]{1,0:T(8,128)}, f32[1024,256]{1,0:T(8,128)}) custom-call(s32[3]{0:T(128)S(1)} %and_select_fusion.where, f32[256,256]{1,0:T(8,128)S(1)} %add_add_fusion.own, f32[256,256]{1,0:T(8,128)S(1)} %collective-permute-done.24.after, f32[256,256]{1,0:T(8,128)S(1)} %collective-permute-done.22.before, f32[1024,256]{1,0:T(8,128)S(1)} %bitcast.66, ...), custom_call_target="tpu_custom_call" | custom-call | tf_op jit(solution)/shard_map/update/pallas_call | solution.py:250
  140.9 2.7 %collective-permute-done.25.far_b = f32[128,256]{1,0:T(8,128)S(1)} collective-permute-done((f32[128,256]{1,0:T(8,128)S(1)}, f32[128,256]{1,0:T(8,128)S(1)}, u32[]{:S(2)}, u32[]{:S(2)}) %collective-permute-start.25) | collective-permute-done | bytes 131104 | tf_op jit(solution)/shard_map/ppermute | solution.py:24
  144.4 1.7 %cast_rows.1 = f32[512,256]{1,0:T(8,128)} custom-call(bf16[512,256]{1,0:T(8,128)(2,1)} %bitcast.82), custom_call_target="tpu_custom_call" | custom-call | tf_op jit(solution)/shard_map/cast_rows/pallas_call | solution.py:272
  (151 shorter events, 31.6 us)
Async XLA Ops:
  7.2 52.7 %all-gather.2.cloned.1.call-start = ((), (), s32[]{:S(2)}) async-start(), calls=%async_computation.4 | async-start | bytes 4718592 | tf_op jit(solution)/shard_map/all_gather | solution.py:296
  9.4 11.7 %collective-permute-start = (bf16[8,32,256]{2,1,0:T(8,128)(2,1)S(1)}, bf16[8,32,256]{2,1,0:T(8,128)(2,1)S(1)}, u32[]{:S(2)}, u32[]{:S(2)}) collective-permute-start(bf16[8,32,256]{2,1,0:T(8,128)(2,1)S(1)} %bitcast.73), channel_id=1, source_target_pairs={{0,32},{32,64},{64,96},{96,128},{128,160},{160,192},{192,224},{224... | collective-permute-start | bytes 393224 | tf_op jit(solution)/shard_map/ppermute | solution.py:24
  11.4 16.8 %collective-permute-start.3 = (bf16[8,32,256]{2,1,0:T(8,128)(2,1)S(1)}, bf16[8,32,256]{2,1,0:T(8,128)(2,1)S(1)}, u32[]{:S(2)}, u32[]{:S(2)}) collective-permute-start(bf16[8,32,256]{2,1,0:T(8,128)(2,1)S(1)} %bitcast.74), channel_id=1, source_target_pairs={{0,224},{32,0},{64,32},{96,64},{128,96},{160,128},{192,160},{224,1... | collective-permute-start | bytes 393224 | tf_op jit(solution)/shard_map/ppermute | solution.py:24
  15.4 6.2 %collective-permute-start.10 = (bf16[8,32,256]{2,1,0:T(8,128)(2,1)S(1)}, bf16[8,32,256]{2,1,0:T(8,128)(2,1)S(1)}, u32[]{:S(2)}, u32[]{:S(2)}) collective-permute-start(bf16[8,32,256]{2,1,0:T(8,128)(2,1)S(1)} %bitcast.70), channel_id=1, source_target_pairs={{0,32},{32,64},{64,96},{96,128},{128,160},{160,192},{192,224},{224... | collective-permute-start | bytes 393224 | tf_op jit(solution)/shard_map/ppermute | solution.py:24
  15.4 16.1 %collective-permute-start.4 = (bf16[8,32,256]{2,1,0:T(8,128)(2,1)S(1)}, bf16[8,32,256]{2,1,0:T(8,128)(2,1)S(1)}, u32[]{:S(2)}, u32[]{:S(2)}) collective-permute-start(bf16[8,32,256]{2,1,0:T(8,128)(2,1)S(1)} %bitcast.71), channel_id=1, source_target_pairs={{0,224},{32,0},{64,32},{96,64},{128,96},{160,128},{192,160},{224,1... | collective-permute-start | bytes 393224 | tf_op jit(solution)/shard_map/ppermute | solution.py:24
  21.1 7.1 %collective-permute-start.1 = (bf16[8,32,256]{2,1,0:T(8,128)(2,1)S(1)}, bf16[8,32,256]{2,1,0:T(8,128)(2,1)S(1)}, u32[]{:S(2)}, u32[]{:S(2)}) collective-permute-start(bf16[8,32,256]{2,1,0:T(8,128)(2,1)S(1)} %collective-permute-done.refs_14_), channel_id=1, source_target_pairs={{0,32},{32,64},{64,96},{96,128},{128,160},{160,192},{192,224},{224... | collective-permute-start | bytes 393224 | tf_op jit(solution)/shard_map/ppermute | solution.py:24
  21.7 10.0 %collective-permute-start.11 = (bf16[8,32,256]{2,1,0:T(8,128)(2,1)S(1)}, bf16[8,32,256]{2,1,0:T(8,128)(2,1)S(1)}, u32[]{:S(2)}, u32[]{:S(2)}) collective-permute-start(bf16[8,32,256]{2,1,0:T(8,128)(2,1)S(1)} %collective-permute-done.10.refs_15_), channel_id=1, source_target_pairs={{0,32},{32,64},{64,96},{96,128},{128,160},{160,192},{192,224},{224... | collective-permute-start | bytes 393224 | tf_op jit(solution)/shard_map/ppermute | solution.py:24
  28.2 6.5 %collective-permute-start.2 = (bf16[8,32,256]{2,1,0:T(8,128)(2,1)S(1)}, bf16[8,32,256]{2,1,0:T(8,128)(2,1)S(1)}, u32[]{:S(2)}, u32[]{:S(2)}) collective-permute-start(bf16[8,32,256]{2,1,0:T(8,128)(2,1)S(1)} %collective-permute-done.1.refs_12_), channel_id=1, source_target_pairs={{0,32},{32,64},{64,96},{96,128},{128,160},{160,192},{192,224},{224... | collective-permute-start | bytes 393224 | tf_op jit(solution)/shard_map/ppermute | solution.py:24
  28.2 12.6 %collective-permute-start.5 = (bf16[8,32,256]{2,1,0:T(8,128)(2,1)S(1)}, bf16[8,32,256]{2,1,0:T(8,128)(2,1)S(1)}, u32[]{:S(2)}, u32[]{:S(2)}) collective-permute-start(bf16[8,32,256]{2,1,0:T(8,128)(2,1)S(1)} %collective-permute-done.3.refs_2_), channel_id=1, source_target_pairs={{0,224},{32,0},{64,32},{96,64},{128,96},{160,128},{192,160},{224,1... | collective-permute-start | bytes 393224 | tf_op jit(solution)/shard_map/ppermute | solution.py:24
  31.6 12.6 %collective-permute-start.6 = (bf16[8,32,256]{2,1,0:T(8,128)(2,1)S(1)}, bf16[8,32,256]{2,1,0:T(8,128)(2,1)S(1)}, u32[]{:S(2)}, u32[]{:S(2)}) collective-permute-start(bf16[8,32,256]{2,1,0:T(8,128)(2,1)S(1)} %collective-permute-done.4.refs_3_), channel_id=1, source_target_pairs={{0,224},{32,0},{64,32},{96,64},{128,96},{160,128},{192,160},{224,1... | collective-permute-start | bytes 393224 | tf_op jit(solution)/shard_map/ppermute | solution.py:24
  31.7 14.5 %collective-permute-start.12 = (bf16[8,32,256]{2,1,0:T(8,128)(2,1)S(1)}, bf16[8,32,256]{2,1,0:T(8,128)(2,1)S(1)}, u32[]{:S(2)}, u32[]{:S(2)}) collective-permute-start(bf16[8,32,256]{2,1,0:T(8,128)(2,1)S(1)} %collective-permute-done.11.refs_13_), channel_id=1, source_target_pairs={{0,32},{32,64},{64,96},{96,128},{128,160},{160,192},{192,224},{224... | collective-permute-start | bytes 393224 | tf_op jit(solution)/shard_map/ppermute | solution.py:24
  35.4 13.3 %all-to-all-start = ((s32[8,1,592]{2,1,0:T(1,128)}), s32[8,1,592]{2,1,0:T(1,128)S(1)}, u32[]{:S(2)}, u32[]{:S(2)}) async-start(s32[8,1,592]{2,1,0:T(1,128)} %copy.51), calls=%async_computation | async-start | bytes 40960 | tf_op jit(solution)/shard_map/all_to_all | solution.py:337
  40.9 10.1 %collective-permute-start.7 = (bf16[8,32,256]{2,1,0:T(8,128)(2,1)S(1)}, bf16[8,32,256]{2,1,0:T(8,128)(2,1)S(1)}, u32[]{:S(2)}, u32[]{:S(2)}) collective-permute-start(bf16[8,32,256]{2,1,0:T(8,128)(2,1)S(1)} %collective-permute-done.5.refs_4_), channel_id=1, source_target_pairs={{0,224},{32,0},{64,32},{96,64},{128,96},{160,128},{192,160},{224,1... | collective-permute-start | bytes 393224 | tf_op jit(solution)/shard_map/ppermute | solution.py:24
  44.2 6.8 %collective-permute-start.8 = (bf16[8,32,256]{2,1,0:T(8,128)(2,1)S(1)}, bf16[8,32,256]{2,1,0:T(8,128)(2,1)S(1)}, u32[]{:S(2)}, u32[]{:S(2)}) collective-permute-start(bf16[8,32,256]{2,1,0:T(8,128)(2,1)S(1)} %collective-permute-done.6.refs_5_), channel_id=1, source_target_pairs={{0,224},{32,0},{64,32},{96,64},{128,96},{160,128},{192,160},{224,1... | collective-permute-start | bytes 393224 | tf_op jit(solution)/shard_map/ppermute | solution.py:24
  45.6 6.2 %collective-permute-start.9 = (bf16[8,32,256]{2,1,0:T(8,128)(2,1)S(1)}, bf16[8,32,256]{2,1,0:T(8,128)(2,1)S(1)}, u32[]{:S(2)}, u32[]{:S(2)}) collective-permute-start(bf16[8,32,256]{2,1,0:T(8,128)(2,1)S(1)} %collective-permute-done.2.refs_10_), channel_id=1, source_target_pairs={{0,32},{32,64},{64,96},{96,128},{128,160},{160,192},{192,224},{224... | collective-permute-start | bytes 393224 | tf_op jit(solution)/shard_map/ppermute | solution.py:24
  46.2 7.0 %collective-permute-start.13 = (bf16[8,32,256]{2,1,0:T(8,128)(2,1)S(1)}, bf16[8,32,256]{2,1,0:T(8,128)(2,1)S(1)}, u32[]{:S(2)}, u32[]{:S(2)}) collective-permute-start(bf16[8,32,256]{2,1,0:T(8,128)(2,1)S(1)} %collective-permute-done.12.refs_11_), channel_id=1, source_target_pairs={{0,32},{32,64},{64,96},{96,128},{128,160},{160,192},{192,224},{224... | collective-permute-start | bytes 393224 | tf_op jit(solution)/shard_map/ppermute | solution.py:24
  55.4 31.7 %all-to-all-start.1 = ((bf16[8,512,256]{2,1,0:T(8,128)(2,1)}), bf16[8,512,256]{2,1,0:T(8,128)(2,1)S(1)}, u32[]{:S(2)}, u32[]{:S(2)}) async-start(bf16[8,512,256]{2,1,0:T(8,128)(2,1)} %pack.1.p_ref), calls=%async_computation.1 | async-start | bytes 4194304 | tf_op jit(solution)/shard_map/all_to_all | solution.py:358
  59.9 84.6 %reduce-scatter.2.cloned.1.call-start = ((), (), s32[]{:S(2)}) async-start(), calls=%async_computation.5 | async-start | bytes 2359296 | tf_op jit(solution)/shard_map/reduce_scatter | solution.py:384
  68.2 8.7 %collective-permute-start.14 = (f32[2,8,1,512]{3,2,1,0:T(1,128)}, f32[2,8,1,512]{3,2,1,0:T(1,128)S(1)}, u32[]{:S(2)}, u32[]{:S(2)}) collective-permute-start(f32[2,8,1,512]{3,2,1,0:T(1,128)} %forward.1), channel_id=1, source_target_pairs={{0,128},{32,160},{64,192},{96,224},{128,0},{160,32},{192,64},{224,... | collective-permute-start | bytes 98312 | tf_op jit(solution)/shard_map/ppermute | solution.py:24
  77.7 4.3 %collective-permute-start.15 = (f32[2,2,8,1,512]{4,3,2,1,0:T(1,128)S(1)}, f32[2,2,8,1,512]{4,3,2,1,0:T(1,128)S(1)}, u32[]{:S(2)}, u32[]{:S(2)}) collective-permute-start(f32[2,2,8,1,512]{4,3,2,1,0:T(1,128)S(1)} %pad_maximum_fusion.2), channel_id=1, source_target_pairs={{0,224},{32,0},{64,32},{96,64},{128,96},{160,128},{192,160},{224,1... | collective-permute-start | bytes 196616 | tf_op jit(solution)/shard_map/ppermute | solution.py:24
  77.8 5.5 %collective-permute-start.16 = (f32[2,2,8,1,512]{4,3,2,1,0:T(1,128)S(1)}, f32[2,2,8,1,512]{4,3,2,1,0:T(1,128)S(1)}, u32[]{:S(2)}, u32[]{:S(2)}) collective-permute-start(f32[2,2,8,1,512]{4,3,2,1,0:T(1,128)S(1)} %pad_maximum_fusion.2), channel_id=1, source_target_pairs={{0,192},{32,224},{64,0},{96,32},{128,64},{160,96},{192,128},{224,1... | collective-permute-start | bytes 196616 | tf_op jit(solution)/shard_map/ppermute | solution.py:24
  78.9 5.5 %collective-permute-start.17 = (f32[2,2,8,1,512]{4,3,2,1,0:T(1,128)S(1)}, f32[2,2,8,1,512]{4,3,2,1,0:T(1,128)S(1)}, u32[]{:S(2)}, u32[]{:S(2)}) collective-permute-start(f32[2,2,8,1,512]{4,3,2,1,0:T(1,128)S(1)} %pad_maximum_fusion.2), channel_id=1, source_target_pairs={{0,32},{32,64},{64,96},{96,128},{128,160},{160,192},{192,224},{224... | collective-permute-start | bytes 196616 | tf_op jit(solution)/shard_map/ppermute | solution.py:24
  98.9 10.1 %all-to-all-start.2 = ((f32[8,2,512]{2,1,0:T(2,128)}), f32[8,2,512]{2,1,0:T(2,128)S(1)}, u32[]{:S(2)}, u32[]{:S(2)}) async-start(f32[8,2,512]{2,1,0:T(2,128)} %pad_maximum_fusion.3.line_ref), calls=%async_computation.2 | async-start | bytes 65536 | tf_op jit(solution)/shard_map/all_to_all | solution.py:385
  110.6 5.8 %collective-permute-start.18 = (f32[128,256]{1,0:T(8,128)S(1)}, f32[128,256]{1,0:T(8,128)S(1)}, u32[]{:S(2)}, u32[]{:S(2)}) collective-permute-start(f32[128,256]{1,0:T(8,128)S(1)} %get-tuple-element.36), channel_id=1, source_target_pairs={{0,1},{1,2},{2,3},{3,0},{4,5},{5,6},{6,7},{7,4},{8,9},{9,10},{10,1... | collective-permute-start | bytes 393224 | tf_op jit(solution)/shard_map/ppermute | solution.py:24
  111.1 6.2 %collective-permute-start.20 = (f32[128,256]{1,0:T(8,128)S(1)}, f32[128,256]{1,0:T(8,128)S(1)}, u32[]{:S(2)}, u32[]{:S(2)}) collective-permute-start(f32[128,256]{1,0:T(8,128)S(1)} %get-tuple-element.38), channel_id=1, source_target_pairs={{0,3},{1,0},{2,1},{3,2},{4,7},{5,4},{6,5},{7,6},{8,11},{9,8},{10,9... | collective-permute-start | bytes 393224 | tf_op jit(solution)/shard_map/ppermute | solution.py:24
  118.1 7.8 %collective-permute-start.19 = (f32[256,256]{1,0:T(8,128)}, f32[256,256]{1,0:T(8,128)}, u32[]{:S(2)}, u32[]{:S(2)}) collective-permute-start(f32[256,256]{1,0:T(8,128)} %pad_maximum_fusion), channel_id=1, source_target_pairs={{0,1},{1,2},{2,3},{3,0},{4,5},{5,6},{6,7},{7,4},{8,9},{9,10},{10,1... | collective-permute-start | bytes 786440 | tf_op jit(solution)/shard_map/ppermute | solution.py:24
  119.6 8.7 %collective-permute-start.21 = (f32[256,256]{1,0:T(8,128)}, f32[256,256]{1,0:T(8,128)}, u32[]{:S(2)}, u32[]{:S(2)}) collective-permute-start(f32[256,256]{1,0:T(8,128)} %pad_maximum_fusion.1), channel_id=1, source_target_pairs={{0,3},{1,0},{2,1},{3,2},{4,7},{5,4},{6,5},{7,6},{8,11},{9,8},{10,9... | collective-permute-start | bytes 786440 | tf_op jit(solution)/shard_map/ppermute | solution.py:24
  124.3 13.8 %copy-start.1 = (f32[1,1024,256]{2,1,0:T(8,128)S(1)}, f32[1,1024,256]{2,1,0:T(8,128)}, u32[]{:S(2)}) copy-start(f32[1,1024,256]{2,1,0:T(8,128)} %param.16) | copy-start | bytes 3145732
  129.4 6.4 %collective-permute-start.22 = (f32[256,256]{1,0:T(8,128)S(1)}, f32[256,256]{1,0:T(8,128)S(1)}, u32[]{:S(2)}, u32[]{:S(2)}) collective-permute-start(f32[256,256]{1,0:T(8,128)S(1)} %add_add_fusion.own), channel_id=1, source_target_pairs={{0,1},{1,2},{2,3},{3,0},{4,5},{5,6},{6,7},{7,4},{8,9},{9,10},{10,1... | collective-permute-start | bytes 786440 | tf_op jit(solution)/shard_map/ppermute | solution.py:24
  129.5 7.8 %collective-permute-start.24 = (f32[256,256]{1,0:T(8,128)S(1)}, f32[256,256]{1,0:T(8,128)S(1)}, u32[]{:S(2)}, u32[]{:S(2)}) collective-permute-start(f32[256,256]{1,0:T(8,128)S(1)} %add_add_fusion.own), channel_id=1, source_target_pairs={{0,3},{1,0},{2,1},{3,2},{4,7},{5,4},{6,5},{7,6},{8,11},{9,8},{10,9... | collective-permute-start | bytes 786440 | tf_op jit(solution)/shard_map/ppermute | solution.py:24
  135.8 5.0 %collective-permute-start.23 = (f32[128,256]{1,0:T(8,128)S(1)}, f32[128,256]{1,0:T(8,128)S(1)}, u32[]{:S(2)}, u32[]{:S(2)}) collective-permute-start(f32[128,256]{1,0:T(8,128)S(1)} %slice.78), channel_id=1, source_target_pairs={{0,1},{1,2},{2,3},{3,0},{4,5},{5,6},{6,7},{7,4},{8,9},{9,10},{10,1... | collective-permute-start | bytes 393224 | tf_op jit(solution)/shard_map/ppermute | solution.py:24
  137.3 6.3 %collective-permute-start.25 = (f32[128,256]{1,0:T(8,128)S(1)}, f32[128,256]{1,0:T(8,128)S(1)}, u32[]{:S(2)}, u32[]{:S(2)}) collective-permute-start(f32[128,256]{1,0:T(8,128)S(1)} %slice.79), channel_id=1, source_target_pairs={{0,3},{1,0},{2,1},{3,2},{4,7},{5,4},{6,5},{7,6},{8,11},{9,8},{10,9... | collective-permute-start | bytes 393224 | tf_op jit(solution)/shard_map/ppermute | solution.py:24
  (8 other events, 78.2 us)
Sparse Core Ops, SparseCore 0:
  10.5 37.5 all-gather.1
  99.0 40.7 reduce-scatter.1
